TPU v7x, 32 devices: a whole 2x2x4 slice. The times are simulated.
32 devices in a mesh: dp: 16 (over z, y, core), blk: 2 (over x).
Axes of the slice: x: 2, y: 2, z: 4, core: 2. Of those that a mesh axis runs over, the one named last changes fastest.
Arguments:
- frames: bfloat16 [8192, 768], P(('dp', 'blk')), may hold values from -6 to 6
- cotangent: bfloat16 [8192, 768], P(('dp', 'blk')), may hold values from -6 to 6
- seq_lengths: int32 [16, 4], P('dp'), may hold values from 32 to 257, as said below
- key_mask: int32 [8192], P(('dp', 'blk')), may hold values 0 or 1
- qkv_weight: bfloat16 [768, 2304], P(None, ('dp', 'blk')), may hold values from -0.21875 to 0.21875
- query_value_bias: bfloat16 [1536], P(('dp', 'blk')), may hold values from -3 to 3
- out_weight: bfloat16 [768, 768], P(None, ('dp', 'blk')), may hold values from -0.875 to 0.875
- out_bias: bfloat16 [768], P(('dp', 'blk')), may hold values from -3 to 3
- up_weight: bfloat16 [768, 3072], P(None, ('dp', 'blk')), may hold values from -0.21875 to 0.21875
- up_bias: bfloat16 [3072], P(('dp', 'blk')), may hold values from -3 to 3
- down_weight: bfloat16 [3072, 768], P(None, ('dp', 'blk')), may hold values from -0.109375 to 0.109375
- down_bias: bfloat16 [768], P(('dp', 'blk')), may hold values from -3 to 3
- first_gain: bfloat16 [768], P(('dp', 'blk')), may hold values from 0.5 to 1.5
- first_shift: bfloat16 [768], P(('dp', 'blk')), may hold values from -3 to 3
- second_gain: bfloat16 [768], P(('dp', 'blk')), may hold values from 0.5 to 1.5
- second_shift: bfloat16 [768], P(('dp', 'blk')), may hold values from -3 to 3
- rel_bias: bfloat16 [321, 12], replicated, may hold values from -4 to 4
Outputs:
- layer_out: float32 [8192, 768], P(('dp', 'blk'))
- frames_grad: float32 [8192, 768], P(('dp', 'blk'))
- qkv_weight_grad: float32 [768, 2304], P(None, ('dp', 'blk'))
- query_value_bias_grad: float32 [1536], P(('dp', 'blk'))
- out_weight_grad: float32 [768, 768], P(None, ('dp', 'blk'))
- out_bias_grad: float32 [768], P(('dp', 'blk'))
- up_weight_grad: float32 [768, 3072], P(None, ('dp', 'blk'))
- up_bias_grad: float32 [3072], P(('dp', 'blk'))
- down_weight_grad: float32 [3072, 768], P(None, ('dp', 'blk'))
- down_bias_grad: float32 [768], P(('dp', 'blk'))
- first_gain_grad: float32 [768], P(('dp', 'blk'))
- first_shift_grad: float32 [768], P(('dp', 'blk'))
- second_gain_grad: float32 [768], P(('dp', 'blk'))
- second_shift_grad: float32 [768], P(('dp', 'blk'))
- rel_bias_grad: float32 [321, 12], replicated
Inputs may be any that keep to these rules, and one draw needn't show every extreme that they name: `seq_lengths`: in each row, the 4 lengths sum to 256 * 2; each row holds one sequence of exactly the largest length.
All inputs are finite; a program needn't handle non-finite values. No bound on the sum of `key_mask` on one device may be relied on, other than what follows from the above.
Results may differ from a plain program's by a relative error of at most 0.014.
Values may be sent and summed in bfloat16 or wider, within the bound.
No kernel may reach another device: no remote copies, remote signals or barrier semaphores. Data moves between devices by JAX's collectives and lax.ppermute only.
A program may use at most 192 MiB of HBM per device.

v0:
```python
import math

import jax
import jax.numpy as jnp
import numpy as np
from jax import lax
from jax.experimental import pallas as pl
from jax.experimental.pallas import tpu as pltpu
from jax.sharding import PartitionSpec as P

H = 12
HD = 64
MAXREL = 160
BLOCK = 256
BUCKETS = 321


EPSILON = 1e-05
MASKED = -2e30
START_PEAK = -1e30
HIGHEST = lax.Precision.HIGHEST


def from_behind(block, axis, distance):
    devices = range(lax.axis_size(axis))
    route = [((i - distance) % len(devices), i) for i in devices]
    return lax.ppermute(block, axis, route)


def layer_norm(values, gain_vec, shift_vec):
    center = values - jnp.mean(values, axis=-1, keepdims=True)
    inv_std = lax.rsqrt(jnp.mean(center * center, axis=-1, keepdims=True) + EPSILON)
    normed = center * inv_std
    return (normed * gain_vec + shift_vec, normed, inv_std)


def norm_back(gradient, normed, inv_std, gain_vec):
    scaled = gradient * gain_vec
    inner = (
        scaled
        - jnp.mean(scaled, axis=-1, keepdims=True)
        - normed * jnp.mean(scaled * normed, axis=-1, keepdims=True)
    )
    return (inner * inv_std, jnp.sum(gradient * normed, axis=0), jnp.sum(gradient, axis=0))


def gelu_parts(values):
    normal_cdf = 0.5 * (1.0 + lax.erf(values * 0.7071067811865476))
    density = jnp.exp(-0.5 * values * values) * 0.3989422804014327
    return (values * normal_cdf, normal_cdf + values * density)


def doc_numbers(seq_ends, positions):
    return jnp.sum((positions[:, None] >= seq_ends[None, :]).astype(jnp.int32), axis=1)


def pair_logits(
    query_block, key_block, query_pos, key_pos, query_doc, key_doc, key_live, table_heads
):
    block_len = query_block.shape[0]
    raw = jnp.einsum(
        "qhd,khd->hqk",
        query_block.reshape(block_len, H, HD),
        key_block.reshape(-1, H, HD),
        preferred_element_type=jnp.float32,
    )
    relative = jnp.clip(key_pos[None, :] - query_pos[:, None], -MAXREL, MAXREL) + MAXREL
    bias = jnp.take(table_heads, relative, axis=1)
    allowed = (query_doc[:, None] == key_doc[None, :]) & (
        (key_live[None, :] > 0.5) | (query_pos[:, None] == key_pos[None, :])
    )
    return jnp.where(allowed[None], raw * (1.0 / math.sqrt(HD)) + bias, MASKED)


def diagonal_sums(gradient, offset):
    heads, block_len, _ = gradient.shape
    flipped = gradient[:, ::-1, :]
    padded = jnp.pad(flipped, ((0, 0), (0, 0), (0, block_len)))
    sheared = padded.reshape(heads, 2 * block_len * block_len)[:, : block_len * (2 * block_len - 1)]
    sheared = sheared.reshape(heads, block_len, 2 * block_len - 1)
    diag_sums = jnp.sum(sheared, axis=1)
    distance = offset + jnp.arange(2 * block_len - 1, dtype=jnp.int32) - (block_len - 1)
    bucket = jnp.clip(distance, -MAXREL, MAXREL) + MAXREL
    onehot = (bucket[:, None] == jnp.arange(BUCKETS, dtype=jnp.int32)[None, :]).astype(jnp.float32)
    return jnp.dot(diag_sums, onehot, precision=HIGHEST)


def body(
    frames,
    cotangent,
    seq_lengths,
    key_mask,
    qkv_weight,
    query_value_bias,
    out_weight,
    out_bias,
    up_weight,
    up_bias,
    down_weight,
    down_bias,
    first_gain,
    first_shift,
    second_gain,
    second_shift,
    rel_bias,
):
    cycle_size = lax.axis_size("blk")
    cycle_place = lax.axis_index("blk")
    shard_len = frames.shape[0]
    width = frames.shape[1]
    block_count = shard_len // BLOCK
    score_scale = 1.0 / math.sqrt(HD)
    seq_ends = jnp.cumsum(seq_lengths[0])
    local_pos = jnp.arange(shard_len, dtype=jnp.int32)
    positions = cycle_place * shard_len + local_pos
    own_docs = doc_numbers(seq_ends, positions)
    table_heads = rel_bias.astype(jnp.float32).T

    def blocked(array):
        return array.reshape((block_count, BLOCK) + array.shape[1:])

    def key_meta(turn):
        source = (cycle_place - turn) % cycle_size
        key_pos = source * shard_len + local_pos
        return (key_pos, doc_numbers(seq_ends, key_pos))

    gathered = (
        lax.all_gather(qkv_weight, ("dp", "blk"), axis=1, tiled=True),
        lax.all_gather(query_value_bias, ("dp", "blk"), axis=0, tiled=True),
        lax.all_gather(out_weight, ("dp", "blk"), axis=1, tiled=True),
        lax.all_gather(out_bias, ("dp", "blk"), axis=0, tiled=True),
        lax.all_gather(up_weight, ("dp", "blk"), axis=1, tiled=True),
        lax.all_gather(up_bias, ("dp", "blk"), axis=0, tiled=True),
        lax.all_gather(down_weight, ("dp", "blk"), axis=1, tiled=True),
        lax.all_gather(down_bias, ("dp", "blk"), axis=0, tiled=True),
        lax.all_gather(first_gain, ("dp", "blk"), axis=0, tiled=True),
        lax.all_gather(first_shift, ("dp", "blk"), axis=0, tiled=True),
        lax.all_gather(second_gain, ("dp", "blk"), axis=0, tiled=True),
        lax.all_gather(second_shift, ("dp", "blk"), axis=0, tiled=True),
    )
    (
        qkv_full,
        qv_bias_full,
        out_full,
        out_bias_full,
        up_full,
        up_bias_full,
        down_full,
        down_bias_full,
        gain_one,
        shift_one,
        gain_two,
        shift_two,
    ) = gathered
    frames_wide = frames.astype(jnp.float32)
    first_out, first_normed, first_inv = layer_norm(
        frames_wide, gain_one.astype(jnp.float32), shift_one.astype(jnp.float32)
    )
    first_low = first_out.astype(jnp.bfloat16)
    projected = jnp.dot(first_low, qkv_full, preferred_element_type=jnp.float32)
    bias_vec = qv_bias_full.astype(jnp.float32)
    queries = (projected[:, :width] + bias_vec[:width]).astype(jnp.bfloat16)
    key_rows = projected[:, width : 2 * width].astype(jnp.bfloat16)
    value_rows = (projected[:, 2 * width :] + bias_vec[width:]).astype(jnp.bfloat16)
    live_rows = key_mask.astype(jnp.bfloat16)
    query_blocks = (blocked(queries), blocked(positions), blocked(own_docs))

    def forward_hop(turn, online_state, key_part, value_part, live_part):
        key_pos, key_doc = key_meta(turn)
        key_items = (
            blocked(key_part),
            blocked(value_part),
            blocked(key_pos),
            blocked(key_doc),
            blocked(live_part),
        )

        def forward_per_query(query_items):
            query_block, query_pos, query_doc, row_peak, row_total, accum = query_items

            def online(carried, key_block_items):
                row_peak, row_total, accum = carried
                key_block, value_block, key_bpos, key_bdoc, key_blive = key_block_items
                logits = pair_logits(
                    query_block,
                    key_block,
                    query_pos,
                    key_bpos,
                    query_doc,
                    key_bdoc,
                    key_blive,
                    table_heads,
                )
                new_peak = jnp.maximum(row_peak, jnp.max(logits, axis=2))
                decay = jnp.exp(row_peak - new_peak)
                weights = jnp.exp(logits - new_peak[:, :, None])
                row_total = row_total * decay + jnp.sum(weights, axis=2)
                accum = accum * decay.T[:, :, None] + jnp.einsum(
                    "hqk,khd->qhd",
                    weights.astype(jnp.bfloat16),
                    value_block.reshape(-1, H, HD),
                    preferred_element_type=jnp.float32,
                )
                return ((new_peak, row_total, accum), None)

            result, unused = lax.scan(online, (row_peak, row_total, accum), key_items)
            return result

        return lax.map(forward_per_query, query_blocks + online_state)

    def cycle_turn(turn, carried):
        online_state, key_part, value_part, live_part = carried
        online_state = forward_hop(turn, online_state, key_part, value_part, live_part)
        key_part, value_part, live_part = from_behind((key_part, value_part, live_part), "blk", 1)
        return (online_state, key_part, value_part, live_part)

    start_state = (
        jnp.full((block_count, H, BLOCK), START_PEAK, jnp.float32),
        jnp.zeros((block_count, H, BLOCK), jnp.float32),
        jnp.zeros((block_count, BLOCK, H, HD), jnp.float32),
    )
    carried = lax.fori_loop(
        0, cycle_size - 1, cycle_turn, (start_state, key_rows, value_rows, live_rows)
    )
    row_peak, row_total, accum = forward_hop(
        cycle_size - 1, carried[0], carried[1], carried[2], carried[3]
    )
    mixed = accum / jnp.transpose(row_total, (0, 2, 1))[:, :, :, None]
    mixed_flat = mixed.reshape(shard_len, width)
    context = mixed_flat.astype(jnp.bfloat16)
    branch = jnp.dot(context, out_full, preferred_element_type=jnp.float32) + out_bias_full.astype(
        jnp.float32
    )
    middle = frames_wide + branch
    second_out, second_normed, second_inv = layer_norm(
        middle, gain_two.astype(jnp.float32), shift_two.astype(jnp.float32)
    )
    second_low = second_out.astype(jnp.bfloat16)
    hidden = jnp.dot(second_low, up_full, preferred_element_type=jnp.float32) + up_bias_full.astype(
        jnp.float32
    )
    active, slope = gelu_parts(hidden)
    active_low = active.astype(jnp.bfloat16)
    layer_out = (
        middle
        + jnp.dot(active_low, down_full, preferred_element_type=jnp.float32)
        + down_bias_full.astype(jnp.float32)
    )
    weights_back = (
        lax.all_gather(qkv_weight, ("dp", "blk"), axis=1, tiled=True),
        lax.all_gather(query_value_bias, ("dp", "blk"), axis=0, tiled=True),
        lax.all_gather(out_weight, ("dp", "blk"), axis=1, tiled=True),
        lax.all_gather(out_bias, ("dp", "blk"), axis=0, tiled=True),
        lax.all_gather(up_weight, ("dp", "blk"), axis=1, tiled=True),
        lax.all_gather(up_bias, ("dp", "blk"), axis=0, tiled=True),
        lax.all_gather(down_weight, ("dp", "blk"), axis=1, tiled=True),
        lax.all_gather(down_bias, ("dp", "blk"), axis=0, tiled=True),
        lax.all_gather(first_gain, ("dp", "blk"), axis=0, tiled=True),
        lax.all_gather(first_shift, ("dp", "blk"), axis=0, tiled=True),
        lax.all_gather(second_gain, ("dp", "blk"), axis=0, tiled=True),
        lax.all_gather(second_shift, ("dp", "blk"), axis=0, tiled=True),
    )
    qkv_back = weights_back[0]
    out_back = weights_back[2]
    up_back = weights_back[4]
    down_back = weights_back[6]
    gain_one_back = weights_back[8].astype(jnp.float32)
    gain_two_back = weights_back[10].astype(jnp.float32)
    grad_wide = cotangent.astype(jnp.float32)
    down_grad = jnp.einsum("tf,td->fd", active_low, cotangent, preferred_element_type=jnp.float32)
    down_bias_grad = jnp.sum(grad_wide, axis=0)
    active_grad = jnp.einsum("td,fd->tf", cotangent, down_back, preferred_element_type=jnp.float32)
    hidden_low = (active_grad * slope).astype(jnp.bfloat16)
    up_grad = jnp.einsum("td,tf->df", second_low, hidden_low, preferred_element_type=jnp.float32)
    up_bias_grad = jnp.sum(hidden_low.astype(jnp.float32), axis=0)
    second_grad = jnp.einsum("tf,df->td", hidden_low, up_back, preferred_element_type=jnp.float32)
    middle_norm, gain_two_grad, shift_two_grad = norm_back(
        second_grad, second_normed, second_inv, gain_two_back
    )
    middle_grad = grad_wide + middle_norm
    branch_low = middle_grad.astype(jnp.bfloat16)
    out_grad = jnp.einsum("td,te->de", context, branch_low, preferred_element_type=jnp.float32)
    out_bias_grad = jnp.sum(branch_low.astype(jnp.float32), axis=0)
    context_low = jnp.einsum(
        "te,de->td", branch_low, out_back, preferred_element_type=jnp.float32
    ).astype(jnp.bfloat16)
    delta = jnp.sum(
        (context_low.astype(jnp.float32) * mixed_flat).reshape(shard_len, H, HD), axis=2
    )
    delta_blocks = jnp.transpose(blocked(delta), (0, 2, 1))
    query_back = (
        blocked(queries),
        blocked(context_low),
        blocked(positions),
        blocked(own_docs),
        row_peak,
        row_total,
        delta_blocks,
    )

    def backward_hop(
        turn, query_grad, table_grad, key_part, value_part, live_part, key_grad, value_grad
    ):
        key_pos, key_doc = key_meta(turn)

        def per_key(carried, key_block_items):
            query_grad, table_grad = carried
            key_block, value_block, key_bpos, key_bdoc, key_blive, key_bgrad, value_bgrad = (
                key_block_items
            )
            key_heads = key_block.reshape(-1, H, HD)
            value_heads = value_block.reshape(-1, H, HD)

            def per_per_query(inner, query_items):
                key_bgrad, value_bgrad, table_grad = inner
                (
                    query_block,
                    dout_block,
                    query_pos,
                    query_doc,
                    peak_block,
                    total_block,
                    delta_block,
                ) = query_items
                logits = pair_logits(
                    query_block,
                    key_block,
                    query_pos,
                    key_bpos,
                    query_doc,
                    key_bdoc,
                    key_blive,
                    table_heads,
                )
                attn_prob = jnp.exp(logits - peak_block[:, :, None]) / total_block[:, :, None]
                dout_heads = dout_block.reshape(-1, H, HD)
                prob_grad = jnp.einsum(
                    "qhd,khd->hqk", dout_heads, value_heads, preferred_element_type=jnp.float32
                )
                logit_grad = attn_prob * (prob_grad - delta_block[:, :, None])
                raw_low = (logit_grad * score_scale).astype(jnp.bfloat16)
                query_part = jnp.einsum(
                    "hqk,khd->qhd", raw_low, key_heads, preferred_element_type=jnp.float32
                ).reshape(-1, width)
                key_bgrad = key_bgrad + jnp.einsum(
                    "hqk,qhd->khd",
                    raw_low,
                    query_block.reshape(-1, H, HD),
                    preferred_element_type=jnp.float32,
                ).reshape(-1, width)
                value_bgrad = value_bgrad + jnp.einsum(
                    "hqk,qhd->khd",
                    attn_prob.astype(jnp.bfloat16),
                    dout_heads,
                    preferred_element_type=jnp.float32,
                ).reshape(-1, width)
                table_grad = table_grad + diagonal_sums(logit_grad, key_bpos[0] - query_pos[0])
                return ((key_bgrad, value_bgrad, table_grad), query_part)

            (key_bgrad, value_bgrad, table_grad), query_parts = lax.scan(
                per_per_query, (key_bgrad, value_bgrad, table_grad), query_back
            )
            return ((query_grad + query_parts, table_grad), (key_bgrad, value_bgrad))

        (query_grad, table_grad), (key_new, value_new) = lax.scan(
            per_key,
            (query_grad, table_grad),
            (
                blocked(key_part),
                blocked(value_part),
                blocked(key_pos),
                blocked(key_doc),
                blocked(live_part),
                blocked(key_grad),
                blocked(value_grad),
            ),
        )
        return (
            query_grad,
            table_grad,
            key_new.reshape(shard_len, width),
            value_new.reshape(shard_len, width),
        )

    def pass_grads(key_grad, value_grad):
        return (
            from_behind(key_grad.astype(jnp.bfloat16), "blk", 1).astype(key_grad.dtype),
            from_behind(value_grad.astype(jnp.bfloat16), "blk", 1).astype(value_grad.dtype),
        )

    def back_turn(turn, carried):
        query_grad, table_grad, key_part, value_part, live_part, key_grad, value_grad = carried
        query_grad, table_grad, key_grad, value_grad = backward_hop(
            turn, query_grad, table_grad, key_part, value_part, live_part, key_grad, value_grad
        )
        key_part, value_part, live_part = from_behind((key_part, value_part, live_part), "blk", 1)
        key_grad, value_grad = pass_grads(key_grad, value_grad)
        return (query_grad, table_grad, key_part, value_part, live_part, key_grad, value_grad)

    zero_rows = jnp.zeros((shard_len, width), jnp.float32)
    back_start = (
        jnp.zeros((block_count, BLOCK, width), jnp.float32),
        jnp.zeros((H, BUCKETS), jnp.float32),
        key_rows,
        value_rows,
        live_rows,
        zero_rows,
        zero_rows,
    )
    carried = lax.fori_loop(0, cycle_size - 1, back_turn, back_start)
    query_grad, table_grad, key_grad, value_grad = backward_hop(
        cycle_size - 1,
        carried[0],
        carried[1],
        carried[2],
        carried[3],
        carried[4],
        carried[5],
        carried[6],
    )
    key_grad, value_grad = pass_grads(key_grad, value_grad)
    query_low = query_grad.reshape(shard_len, width).astype(jnp.bfloat16)
    key_low = key_grad.astype(jnp.bfloat16)
    value_low = value_grad.astype(jnp.bfloat16)
    qkv_low = jnp.concatenate([query_low, key_low, value_low], axis=1)
    qkv_grad = jnp.einsum("td,te->de", first_low, qkv_low, preferred_element_type=jnp.float32)
    query_value_grad = jnp.concatenate(
        [
            jnp.sum(query_low.astype(jnp.float32), axis=0),
            jnp.sum(value_low.astype(jnp.float32), axis=0),
        ]
    )
    first_grad = jnp.einsum("te,de->td", qkv_low, qkv_back, preferred_element_type=jnp.float32)
    frames_norm, gain_one_grad, shift_one_grad = norm_back(
        first_grad, first_normed, first_inv, gain_one_back
    )
    frames_grad = middle_grad + frames_norm
    summed = (
        lax.psum_scatter(qkv_grad, ("dp", "blk"), scatter_dimension=1, tiled=True),
        lax.psum_scatter(query_value_grad, ("dp", "blk"), scatter_dimension=0, tiled=True),
        lax.psum_scatter(out_grad, ("dp", "blk"), scatter_dimension=1, tiled=True),
        lax.psum_scatter(out_bias_grad, ("dp", "blk"), scatter_dimension=0, tiled=True),
        lax.psum_scatter(up_grad, ("dp", "blk"), scatter_dimension=1, tiled=True),
        lax.psum_scatter(up_bias_grad, ("dp", "blk"), scatter_dimension=0, tiled=True),
        lax.psum_scatter(down_grad, ("dp", "blk"), scatter_dimension=1, tiled=True),
        lax.psum_scatter(down_bias_grad, ("dp", "blk"), scatter_dimension=0, tiled=True),
        lax.psum_scatter(gain_one_grad, ("dp", "blk"), scatter_dimension=0, tiled=True),
        lax.psum_scatter(shift_one_grad, ("dp", "blk"), scatter_dimension=0, tiled=True),
        lax.psum_scatter(gain_two_grad, ("dp", "blk"), scatter_dimension=0, tiled=True),
        lax.psum_scatter(shift_two_grad, ("dp", "blk"), scatter_dimension=0, tiled=True),
    )
    table_sum = lax.psum(table_grad, ("dp", "blk"))
    return (
        layer_out,
        frames_grad,
        summed[0],
        summed[1],
        summed[2],
        summed[3],
        summed[4],
        summed[5],
        summed[6],
        summed[7],
        summed[8],
        summed[9],
        summed[10],
        summed[11],
        table_sum.T,
    )


AXES = ("dp", "blk")
F32 = jnp.float32
LOW = jnp.bfloat16
LANES = 128
NARROW = 6
PAD = 8


def route(move):
    n_dp, n_blk = lax.axis_size("dp"), lax.axis_size("blk")
    pairs = []
    for d in range(n_dp):
        d_bits, b_bits = move[d % 2]
        for b in range(n_blk):
            pairs.append((d * n_blk + b, (d ^ d_bits) * n_blk + (b ^ b_bits)))
    return pairs


def shift(array, move, name="swap"):
    with jax.named_scope(name):
        return lax.ppermute(array, AXES, route(move))


CORE = ((1, 0), (1, 0))
SIDE = ((0, 1), (2, 0))
OTHER_SIDE = ((2, 0), (0, 1))
PACK = ((0, 1), (0, 1))
ALONG_Z = tuple(((4 * turn, 0), (4 * turn, 0)) for turn in (1, 2, 3))


def tied(value, *after):
    return lax.optimization_barrier((value,) + after)[0]


def joined(*groups):
    return lax.optimization_barrier(groups)


def twin(array, name="twin"):
    return shift(array, CORE, name)


def along_z(unit, name):
    return tuple(shift(unit, move, name + "_z") for move in ALONG_Z)


def z_sends(plane, name):
    low = plane.astype(LOW)
    return tuple(shift(low[n + 1], move, name + "_z") for n, move in enumerate(ALONG_Z))


def z_sum(plane, arrived):
    return plane[0] + sum(part.astype(F32) for part in arrived)


def unit_of(place, x_turn, y_turn, z_turn, c):
    x, y, z = place[0] ^ x_turn, place[1] ^ y_turn, place[2] ^ z_turn
    return ((z * 2 + y) * 2 + c) * 2 + x


def planes_of(place):
    c0 = place[3]
    found = []
    for plane in range(2):
        c = c0 if plane == 0 else 1 - c0
        for z in range(4):
            for n, (x_turn, y_turn) in enumerate(((0, 0), (1 - c, c), (c, 1 - c), (1, 1))):
                found.append((4 * plane + n, z, unit_of(place, x_turn, y_turn, z, c)))
    return found


def load_units(place, pieces, stage, sems):
    copies = [
        pltpu.make_async_copy(pieces[array].at[z], stage.at[unit], sems.at[n])
        for n, (array, z, unit) in enumerate(planes_of(place))
    ]
    for copy in copies:
        copy.start()
    return copies


def take_columns(place, array, pair, taken, top):
    for c in range(2):

        @pl.when(place[3] == c)
        def _():
            taken[top : top + array.shape[0], :] = jnp.concatenate(
                [
                    array[:, (2 * n + c) * pair : (2 * n + c + 1) * pair]
                    for n in range(array.shape[1] // (2 * pair))
                ],
                axis=1,
            )


def give_units(place, stage, parts):
    c = place[3]
    for part, (x_turn, y_turn) in zip(parts, ((0, 0), (1 - c, c), (c, 1 - c), (1, 1))):
        for turn in range(4):
            unit = ((place[2] ^ turn) * 2 + (place[1] ^ y_turn)) * 2 + (place[0] ^ x_turn)
            if isinstance(part, tuple):
                part[turn // 2][turn % 2] = stage[unit].astype(LOW)
            else:
                part[turn] = stage[unit].astype(LOW)


def part_shapes(rows, width):
    return [jax.ShapeDtypeStruct((4, rows, width), LOW)] * 4


def dot_nn(a, b):
    return lax.dot_general(a, b, (((1,), (0,)), ((), ())), preferred_element_type=F32)


def dot_nt(a, b):
    return lax.dot_general(a, b, (((1,), (1,)), ((), ())), preferred_element_type=F32)


def dot_tn(a, b):
    return lax.dot_general(a, b, (((0,), (0,)), ((), ())), preferred_element_type=F32)


HBM = pl.BlockSpec(memory_space=pltpu.HBM)
SMEM = pl.BlockSpec(memory_space=pltpu.SMEM)
VMEM = pl.BlockSpec(memory_space=pltpu.VMEM)


def call(kernel, in_specs, outs, out_specs, scratch, args, flops, limit=56, **kwargs):
    moved = sum(math.prod(a.shape) * a.dtype.itemsize for a in list(args) + list(outs))
    return pl.pallas_call(
        kernel,
        out_shape=outs,
        in_specs=in_specs,
        out_specs=out_specs,
        scratch_shapes=scratch,
        compiler_params=pltpu.CompilerParams(vmem_limit_bytes=limit * 1024 * 1024),
        cost_estimate=pl.CostEstimate(flops=flops, bytes_accessed=moved, transcendentals=0),
        **kwargs,
    )(*args)


def spread_tables(units, width):
    tables = []
    for n in (width // units, 2 * width // units, 4 * width // units):
        lane = np.arange(units * n)
        keep = lane[None, :] // n == np.arange(units)[:, None]
        pick = lane[None, :] % n == np.arange(LANES)[:, None]
        tables.append(jnp.asarray(np.concatenate([keep, pick]), LOW))
    return tables


def project_kernel(
    place, own, other, p0, p1, p2, p3, p4, p5, p6, p7, wide_one, wide_two, wide_four,
    first, queries, keys, values, weight, vectors, up_bias, mate_live, stage, small, sems,
):
    units = stage.shape[0]
    width = own.shape[1]
    rows = stage.shape[1] - PAD
    shard_len = own.shape[0]
    copies = load_units(place, (p0, p1, p2, p3, p4, p5, p6, p7), stage, sems)

    def normed(frames):
        wide = frames.astype(F32)
        center = wide - jnp.mean(wide, axis=1, keepdims=True)
        return center * lax.rsqrt(jnp.mean(center * center, axis=1, keepdims=True) + EPSILON)

    own_normed, mate_normed = normed(own[...]), normed(other[...])
    for copy in copies:
        copy.wait()
    for unit in range(units):
        top = stage[unit, rows : rows + PAD, :].astype(F32)
        small[0, unit : unit + 1, :] = top[0:1]
        small[1, unit : unit + 1, :] = top[1:2]

    mate = unit_of(place, 1, 0, 0, place[3])
    mate_live[...] = stage[mate, rows : rows + PAD, : mate_live.shape[1]].astype(F32)

    def spread(row, slot, table):
        held = small[row, :, slot * LANES : (slot + 1) * LANES].astype(LOW)
        laid = dot_nn(held, table[units:, :]) * table[:units, :].astype(F32)
        return jnp.sum(laid, axis=0, keepdims=True)

    for n in range(NARROW):
        vectors[n : n + 1, :] = spread(0, n, wide_one)
    qv_bias = spread(1, 0, wide_two)
    up_bias[...] = jnp.broadcast_to(spread(1, 1, wide_four), up_bias.shape)
    vectors[NARROW : NARROW + 1, :] = qv_bias[:, :width]
    vectors[NARROW + 1 : NARROW + 2, :] = qv_bias[:, width:]

    def join(pair, _):
        both = jnp.concatenate(
            [stage[2 * pair, :rows, :].astype(F32), stage[2 * pair + 1, :rows, :].astype(F32)], axis=0
        )
        weight[pl.ds(pl.multiple_of(2 * rows * pair, 2 * rows), 2 * rows), :] = both.astype(LOW)
        return 0

    lax.fori_loop(0, units // 2, join, 0)
    gain, offset = vectors[0:1, :], vectors[1:2, :]
    x = place[0]
    own_at = pl.multiple_of(x * shard_len, shard_len)
    mate_at = pl.multiple_of((1 - x) * shard_len, shard_len)
    first[pl.ds(own_at, shard_len), :] = (own_normed * gain + offset).astype(LOW)
    first[pl.ds(mate_at, shard_len), :] = (mate_normed * gain + offset).astype(LOW)
    mine = first[pl.ds(own_at, shard_len), :]
    queries[...] = (dot_nt(mine, weight[:width, :]) + vectors[NARROW : NARROW + 1, :]).astype(LOW)
    keys[...] = dot_nt(first[...], weight[width : 2 * width, :]).astype(LOW)
    values[...] = (
        dot_nt(first[...], weight[2 * width :, :]) + vectors[NARROW + 1 : NARROW + 2, :]
    ).astype(LOW)


def half_mask(shape, head):
    return (lax.broadcasted_iota(jnp.int32, shape, 1) // HD) == head


def attend_kernel(
    place, lengths, queries, keys, values, curve, own_live, mate_live, probs, mixed, hidden_pairs
):
    q, k, v = queries[...], keys[...], values[...]
    block_len, span = hidden_pairs.shape
    step = pl.program_id(0)

    @pl.when(step == 0)
    def _():
        start = place[0] * block_len
        key_pos = lax.broadcasted_iota(jnp.int32, (1, span), 1)
        query_pos = lax.broadcasted_iota(jnp.int32, (block_len, 1), 0) + start
        key_doc, query_doc = jnp.zeros_like(key_pos), jnp.zeros_like(query_pos)
        end = 0
        for n in range(lengths.shape[1]):
            end = end + lengths[0, n]
            key_doc = key_doc + (key_pos >= end).astype(jnp.int32)
            query_doc = query_doc + (query_pos >= end).astype(jnp.int32)
        one, two = own_live[...].astype(F32), mate_live[2:3, :]
        live = jnp.where(
            place[0] == 0, jnp.concatenate([one, two], axis=1), jnp.concatenate([two, one], axis=1)
        )
        allowed = (query_doc == key_doc) & ((live > 0.5) | (query_pos == key_pos))
        hidden_pairs[...] = jnp.where(allowed, 0.0, MASKED)

    total = jnp.zeros(q.shape, F32)
    for head in range(2):
        q_head = jnp.where(half_mask(q.shape, head), q, 0) * (1.0 / math.sqrt(HD))
        bias = pltpu.roll(
            jnp.broadcast_to(curve[pl.ds(2 * step + head, 1), :], (block_len, block_len + span)),
            span + 1, 1, stride=1, stride_axis=0,
        )[:, :span]
        logits = dot_nt(q_head.astype(LOW), k) + bias + hidden_pairs[...]
        weights = jnp.exp(logits - jnp.max(logits, axis=1, keepdims=True))
        prob = (weights * (1.0 / jnp.sum(weights, axis=1, keepdims=True))).astype(LOW)
        probs[head] = prob
        total = total + dot_nn(prob, jnp.where(half_mask(v.shape, head), v, 0))
    mixed[...] = total


def load_mixed(place, pieces, up, kept, sems, kept_sems):
    rows = pieces[0].shape[1] - kept.shape[1]
    first, later = [], []
    for n, (array, z, unit) in enumerate(planes_of(place)):
        ref = pieces[array].at[z]
        at = pl.multiple_of(unit * rows, rows)
        first.append(pltpu.make_async_copy(ref.at[rows:], kept.at[unit], kept_sems.at[n]))
        later.append(pltpu.make_async_copy(ref.at[:rows], up.at[pl.ds(at, rows)], sems.at[n]))
    for copy in first + later:
        copy.start()
    return first, later


def join_units(kept, out):
    units = kept.shape[0]
    each = out.shape[0] // units

    def join(pair, _):
        both = jnp.concatenate(
            [kept[2 * pair].astype(F32)[:each], kept[2 * pair + 1].astype(F32)[:each]], axis=0
        )
        out[pl.ds(pl.multiple_of(2 * each * pair, 2 * each), 2 * each), :] = both.astype(LOW)
        return 0

    lax.fori_loop(0, units // 2, join, 0)


def expand_kernel(
    place, frames, mixed, vectors, up_bias, p0, p1, p2, p3, p4, p5, p6, p7,
    middle, second, context, active, slope, up, kept, out, sems, kept_sems,
):
    width = frames.shape[1]
    first, later = load_mixed(place, (p0, p1, p2, p3, p4, p5, p6, p7), up, kept, sems, kept_sems)
    context[...] = mixed[...].astype(LOW)
    for copy in first:
        copy.wait()
    join_units(kept, out)
    mid = frames[...].astype(F32) + (dot_nt(context[...], out[...]) + vectors[4:5, :])
    middle[...] = mid
    center = mid - jnp.mean(mid, axis=1, keepdims=True)
    normed = center * lax.rsqrt(jnp.mean(center * center, axis=1, keepdims=True) + EPSILON)
    second[...] = (normed * vectors[2:3, :] + vectors[3:4, :]).astype(LOW)
    for copy in later:
        copy.wait()
    for n in range(up.shape[0] // width):
        at = slice(n * width, (n + 1) * width)
        hidden = dot_nt(second[...], up[at, :]) + up_bias[0:1, at]
        cdf = 0.5 * (1.0 + lax.erf(hidden * 0.7071067811865476))
        density = jnp.exp(-0.5 * hidden * hidden) * 0.3989422804014327
        active[:, at] = (hidden * cdf).astype(LOW)
        slope[:, at] = cdf + hidden * density


def down_grad_kernel(
    place, active, active_twin, cotangent, cotangent_twin, o0, o1, o2, o3, bias_grad, taken, wide,
):
    units, rows, width = wide.shape
    each = width // (2 * units)
    bias_grad[...] = jnp.broadcast_to(
        jnp.sum(cotangent[...].astype(F32), axis=0, keepdims=True), bias_grad.shape
    )

    shard_len = cotangent.shape[0]
    take_columns(place, cotangent, 2 * each, taken, 0)
    take_columns(place, cotangent_twin, 2 * each, taken, shard_len)
    dy, dy_twin = taken[:shard_len, :], taken[shard_len:, :]
    for fold in range(rows // each):
        at = slice(fold * width, (fold + 1) * width)
        grad = dot_tn(dy, active[:, at]) + dot_tn(dy_twin, active_twin[:, at])
        for unit in range(units):
            wide[unit, fold * each : (fold + 1) * each, :] = grad[unit * each : (unit + 1) * each]
    give_units(place, wide, (o0, o1, o2, o3))


def unfold_units(stage, down):
    units, rows, width = stage.shape
    each = down.shape[0] // units

    def unfold(pair, _):
        one, two = stage[2 * pair].astype(F32), stage[2 * pair + 1].astype(F32)
        at = pl.multiple_of(2 * each * pair, 2 * each)
        for fold in range(rows // each):
            both = jnp.concatenate(
                [one[fold * each : (fold + 1) * each], two[fold * each : (fold + 1) * each]], axis=0
            )
            down[pl.ds(at, 2 * each), fold * width : (fold + 1) * width] = both.astype(LOW)
        return 0

    lax.fori_loop(0, units // 2, unfold, 0)


def back_kernel(
    place, cotangent, slope, middle, vectors, p0, p1, p2, p3, p4, p5, p6, p7, u0, u1, u2, u3, u4, u5, u6, u7,
    middle_grad, context_grad, vector_grads, branch_grad, up_bias_grad, hidden_grad,
    stage, down, up, kept, out, stage_sems, sems, kept_sems,
):
    width = cotangent.shape[1]
    down_copies = load_units(place, (p0, p1, p2, p3, p4, p5, p6, p7), stage, stage_sems)
    kept_copies, up_copies = load_mixed(
        place, (u0, u1, u2, u3, u4, u5, u6, u7), up, kept, sems, kept_sems
    )
    for copy in down_copies:
        copy.wait()
    unfold_units(stage, down)
    dy = cotangent[...]
    for n in range(hidden_grad.shape[1] // width):
        at = slice(n * width, (n + 1) * width)
        grad = (dot_nn(dy, down[:, at]) * slope[:, at]).astype(LOW)
        hidden_grad[:, at] = grad
        up_bias_grad[:, at] = jnp.broadcast_to(
            jnp.sum(grad.astype(F32), axis=0, keepdims=True), (up_bias_grad.shape[0], width)
        )
    for copy in kept_copies:
        copy.wait()
    join_units(kept, out)
    for copy in up_copies:
        copy.wait()
    second_grad = dot_nn(hidden_grad[...], up[...])
    mid = middle[...]
    center = mid - jnp.mean(mid, axis=1, keepdims=True)
    inv_std = lax.rsqrt(jnp.mean(center * center, axis=1, keepdims=True) + EPSILON)
    normed = center * inv_std
    scaled = second_grad * vectors[2:3, :]
    inner = (
        scaled
        - jnp.mean(scaled, axis=1, keepdims=True)
        - normed * jnp.mean(scaled * normed, axis=1, keepdims=True)
    )
    mid_grad = cotangent[...].astype(F32) + inner * inv_std
    middle_grad[...] = mid_grad
    branch = mid_grad.astype(LOW)
    vector_grads[...] = jnp.concatenate(
        [
            jnp.sum(second_grad * normed, axis=0, keepdims=True),
            jnp.sum(second_grad, axis=0, keepdims=True),
            jnp.sum(branch.astype(F32), axis=0, keepdims=True),
            jnp.zeros((5, width), F32),
        ],
        axis=0,
    )
    branch_grad[...] = branch
    context_grad[...] = dot_nn(branch, out[...]).astype(LOW)


def up_grad_kernel(
    place, hidden, hidden_twin, second, second_twin, branch, branch_twin, context, context_twin,
    o0, o1, o2, o3, o4, taken, taken_branch, stage,
):
    units, rows, width = stage.shape
    each = width // (2 * units)
    up_rows = hidden.shape[1] // (2 * units)

    shard_len = second.shape[0]
    take_columns(place, branch, 2 * each, taken_branch, 0)
    take_columns(place, branch_twin, 2 * each, taken_branch, shard_len)
    take_columns(place, hidden, 2 * up_rows, taken, 0)
    take_columns(place, hidden_twin, 2 * up_rows, taken, shard_len)
    out_grad = dot_tn(taken_branch[:shard_len, :], context[...]) + dot_tn(
        taken_branch[shard_len:, :], context_twin[...]
    )
    blank = jnp.zeros((rows - up_rows - each, width), F32)
    quarter = units // 4
    for z in range(4):
        at = slice(z * quarter * up_rows, (z + 1) * quarter * up_rows)
        grad = dot_tn(taken[:shard_len, at], second[...]) + dot_tn(taken[shard_len:, at], second_twin[...])
        for n in range(quarter):
            unit = z * quarter + n
            stage[unit] = jnp.concatenate(
                [
                    grad[n * up_rows : (n + 1) * up_rows],
                    out_grad[unit * each : (unit + 1) * each],
                    blank,
                ],
                axis=0,
            ).astype(LOW)
    give_units(place, stage, (o0, o1, (o2, o3), o4))


def rows_left(each):
    return -each % 16


def finish_kernel(
    place, active, middle, vectors, p0, p1, p2, p3, p4, p5, p6, p7, layer_out, stage, down, sems
):
    copies = load_units(place, (p0, p1, p2, p3, p4, p5, p6, p7), stage, sems)
    for copy in copies:
        copy.wait()
    unfold_units(stage, down)
    layer_out[...] = middle[...] + dot_nt(active[...], down[...]) + vectors[5:6, :]


def attend_back_kernel(
    place, queries, keys, values, context_grad, mixed, probs, grads, diagonals
):
    q, k, v, dout = queries[...], keys[...], values[...], context_grad[...]
    block_len, span = probs.shape[1:]
    weighted = dout.astype(F32) * mixed[...]
    row = lax.broadcasted_iota(jnp.int32, (block_len, block_len), 0)
    lane = lax.broadcasted_iota(jnp.int32, (block_len, block_len), 1)
    turn = (row + lane == block_len - 1).astype(LOW)
    blank = jnp.zeros((block_len, block_len), F32)
    dq, dk, dv = jnp.zeros(q.shape, F32), jnp.zeros(k.shape, F32), jnp.zeros(v.shape, F32)
    for head in range(2):
        mine = half_mask(q.shape, head)
        dout_head = jnp.where(mine, dout, 0)
        delta = jnp.sum(jnp.where(mine, weighted, 0.0), axis=1, keepdims=True)
        prob = probs[head]
        grad = prob.astype(F32) * (dot_nt(dout_head, v) - delta)
        raw = (grad * (1.0 / math.sqrt(HD))).astype(LOW)
        dq = dq + dot_nn(raw, jnp.where(half_mask(k.shape, head), k, 0))
        dk = dk + dot_tn(raw, jnp.where(mine, q, 0))
        dv = dv + dot_tn(prob, dout_head)
        turned = jnp.concatenate([dot_nn(turn, raw), blank], axis=1)
        sheared = pltpu.roll(turned, 0, 1, stride=1, stride_axis=0)
        diagonals[pl.ds(2 * pl.program_id(0) + head, 1), :] = jnp.sum(sheared, axis=0, keepdims=True) * math.sqrt(HD)
    own_at = pl.multiple_of(place[0] * block_len, block_len)
    grads[0] = jnp.zeros(k.shape, LOW)
    grads[0, pl.ds(own_at, block_len), :] = dq.astype(LOW)
    grads[1] = dk.astype(LOW)
    grads[2] = dv.astype(LOW)


def total(array):
    return jnp.sum(array, axis=0, keepdims=True)


def norm_parts(frames):
    wide = frames.astype(F32)
    center = wide - jnp.mean(wide, axis=1, keepdims=True)
    inv_std = lax.rsqrt(jnp.mean(center * center, axis=1, keepdims=True) + EPSILON)
    return center * inv_std, inv_std


def first_grad_kernel(
    place, own_frames, mate_frames, grads, weight_in, diagonals, vector_grads, down_bias_grad, up_bias_grad,
    own_grad, mate_grad, small, weight, sems,
):
    copy = pltpu.make_async_copy(weight_in, weight, sems.at[0])
    copy.start()
    shard_len, width = own_frames.shape
    x = place[0]
    own_at = pl.multiple_of(x * shard_len, shard_len)
    mate_at = pl.multiple_of((1 - x) * shard_len, shard_len)
    own_normed, _ = norm_parts(own_frames[...])
    mate_normed, _ = norm_parts(mate_frames[...])
    dq = grads[0, pl.ds(own_at, shard_len), :]
    small[4:5, :] = vector_grads[2:3, :]
    small[2:4, :] = vector_grads[0:2, :]
    small[5:6, :] = down_bias_grad[0:1, :]
    small[6:7, :] = total(dq.astype(F32))
    small[7:8, :] = total(grads[2].astype(F32))
    for n in range(up_bias_grad.shape[1] // width):
        small[8 + n : 9 + n, :] = up_bias_grad[0:1, n * width : (n + 1) * width]
    small[12:, :] = diagonals[...]
    copy.wait()

    def from_keys(at):
        return dot_nn(grads[1, pl.ds(at, shard_len), :], weight[width : 2 * width, :]) + dot_nn(
            grads[2, pl.ds(at, shard_len), :], weight[2 * width :, :]
        )

    of_own = from_keys(own_at) + dot_nn(dq, weight[:width, :])
    of_mate = from_keys(mate_at)
    own_grad[...] = of_own
    mate_grad[...] = of_mate
    small[0:1, :] = total(of_own * own_normed) + total(of_mate * mate_normed)
    small[1:2, :] = total(of_own) + total(of_mate)


def qkv_grad_kernel(
    place, grads, grads_twin, first, first_twin, small_own, small_twin, wide_one, wide_two, wide_four,
    o0, o1, o2, o3, taken, sums, small, stage,
):
    units, full, width = stage.shape
    rows = full - PAD
    span = first.shape[0]
    shard_len = span // 2
    x = place[0]
    summed = small_own[...] + small_twin[...]

    def fold(vector, table):
        kept = (vector * table[: 2 * units, :].astype(F32)).astype(LOW)
        return dot_nt(kept, table[2 * units :, :])

    for n in range(NARROW):
        small[0, :, n * LANES : (n + 1) * LANES] = fold(summed[n : n + 1, :], wide_one)
    small[1, :, :] = jnp.zeros((2 * units, width), F32)
    both = jnp.concatenate([summed[6:7, :], summed[7:8, :]], axis=1)
    small[1, :, :LANES] = fold(both, wide_two)
    four = jnp.concatenate([summed[8 + n : 9 + n, :] for n in range(4)], axis=1)
    small[1, :, LANES : 2 * LANES] = fold(four, wide_four)
    lanes = 3 * LANES
    distance = (
        lax.broadcasted_iota(jnp.int32, (shard_len + span, lanes), 0) - (shard_len - 1) - x * shard_len
    )
    bucket = jnp.clip(distance, -MAXREL, MAXREL) + MAXREL
    here = (bucket == lax.broadcasted_iota(jnp.int32, (shard_len + span, lanes), 1)).astype(F32).astype(LOW)
    diagonals = summed[12:, :]
    high = diagonals.astype(LOW)
    table = dot_nn(high, here) + dot_nn((diagonals - high.astype(F32)).astype(LOW), here)
    table = jnp.concatenate([table[: H // 2], table[H // 2 :]], axis=1)
    for n, array in enumerate((grads, grads_twin)):
        columns = jnp.concatenate([array[part] for part in range(3)], axis=1)
        take_columns(place, columns, 2 * rows, taken, n * span)
    sums[...] = dot_tn(taken[:span, :], first[...]) + dot_tn(taken[span:, :], first_twin[...])
    for unit in range(units):
        at = 4 * (unit // 2) + 2 * place[3] + unit % 2
        stage[unit] = jnp.concatenate(
            [
                sums[unit * rows : (unit + 1) * rows, :],
                small[0, pl.ds(at, 1), :],
                small[1, pl.ds(at, 1), :],
                table,
            ],
            axis=0,
        ).astype(LOW)
    give_units(place, stage, (o0, o1, o2, o3))


def input_grad_kernel(frames, mate_frames, own_grad, mate_grad, middle_grad, vectors, own_part, mate_part):
    def through_norm(of_frames, grad):
        normed, inv_std = norm_parts(of_frames)
        scaled = grad * vectors[0:1, :]
        inner = (
            scaled
            - jnp.mean(scaled, axis=1, keepdims=True)
            - normed * jnp.mean(scaled * normed, axis=1, keepdims=True)
        )
        return inner * inv_std

    own_part[...] = middle_grad[...] + through_norm(frames[...], own_grad[...])
    mate_part[...] = through_norm(mate_frames[...], mate_grad[...]).astype(LOW)


def last_kernel(
    own, z1, z2, z3, own_part, mate_part, qkv, qv_bias, up_bias, table, frames_grad, n0, n1, n2, n3, n4, n5
):
    frames_grad[...] = own_part[...] + mate_part[...].astype(F32)
    rows = qkv.shape[0]
    total = own[...] + z1[...].astype(F32) + z2[...].astype(F32) + z3[...].astype(F32)
    qkv[...] = total[:rows]
    for n, narrow in enumerate((n0, n1, n2, n3, n4, n5)):
        narrow[...] = total[rows : rows + 1, n * LANES : n * LANES + narrow.shape[1]]
    qv_bias[...] = total[rows + 1 : rows + 2, : qv_bias.shape[1]]
    up_bias[...] = total[rows + 1 : rows + 2, LANES : LANES + up_bias.shape[1]]
    for half in range(2):
        at = 3 * LANES * half
        table[half * (H // 2) : (half + 1) * (H // 2), :] = total[rows + 2 : rows + PAD, at : at + BUCKETS]


def pack_kernel(
    live, qkv, out, up, down, first_gain, first_shift, second_gain, second_shift, out_bias,
    down_bias, qv_bias, up_bias, qkv_unit, up_unit, down_unit,
):
    each, width = out.shape

    def slots(vectors):
        parts = []
        for vector in vectors:
            wide = vector[...].astype(F32)
            parts += [wide, jnp.zeros((1, LANES - wide.shape[1]), F32)]
        left = width - LANES * len(vectors)
        if left:
            parts.append(jnp.zeros((1, left), F32))
        return jnp.concatenate(parts, axis=1)

    narrow = slots((first_gain, first_shift, second_gain, second_shift, out_bias, down_bias))
    wide = slots((qv_bias, up_bias))
    seen = live[...].astype(F32)
    seen = jnp.concatenate([seen, jnp.zeros((1, width - seen.shape[1]), F32)], axis=1)
    blank = jnp.zeros((PAD - 3, width), F32)
    qkv_unit[...] = jnp.concatenate([qkv[...].astype(F32), narrow, wide, seen, blank], axis=0).astype(LOW)
    blank = jnp.zeros((up_unit.shape[0] - up.shape[0] - each, width), F32)
    up_unit[...] = jnp.concatenate(
        [up[...].astype(F32), out[...].astype(F32), blank], axis=0
    ).astype(LOW)
    down_unit[...] = jnp.concatenate(
        [
            down[:, fold * width : (fold + 1) * width].astype(F32)
            for fold in range(down.shape[1] // width)
        ],
        axis=0,
    ).astype(LOW)


def paired_body(
    frames, cotangent, seq_lengths, key_mask, qkv_weight, query_value_bias, out_weight, out_bias,
    up_weight, up_bias, down_weight, down_bias, first_gain, first_shift, second_gain, second_shift,
    rel_bias,
):
    shard_len, width = frames.shape
    x = lax.axis_index("blk")
    d = lax.axis_index("dp")
    core = d % 2
    units = lax.axis_size("dp") * lax.axis_size("blk")
    span = shard_len * lax.axis_size("blk")
    place = jnp.stack([x, (d // 2) % 2, d // 4, core]).astype(jnp.int32)
    each = width // units
    ff = up_weight.shape[1] * units
    qkv_rows, up_rows = qkv_weight.shape[1], up_weight.shape[1]
    folds = ff // width
    down_rows = each * folds
    out_rows = each + rows_left(each)

    def shape(*dims, kind=LOW):
        return jax.ShapeDtypeStruct(dims, kind)

    def row(vector):
        return vector.reshape(1, vector.shape[0])

    packed = (
        row(key_mask), qkv_weight.T, out_weight.T, up_weight.T, down_weight.T, row(first_gain),
        row(first_shift), row(second_gain), row(second_shift), row(out_bias), row(down_bias),
        row(query_value_bias), row(up_bias),
    )
    qkv_unit, up_unit, down_unit = call(
        pack_kernel,
        [VMEM] * len(packed),
        [shape(qkv_rows + PAD, width), shape(up_rows + out_rows, width), shape(down_rows, width)],
        [VMEM] * 3,
        [],
        packed,
        0,
        name="pack",
    )
    def twins(pieces):
        return tuple(pieces) + tuple(twin(piece) for piece in pieces)

    cotangent_twin = twin(cotangent)
    qkv_z = along_z(qkv_unit, "qkv")
    mate_frames = shift(tied(frames, qkv_unit), PACK, "frames_pack")
    qkv_z, mate_frames = joined(qkv_z, mate_frames)
    qkv_own = jnp.stack((qkv_unit,) + qkv_z)
    qkv_side = shift(qkv_own, SIDE, "qkv_1")
    up_first = tied(up_unit, *qkv_z)
    up_z = [shift(up_first, move, "up_z") for move in ALONG_Z[:2]]
    qkv_side, up_z, cotangent_twin = joined(qkv_side, up_z, cotangent_twin)
    qkv_other = shift(qkv_own, OTHER_SIDE, "qkv_2")
    qkv_across = shift(qkv_side, OTHER_SIDE, "qkv_3")
    up_z.append(shift(tied(up_unit, qkv_side), ALONG_Z[2], "up_z"))
    up_z, qkv_other, qkv_across = joined(up_z, qkv_other, qkv_across)
    qkv_pieces = twins((qkv_own, qkv_side, qkv_other, qkv_across))
    up_own = jnp.stack([up_unit] + up_z)
    up_side = shift(up_own, SIDE, "up_1")
    down_first = tied(down_unit, up_own)
    down_z = [shift(down_first, move, "down_z") for move in ALONG_Z[:2]]

    distance = jnp.arange(span + shard_len, dtype=jnp.int32) - (shard_len - 1) - x * shard_len
    bucket = jnp.clip(distance, -MAXREL, MAXREL) + MAXREL
    bucket_lanes = 3 * LANES
    buckets = (bucket[:, None] == jnp.arange(bucket_lanes, dtype=jnp.int32)[None, :]).astype(LOW)
    curve = lax.dot_general(
        rel_bias, buckets[:, :BUCKETS], (((0,), (1,)), ((), ())), preferred_element_type=F32
    )
    spreads = spread_tables(units, width)
    unit_sems = pltpu.SemaphoreType.DMA((units,))
    first, queries, keys, values, weight, vectors, up_bias_all, mate_live = call(
        project_kernel,
        [SMEM, VMEM, VMEM] + [HBM] * 8 + [VMEM] * 3,
        [
            shape(span, width), shape(shard_len, width), shape(span, width), shape(span, width),
            shape(3 * width, width), shape(8, width, kind=F32), shape(8, ff, kind=F32),
            shape(PAD, shard_len, kind=F32),
        ],
        [VMEM] * 8,
        [
            pltpu.VMEM((units, qkv_rows + PAD, width), LOW), pltpu.VMEM((2, units, width), F32), unit_sems,
        ],
        (tied(place, up_own), frames, mate_frames) + qkv_pieces + tuple(spreads),
        2 * shard_len * width * 5 * width,
        name="project",
    )
    up_side, keys, down_z = joined(up_side, keys, down_z)
    up_other = shift(up_own, OTHER_SIDE, "up_2")
    up_across = shift(up_side, OTHER_SIDE, "up_3")
    down_z.append(shift(tied(down_unit, keys), ALONG_Z[2], "down_z"))
    pairs = H // 2
    pair_lanes = 2 * HD

    def lanes_of(rows):
        return pl.BlockSpec((rows, pair_lanes), lambda n: (0, n))

    def heads_of(*dims):
        return pl.BlockSpec(dims, lambda n: (n,) + (0,) * (len(dims) - 1))

    def whole(*dims):
        return pl.BlockSpec(dims, lambda n: (0,) * len(dims))

    probs, mixed = call(
        attend_kernel,
        [
            SMEM, SMEM, lanes_of(shard_len), lanes_of(span), lanes_of(span), whole(H, span + shard_len),
            whole(1, shard_len), whole(PAD, shard_len),
        ],
        [shape(H, shard_len, span), shape(shard_len, width, kind=F32)],
        [heads_of(2, shard_len, span), lanes_of(shard_len)],
        [pltpu.VMEM((shard_len, span), F32)],
        (
            tied(place, up_side), seq_lengths, queries, keys, values, curve, row(key_mask), mate_live,
        ),
        8 * shard_len * span * width,
        grid=(pairs,),
        name="attend",
    )
    up_other, up_across, mixed, down_z = joined(up_other, up_across, mixed, down_z)
    up_pieces = twins((up_own, up_side, up_other, up_across))
    down_own = jnp.stack([down_unit] + down_z)
    down_side = shift(down_own, SIDE, "down_1")
    down_other = shift(down_own, OTHER_SIDE, "down_2")
    middle, second, context, active, slope = call(
        expand_kernel,
        [SMEM] + [VMEM] * 4 + [HBM] * 8,
        [
            shape(shard_len, width, kind=F32), shape(shard_len, width), shape(shard_len, width),
            shape(shard_len, ff), shape(shard_len, ff, kind=F32),
        ],
        [VMEM] * 5,
        [
            pltpu.VMEM((ff, width), LOW), pltpu.VMEM((units, out_rows, width), LOW),
            pltpu.VMEM((width, width), LOW), unit_sems, unit_sems,
        ],
        (tied(place, down_own), frames, mixed, vectors, up_bias_all) + up_pieces,
        2 * shard_len * width * (width + ff),
        name="expand",
    )
    down_side, down_other, active = joined(down_side, down_other, active)
    down_across = shift(down_side, OTHER_SIDE, "down_3")
    active_twin, context_twin, second_twin = twin(active), twin(context), twin(second)
    first_twin = twin(first)
    down_parts = call(
        down_grad_kernel,
        [SMEM] + [VMEM] * 4,
        part_shapes(down_rows, width) + [shape(8, width, kind=F32)],
        [VMEM] * 5,
        [
            pltpu.VMEM((span, width // 2), LOW), pltpu.VMEM((units // 2, down_rows, width), F32),
        ],
        (tied(place, down_side), active, active_twin, cotangent, cotangent_twin),
        2 * shard_len * width * ff,
        name="down_grad", limit=24,
    )
    down_across, down_parts = joined(down_across, down_parts)
    down_bias_grad = down_parts[4]
    down_pieces = twins((down_own, down_side, down_other, down_across))
    turned = shift(down_parts[3], OTHER_SIDE, "rs_down_3")
    down_two = shift(down_parts[2], OTHER_SIDE, "rs_down_2")
    middle_grad, context_grad, vector_grads, branch_grad, up_bias_grad, hidden_grad = call(
        back_kernel,
        [SMEM] + [VMEM] * 4 + [HBM] * 16,
        [
            shape(shard_len, width, kind=F32), shape(shard_len, width), shape(8, width, kind=F32),
            shape(shard_len, width), shape(8, ff, kind=F32), shape(shard_len, ff),
        ],
        [VMEM] * 6,
        [
            pltpu.VMEM((units, down_rows, width), LOW), pltpu.VMEM((width, ff), LOW),
            pltpu.VMEM((ff, width), LOW), pltpu.VMEM((units, out_rows, width), LOW),
            pltpu.VMEM((width, width), LOW), unit_sems, unit_sems, unit_sems,
        ],
        (tied(place, down_parts[0]), cotangent, slope, middle, vectors) + down_pieces + up_pieces,
        2 * shard_len * width * (2 * ff + width),
        name="back",
    )
    turned, down_two, hidden_grad, context_twin, second_twin, first_twin = joined(
        turned, down_two, hidden_grad, context_twin, second_twin, first_twin
    )
    side = (down_parts[1].astype(F32) + turned.astype(F32)).astype(LOW)
    down_one = shift(side, SIDE, "rs_down_1")
    hidden_twin = twin(hidden_grad)
    branch_twin = twin(branch_grad)
    down_sum = down_parts[0].astype(F32) + down_two.astype(F32)
    up_parts = call(
        up_grad_kernel,
        [SMEM] + [VMEM] * 8,
        [shape(n, up_rows + out_rows, width) for n in (4, 4, 2, 2, 4)],
        [VMEM] * 5,
        [
            pltpu.VMEM((span, ff // 2), LOW), pltpu.VMEM((span, width // 2), LOW),
            pltpu.VMEM((units // 2, up_rows + out_rows, width), LOW),
        ],
        (
            tied(place, down_sum, side), hidden_grad, hidden_twin, second, second_twin, branch_grad, branch_twin,
            context, context_twin,
        ),
        2 * shard_len * width * (ff + width),
        name="up_grad", limit=28,
    )
    down_one, up_parts = joined(down_one, up_parts)
    turned = shift(up_parts[4], OTHER_SIDE, "rs_up_3")
    up_two = shift(up_parts[2], OTHER_SIDE, "rs_up_2a")
    down_sum = down_sum + down_one.astype(F32)
    down_low = down_sum.astype(LOW)
    down_z = [shift(down_low[n + 1], ALONG_Z[n], "rs_down_z") for n in range(2)]
    grads, diagonals = call(
        attend_back_kernel,
        [
            SMEM, lanes_of(shard_len), lanes_of(span), lanes_of(span), lanes_of(shard_len), lanes_of(shard_len),
            heads_of(2, shard_len, span),
        ],
        [shape(3, span, width), shape(H, span + shard_len, kind=F32)],
        [pl.BlockSpec((3, span, pair_lanes), lambda n: (0, 0, n)), whole(H, span + shard_len)],
        [],
        (place, queries, keys, values, tied(context_grad, up_parts[0]), mixed, probs),
        16 * shard_len * span * width,
        grid=(pairs,),
        name="attend_back", limit=24,
    )
    turned, up_two, down_z, grads = joined(turned, up_two, down_z, grads)
    up_rest = shift(up_parts[3], OTHER_SIDE, "rs_up_2b")
    grads_twin = twin(grads)
    side = (up_parts[1].astype(F32) + turned.astype(F32)).astype(LOW)
    up_one = shift(side, SIDE, "rs_up_1")
    own_grad, mate_grad, small = call(
        first_grad_kernel,
        [SMEM] + [VMEM] * 3 + [HBM] + [VMEM] * 4,
        [
            shape(shard_len, width, kind=F32), shape(shard_len, width, kind=F32),
            shape(12 + H, width, kind=F32),
        ],
        [VMEM] * 3,
        [pltpu.VMEM((3 * width, width), LOW), pltpu.SemaphoreType.DMA((1,))],
        (
            tied(place, side), frames, mate_frames, grads, weight, diagonals, vector_grads,
            down_bias_grad, up_bias_grad,
        ),
        2 * shard_len * width * 5 * width,
        name="first_grad", limit=24,
    )
    grads_twin, small = joined(grads_twin, small)
    down_z.append(shift(tied(down_low[3], small), ALONG_Z[2], "rs_down_z"))
    small_twin = twin(small)
    qkv_parts = call(
        qkv_grad_kernel,
        [SMEM] + [VMEM] * 9,
        part_shapes(qkv_rows + PAD, width),
        [VMEM] * 4,
        [
            pltpu.VMEM((2 * span, 3 * width // 2), LOW), pltpu.VMEM((3 * width // 2, width), F32),
            pltpu.VMEM((2, units, width), F32), pltpu.VMEM((units // 2, qkv_rows + PAD, width), LOW),
        ],
        (place, grads, grads_twin, first, first_twin, small, small_twin) + tuple(spreads),
        2 * shard_len * width * 6 * width,
        name="qkv_grad", limit=28,
    )
    up_one, up_rest, down_z, qkv_parts = joined(up_one, up_rest, down_z, qkv_parts)
    turned = shift(qkv_parts[3], OTHER_SIDE, "rs_qkv_3")
    qkv_two = shift(qkv_parts[2], OTHER_SIDE, "rs_qkv_2")
    up_sum = [
        up_parts[0][n].astype(F32) + up_one[n].astype(F32) + (up_two, up_rest)[n // 2][n % 2].astype(F32)
        for n in range(4)
    ]
    up_low = [part.astype(LOW) for part in up_sum]
    up_z = [shift(up_low[n + 1], ALONG_Z[n], "rs_up_z") for n in range(2)]
    down_sum = z_sum(down_sum, down_z)
    own_part, mate_part = call(
        input_grad_kernel,
        [VMEM] * 6,
        [shape(shard_len, width, kind=F32), shape(shard_len, width)],
        [VMEM] * 2,
        [],
        (frames, mate_frames, own_grad, tied(mate_grad, *up_low), middle_grad, vectors),
        0,
        name="input_grad", limit=12,
    )
    turned, mate_part = joined(turned, mate_part)
    side = (qkv_parts[1].astype(F32) + turned.astype(F32)).astype(LOW)
    qkv_one = shift(side, SIDE, "rs_qkv_1")
    up_z, side_after = joined(up_z, side)
    up_z.append(shift(tied(up_low[3], side_after), ALONG_Z[2], "rs_up_z"))
    layer_out = call(
        finish_kernel,
        [SMEM] + [VMEM] * 3 + [HBM] * 8,
        [shape(shard_len, width, kind=F32)],
        [VMEM],
        [pltpu.VMEM((units, down_rows, width), LOW), pltpu.VMEM((width, ff), LOW), unit_sems],
        (tied(place, side_after), active, middle, vectors) + down_pieces,
        2 * shard_len * width * ff,
        name="finish",
    )[0]
    qkv_one, qkv_two, up_z, layer_out = joined(qkv_one, qkv_two, up_z, layer_out)
    qkv_sum = qkv_parts[0].astype(F32) + qkv_one.astype(F32) + qkv_two.astype(F32)
    qkv_z = z_sends(qkv_sum, "rs_qkv")
    mate_part = shift(tied(mate_part, qkv_sum), PACK, "grad_pack")
    up_sum = z_sum(tied(up_sum[:1], qkv_sum), up_z)
    up_sum, qkv_z = joined(up_sum, qkv_z)
    last = call(
        last_kernel,
        [VMEM] * 6,
        [
            shape(qkv_rows, width, kind=F32), shape(1, 2 * each, kind=F32), shape(1, up_rows, kind=F32),
            shape(H, BUCKETS, kind=F32), shape(shard_len, width, kind=F32),
        ]
        + [shape(1, each, kind=F32)] * NARROW,
        [VMEM] * (5 + NARROW),
        [],
        (qkv_sum[0],) + tuple(qkv_z) + (own_part, mate_part),
        0,
        name="last", limit=8,
    )
    qkv_grad, qv_bias_grad, up_bias_sum, table, frames_grad = last[:5]
    pieces = [piece.reshape(each) for piece in last[5:]]

    down_grad = jnp.concatenate(
        [down_sum[fold * each : (fold + 1) * each] for fold in range(folds)], axis=1
    )
    return (
        layer_out, frames_grad, qkv_grad.T, qv_bias_grad.reshape(2 * each),
        up_sum[up_rows : up_rows + each].T, pieces[4], up_sum[:up_rows].T, up_bias_sum.reshape(up_rows),
        down_grad.T, pieces[5], pieces[0], pieces[1], pieces[2], pieces[3], table.T,
    )


def paired(mesh):
    return mesh.shape["blk"] == 2 and mesh.shape["dp"] == 16


def solution(mesh):
    placed = (
        P(("dp", "blk"), None),
        P(("dp", "blk"), None),
        P("dp", None),
        P(("dp", "blk")),
        P(None, ("dp", "blk")),
        P(("dp", "blk")),
        P(None, ("dp", "blk")),
        P(("dp", "blk")),
        P(None, ("dp", "blk")),
        P(("dp", "blk")),
        P(None, ("dp", "blk")),
        P(("dp", "blk")),
        P(("dp", "blk")),
        P(("dp", "blk")),
        P(("dp", "blk")),
        P(("dp", "blk")),
        P(),
    )
    return jax.shard_map(
        paired_body if paired(mesh) else body,
        mesh=mesh,
        in_specs=placed,
        out_specs=(
            P(("dp", "blk"), None),
            P(("dp", "blk"), None),
            P(None, ("dp", "blk")),
            P(("dp", "blk")),
            P(None, ("dp", "blk")),
            P(("dp", "blk")),
            P(None, ("dp", "blk")),
            P(("dp", "blk")),
            P(None, ("dp", "blk")),
            P(("dp", "blk")),
            P(("dp", "blk")),
            P(("dp", "blk")),
            P(("dp", "blk")),
            P(("dp", "blk")),
            P(),
        ),
        check_vma=False,
    )
```

profile of v0, /device:TPU:0, one launch (start us, length us, event | category | flops | bytes accessed | tf_op | source)
XLA Modules:
  0.0 205.2 jit_solution(3806088171017092176)
XLA Ops:
  0.7 2.0 pack.1
  2.7 2.9 %collective-permute-start.3 = (bf16[256,768]{1,0:T(8,128)(2,1)}, bf16[256,768]{1,0:T(8,128)(2,1)S(1)}, u32[]{:S(2)}, u32[]{:S(2)}) collective-permute-start(bf16[256,768]{1,0:T(8,128)(2,1)} %frames.3), channel_id=1, source_target_pairs={{0,1},{1,0},{2,3},{3,2},{4,5},{5,4},{6,7},{7,6},{8,9},{9,8},{10,11... | collective-permute-start | bytes 1179656 | tf_op jit(solution)/shard_map/frames_pack/ppermute | solution.py:492
  5.6 1.6 collective-permute-start
  7.2 2.6 %collective-permute-start.1 = (bf16[80,768]{1,0:T(8,128)(2,1)}, bf16[80,768]{1,0:T(8,128)(2,1)S(1)}, u32[]{:S(2)}, u32[]{:S(2)}) collective-permute-start(bf16[80,768]{1,0:T(8,128)(2,1)} %get-tuple-element.167), channel_id=1, source_target_pairs={{0,16},{1,17},{2,18},{3,19},{4,20},{5,21},{6,22},{7,23},{8,24},{9,... | collective-permute-start | bytes 368648 | tf_op jit(solution)/shard_map/qkv_z/ppermute | solution.py:492
  10.0 2.0 collective-permute-done
  12.0 7.4 %collective-permute-done.1 = bf16[80,768]{1,0:T(8,128)(2,1)S(1)} collective-permute-done((bf16[80,768]{1,0:T(8,128)(2,1)}, bf16[80,768]{1,0:T(8,128)(2,1)S(1)}, u32[]{:S(2)}, u32[]{:S(2)}) %collective-permute-start.1) | collective-permute-done | bytes 122912 | tf_op jit(solution)/shard_map/qkv_z/ppermute | solution.py:492
  19.4 1.1 pad_maximum_fusion.2.p0
  21.2 1.9 collective-permute-start.5
  23.1 1.2 collective-permute-start.6
  24.2 1.5 collective-permute-start.9
  25.7 7.2 %collective-permute-done.5 = bf16[128,768]{1,0:T(8,128)(2,1)S(1)} collective-permute-done((bf16[128,768]{1,0:T(8,128)(2,1)}, bf16[128,768]{1,0:T(8,128)(2,1)S(1)}, u32[]{:S(2)}, u32[]{:S(2)}) %collective-permute-start.5) | collective-permute-done | bytes 196640 | tf_op jit(solution)/shard_map/up_z/ppermute | solution.py:492
  32.9 2.5 %collective-permute-done.6 = bf16[128,768]{1,0:T(8,128)(2,1)S(1)} collective-permute-done((bf16[128,768]{1,0:T(8,128)(2,1)}, bf16[128,768]{1,0:T(8,128)(2,1)S(1)}, u32[]{:S(2)}, u32[]{:S(2)}) %collective-permute-start.6) | collective-permute-done | bytes 196640 | tf_op jit(solution)/shard_map/up_z/ppermute | solution.py:492
  35.5 1.5 collective-permute-start.10
  37.0 2.5 %collective-permute-start.8 = (bf16[128,768]{1,0:T(8,128)(2,1)}, bf16[128,768]{1,0:T(8,128)(2,1)S(1)}, u32[]{:S(2)}, u32[]{:S(2)}) collective-permute-start(bf16[128,768]{1,0:T(8,128)(2,1)} %get-tuple-element.176), channel_id=1, source_target_pairs={{0,24},{1,25},{2,26},{3,27},{4,28},{5,29},{6,30},{7,31},{8,16},{9,... | collective-permute-start | bytes 589832 | tf_op jit(solution)/shard_map/up_z/ppermute | solution.py:492
  39.4 5.3 %collective-permute-done.8 = bf16[128,768]{1,0:T(8,128)(2,1)S(1)} collective-permute-done((bf16[128,768]{1,0:T(8,128)(2,1)}, bf16[128,768]{1,0:T(8,128)(2,1)S(1)}, u32[]{:S(2)}, u32[]{:S(2)}) %collective-permute-start.8) | collective-permute-done | bytes 196640 | tf_op jit(solution)/shard_map/up_z/ppermute | solution.py:492
  44.8 1.0 pad_maximum_fusion.p0.u0
  45.8 1.6 collective-permute-start.12
  48.4 1.6 collective-permute-done.13.p4
  50.0 1.6 collective-permute-start.17
  51.7 1.4 collective-permute-start.18
  53.7 1.4 collective-permute-start.11
  55.0 9.0 %project.1 = (bf16[512,768]{1,0:T(8,128)(2,1)}, bf16[256,768]{1,0:T(8,128)(2,1)}, bf16[512,768]{1,0:T(8,128)(2,1)}, bf16[512,768]{1,0:T(8,128)(2,1)}, bf16[2304,...) custom-call(s32[4]{0:T(128)} %pad_add_fusion.place, bf16[256,768]{1,0:T(8,128)(2,1)} %frames.3, ...), custom_call_target="tpu_custom_call" | custom-call | flops 1509949440 | bytes 12861456 | tf_op jit(solution)/shard_map/project/pallas_call | solution.py:601
  64.8 1.9 collective-permute-start.20
  66.7 1.0 fusion.1.curve
  67.9 9.7 %attend.1 = (bf16[12,256,512]{2,1,0:T(8,128)(2,1)}, f32[256,768]{1,0:T(8,128)}) custom-call(s32[4]{0:T(128)} %pad_add_fusion.place, s32[1,4]{1,0:T(1,128)} %lengths.1, bf16[256,768]{1,0:T(8,128)(2,1)} %get-tuple-element.188.queries, bf16[512,768]{1,0:T(8,128)(2,1)} %get-tuple-element.189.keys, bf16[512,768]{1,0:T(8,128)(2,1)} %get-tuple-element.190.values, ...), custom_call_target="tpu_custom_call" | custom-call | flops 805306368 | bytes 5944352 | tf_op jit(solution)/shard_map/attend/pallas_call | solution.py:601
  79.1 1.5 collective-permute-start.21
  80.6 1.5 collective-permute-start.22
  83.6 9.9 %expand.1 = (f32[256,768]{1,0:T(8,128)}, bf16[256,768]{1,0:T(8,128)(2,1)}, bf16[256,768]{1,0:T(8,128)(2,1)}, bf16[256,3072]{1,0:T(8,128)(2,1)}, f32[256,3072]{1,0:T(8,128)}) custom-call(s32[4]{0:T(128)} %pad_add_fusion.place, bf16[256,768]{1,0:T(8,128)(2,1)} %frames.3, f32[256,768]{1,0:T(8,128)} %get-tuple-element.200.mixed, ...), custom_call_target="tpu_custom_call" | custom-call | flops 1509949440 | bytes 13885456 | tf_op jit(solution)/shard_map/expand/pallas_call | solution.py:601
  93.5 1.6 collective-permute-done.21.p1
  95.4 1.5 collective-permute-start.27
  97.4 1.4 collective-permute-done.28.active_twin
  98.7 1.4 copy-done.10
  100.2 2.9 %down_grad.1 = (bf16[4,96,768]{2,1,0:T(8,128)(2,1)S(1)}, bf16[4,96,768]{2,1,0:T(8,128)(2,1)S(1)}, bf16[4,96,768]{2,1,0:T(8,128)(2,1)S(1)}, bf16[4,96,768]{2,1,0:T(8,128)(2,1)S(1)}, f32[8,768]{1,0:T(8,128)S(1)}) custom-call(s32[4]{0:T(128)S(1)} %copy-done.21, bf16[256,3072]{1,0:T(8,128)(2,1)S(1)} %copy-done.10, ...), custom_call_target="tpu_custom_call" | custom-call | flops 1207959552 | bytes 6316048 | tf_op jit(solution)/shard_map/down_grad/pallas_call | solution.py:601
  103.1 2.4 %collective-permute-done.27.p3 = bf16[4,96,768]{2,1,0:T(8,128)(2,1)S(1)} collective-permute-done((bf16[4,96,768]{2,1,0:T(8,128)(2,1)}, bf16[4,96,768]{2,1,0:T(8,128)(2,1)S(1)}, u32[]{:S(2)}, u32[]{:S(2)}) %collective-permute-start.27) | collective-permute-done | bytes 589856 | tf_op jit(solution)/shard_map/down_3/ppermute | solution.py:492
  106.0 1.5 collective-permute-start.29
  109.1 12.8 %back.1 = (f32[256,768]{1,0:T(8,128)}, bf16[256,768]{1,0:T(8,128)(2,1)}, f32[8,768]{1,0:T(8,128)}, bf16[256,768]{1,0:T(8,128)(2,1)}, f32[8,3072]{1,0:T(8,128)}, /*index=5*/bf16[256,3072]{1,0:T(8,128)(2,1)}) custom-call(s32[4]{0:T(128)} %pad_add_fusion.place, bf16[256,768]{1,0:T(8,128)(2,1)} %cotangent.3, f32[256,3072]{1,0:T(8,128)} %get-tuple-element.220.slope, ...), custom_call_target="tpu_custom_call" | custom-call | flops 2717908992 | bytes 18628624 | tf_op jit(solution)/shard_map/back/pallas_call | solution.py:601
  122.4 1.2 add_convert_fusion.1
  123.6 1.5 collective-permute-start.38
  125.2 1.9 collective-permute-done.40.branch_twin
  128.1 3.6 %up_grad.1 = (bf16[4,128,768]{2,1,0:T(8,128)(2,1)S(1)}, bf16[4,128,768]{2,1,0:T(8,128)(2,1)S(1)}, bf16[2,128,768]{2,1,0:T(8,128)(2,1)S(1)}, bf16[2,128,768]{2,1,0:T(8,128)(2,1)S(1)}, bf16[4,128,768]{2,1,0:T(8,128)(2,1)S(1)}) custom-call(s32[4]{0:T(128)S(1)} %copy-done.22, bf16[256,3072]{1,0:T(8,128)(2,1)S(1)} %copy-done.24, ...), custom_call_target="tpu_custom_call" | custom-call | flops 1509949440 | bytes 8650768 | tf_op jit(solution)/shard_map/up_grad/pallas_call | solution.py:601
  131.7 1.9 collective-permute-done.38
  133.6 1.5 collective-permute-start.41
  136.4 2.0 collective-permute-start.44
  138.5 8.9 %attend_back.1 = (bf16[3,512,768]{2,1,0:T(8,128)(2,1)S(1)}, f32[12,768]{1,0:T(8,128)S(1)}) custom-call(s32[4]{0:T(128)S(1)} %copy-done.22, bf16[256,768]{1,0:T(8,128)(2,1)S(1)} %copy-done.17, bf16[512,768]{1,0:T(8,128)(2,1)S(1)} %copy-done.13, bf16[512,768]{1,0:T(8,128)(2,1)S(1)} %copy-done.14, bf16[256,768]{1,0:T(8,128)(2,1)S(1)} %copy-done.18, ...), custom_call_target="tpu_custom_call" | custom-call | flops 1610612736 | bytes 8687632 | tf_op jit(solution)/shard_map/attend_back/pallas_call | solution.py:601
  147.4 2.4 %collective-permute-done.42 = bf16[2,128,768]{2,1,0:T(8,128)(2,1)S(1)} collective-permute-done((bf16[2,128,768]{2,1,0:T(8,128)(2,1)S(1)}, bf16[2,128,768]{2,1,0:T(8,128)(2,1)S(1)}, u32[]{:S(2)}, u32[]{:S(2)}) %collective-permute-start.42) | collective-permute-done | bytes 393248 | tf_op jit(solution)/shard_map/rs_up_2a/ppermute | solution.py:492
  150.1 1.5 collective-permute-start.45
  151.6 1.5 collective-permute-start.46
  153.2 3.4 %first_grad.1 = (f32[256,768]{1,0:T(8,128)S(1)}, f32[256,768]{1,0:T(8,128)S(1)}, f32[24,768]{1,0:T(8,128)S(1)}) custom-call(s32[4]{0:T(128)S(1)} %copy-done.22, bf16[256,768]{1,0:T(8,128)(2,1)S(1)} %copy-done.2, bf16[256,768]{1,0:T(8,128)(2,1)S(1)} %copy-done.6, bf16[3,512,768]{2,1,0:T(8,128)(2,1)S(1)} %get-tuple-element.253.grads, ...), custom_call_target="tpu_custom_call" | custom-call | flops 1509949440 | bytes 8515600 | tf_op jit(solution)/shard_map/first_grad/pallas_call | solution.py:601
  156.6 1.5 collective-permute-start.48
  158.1 5.4 %qkv_grad.1 = (bf16[4,80,768]{2,1,0:T(8,128)(2,1)S(1)}, bf16[4,80,768]{2,1,0:T(8,128)(2,1)S(1)}, bf16[4,80,768]{2,1,0:T(8,128)(2,1)S(1)}, bf16[4,80,768]{2,1,0:T(8,128)(2,1)S(1)}) custom-call(s32[4]{0:T(128)S(1)} %copy-done.22, bf16[3,512,768]{2,1,0:T(8,128)(2,1)S(1)} %get-tuple-element.253.grads, ...), custom_call_target="tpu_custom_call" | custom-call | flops 1811939328 | bytes 10125328 | tf_op jit(solution)/shard_map/qkv_grad/pallas_call | solution.py:601
  163.7 2.7 %collective-permute-done.45 = bf16[4,128,768]{2,1,0:T(8,128)(2,1)S(1)} collective-permute-done((bf16[4,128,768]{2,1,0:T(8,128)(2,1)S(1)}, bf16[4,128,768]{2,1,0:T(8,128)(2,1)S(1)}, u32[]{:S(2)}, u32[]{:S(2)}) %collective-permute-start.45) | collective-permute-done | bytes 786464 | tf_op jit(solution)/shard_map/rs_up_1/ppermute | solution.py:492
  166.4 1.3 collective-permute-start.50
  168.7 1.9 collective-permute-start.54
  171.3 1.0 input_grad.1
  172.4 2.8 %collective-permute-done.50 = bf16[4,80,768]{2,1,0:T(8,128)(2,1)S(1)} collective-permute-done((bf16[4,80,768]{2,1,0:T(8,128)(2,1)S(1)}, bf16[4,80,768]{2,1,0:T(8,128)(2,1)S(1)}, u32[]{:S(2)}, u32[]{:S(2)}) %collective-permute-start.50) | collective-permute-done | bytes 491552 | tf_op jit(solution)/shard_map/rs_qkv_3/ppermute | solution.py:492
  175.4 1.5 collective-permute-start.51
  177.5 2.7 %collective-permute-done.54 = bf16[128,768]{1,0:T(8,128)(2,1)S(1)} collective-permute-done((bf16[128,768]{1,0:T(8,128)(2,1)S(1)}, bf16[128,768]{1,0:T(8,128)(2,1)S(1)}, u32[]{:S(2)}, u32[]{:S(2)}) %collective-permute-start.54) | collective-permute-done | bytes 196640 | tf_op jit(solution)/shard_map/rs_up_z/ppermute | solution.py:492
  180.2 1.5 collective-permute-start.55
  182.4 7.0 %finish.1 = f32[256,768]{1,0:T(8,128)} custom-call(s32[4]{0:T(128)} %pad_add_fusion.place, bf16[256,3072]{1,0:T(8,128)(2,1)} %get-tuple-element.208.active, f32[256,768]{1,0:T(8,128)} %get-tuple-element.221.middle, f32[8,768]{1,0:T(8,128)} %get-tuple-element.201.vectors, bf16[4,96,768]{2,1,0:T(8,128)(2,1)} %pad_maximum_fusion.1.p0, ...), custom_call_target="tpu_custom_call" | custom-call | flops 1207959552 | bytes 7888912 | tf_op jit(solution)/shard_map/finish/pallas_call | solution.py:601
  189.6 1.6 collective-permute-start.59
  191.3 2.3 %collective-permute-start.57 = (bf16[80,768]{1,0:T(8,128)(2,1)S(1)}, bf16[80,768]{1,0:T(8,128)(2,1)S(1)}, u32[]{:S(2)}, u32[]{:S(2)}) collective-permute-start(bf16[80,768]{1,0:T(8,128)(2,1)S(1)} %get-tuple-element.329), channel_id=1, source_target_pairs={{0,16},{1,17},{2,18},{3,19},{4,20},{5,21},{6,22},{7,23},{8,24},{9,... | collective-permute-start | bytes 368648 | tf_op jit(solution)/shard_map/rs_qkv_z/ppermute | solution.py:492
  193.6 2.1 %collective-permute-start.58 = (bf16[80,768]{1,0:T(8,128)(2,1)S(1)}, bf16[80,768]{1,0:T(8,128)(2,1)S(1)}, u32[]{:S(2)}, u32[]{:S(2)}) collective-permute-start(bf16[80,768]{1,0:T(8,128)(2,1)S(1)} %get-tuple-element.328), channel_id=1, source_target_pairs={{0,24},{1,25},{2,26},{3,27},{4,28},{5,29},{6,30},{7,31},{8,16},{9,... | collective-permute-start | bytes 368648 | tf_op jit(solution)/shard_map/rs_qkv_z/ppermute | solution.py:492
  196.4 6.1 %collective-permute-done.57.z2 = bf16[80,768]{1,0:T(8,128)(2,1)S(1)} collective-permute-done((bf16[80,768]{1,0:T(8,128)(2,1)S(1)}, bf16[80,768]{1,0:T(8,128)(2,1)S(1)}, u32[]{:S(2)}, u32[]{:S(2)}) %collective-permute-start.57) | collective-permute-done | bytes 122912 | tf_op jit(solution)/shard_map/rs_qkv_z/ppermute | solution.py:492
  204.0 1.1 last.1
  (172 shorter events, 18.1 us)
Async XLA Ops:
  0.7 66.1 %copy-start = (bf16[321,12]{0,1:T(8,128)(2,1)S(1)}, bf16[321,12]{0,1:T(8,128)(2,1)}, u32[]{:S(2)}) copy-start(bf16[321,12]{0,1:T(8,128)(2,1)} %param.36) | copy-start | bytes 23116
  2.7 16.8 %collective-permute-start.3 = (bf16[256,768]{1,0:T(8,128)(2,1)}, bf16[256,768]{1,0:T(8,128)(2,1)S(1)}, u32[]{:S(2)}, u32[]{:S(2)}) collective-permute-start(bf16[256,768]{1,0:T(8,128)(2,1)} %frames.3), channel_id=1, source_target_pairs={{0,1},{1,0},{2,3},{3,2},{4,5},{5,4},{6,7},{7,6},{8,9},{9,8},{10,11... | collective-permute-start | bytes 1179656 | tf_op jit(solution)/shard_map/frames_pack/ppermute | solution.py:492
  5.6 6.4 %collective-permute-start = (bf16[80,768]{1,0:T(8,128)(2,1)}, bf16[80,768]{1,0:T(8,128)(2,1)S(1)}, u32[]{:S(2)}, u32[]{:S(2)}) collective-permute-start(bf16[80,768]{1,0:T(8,128)(2,1)} %get-tuple-element.167), channel_id=1, source_target_pairs={{0,8},{1,9},{2,10},{3,11},{4,12},{5,13},{6,14},{7,15},{8,0},{9,1},... | collective-permute-start | bytes 368648 | tf_op jit(solution)/shard_map/qkv_z/ppermute | solution.py:492
  7.2 12.3 %collective-permute-start.1 = (bf16[80,768]{1,0:T(8,128)(2,1)}, bf16[80,768]{1,0:T(8,128)(2,1)S(1)}, u32[]{:S(2)}, u32[]{:S(2)}) collective-permute-start(bf16[80,768]{1,0:T(8,128)(2,1)} %get-tuple-element.167), channel_id=1, source_target_pairs={{0,16},{1,17},{2,18},{3,19},{4,20},{5,21},{6,22},{7,23},{8,24},{9,... | collective-permute-start | bytes 368648 | tf_op jit(solution)/shard_map/qkv_z/ppermute | solution.py:492
  9.8 9.7 %collective-permute-start.2 = (bf16[80,768]{1,0:T(8,128)(2,1)}, bf16[80,768]{1,0:T(8,128)(2,1)S(1)}, u32[]{:S(2)}, u32[]{:S(2)}) collective-permute-start(bf16[80,768]{1,0:T(8,128)(2,1)} %get-tuple-element.167), channel_id=1, source_target_pairs={{0,24},{1,25},{2,26},{3,27},{4,28},{5,29},{6,30},{7,31},{8,16},{9,... | collective-permute-start | bytes 368648 | tf_op jit(solution)/shard_map/qkv_z/ppermute | solution.py:492
  19.4 26.4 %copy-start.5 = (bf16[256,768]{1,0:T(8,128)(2,1)}, bf16[256,768]{1,0:T(8,128)(2,1)S(1)}, u32[]{:S(2)}) copy-start(bf16[256,768]{1,0:T(8,128)(2,1)S(1)} %collective-permute-done.3.other.mate_frames) | copy-start | bytes 1179652
  19.4 30.6 %copy-start.40 = (bf16[96,768]{1,0:T(8,128)(2,1)S(1)}, bf16[96,768]{1,0:T(8,128)(2,1)}, u32[]{:S(2)}) copy-start(bf16[96,768]{1,0:T(8,128)(2,1)} %get-tuple-element.195) | copy-start | bytes 442372
  20.6 34.4 %copy-start.39 = (bf16[4,80,768]{2,1,0:T(8,128)(2,1)}, bf16[4,80,768]{2,1,0:T(8,128)(2,1)S(1)}, u32[]{:S(2)}) copy-start(bf16[4,80,768]{2,1,0:T(8,128)(2,1)S(1)} %pad_maximum_fusion.2.p0) | copy-start | bytes 1474564
  20.6 14.9 %collective-permute-start.4 = (bf16[4,80,768]{2,1,0:T(8,128)(2,1)S(1)}, bf16[4,80,768]{2,1,0:T(8,128)(2,1)}, u32[]{:S(2)}, u32[]{:S(2)}) collective-permute-start(bf16[4,80,768]{2,1,0:T(8,128)(2,1)S(1)} %pad_maximum_fusion.2.p0), channel_id=1, source_target_pairs={{0,1},{1,0},{2,6},{3,7},{4,5},{5,4},{6,2},{7,3},{8,9},{9,8},{10,14... | collective-permute-start | bytes 1474568 | tf_op jit(solution)/shard_map/qkv_1/ppermute | solution.py:492
  21.2 4.5 %collective-permute-start.7 = (bf16[256,768]{1,0:T(8,128)(2,1)S(1)}, bf16[256,768]{1,0:T(8,128)(2,1)S(1)}, u32[]{:S(2)}, u32[]{:S(2)}) collective-permute-start(bf16[256,768]{1,0:T(8,128)(2,1)S(1)} %copy-done.19), channel_id=1, source_target_pairs={{0,2},{1,3},{2,0},{3,1},{4,6},{5,7},{6,4},{7,5},{8,10},{9,11},{10,... | collective-permute-start | bytes 1179656 | tf_op jit(solution)/shard_map/twin/ppermute | solution.py:492
  21.2 11.7 %collective-permute-start.5 = (bf16[128,768]{1,0:T(8,128)(2,1)}, bf16[128,768]{1,0:T(8,128)(2,1)S(1)}, u32[]{:S(2)}, u32[]{:S(2)}) collective-permute-start(bf16[128,768]{1,0:T(8,128)(2,1)} %get-tuple-element.176), channel_id=1, source_target_pairs={{0,8},{1,9},{2,10},{3,11},{4,12},{5,13},{6,14},{7,15},{8,0},{9,1},... | collective-permute-start | bytes 589832 | tf_op jit(solution)/shard_map/up_z/ppermute | solution.py:492
  23.1 12.4 %collective-permute-start.6 = (bf16[128,768]{1,0:T(8,128)(2,1)}, bf16[128,768]{1,0:T(8,128)(2,1)S(1)}, u32[]{:S(2)}, u32[]{:S(2)}) collective-permute-start(bf16[128,768]{1,0:T(8,128)(2,1)} %get-tuple-element.176), channel_id=1, source_target_pairs={{0,16},{1,17},{2,18},{3,19},{4,20},{5,21},{6,22},{7,23},{8,24},{9,... | collective-permute-start | bytes 589832 | tf_op jit(solution)/shard_map/up_z/ppermute | solution.py:492
  24.2 15.2 %collective-permute-start.9 = (bf16[4,80,768]{2,1,0:T(8,128)(2,1)S(1)}, bf16[4,80,768]{2,1,0:T(8,128)(2,1)}, u32[]{:S(2)}, u32[]{:S(2)}) collective-permute-start(bf16[4,80,768]{2,1,0:T(8,128)(2,1)S(1)} %pad_maximum_fusion.2.p0), channel_id=1, source_target_pairs={{0,4},{1,5},{2,3},{3,2},{4,0},{5,1},{6,7},{7,6},{8,12},{9,13},{10,... | collective-permute-start | bytes 1474568 | tf_op jit(solution)/shard_map/qkv_2/ppermute | solution.py:492
  35.5 9.3 %collective-permute-start.10 = (bf16[4,80,768]{2,1,0:T(8,128)(2,1)}, bf16[4,80,768]{2,1,0:T(8,128)(2,1)}, u32[]{:S(2)}, u32[]{:S(2)}) collective-permute-start(bf16[4,80,768]{2,1,0:T(8,128)(2,1)} %collective-permute-done.4.p1), channel_id=1, source_target_pairs={{0,4},{1,5},{2,3},{3,2},{4,0},{5,1},{6,7},{7,6},{8,12},{9,13},{10,... | collective-permute-start | bytes 1474568 | tf_op jit(solution)/shard_map/qkv_3/ppermute | solution.py:492
  37.0 7.8 %collective-permute-start.8 = (bf16[128,768]{1,0:T(8,128)(2,1)}, bf16[128,768]{1,0:T(8,128)(2,1)S(1)}, u32[]{:S(2)}, u32[]{:S(2)}) collective-permute-start(bf16[128,768]{1,0:T(8,128)(2,1)} %get-tuple-element.176), channel_id=1, source_target_pairs={{0,24},{1,25},{2,26},{3,27},{4,28},{5,29},{6,30},{7,31},{8,16},{9,... | collective-permute-start | bytes 589832 | tf_op jit(solution)/shard_map/up_z/ppermute | solution.py:492
  45.8 18.2 %collective-permute-start.12 = (bf16[4,128,768]{2,1,0:T(8,128)(2,1)S(1)}, bf16[4,128,768]{2,1,0:T(8,128)(2,1)S(1)}, u32[]{:S(2)}, u32[]{:S(2)}) collective-permute-start(bf16[4,128,768]{2,1,0:T(8,128)(2,1)S(1)} %pad_maximum_fusion.p0.u0), channel_id=1, source_target_pairs={{0,1},{1,0},{2,6},{3,7},{4,5},{5,4},{6,2},{7,3},{8,9},{9,8},{10,14... | collective-permute-start | bytes 2359304 | tf_op jit(solution)/shard_map/up_1/ppermute | solution.py:492
  47.4 2.7 %collective-permute-start.13 = (bf16[4,80,768]{2,1,0:T(8,128)(2,1)S(1)}, bf16[4,80,768]{2,1,0:T(8,128)(2,1)}, u32[]{:S(2)}, u32[]{:S(2)}) collective-permute-start(bf16[4,80,768]{2,1,0:T(8,128)(2,1)S(1)} %pad_maximum_fusion.2.p0), channel_id=1, source_target_pairs={{0,2},{1,3},{2,0},{3,1},{4,6},{5,7},{6,4},{7,5},{8,10},{9,11},{10,... | collective-permute-start | bytes 1474568 | tf_op jit(solution)/shard_map/twin/ppermute | solution.py:492
  47.4 4.3 %collective-permute-start.14 = (bf16[4,80,768]{2,1,0:T(8,128)(2,1)}, bf16[4,80,768]{2,1,0:T(8,128)(2,1)}, u32[]{:S(2)}, u32[]{:S(2)}) collective-permute-start(bf16[4,80,768]{2,1,0:T(8,128)(2,1)} %collective-permute-done.4.p1), channel_id=1, source_target_pairs={{0,2},{1,3},{2,0},{3,1},{4,6},{5,7},{6,4},{7,5},{8,10},{9,11},{10,... | collective-permute-start | bytes 1474568 | tf_op jit(solution)/shard_map/twin/ppermute | solution.py:492
  47.9 5.8 %collective-permute-start.15 = (bf16[4,80,768]{2,1,0:T(8,128)(2,1)}, bf16[4,80,768]{2,1,0:T(8,128)(2,1)}, u32[]{:S(2)}, u32[]{:S(2)}) collective-permute-start(bf16[4,80,768]{2,1,0:T(8,128)(2,1)} %collective-permute-done.9.p2), channel_id=1, source_target_pairs={{0,2},{1,3},{2,0},{3,1},{4,6},{5,7},{6,4},{7,5},{8,10},{9,11},{10,... | collective-permute-start | bytes 1474568 | tf_op jit(solution)/shard_map/twin/ppermute | solution.py:492
  47.9 7.1 %collective-permute-start.16 = (bf16[4,80,768]{2,1,0:T(8,128)(2,1)}, bf16[4,80,768]{2,1,0:T(8,128)(2,1)}, u32[]{:S(2)}, u32[]{:S(2)}) collective-permute-start(bf16[4,80,768]{2,1,0:T(8,128)(2,1)} %collective-permute-done.10.p3), channel_id=1, source_target_pairs={{0,2},{1,3},{2,0},{3,1},{4,6},{5,7},{6,4},{7,5},{8,10},{9,11},{10,... | collective-permute-start | bytes 1474568 | tf_op jit(solution)/shard_map/twin/ppermute | solution.py:492
  50.0 14.0 %collective-permute-start.17 = (bf16[96,768]{1,0:T(8,128)(2,1)S(1)}, bf16[96,768]{1,0:T(8,128)(2,1)S(1)}, u32[]{:S(2)}, u32[]{:S(2)}) collective-permute-start(bf16[96,768]{1,0:T(8,128)(2,1)S(1)} %copy-done.40), channel_id=1, source_target_pairs={{0,8},{1,9},{2,10},{3,11},{4,12},{5,13},{6,14},{7,15},{8,0},{9,1},... | collective-permute-start | bytes 442376 | tf_op jit(solution)/shard_map/down_z/ppermute | solution.py:492
  51.7 12.4 %collective-permute-start.18 = (bf16[96,768]{1,0:T(8,128)(2,1)S(1)}, bf16[96,768]{1,0:T(8,128)(2,1)S(1)}, u32[]{:S(2)}, u32[]{:S(2)}) collective-permute-start(bf16[96,768]{1,0:T(8,128)(2,1)S(1)} %copy-done.40), channel_id=1, source_target_pairs={{0,16},{1,17},{2,18},{3,19},{4,20},{5,21},{6,22},{7,23},{8,24},{9,... | collective-permute-start | bytes 442376 | tf_op jit(solution)/shard_map/down_z/ppermute | solution.py:492
  53.7 24.0 %collective-permute-start.11 = (bf16[4,128,768]{2,1,0:T(8,128)(2,1)S(1)}, bf16[4,128,768]{2,1,0:T(8,128)(2,1)}, u32[]{:S(2)}, u32[]{:S(2)}) collective-permute-start(bf16[4,128,768]{2,1,0:T(8,128)(2,1)S(1)} %pad_maximum_fusion.p0.u0), channel_id=1, source_target_pairs={{0,4},{1,5},{2,3},{3,2},{4,0},{5,1},{6,7},{7,6},{8,12},{9,13},{10,... | collective-permute-start | bytes 2359304 | tf_op jit(solution)/shard_map/up_2/ppermute | solution.py:492
  64.1 13.6 %collective-permute-start.19 = (bf16[4,128,768]{2,1,0:T(8,128)(2,1)S(1)}, bf16[4,128,768]{2,1,0:T(8,128)(2,1)}, u32[]{:S(2)}, u32[]{:S(2)}) collective-permute-start(bf16[4,128,768]{2,1,0:T(8,128)(2,1)S(1)} %collective-permute-done.12.p1.u1), channel_id=1, source_target_pairs={{0,4},{1,5},{2,3},{3,2},{4,0},{5,1},{6,7},{7,6},{8,12},{9,13},{10,... | collective-permute-start | bytes 2359304 | tf_op jit(solution)/shard_map/up_3/ppermute | solution.py:492
  64.8 15.8 %collective-permute-start.23 = (bf16[4,128,768]{2,1,0:T(8,128)(2,1)S(1)}, bf16[4,128,768]{2,1,0:T(8,128)(2,1)}, u32[]{:S(2)}, u32[]{:S(2)}) collective-permute-start(bf16[4,128,768]{2,1,0:T(8,128)(2,1)S(1)} %pad_maximum_fusion.p0.u0), channel_id=1, source_target_pairs={{0,2},{1,3},{2,0},{3,1},{4,6},{5,7},{6,4},{7,5},{8,10},{9,11},{10,... | collective-permute-start | bytes 2359304 | tf_op jit(solution)/shard_map/twin/ppermute | solution.py:492
  64.8 12.8 %collective-permute-start.20 = (bf16[96,768]{1,0:T(8,128)(2,1)S(1)}, bf16[96,768]{1,0:T(8,128)(2,1)S(1)}, u32[]{:S(2)}, u32[]{:S(2)}) collective-permute-start(bf16[96,768]{1,0:T(8,128)(2,1)S(1)} %copy-done.40), channel_id=1, source_target_pairs={{0,24},{1,25},{2,26},{3,27},{4,28},{5,29},{6,30},{7,31},{8,16},{9,... | collective-permute-start | bytes 442376 | tf_op jit(solution)/shard_map/down_z/ppermute | solution.py:492
  67.8 14.4 %collective-permute-start.24 = (bf16[4,128,768]{2,1,0:T(8,128)(2,1)S(1)}, bf16[4,128,768]{2,1,0:T(8,128)(2,1)S(1)}, u32[]{:S(2)}, u32[]{:S(2)}) collective-permute-start(bf16[4,128,768]{2,1,0:T(8,128)(2,1)S(1)} %collective-permute-done.12.p1.u1), channel_id=1, source_target_pairs={{0,2},{1,3},{2,0},{3,1},{4,6},{5,7},{6,4},{7,5},{8,10},{9,11},{10,... | collective-permute-start | bytes 2359304 | tf_op jit(solution)/shard_map/twin/ppermute | solution.py:492
  77.7 4.5 %collective-permute-start.25 = (bf16[4,128,768]{2,1,0:T(8,128)(2,1)}, bf16[4,128,768]{2,1,0:T(8,128)(2,1)S(1)}, u32[]{:S(2)}, u32[]{:S(2)}) collective-permute-start(bf16[4,128,768]{2,1,0:T(8,128)(2,1)} %collective-permute-done.11.p2.u2), channel_id=1, source_target_pairs={{0,2},{1,3},{2,0},{3,1},{4,6},{5,7},{6,4},{7,5},{8,10},{9,11},{10,... | collective-permute-start | bytes 2359304 | tf_op jit(solution)/shard_map/twin/ppermute | solution.py:492
  78.1 4.1 %collective-permute-start.26 = (bf16[4,128,768]{2,1,0:T(8,128)(2,1)}, bf16[4,128,768]{2,1,0:T(8,128)(2,1)S(1)}, u32[]{:S(2)}, u32[]{:S(2)}) collective-permute-start(bf16[4,128,768]{2,1,0:T(8,128)(2,1)} %collective-permute-done.19.p3.u3), channel_id=1, source_target_pairs={{0,2},{1,3},{2,0},{3,1},{4,6},{5,7},{6,4},{7,5},{8,10},{9,11},{10,... | collective-permute-start | bytes 2359304 | tf_op jit(solution)/shard_map/twin/ppermute | solution.py:492
  79.1 16.0 %collective-permute-start.21 = (bf16[4,96,768]{2,1,0:T(8,128)(2,1)}, bf16[4,96,768]{2,1,0:T(8,128)(2,1)}, u32[]{:S(2)}, u32[]{:S(2)}) collective-permute-start(bf16[4,96,768]{2,1,0:T(8,128)(2,1)} %pad_maximum_fusion.1.p0), channel_id=1, source_target_pairs={{0,1},{1,0},{2,6},{3,7},{4,5},{5,4},{6,2},{7,3},{8,9},{9,8},{10,14... | collective-permute-start | bytes 1769480 | tf_op jit(solution)/shard_map/down_1/ppermute | solution.py:492
  80.6 14.5 %collective-permute-start.22 = (bf16[4,96,768]{2,1,0:T(8,128)(2,1)}, bf16[4,96,768]{2,1,0:T(8,128)(2,1)S(1)}, u32[]{:S(2)}, u32[]{:S(2)}) collective-permute-start(bf16[4,96,768]{2,1,0:T(8,128)(2,1)} %pad_maximum_fusion.1.p0), channel_id=1, source_target_pairs={{0,4},{1,5},{2,3},{3,2},{4,0},{5,1},{6,7},{7,6},{8,12},{9,13},{10,... | collective-permute-start | bytes 1769480 | tf_op jit(solution)/shard_map/down_2/ppermute | solution.py:492
  95.1 3.6 %collective-permute-start.28 = (bf16[256,3072]{1,0:T(8,128)(2,1)}, bf16[256,3072]{1,0:T(8,128)(2,1)S(1)}, u32[]{:S(2)}, u32[]{:S(2)}) collective-permute-start(bf16[256,3072]{1,0:T(8,128)(2,1)} %get-tuple-element.208.active), channel_id=1, source_target_pairs={{0,2},{1,3},{2,0},{3,1},{4,6},{5,7},{6,4},{7,5},{8,10},{9,11},{10,... | collective-permute-start | bytes 4718600 | tf_op jit(solution)/shard_map/twin/ppermute | solution.py:492
  95.4 10.1 %collective-permute-start.27 = (bf16[4,96,768]{2,1,0:T(8,128)(2,1)}, bf16[4,96,768]{2,1,0:T(8,128)(2,1)S(1)}, u32[]{:S(2)}, u32[]{:S(2)}) collective-permute-start(bf16[4,96,768]{2,1,0:T(8,128)(2,1)} %collective-permute-done.21.p1), channel_id=1, source_target_pairs={{0,4},{1,5},{2,3},{3,2},{4,0},{5,1},{6,7},{7,6},{8,12},{9,13},{10,... | collective-permute-start | bytes 1769480 | tf_op jit(solution)/shard_map/down_3/ppermute | solution.py:492
  96.9 9.1 %collective-permute-start.31 = (bf16[4,96,768]{2,1,0:T(8,128)(2,1)}, bf16[4,96,768]{2,1,0:T(8,128)(2,1)S(1)}, u32[]{:S(2)}, u32[]{:S(2)}) collective-permute-start(bf16[4,96,768]{2,1,0:T(8,128)(2,1)} %pad_maximum_fusion.1.p0), channel_id=1, source_target_pairs={{0,2},{1,3},{2,0},{3,1},{4,6},{5,7},{6,4},{7,5},{8,10},{9,11},{10,... | collective-permute-start | bytes 1769480 | tf_op jit(solution)/shard_map/twin/ppermute | solution.py:492
  96.9 10.6 %collective-permute-start.32 = (bf16[4,96,768]{2,1,0:T(8,128)(2,1)}, bf16[4,96,768]{2,1,0:T(8,128)(2,1)S(1)}, u32[]{:S(2)}, u32[]{:S(2)}) collective-permute-start(bf16[4,96,768]{2,1,0:T(8,128)(2,1)} %collective-permute-done.21.p1), channel_id=1, source_target_pairs={{0,2},{1,3},{2,0},{3,1},{4,6},{5,7},{6,4},{7,5},{8,10},{9,11},{10,... | collective-permute-start | bytes 1769480 | tf_op jit(solution)/shard_map/twin/ppermute | solution.py:492
  97.4 10.7 %collective-permute-start.33 = (bf16[4,96,768]{2,1,0:T(8,128)(2,1)S(1)}, bf16[4,96,768]{2,1,0:T(8,128)(2,1)S(1)}, u32[]{:S(2)}, u32[]{:S(2)}) collective-permute-start(bf16[4,96,768]{2,1,0:T(8,128)(2,1)S(1)} %collective-permute-done.22.p2), channel_id=1, source_target_pairs={{0,2},{1,3},{2,0},{3,1},{4,6},{5,7},{6,4},{7,5},{8,10},{9,11},{10,... | collective-permute-start | bytes 1769480 | tf_op jit(solution)/shard_map/twin/ppermute | solution.py:492
  105.5 2.6 %collective-permute-start.34 = (bf16[4,96,768]{2,1,0:T(8,128)(2,1)S(1)}, bf16[4,96,768]{2,1,0:T(8,128)(2,1)S(1)}, u32[]{:S(2)}, u32[]{:S(2)}) collective-permute-start(bf16[4,96,768]{2,1,0:T(8,128)(2,1)S(1)} %collective-permute-done.27.p3), channel_id=1, source_target_pairs={{0,2},{1,3},{2,0},{3,1},{4,6},{5,7},{6,4},{7,5},{8,10},{9,11},{10,... | collective-permute-start | bytes 1769480 | tf_op jit(solution)/shard_map/twin/ppermute | solution.py:492
  105.5 16.4 %collective-permute-start.37 = (bf16[512,768]{1,0:T(8,128)(2,1)S(1)}, bf16[512,768]{1,0:T(8,128)(2,1)S(1)}, u32[]{:S(2)}, u32[]{:S(2)}) collective-permute-start(bf16[512,768]{1,0:T(8,128)(2,1)S(1)} %copy-done.12), channel_id=1, source_target_pairs={{0,2},{1,3},{2,0},{3,1},{4,6},{5,7},{6,4},{7,5},{8,10},{9,11},{10,... | collective-permute-start | bytes 2359304 | tf_op jit(solution)/shard_map/twin/ppermute | solution.py:492
  106.0 15.9 %collective-permute-start.29 = (bf16[4,96,768]{2,1,0:T(8,128)(2,1)S(1)}, bf16[4,96,768]{2,1,0:T(8,128)(2,1)}, u32[]{:S(2)}, u32[]{:S(2)}) collective-permute-start(bf16[4,96,768]{2,1,0:T(8,128)(2,1)S(1)} %get-tuple-element.216), channel_id=1, source_target_pairs={{0,4},{1,5},{2,3},{3,2},{4,0},{5,1},{6,7},{7,6},{8,12},{9,13},{10,... | collective-permute-start | bytes 1769480 | tf_op jit(solution)/shard_map/rs_down_3/ppermute | solution.py:492
  107.5 14.7 %collective-permute-start.30 = (bf16[4,96,768]{2,1,0:T(8,128)(2,1)S(1)}, bf16[4,96,768]{2,1,0:T(8,128)(2,1)S(1)}, u32[]{:S(2)}, u32[]{:S(2)}) collective-permute-start(bf16[4,96,768]{2,1,0:T(8,128)(2,1)S(1)} %get-tuple-element.217), channel_id=1, source_target_pairs={{0,4},{1,5},{2,3},{3,2},{4,0},{5,1},{6,7},{7,6},{8,12},{9,13},{10,... | collective-permute-start | bytes 1769480 | tf_op jit(solution)/shard_map/rs_down_2/ppermute | solution.py:492
  108.0 13.9 %collective-permute-start.35 = (bf16[256,768]{1,0:T(8,128)(2,1)S(1)}, bf16[256,768]{1,0:T(8,128)(2,1)S(1)}, u32[]{:S(2)}, u32[]{:S(2)}) collective-permute-start(bf16[256,768]{1,0:T(8,128)(2,1)S(1)} %copy-done.26), channel_id=1, source_target_pairs={{0,2},{1,3},{2,0},{3,1},{4,6},{5,7},{6,4},{7,5},{8,10},{9,11},{10,... | collective-permute-start | bytes 1179656 | tf_op jit(solution)/shard_map/twin/ppermute | solution.py:492
  108.2 13.8 %collective-permute-start.36 = (bf16[256,768]{1,0:T(8,128)(2,1)S(1)}, bf16[256,768]{1,0:T(8,128)(2,1)S(1)}, u32[]{:S(2)}, u32[]{:S(2)}) collective-permute-start(bf16[256,768]{1,0:T(8,128)(2,1)S(1)} %copy-done.25), channel_id=1, source_target_pairs={{0,2},{1,3},{2,0},{3,1},{4,6},{5,7},{6,4},{7,5},{8,10},{9,11},{10,... | collective-permute-start | bytes 1179656 | tf_op jit(solution)/shard_map/twin/ppermute | solution.py:492
  122.2 4.9 %collective-permute-start.39 = (bf16[256,3072]{1,0:T(8,128)(2,1)}, bf16[256,3072]{1,0:T(8,128)(2,1)S(1)}, u32[]{:S(2)}, u32[]{:S(2)}) collective-permute-start(bf16[256,3072]{1,0:T(8,128)(2,1)} %get-tuple-element.231.hidden), channel_id=1, source_target_pairs={{0,2},{1,3},{2,0},{3,1},{4,6},{5,7},{6,4},{7,5},{8,10},{9,11},{10,... | collective-permute-start | bytes 4718600 | tf_op jit(solution)/shard_map/twin/ppermute | solution.py:492
  123.6 9.9 %collective-permute-start.38 = (bf16[4,96,768]{2,1,0:T(8,128)(2,1)S(1)}, bf16[4,96,768]{2,1,0:T(8,128)(2,1)S(1)}, u32[]{:S(2)}, u32[]{:S(2)}) collective-permute-start(bf16[4,96,768]{2,1,0:T(8,128)(2,1)S(1)} %add_convert_fusion.1), channel_id=1, source_target_pairs={{0,1},{1,0},{2,6},{3,7},{4,5},{5,4},{6,2},{7,3},{8,9},{9,8},{10,14... | collective-permute-start | bytes 1769480 | tf_op jit(solution)/shard_map/rs_down_1/ppermute | solution.py:492
  125.2 1.9 collective-permute-start.40
  133.6 16.2 %collective-permute-start.41 = (bf16[4,128,768]{2,1,0:T(8,128)(2,1)S(1)}, bf16[4,128,768]{2,1,0:T(8,128)(2,1)S(1)}, u32[]{:S(2)}, u32[]{:S(2)}) collective-permute-start(bf16[4,128,768]{2,1,0:T(8,128)(2,1)S(1)} %get-tuple-element.241), channel_id=1, source_target_pairs={{0,4},{1,5},{2,3},{3,2},{4,0},{5,1},{6,7},{7,6},{8,12},{9,13},{10,... | collective-permute-start | bytes 2359304 | tf_op jit(solution)/shard_map/rs_up_3/ppermute | solution.py:492
  135.1 14.7 %collective-permute-start.42 = (bf16[2,128,768]{2,1,0:T(8,128)(2,1)S(1)}, bf16[2,128,768]{2,1,0:T(8,128)(2,1)S(1)}, u32[]{:S(2)}, u32[]{:S(2)}) collective-permute-start(bf16[2,128,768]{2,1,0:T(8,128)(2,1)S(1)} %get-tuple-element.242), channel_id=1, source_target_pairs={{0,4},{1,5},{2,3},{3,2},{4,0},{5,1},{6,7},{7,6},{8,12},{9,13},{10,... | collective-permute-start | bytes 1179656 | tf_op jit(solution)/shard_map/rs_up_2a/ppermute | solution.py:492
  135.9 11.5 %collective-permute-start.43 = (bf16[96,768]{1,0:T(8,128)(2,1)S(1)}, bf16[96,768]{1,0:T(8,128)(2,1)S(1)}, u32[]{:S(2)}, u32[]{:S(2)}) collective-permute-start(bf16[96,768]{1,0:T(8,128)(2,1)S(1)} %get-tuple-element.327), channel_id=1, source_target_pairs={{0,8},{1,9},{2,10},{3,11},{4,12},{5,13},{6,14},{7,15},{8,0},{9,1},... | collective-permute-start | bytes 442376 | tf_op jit(solution)/shard_map/rs_down_z/ppermute | solution.py:492
  136.4 11.0 %collective-permute-start.44 = (bf16[96,768]{1,0:T(8,128)(2,1)S(1)}, bf16[96,768]{1,0:T(8,128)(2,1)S(1)}, u32[]{:S(2)}, u32[]{:S(2)}) collective-permute-start(bf16[96,768]{1,0:T(8,128)(2,1)S(1)} %get-tuple-element.326), channel_id=1, source_target_pairs={{0,16},{1,17},{2,18},{3,19},{4,20},{5,21},{6,22},{7,23},{8,24},{9,... | collective-permute-start | bytes 442376 | tf_op jit(solution)/shard_map/rs_down_z/ppermute | solution.py:492
  149.8 6.8 %collective-permute-start.47 = (bf16[3,512,768]{2,1,0:T(8,128)(2,1)S(1)}, bf16[3,512,768]{2,1,0:T(8,128)(2,1)S(1)}, u32[]{:S(2)}, u32[]{:S(2)}) collective-permute-start(bf16[3,512,768]{2,1,0:T(8,128)(2,1)S(1)} %get-tuple-element.253.grads), channel_id=1, source_target_pairs={{0,2},{1,3},{2,0},{3,1},{4,6},{5,7},{6,4},{7,5},{8,10},{9,11},{10,... | collective-permute-start | bytes 7077896 | tf_op jit(solution)/shard_map/twin/ppermute | solution.py:492
  150.1 16.3 %collective-permute-start.45 = (bf16[4,128,768]{2,1,0:T(8,128)(2,1)S(1)}, bf16[4,128,768]{2,1,0:T(8,128)(2,1)S(1)}, u32[]{:S(2)}, u32[]{:S(2)}) collective-permute-start(bf16[4,128,768]{2,1,0:T(8,128)(2,1)S(1)} %add_convert_fusion), channel_id=1, source_target_pairs={{0,1},{1,0},{2,6},{3,7},{4,5},{5,4},{6,2},{7,3},{8,9},{9,8},{10,14... | collective-permute-start | bytes 2359304 | tf_op jit(solution)/shard_map/rs_up_1/ppermute | solution.py:492
  151.6 12.1 %collective-permute-start.46 = (bf16[2,128,768]{2,1,0:T(8,128)(2,1)S(1)}, bf16[2,128,768]{2,1,0:T(8,128)(2,1)S(1)}, u32[]{:S(2)}, u32[]{:S(2)}) collective-permute-start(bf16[2,128,768]{2,1,0:T(8,128)(2,1)S(1)} %get-tuple-element.250), channel_id=1, source_target_pairs={{0,4},{1,5},{2,3},{3,2},{4,0},{5,1},{6,7},{7,6},{8,12},{9,13},{10,... | collective-permute-start | bytes 1179656 | tf_op jit(solution)/shard_map/rs_up_2b/ppermute | solution.py:492
  156.6 1.5 collective-permute-start.49
  156.6 9.7 %collective-permute-start.48 = (bf16[96,768]{1,0:T(8,128)(2,1)S(1)}, bf16[96,768]{1,0:T(8,128)(2,1)S(1)}, u32[]{:S(2)}, u32[]{:S(2)}) collective-permute-start(bf16[96,768]{1,0:T(8,128)(2,1)S(1)} %get-tuple-element.262), channel_id=1, source_target_pairs={{0,24},{1,25},{2,26},{3,27},{4,28},{5,29},{6,30},{7,31},{8,16},{9,... | collective-permute-start | bytes 442376 | tf_op jit(solution)/shard_map/rs_down_z/ppermute | solution.py:492
  166.4 8.9 %collective-permute-start.50 = (bf16[4,80,768]{2,1,0:T(8,128)(2,1)S(1)}, bf16[4,80,768]{2,1,0:T(8,128)(2,1)S(1)}, u32[]{:S(2)}, u32[]{:S(2)}) collective-permute-start(bf16[4,80,768]{2,1,0:T(8,128)(2,1)S(1)} %get-tuple-element.270), channel_id=1, source_target_pairs={{0,4},{1,5},{2,3},{3,2},{4,0},{5,1},{6,7},{7,6},{8,12},{9,13},{10,... | collective-permute-start | bytes 1474568 | tf_op jit(solution)/shard_map/rs_qkv_3/ppermute | solution.py:492
  168.0 9.5 %collective-permute-start.53 = (bf16[128,768]{1,0:T(8,128)(2,1)S(1)}, bf16[128,768]{1,0:T(8,128)(2,1)S(1)}, u32[]{:S(2)}, u32[]{:S(2)}) collective-permute-start(bf16[128,768]{1,0:T(8,128)(2,1)S(1)} %get-tuple-element.320), channel_id=1, source_target_pairs={{0,8},{1,9},{2,10},{3,11},{4,12},{5,13},{6,14},{7,15},{8,0},{9,1},... | collective-permute-start | bytes 589832 | tf_op jit(solution)/shard_map/rs_up_z/ppermute | solution.py:492
  168.7 11.5 %collective-permute-start.54 = (bf16[128,768]{1,0:T(8,128)(2,1)S(1)}, bf16[128,768]{1,0:T(8,128)(2,1)S(1)}, u32[]{:S(2)}, u32[]{:S(2)}) collective-permute-start(bf16[128,768]{1,0:T(8,128)(2,1)S(1)} %get-tuple-element.323), channel_id=1, source_target_pairs={{0,16},{1,17},{2,18},{3,19},{4,20},{5,21},{6,22},{7,23},{8,24},{9,... | collective-permute-start | bytes 589832 | tf_op jit(solution)/shard_map/rs_up_z/ppermute | solution.py:492
  170.5 18.9 %collective-permute-start.52 = (bf16[4,80,768]{2,1,0:T(8,128)(2,1)S(1)}, bf16[4,80,768]{2,1,0:T(8,128)(2,1)S(1)}, u32[]{:S(2)}, u32[]{:S(2)}) collective-permute-start(bf16[4,80,768]{2,1,0:T(8,128)(2,1)S(1)} %get-tuple-element.280), channel_id=1, source_target_pairs={{0,4},{1,5},{2,3},{3,2},{4,0},{5,1},{6,7},{7,6},{8,12},{9,13},{10,... | collective-permute-start | bytes 1474568 | tf_op jit(solution)/shard_map/rs_qkv_2/ppermute | solution.py:492
  175.4 14.1 %collective-permute-start.51 = (bf16[4,80,768]{2,1,0:T(8,128)(2,1)S(1)}, bf16[4,80,768]{2,1,0:T(8,128)(2,1)S(1)}, u32[]{:S(2)}, u32[]{:S(2)}) collective-permute-start(bf16[4,80,768]{2,1,0:T(8,128)(2,1)S(1)} %add_convert_fusion.2), channel_id=1, source_target_pairs={{0,1},{1,0},{2,6},{3,7},{4,5},{5,4},{6,2},{7,3},{8,9},{9,8},{10,14... | collective-permute-start | bytes 1474568 | tf_op jit(solution)/shard_map/rs_qkv_1/ppermute | solution.py:492
  180.2 9.3 %collective-permute-start.55 = (bf16[128,768]{1,0:T(8,128)(2,1)S(1)}, bf16[128,768]{1,0:T(8,128)(2,1)S(1)}, u32[]{:S(2)}, u32[]{:S(2)}) collective-permute-start(bf16[128,768]{1,0:T(8,128)(2,1)S(1)} %get-tuple-element.284), channel_id=1, source_target_pairs={{0,24},{1,25},{2,26},{3,27},{4,28},{5,29},{6,30},{7,31},{8,16},{9,... | collective-permute-start | bytes 589832 | tf_op jit(solution)/shard_map/rs_up_z/ppermute | solution.py:492
  189.6 14.3 %collective-permute-start.59 = (bf16[256,768]{1,0:T(8,128)(2,1)S(1)}, bf16[256,768]{1,0:T(8,128)(2,1)S(1)}, u32[]{:S(2)}, u32[]{:S(2)}) collective-permute-start(bf16[256,768]{1,0:T(8,128)(2,1)S(1)} %get-tuple-element.299), channel_id=1, source_target_pairs={{0,1},{1,0},{2,3},{3,2},{4,5},{5,4},{6,7},{7,6},{8,9},{9,8},{10,11... | collective-permute-start | bytes 1179656 | tf_op jit(solution)/shard_map/grad_pack/ppermute | solution.py:492
  191.3 5.2 %collective-permute-start.56 = (bf16[80,768]{1,0:T(8,128)(2,1)S(1)}, bf16[80,768]{1,0:T(8,128)(2,1)S(1)}, u32[]{:S(2)}, u32[]{:S(2)}) collective-permute-start(bf16[80,768]{1,0:T(8,128)(2,1)S(1)} %get-tuple-element.330), channel_id=1, source_target_pairs={{0,8},{1,9},{2,10},{3,11},{4,12},{5,13},{6,14},{7,15},{8,0},{9,1},... | collective-permute-start | bytes 368648 | tf_op jit(solution)/shard_map/rs_qkv_z/ppermute | solution.py:492
  191.3 11.2 %collective-permute-start.57 = (bf16[80,768]{1,0:T(8,128)(2,1)S(1)}, bf16[80,768]{1,0:T(8,128)(2,1)S(1)}, u32[]{:S(2)}, u32[]{:S(2)}) collective-permute-start(bf16[80,768]{1,0:T(8,128)(2,1)S(1)} %get-tuple-element.329), channel_id=1, source_target_pairs={{0,16},{1,17},{2,18},{3,19},{4,20},{5,21},{6,22},{7,23},{8,24},{9,... | collective-permute-start | bytes 368648 | tf_op jit(solution)/shard_map/rs_qkv_z/ppermute | solution.py:492
  193.6 9.0 %collective-permute-start.58 = (bf16[80,768]{1,0:T(8,128)(2,1)S(1)}, bf16[80,768]{1,0:T(8,128)(2,1)S(1)}, u32[]{:S(2)}, u32[]{:S(2)}) collective-permute-start(bf16[80,768]{1,0:T(8,128)(2,1)S(1)} %get-tuple-element.328), channel_id=1, source_target_pairs={{0,24},{1,25},{2,26},{3,27},{4,28},{5,29},{6,30},{7,31},{8,16},{9,... | collective-permute-start | bytes 368648 | tf_op jit(solution)/shard_map/rs_qkv_z/ppermute | solution.py:492
  (37 other events, 234.7 us)
where the time goes:
time: 206 us; the launch traced here: 205 us
  Pallas kernels  76.7 us (37%)
  starting transfers between devices  59.9 us (29%)
  waiting for transfers between devices  53.5 us (26%)
  other arithmetic  6.76 us (3%)
  local copies, waits for them, and re-layouts  5.78 us (3%)
    pallas_call x13, Pallas kernels, call(): pl.pallas_call(kernel, out_shape=outs, in_specs=in_specs, out_specs=out_s...  76.7 us
    ppermute x60, starting transfers between devices, shift(): return lax.ppermute(array, AXES, route(move))  59.9 us
    ppermute x60, waiting for transfers between devices, shift(): return lax.ppermute(array, AXES, route(move))  53.5 us
    unnamed x82, local copies, waits for them, and re-layouts  4.32 us
  transfers between devices with their start and end apart: 60, of which 20 were waited for; matrix products, arithmetic and copies ran while one was open for 3% of the time, Pallas kernels for 36%

commit v1 on v0

--- a/solution.py
+++ b/solution.py
@@ -529,25 +529,15 @@
     return ((z * 2 + y) * 2 + c) * 2 + x
 
 
-def planes_of(place):
-    c0 = place[3]
-    found = []
-    for plane in range(2):
-        c = c0 if plane == 0 else 1 - c0
-        for z in range(4):
+def each_unit(place, visit):
+    def step(z, _):
+        for plane in range(2):
+            c = place[3] if plane == 0 else 1 - place[3]
             for n, (x_turn, y_turn) in enumerate(((0, 0), (1 - c, c), (c, 1 - c), (1, 1))):
-                found.append((4 * plane + n, z, unit_of(place, x_turn, y_turn, z, c)))
-    return found
-
-
-def load_units(place, pieces, stage, sems):
-    copies = [
-        pltpu.make_async_copy(pieces[array].at[z], stage.at[unit], sems.at[n])
-        for n, (array, z, unit) in enumerate(planes_of(place))
-    ]
-    for copy in copies:
-        copy.start()
-    return copies
+                visit(4 * plane + n, z, unit_of(place, x_turn, y_turn, z, c))
+        return 0
+
+    lax.fori_loop(0, 4, step, 0)
 
 
 def take_columns(place, array, pair, taken, top):
@@ -567,12 +557,16 @@
 def give_units(place, stage, parts):
     c = place[3]
     for part, (x_turn, y_turn) in zip(parts, ((0, 0), (1 - c, c), (c, 1 - c), (1, 1))):
-        for turn in range(4):
-            unit = ((place[2] ^ turn) * 2 + (place[1] ^ y_turn)) * 2 + (place[0] ^ x_turn)
-            if isinstance(part, tuple):
-                part[turn // 2][turn % 2] = stage[unit].astype(LOW)
-            else:
-                part[turn] = stage[unit].astype(LOW)
+        halves = part if isinstance(part, tuple) else (part,)
+        for half, ref in enumerate(halves):
+            start = half * ref.shape[0]
+
+            def give(turn, _, ref=ref, start=start, x_turn=x_turn, y_turn=y_turn):
+                unit = ((place[2] ^ (start + turn)) * 2 + (place[1] ^ y_turn)) * 2 + (place[0] ^ x_turn)
+                ref[turn] = stage[unit].astype(LOW)
+                return 0
+
+            lax.fori_loop(0, ref.shape[0], give, 0)
 
 
 def part_shapes(rows, width):
@@ -610,25 +604,31 @@
     )(*args)
 
 
-def spread_tables(units, width):
+def spread_tables(units, width, lanes):
     tables = []
     for n in (width // units, 2 * width // units, 4 * width // units):
-        lane = np.arange(units * n)
-        keep = lane[None, :] // n == np.arange(units)[:, None]
-        pick = lane[None, :] % n == np.arange(LANES)[:, None]
-        tables.append(jnp.asarray(np.concatenate([keep, pick]), LOW))
+        lane = lanes[None, : units * n]
+        row = jnp.arange(units + LANES, dtype=jnp.int32)[:, None]
+        tables.append(
+            jnp.where(row < units, lane // n == row, lane % n == row - units).astype(F32).astype(LOW)
+        )
     return tables
 
 
 def project_kernel(
     place, own, other, p0, p1, p2, p3, p4, p5, p6, p7, wide_one, wide_two, wide_four,
-    first, queries, keys, values, weight, vectors, up_bias, mate_live, stage, small, sems,
+    first, queries, keys, values, vectors, up_bias, mate_live, weight_out, stage, small, weight, sems,
 ):
     units = stage.shape[0]
     width = own.shape[1]
     rows = stage.shape[1] - PAD
     shard_len = own.shape[0]
-    copies = load_units(place, (p0, p1, p2, p3, p4, p5, p6, p7), stage, sems)
+    pieces = (p0, p1, p2, p3, p4, p5, p6, p7)
+
+    def fill(array, z, unit):
+        stage[unit] = pieces[array][z]
+
+    each_unit(place, fill)
 
     def normed(frames):
         wide = frames.astype(F32)
@@ -636,8 +636,6 @@
         return center * lax.rsqrt(jnp.mean(center * center, axis=1, keepdims=True) + EPSILON)
 
     own_normed, mate_normed = normed(own[...]), normed(other[...])
-    for copy in copies:
-        copy.wait()
     for unit in range(units):
         top = stage[unit, rows : rows + PAD, :].astype(F32)
         small[0, unit : unit + 1, :] = top[0:1]
@@ -666,6 +664,8 @@
         return 0
 
     lax.fori_loop(0, units // 2, join, 0)
+    copy = pltpu.make_async_copy(weight, weight_out, sems.at[0])
+    copy.start()
     gain, offset = vectors[0:1, :], vectors[1:2, :]
     x = place[0]
     own_at = pl.multiple_of(x * shard_len, shard_len)
@@ -678,20 +678,32 @@
     values[...] = (
         dot_nt(first[...], weight[2 * width :, :]) + vectors[NARROW + 1 : NARROW + 2, :]
     ).astype(LOW)
+    copy.wait()
 
 
 def half_mask(shape, head):
     return (lax.broadcasted_iota(jnp.int32, shape, 1) // HD) == head
 
 
+def bias_kernel(curve, bias):
+    heads, block_len, span = bias.shape
+
+    def shear(head, _):
+        bias[head] = pltpu.roll(
+            jnp.broadcast_to(curve[pl.ds(head, 1), :], (block_len, block_len + span)),
+            span + 1, 1, stride=1, stride_axis=0,
+        )[:, :span].astype(LOW)
+        return 0
+
+    lax.fori_loop(0, heads, shear, 0)
+
+
 def attend_kernel(
-    place, lengths, queries, keys, values, curve, own_live, mate_live, probs, mixed, hidden_pairs
+    place, lengths, queries, keys, values, bias, own_live, mate_live, probs, mixed, hidden_pairs
 ):
-    q, k, v = queries[...], keys[...], values[...]
     block_len, span = hidden_pairs.shape
-    step = pl.program_id(0)
-
-    @pl.when(step == 0)
+
+    @pl.when(pl.program_id(0) == 0)
     def _():
         start = place[0] * block_len
         key_pos = lax.broadcasted_iota(jnp.int32, (1, span), 1)
@@ -709,32 +721,19 @@
         allowed = (query_doc == key_doc) & ((live > 0.5) | (query_pos == key_pos))
         hidden_pairs[...] = jnp.where(allowed, 0.0, MASKED)
 
-    total = jnp.zeros(q.shape, F32)
-    for head in range(2):
-        q_head = jnp.where(half_mask(q.shape, head), q, 0) * (1.0 / math.sqrt(HD))
-        bias = pltpu.roll(
-            jnp.broadcast_to(curve[pl.ds(2 * step + head, 1), :], (block_len, block_len + span)),
-            span + 1, 1, stride=1, stride_axis=0,
-        )[:, :span]
-        logits = dot_nt(q_head.astype(LOW), k) + bias + hidden_pairs[...]
-        weights = jnp.exp(logits - jnp.max(logits, axis=1, keepdims=True))
-        prob = (weights * (1.0 / jnp.sum(weights, axis=1, keepdims=True))).astype(LOW)
-        probs[head] = prob
-        total = total + dot_nn(prob, jnp.where(half_mask(v.shape, head), v, 0))
-    mixed[...] = total
-
-
-def load_mixed(place, pieces, up, kept, sems, kept_sems):
-    rows = pieces[0].shape[1] - kept.shape[1]
-    first, later = [], []
-    for n, (array, z, unit) in enumerate(planes_of(place)):
-        ref = pieces[array].at[z]
-        at = pl.multiple_of(unit * rows, rows)
-        first.append(pltpu.make_async_copy(ref.at[rows:], kept.at[unit], kept_sems.at[n]))
-        later.append(pltpu.make_async_copy(ref.at[:rows], up.at[pl.ds(at, rows)], sems.at[n]))
-    for copy in first + later:
-        copy.start()
-    return first, later
+    for pair in range(queries.shape[1] // (2 * HD)):
+        lane = slice(2 * HD * pair, 2 * HD * (pair + 1))
+        q, k, v = queries[:, lane], keys[:, lane], values[:, lane]
+        total = jnp.zeros(q.shape, F32)
+        for head in range(2):
+            n = 2 * pair + head
+            q_head = jnp.where(half_mask(q.shape, head), q, 0) * (1.0 / math.sqrt(HD))
+            logits = dot_nt(q_head.astype(LOW), k) + bias[n].astype(F32) + hidden_pairs[...]
+            weights = jnp.exp(logits - jnp.max(logits, axis=1, keepdims=True))
+            prob = (weights * (1.0 / jnp.sum(weights, axis=1, keepdims=True))).astype(LOW)
+            probs[n] = prob
+            total = total + dot_nn(prob, jnp.where(half_mask(v.shape, head), v, 0))
+        mixed[:, lane] = total
 
 
 def join_units(kept, out):
@@ -753,21 +752,24 @@
 
 def expand_kernel(
     place, frames, mixed, vectors, up_bias, p0, p1, p2, p3, p4, p5, p6, p7,
-    middle, second, context, active, slope, up, kept, out, sems, kept_sems,
+    middle, second, context, active, slope, up, kept, out,
 ):
     width = frames.shape[1]
-    first, later = load_mixed(place, (p0, p1, p2, p3, p4, p5, p6, p7), up, kept, sems, kept_sems)
+    pieces = (p0, p1, p2, p3, p4, p5, p6, p7)
+    rows = p0.shape[1] - kept.shape[1]
+
+    def fill(array, z, unit):
+        kept[unit] = pieces[array][z, rows:]
+        up[pl.ds(pl.multiple_of(unit * rows, rows), rows), :] = pieces[array][z, :rows]
+
+    each_unit(place, fill)
     context[...] = mixed[...].astype(LOW)
-    for copy in first:
-        copy.wait()
     join_units(kept, out)
     mid = frames[...].astype(F32) + (dot_nt(context[...], out[...]) + vectors[4:5, :])
     middle[...] = mid
     center = mid - jnp.mean(mid, axis=1, keepdims=True)
     normed = center * lax.rsqrt(jnp.mean(center * center, axis=1, keepdims=True) + EPSILON)
     second[...] = (normed * vectors[2:3, :] + vectors[3:4, :]).astype(LOW)
-    for copy in later:
-        copy.wait()
     for n in range(up.shape[0] // width):
         at = slice(n * width, (n + 1) * width)
         hidden = dot_nt(second[...], up[at, :]) + up_bias[0:1, at]
@@ -818,15 +820,18 @@
 def back_kernel(
     place, cotangent, slope, middle, vectors, p0, p1, p2, p3, p4, p5, p6, p7, u0, u1, u2, u3, u4, u5, u6, u7,
     middle_grad, context_grad, vector_grads, branch_grad, up_bias_grad, hidden_grad,
-    stage, down, up, kept, out, stage_sems, sems, kept_sems,
+    stage, down, up, kept, out,
 ):
     width = cotangent.shape[1]
-    down_copies = load_units(place, (p0, p1, p2, p3, p4, p5, p6, p7), stage, stage_sems)
-    kept_copies, up_copies = load_mixed(
-        place, (u0, u1, u2, u3, u4, u5, u6, u7), up, kept, sems, kept_sems
-    )
-    for copy in down_copies:
-        copy.wait()
+    down_pieces, up_pieces = (p0, p1, p2, p3, p4, p5, p6, p7), (u0, u1, u2, u3, u4, u5, u6, u7)
+    rows = u0.shape[1] - kept.shape[1]
+
+    def fill(array, z, unit):
+        stage[unit] = down_pieces[array][z]
+        kept[unit] = up_pieces[array][z, rows:]
+        up[pl.ds(pl.multiple_of(unit * rows, rows), rows), :] = up_pieces[array][z, :rows]
+
+    each_unit(place, fill)
     unfold_units(stage, down)
     dy = cotangent[...]
     for n in range(hidden_grad.shape[1] // width):
@@ -836,11 +841,7 @@
         up_bias_grad[:, at] = jnp.broadcast_to(
             jnp.sum(grad.astype(F32), axis=0, keepdims=True), (up_bias_grad.shape[0], width)
         )
-    for copy in kept_copies:
-        copy.wait()
     join_units(kept, out)
-    for copy in up_copies:
-        copy.wait()
     second_grad = dot_nn(hidden_grad[...], up[...])
     mid = middle[...]
     center = mid - jnp.mean(mid, axis=1, keepdims=True)
@@ -907,11 +908,14 @@
 
 
 def finish_kernel(
-    place, active, middle, vectors, p0, p1, p2, p3, p4, p5, p6, p7, layer_out, stage, down, sems
+    place, active, middle, vectors, p0, p1, p2, p3, p4, p5, p6, p7, layer_out, stage, down
 ):
-    copies = load_units(place, (p0, p1, p2, p3, p4, p5, p6, p7), stage, sems)
-    for copy in copies:
-        copy.wait()
+    pieces = (p0, p1, p2, p3, p4, p5, p6, p7)
+
+    def fill(array, z, unit):
+        stage[unit] = pieces[array][z]
+
+    each_unit(place, fill)
     unfold_units(stage, down)
     layer_out[...] = middle[...] + dot_nt(active[...], down[...]) + vectors[5:6, :]
 
@@ -996,7 +1000,7 @@
 
 def qkv_grad_kernel(
     place, grads, grads_twin, first, first_twin, small_own, small_twin, wide_one, wide_two, wide_four,
-    o0, o1, o2, o3, taken, sums, small, stage,
+    o0, o1, o2, o3, taken, sums, small, tables, stage,
 ):
     units, full, width = stage.shape
     rows = full - PAD
@@ -1030,17 +1034,22 @@
         columns = jnp.concatenate([array[part] for part in range(3)], axis=1)
         take_columns(place, columns, 2 * rows, taken, n * span)
     sums[...] = dot_tn(taken[:span, :], first[...]) + dot_tn(taken[span:, :], first_twin[...])
-    for unit in range(units):
+
+    def pack(unit, _):
         at = 4 * (unit // 2) + 2 * place[3] + unit % 2
         stage[unit] = jnp.concatenate(
             [
-                sums[unit * rows : (unit + 1) * rows, :],
+                sums[pl.ds(pl.multiple_of(unit * rows, rows), rows), :],
                 small[0, pl.ds(at, 1), :],
                 small[1, pl.ds(at, 1), :],
-                table,
+                tables[...],
             ],
             axis=0,
         ).astype(LOW)
+        return 0
+
+    tables[...] = table
+    lax.fori_loop(0, units, pack, 0)
     give_units(place, stage, (o0, o1, o2, o3))
 
 
@@ -1153,10 +1162,21 @@
     def twins(pieces):
         return tuple(pieces) + tuple(twin(piece) for piece in pieces)
 
+    distance = jnp.arange(span + shard_len, dtype=jnp.int32) - (shard_len - 1) - x * shard_len
+    bucket = jnp.clip(distance, -MAXREL, MAXREL) + MAXREL
+    bucket_lanes = 3 * LANES
+    buckets = (bucket[:, None] == jnp.arange(bucket_lanes, dtype=jnp.int32)[None, :]).astype(LOW)
+    curve = lax.dot_general(
+        rel_bias, buckets[:, :BUCKETS], (((0,), (1,)), ((), ())), preferred_element_type=F32
+    )
+    bias = call(
+        bias_kernel, [VMEM], [shape(H, shard_len, span)], [VMEM], [], (tied(curve, qkv_unit),), 0, name="bias"
+    )[0]
+    spreads = spread_tables(units, width, tied(jnp.arange(ff, dtype=jnp.int32), qkv_unit))
     cotangent_twin = twin(cotangent)
     qkv_z = along_z(qkv_unit, "qkv")
     mate_frames = shift(tied(frames, qkv_unit), PACK, "frames_pack")
-    qkv_z, mate_frames = joined(qkv_z, mate_frames)
+    qkv_z, mate_frames, bias, place, spreads = joined(qkv_z, mate_frames, bias, place, spreads)
     qkv_own = jnp.stack((qkv_unit,) + qkv_z)
     qkv_side = shift(qkv_own, SIDE, "qkv_1")
     up_first = tied(up_unit, *qkv_z)
@@ -1172,26 +1192,19 @@
     down_first = tied(down_unit, up_own)
     down_z = [shift(down_first, move, "down_z") for move in ALONG_Z[:2]]
 
-    distance = jnp.arange(span + shard_len, dtype=jnp.int32) - (shard_len - 1) - x * shard_len
-    bucket = jnp.clip(distance, -MAXREL, MAXREL) + MAXREL
-    bucket_lanes = 3 * LANES
-    buckets = (bucket[:, None] == jnp.arange(bucket_lanes, dtype=jnp.int32)[None, :]).astype(LOW)
-    curve = lax.dot_general(
-        rel_bias, buckets[:, :BUCKETS], (((0,), (1,)), ((), ())), preferred_element_type=F32
-    )
-    spreads = spread_tables(units, width)
     unit_sems = pltpu.SemaphoreType.DMA((units,))
-    first, queries, keys, values, weight, vectors, up_bias_all, mate_live = call(
+    first, queries, keys, values, vectors, up_bias_all, mate_live, weight = call(
         project_kernel,
-        [SMEM, VMEM, VMEM] + [HBM] * 8 + [VMEM] * 3,
+        [SMEM] + [VMEM] * 13,
         [
             shape(span, width), shape(shard_len, width), shape(span, width), shape(span, width),
-            shape(3 * width, width), shape(8, width, kind=F32), shape(8, ff, kind=F32),
-            shape(PAD, shard_len, kind=F32),
+            shape(8, width, kind=F32), shape(8, ff, kind=F32), shape(PAD, shard_len, kind=F32),
+            shape(3 * width, width),
         ],
-        [VMEM] * 8,
+        [VMEM] * 7 + [HBM],
         [
-            pltpu.VMEM((units, qkv_rows + PAD, width), LOW), pltpu.VMEM((2, units, width), F32), unit_sems,
+            pltpu.VMEM((units, qkv_rows + PAD, width), LOW), pltpu.VMEM((2, units, width), F32),
+            pltpu.VMEM((3 * width, width), LOW), pltpu.SemaphoreType.DMA((1,)),
         ],
         (tied(place, up_own), frames, mate_frames) + qkv_pieces + tuple(spreads),
         2 * shard_len * width * 5 * width,
@@ -1204,8 +1217,8 @@
     pairs = H // 2
     pair_lanes = 2 * HD
 
-    def lanes_of(rows):
-        return pl.BlockSpec((rows, pair_lanes), lambda n: (0, n))
+    def lanes_of(rows, count=1):
+        return pl.BlockSpec((rows, count * pair_lanes), lambda n: (0, n))
 
     def heads_of(*dims):
         return pl.BlockSpec(dims, lambda n: (n,) + (0,) * (len(dims) - 1))
@@ -1216,17 +1229,17 @@
     probs, mixed = call(
         attend_kernel,
         [
-            SMEM, SMEM, lanes_of(shard_len), lanes_of(span), lanes_of(span), whole(H, span + shard_len),
-            whole(1, shard_len), whole(PAD, shard_len),
+            SMEM, SMEM, lanes_of(shard_len, 2), lanes_of(span, 2), lanes_of(span, 2),
+            heads_of(4, shard_len, span), whole(1, shard_len), whole(PAD, shard_len),
         ],
         [shape(H, shard_len, span), shape(shard_len, width, kind=F32)],
-        [heads_of(2, shard_len, span), lanes_of(shard_len)],
+        [heads_of(4, shard_len, span), lanes_of(shard_len, 2)],
         [pltpu.VMEM((shard_len, span), F32)],
         (
-            tied(place, up_side), seq_lengths, queries, keys, values, curve, row(key_mask), mate_live,
+            tied(place, up_side), seq_lengths, queries, keys, values, bias, row(key_mask), mate_live,
         ),
         8 * shard_len * span * width,
-        grid=(pairs,),
+        grid=(pairs // 2,),
         name="attend",
     )
     up_other, up_across, mixed, down_z = joined(up_other, up_across, mixed, down_z)
@@ -1236,7 +1249,7 @@
     down_other = shift(down_own, OTHER_SIDE, "down_2")
     middle, second, context, active, slope = call(
         expand_kernel,
-        [SMEM] + [VMEM] * 4 + [HBM] * 8,
+        [SMEM] + [VMEM] * 12,
         [
             shape(shard_len, width, kind=F32), shape(shard_len, width), shape(shard_len, width),
             shape(shard_len, ff), shape(shard_len, ff, kind=F32),
@@ -1244,11 +1257,11 @@
         [VMEM] * 5,
         [
             pltpu.VMEM((ff, width), LOW), pltpu.VMEM((units, out_rows, width), LOW),
-            pltpu.VMEM((width, width), LOW), unit_sems, unit_sems,
+            pltpu.VMEM((width, width), LOW),
         ],
         (tied(place, down_own), frames, mixed, vectors, up_bias_all) + up_pieces,
         2 * shard_len * width * (width + ff),
-        name="expand",
+        name="expand", limit=36,
     )
     down_side, down_other, active = joined(down_side, down_other, active)
     down_across = shift(down_side, OTHER_SIDE, "down_3")
@@ -1273,7 +1286,7 @@
     down_two = shift(down_parts[2], OTHER_SIDE, "rs_down_2")
     middle_grad, context_grad, vector_grads, branch_grad, up_bias_grad, hidden_grad = call(
         back_kernel,
-        [SMEM] + [VMEM] * 4 + [HBM] * 16,
+        [SMEM] + [VMEM] * 20,
         [
             shape(shard_len, width, kind=F32), shape(shard_len, width), shape(8, width, kind=F32),
             shape(shard_len, width), shape(8, ff, kind=F32), shape(shard_len, ff),
@@ -1282,11 +1295,11 @@
         [
             pltpu.VMEM((units, down_rows, width), LOW), pltpu.VMEM((width, ff), LOW),
             pltpu.VMEM((ff, width), LOW), pltpu.VMEM((units, out_rows, width), LOW),
-            pltpu.VMEM((width, width), LOW), unit_sems, unit_sems, unit_sems,
+            pltpu.VMEM((width, width), LOW),
         ],
         (tied(place, down_parts[0]), cotangent, slope, middle, vectors) + down_pieces + up_pieces,
         2 * shard_len * width * (2 * ff + width),
-        name="back",
+        name="back", limit=48,
     )
     turned, down_two, hidden_grad, context_twin, second_twin, first_twin = joined(
         turned, down_two, hidden_grad, context_twin, second_twin, first_twin
@@ -1363,7 +1376,8 @@
         [VMEM] * 4,
         [
             pltpu.VMEM((2 * span, 3 * width // 2), LOW), pltpu.VMEM((3 * width // 2, width), F32),
-            pltpu.VMEM((2, units, width), F32), pltpu.VMEM((units // 2, qkv_rows + PAD, width), LOW),
+            pltpu.VMEM((2, units, width), F32), pltpu.VMEM((H // 2, width), F32),
+            pltpu.VMEM((units // 2, qkv_rows + PAD, width), LOW),
         ],
         (place, grads, grads_twin, first, first_twin, small, small_twin) + tuple(spreads),
         2 * shard_len * width * 6 * width,
@@ -1396,10 +1410,10 @@
     up_z.append(shift(tied(up_low[3], side_after), ALONG_Z[2], "rs_up_z"))
     layer_out = call(
         finish_kernel,
-        [SMEM] + [VMEM] * 3 + [HBM] * 8,
+        [SMEM] + [VMEM] * 11,
         [shape(shard_len, width, kind=F32)],
         [VMEM],
-        [pltpu.VMEM((units, down_rows, width), LOW), pltpu.VMEM((width, ff), LOW), unit_sems],
+        [pltpu.VMEM((units, down_rows, width), LOW), pltpu.VMEM((width, ff), LOW)],
         (tied(place, side_after), active, middle, vectors) + down_pieces,
         2 * shard_len * width * ff,
         name="finish",
@@ -1407,8 +1421,8 @@
     qkv_one, qkv_two, up_z, layer_out = joined(qkv_one, qkv_two, up_z, layer_out)
     qkv_sum = qkv_parts[0].astype(F32) + qkv_one.astype(F32) + qkv_two.astype(F32)
     qkv_z = z_sends(qkv_sum, "rs_qkv")
-    mate_part = shift(tied(mate_part, qkv_sum), PACK, "grad_pack")
     up_sum = z_sum(tied(up_sum[:1], qkv_sum), up_z)
+    mate_part = shift(tied(mate_part, up_sum), PACK, "grad_pack")
     up_sum, qkv_z = joined(up_sum, qkv_z)
     last = call(
         last_kernel,

time: 206 us -> 198 us (0.961)
  Pallas kernels: 76.7 us -> 68.8 us
    pallas_call x13 -> x14, Pallas kernels: 76.7 us -> 68.8 us  [call(): pl.pallas_call(kernel, out_shape=outs, in_specs=in_specs, out_specs=out_s...]
    convert_element_type x0 -> x3, other arithmetic: none -> 3.45 us  [spread_tables(): jnp.where(row < units, lane // n == row, lane % n == row - units)]
    unnamed x82 -> x108, local copies, waits for them, and re-layouts: 4.32 us -> 4.71 us
  transfers between devices with their start and end apart: 60 -> 60, of which waited for: 20 -> 19; matrix products, arithmetic and copies ran while one was open for 3% -> 4% of each run, Pallas kernels for 36% -> 33%
where the time goes in v1:
time: 198 us
  Pallas kernels  68.8 us (35%)
  starting transfers between devices  59 us (30%)
  waiting for transfers between devices  54.7 us (28%)
  other arithmetic  6.39 us (3%)
  local copies, waits for them, and re-layouts  6.18 us (3%)
    pallas_call x14, Pallas kernels, call(): pl.pallas_call(kernel, out_shape=outs, in_specs=in_specs, out_specs=out_s...  68.8 us
    ppermute x60, starting transfers between devices, shift(): return lax.ppermute(array, AXES, route(move))  59 us
    ppermute x60, waiting for transfers between devices, shift(): return lax.ppermute(array, AXES, route(move))  54.7 us
    unnamed x108, local copies, waits for them, and re-layouts  4.71 us
  transfers between devices with their start and end apart: 60, of which 19 were waited for; matrix products, arithmetic and copies ran while one was open for 4% of the time, Pallas kernels for 33%

profile of v1, /device:TPU:0, one launch (start us, length us, event | category | flops | bytes accessed | tf_op | source)
XLA Modules:
  0.0 197.7 jit_solution(4081200039314055688)
XLA Ops:
  0.7 1.9 pack.1
  2.6 3.0 %collective-permute-start = (bf16[80,768]{1,0:T(8,128)(2,1)}, bf16[80,768]{1,0:T(8,128)(2,1)S(1)}, u32[]{:S(2)}, u32[]{:S(2)}) collective-permute-start(bf16[80,768]{1,0:T(8,128)(2,1)} %get-tuple-element.174), channel_id=1, source_target_pairs={{0,8},{1,9},{2,10},{3,11},{4,12},{5,13},{6,14},{7,15},{8,0},{9,1},... | collective-permute-start | bytes 368648 | tf_op jit(solution)/shard_map/qkv_z/ppermute | solution.py:492
  5.6 2.6 %collective-permute-start.1 = (bf16[80,768]{1,0:T(8,128)(2,1)}, bf16[80,768]{1,0:T(8,128)(2,1)S(1)}, u32[]{:S(2)}, u32[]{:S(2)}) collective-permute-start(bf16[80,768]{1,0:T(8,128)(2,1)} %get-tuple-element.174), channel_id=1, source_target_pairs={{0,16},{1,17},{2,18},{3,19},{4,20},{5,21},{6,22},{7,23},{8,24},{9,... | collective-permute-start | bytes 368648 | tf_op jit(solution)/shard_map/qkv_z/ppermute | solution.py:492
  8.2 1.7 collective-permute-start.3
  10.0 1.5 convert_convert_fusion.wide_four
  11.5 1.1 convert_convert_fusion.1.wide_two
  13.5 1.0 fusion.2.curve
  14.5 4.0 %bias.1 = bf16[12,256,512]{2,1,0:T(8,128)(2,1)} custom-call(f32[12,768]{1,0:T(8,128)} %fusion.2.curve), custom_call_target="tpu_custom_call" | custom-call | bytes 3182592 | tf_op jit(solution)/shard_map/bias/pallas_call | solution.py:595
  19.2 1.1 collective-permute-start.4
  20.4 1.4 collective-permute-start.5
  21.8 2.8 %collective-permute-start.6 = (bf16[128,768]{1,0:T(8,128)(2,1)S(1)}, bf16[128,768]{1,0:T(8,128)(2,1)S(1)}, u32[]{:S(2)}, u32[]{:S(2)}) collective-permute-start(bf16[128,768]{1,0:T(8,128)(2,1)S(1)} %copy-done.51), channel_id=1, source_target_pairs={{0,16},{1,17},{2,18},{3,19},{4,20},{5,21},{6,22},{7,23},{8,24},{9,... | collective-permute-start | bytes 589832 | tf_op jit(solution)/shard_map/up_z/ppermute | solution.py:492
  24.5 1.5 collective-permute-start.9
  26.8 4.8 %collective-permute-done.5 = bf16[128,768]{1,0:T(8,128)(2,1)S(1)} collective-permute-done((bf16[128,768]{1,0:T(8,128)(2,1)S(1)}, bf16[128,768]{1,0:T(8,128)(2,1)S(1)}, u32[]{:S(2)}, u32[]{:S(2)}) %collective-permute-start.5) | collective-permute-done | bytes 196640 | tf_op jit(solution)/shard_map/up_z/ppermute | solution.py:492
  31.7 2.4 %collective-permute-done.6 = bf16[128,768]{1,0:T(8,128)(2,1)S(1)} collective-permute-done((bf16[128,768]{1,0:T(8,128)(2,1)S(1)}, bf16[128,768]{1,0:T(8,128)(2,1)S(1)}, u32[]{:S(2)}, u32[]{:S(2)}) %collective-permute-start.6) | collective-permute-done | bytes 196640 | tf_op jit(solution)/shard_map/up_z/ppermute | solution.py:492
  34.0 1.5 collective-permute-start.10
  35.5 2.4 %collective-permute-start.8 = (bf16[128,768]{1,0:T(8,128)(2,1)S(1)}, bf16[128,768]{1,0:T(8,128)(2,1)S(1)}, u32[]{:S(2)}, u32[]{:S(2)}) collective-permute-start(bf16[128,768]{1,0:T(8,128)(2,1)S(1)} %copy-done.51), channel_id=1, source_target_pairs={{0,24},{1,25},{2,26},{3,27},{4,28},{5,29},{6,30},{7,31},{8,16},{9,... | collective-permute-start | bytes 589832 | tf_op jit(solution)/shard_map/up_z/ppermute | solution.py:492
  37.9 5.2 %collective-permute-done.8 = bf16[128,768]{1,0:T(8,128)(2,1)S(1)} collective-permute-done((bf16[128,768]{1,0:T(8,128)(2,1)S(1)}, bf16[128,768]{1,0:T(8,128)(2,1)S(1)}, u32[]{:S(2)}, u32[]{:S(2)}) %collective-permute-start.8) | collective-permute-done | bytes 196640 | tf_op jit(solution)/shard_map/up_z/ppermute | solution.py:492
  43.2 1.5 collective-permute-start.12
  46.6 2.2 %collective-permute-start.17 = (bf16[96,768]{1,0:T(8,128)(2,1)S(1)}, bf16[96,768]{1,0:T(8,128)(2,1)S(1)}, u32[]{:S(2)}, u32[]{:S(2)}) collective-permute-start(bf16[96,768]{1,0:T(8,128)(2,1)S(1)} %copy-done.52), channel_id=1, source_target_pairs={{0,8},{1,9},{2,10},{3,11},{4,12},{5,13},{6,14},{7,15},{8,0},{9,1},... | collective-permute-start | bytes 442376 | tf_op jit(solution)/shard_map/down_z/ppermute | solution.py:492
  49.4 1.5 collective-permute-start.11
  51.7 8.0 %project.1 = (bf16[512,768]{1,0:T(8,128)(2,1)}, bf16[256,768]{1,0:T(8,128)(2,1)}, bf16[512,768]{1,0:T(8,128)(2,1)}, bf16[512,768]{1,0:T(8,128)(2,1)}, f32[8,768]...) custom-call(s32[4]{0:T(128)} %pad_add_fusion.place, bf16[256,768]{1,0:T(8,128)(2,1)} %frames.3, ...), custom_call_target="tpu_custom_call" | custom-call | flops 1509949440 | bytes 12861456 | tf_op jit(solution)/shard_map/project/pallas_call | solution.py:595
  60.5 2.5 %collective-permute-start.20 = (bf16[96,768]{1,0:T(8,128)(2,1)S(1)}, bf16[96,768]{1,0:T(8,128)(2,1)S(1)}, u32[]{:S(2)}, u32[]{:S(2)}) collective-permute-start(bf16[96,768]{1,0:T(8,128)(2,1)S(1)} %copy-done.52), channel_id=1, source_target_pairs={{0,24},{1,25},{2,26},{3,27},{4,28},{5,29},{6,30},{7,31},{8,16},{9,... | collective-permute-start | bytes 442376 | tf_op jit(solution)/shard_map/down_z/ppermute | solution.py:492
  63.3 7.5 %attend.1 = (bf16[12,256,512]{2,1,0:T(8,128)(2,1)}, f32[256,768]{1,0:T(8,128)}) custom-call(s32[4]{0:T(128)} %pad_add_fusion.place, s32[1,4]{1,0:T(1,128)} %lengths.1, bf16[256,768]{1,0:T(8,128)(2,1)} %get-tuple-element.201.queries, bf16[512,768]{1,0:T(8,128)(2,1)} %get-tuple-element.202.keys, bf16[512,768]{1,0:T(8,128)(2,1)} %get-tuple-element.203.values, ...), custom_call_target="tpu_custom_call" | custom-call | flops 805306368 | bytes 9053216 | tf_op jit(solution)/shard_map/attend/pallas_call | solution.py:595
  70.8 1.0 collective-permute-done.19.p3.u3
  72.4 1.2 collective-permute-start.21
  73.6 1.3 collective-permute-start.22
  75.3 4.0 %expand.1 = (f32[256,768]{1,0:T(8,128)S(1)}, bf16[256,768]{1,0:T(8,128)(2,1)S(1)}, bf16[256,768]{1,0:T(8,128)(2,1)S(1)}, bf16[256,3072]{1,0:T(8,128)(2,1)S(1)}, f32[256,3072]{1,0:T(8,128)S(1)}) custom-call(s32[4]{0:T(128)S(1)} %copy-done.39, bf16[256,768]{1,0:T(8,128)(2,1)S(1)} %copy-done.4, f32[256,768]{1,0:T(8,128)S(1)} %copy-done.21, ...), custom_call_target="tpu_custom_call" | custom-call | flops 1509949440 | bytes 13885456 | tf_op jit(solution)/shard_map/expand/pallas_call | solution.py:595
  79.4 9.1 %collective-permute-done.21.p1 = bf16[4,96,768]{2,1,0:T(8,128)(2,1)S(1)} collective-permute-done((bf16[4,96,768]{2,1,0:T(8,128)(2,1)S(1)}, bf16[4,96,768]{2,1,0:T(8,128)(2,1)S(1)}, u32[]{:S(2)}, u32[]{:S(2)}) %collective-permute-start.21) | collective-permute-done | bytes 589856 | tf_op jit(solution)/shard_map/down_1/ppermute | solution.py:492
  88.6 1.0 collective-permute-start.27
  90.2 1.8 collective-permute-done.28.active_twin
  92.0 3.1 %down_grad.1 = (bf16[4,96,768]{2,1,0:T(8,128)(2,1)S(1)}, bf16[4,96,768]{2,1,0:T(8,128)(2,1)S(1)}, bf16[4,96,768]{2,1,0:T(8,128)(2,1)S(1)}, bf16[4,96,768]{2,1,0:T(8,128)(2,1)S(1)}, f32[8,768]{1,0:T(8,128)S(1)}) custom-call(s32[4]{0:T(128)S(1)} %copy-done.39, bf16[256,3072]{1,0:T(8,128)(2,1)S(1)} %get-tuple-element.222.active, ...), custom_call_target="tpu_custom_call" | custom-call | flops 1207959552 | bytes 6316048 | tf_op jit(solution)/shard_map/down_grad/pallas_call | solution.py:595
  95.0 1.2 copy-done.32
  96.3 2.3 %collective-permute-done.27.p3 = bf16[4,96,768]{2,1,0:T(8,128)(2,1)S(1)} collective-permute-done((bf16[4,96,768]{2,1,0:T(8,128)(2,1)S(1)}, bf16[4,96,768]{2,1,0:T(8,128)(2,1)S(1)}, u32[]{:S(2)}, u32[]{:S(2)}) %collective-permute-start.27) | collective-permute-done | bytes 589856 | tf_op jit(solution)/shard_map/down_3/ppermute | solution.py:492
  99.1 1.0 collective-permute-start.29
  100.1 1.0 collective-permute-start.30
  101.6 10.2 %back.1 = (f32[256,768]{1,0:T(8,128)}, bf16[256,768]{1,0:T(8,128)(2,1)S(1)}, f32[8,768]{1,0:T(8,128)S(1)}, bf16[256,768]{1,0:T(8,128)(2,1)S(1)}, f32[8,3072]{1,0:T(8,128)S(1)}, /*index=5*/bf16[256,3072]{1,0:T(8,128)(2,1)}) custom-call(s32[4]{0:T(128)S(1)} %copy-done.39, bf16[256,768]{1,0:T(8,128)(2,1)S(1)} %copy-done.37, f32[256,3072]{1,0:T(8,128)} %copy-done.18, ...), custom_call_target="tpu_custom_call" | custom-call | flops 2717908992 | bytes 18628624 | tf_op jit(solution)/shard_map/back/pallas_call | solution.py:595
  113.7 1.6 collective-permute-done.30
  115.4 1.0 collective-permute-start.38
  116.7 2.5 %collective-permute-done.40.branch_twin = bf16[256,768]{1,0:T(8,128)(2,1)S(1)} collective-permute-done((bf16[256,768]{1,0:T(8,128)(2,1)S(1)}, bf16[256,768]{1,0:T(8,128)(2,1)S(1)}, u32[]{:S(2)}, u32[]{:S(2)}) %collective-permute-start.40) | collective-permute-done | bytes 393248 | tf_op jit(solution)/shard_map/twin/ppermute | solution.py:492
  119.2 3.7 %up_grad.1 = (bf16[4,128,768]{2,1,0:T(8,128)(2,1)S(1)}, bf16[4,128,768]{2,1,0:T(8,128)(2,1)S(1)}, bf16[2,128,768]{2,1,0:T(8,128)(2,1)S(1)}, bf16[2,128,768]{2,1,0:T(8,128)(2,1)S(1)}, bf16[4,128,768]{2,1,0:T(8,128)(2,1)S(1)}) custom-call(s32[4]{0:T(128)S(1)} %copy-done.39, bf16[256,3072]{1,0:T(8,128)(2,1)S(1)} %copy-done.40, ...), custom_call_target="tpu_custom_call" | custom-call | flops 1509949440 | bytes 8650768 | tf_op jit(solution)/shard_map/up_grad/pallas_call | solution.py:595
  123.0 2.4 %collective-permute-done.38 = bf16[4,96,768]{2,1,0:T(8,128)(2,1)S(1)} collective-permute-done((bf16[4,96,768]{2,1,0:T(8,128)(2,1)S(1)}, bf16[4,96,768]{2,1,0:T(8,128)(2,1)S(1)}, u32[]{:S(2)}, u32[]{:S(2)}) %collective-permute-start.38) | collective-permute-done | bytes 589856 | tf_op jit(solution)/shard_map/rs_down_1/ppermute | solution.py:492
  125.4 1.0 collective-permute-start.41
  126.4 1.0 collective-permute-start.42
  127.6 3.3 %collective-permute-start.43 = (bf16[96,768]{1,0:T(8,128)(2,1)S(1)}, bf16[96,768]{1,0:T(8,128)(2,1)S(1)}, u32[]{:S(2)}, u32[]{:S(2)}) collective-permute-start(bf16[96,768]{1,0:T(8,128)(2,1)S(1)} %get-tuple-element.341), channel_id=1, source_target_pairs={{0,8},{1,9},{2,10},{3,11},{4,12},{5,13},{6,14},{7,15},{8,0},{9,1},... | collective-permute-start | bytes 442376 | tf_op jit(solution)/shard_map/rs_down_z/ppermute | solution.py:492
  131.0 8.8 %attend_back.1 = (bf16[3,512,768]{2,1,0:T(8,128)(2,1)S(1)}, f32[12,768]{1,0:T(8,128)S(1)}) custom-call(s32[4]{0:T(128)S(1)} %copy-done.39, bf16[256,768]{1,0:T(8,128)(2,1)S(1)} %copy-done.31, bf16[512,768]{1,0:T(8,128)(2,1)S(1)} %copy-done.19, bf16[512,768]{1,0:T(8,128)(2,1)S(1)} %copy-done.20, bf16[256,768]{1,0:T(8,128)(2,1)S(1)} %get-tuple-element.260.context_grad, ...), custom_call_target="tpu_custom_call" | custom-call | flops 1610612736 | bytes 8687632 | tf_op jit(solution)/shard_map/attend_back/pallas_call | solution.py:595
  139.9 1.7 collective-permute-done.42
  141.8 1.0 collective-permute-start.45
  142.8 1.5 collective-permute-start.46
  144.3 3.4 %first_grad.1 = (f32[256,768]{1,0:T(8,128)S(1)}, f32[256,768]{1,0:T(8,128)S(1)}, f32[24,768]{1,0:T(8,128)S(1)}) custom-call(s32[4]{0:T(128)S(1)} %copy-done.39, bf16[256,768]{1,0:T(8,128)(2,1)S(1)} %copy-done.4, bf16[256,768]{1,0:T(8,128)(2,1)S(1)} %copy-done.9, bf16[3,512,768]{2,1,0:T(8,128)(2,1)S(1)} %get-tuple-element.267.grads, ...), custom_call_target="tpu_custom_call" | custom-call | flops 1509949440 | bytes 8515600 | tf_op jit(solution)/shard_map/first_grad/pallas_call | solution.py:595
  147.8 2.1 %collective-permute-start.48 = (bf16[96,768]{1,0:T(8,128)(2,1)S(1)}, bf16[96,768]{1,0:T(8,128)(2,1)S(1)}, u32[]{:S(2)}, u32[]{:S(2)}) collective-permute-start(bf16[96,768]{1,0:T(8,128)(2,1)S(1)} %get-tuple-element.276), channel_id=1, source_target_pairs={{0,24},{1,25},{2,26},{3,27},{4,28},{5,29},{6,30},{7,31},{8,16},{9,... | collective-permute-start | bytes 442376 | tf_op jit(solution)/shard_map/rs_down_z/ppermute | solution.py:492
  149.9 5.9 %qkv_grad.1 = (bf16[4,80,768]{2,1,0:T(8,128)(2,1)S(1)}, bf16[4,80,768]{2,1,0:T(8,128)(2,1)S(1)}, bf16[4,80,768]{2,1,0:T(8,128)(2,1)S(1)}, bf16[4,80,768]{2,1,0:T(8,128)(2,1)S(1)}) custom-call(s32[4]{0:T(128)S(1)} %copy-done.39, bf16[3,512,768]{2,1,0:T(8,128)(2,1)S(1)} %get-tuple-element.267.grads, ...), custom_call_target="tpu_custom_call" | custom-call | flops 1811939328 | bytes 10125328 | tf_op jit(solution)/shard_map/qkv_grad/pallas_call | solution.py:595
  155.9 2.2 %collective-permute-done.45 = bf16[4,128,768]{2,1,0:T(8,128)(2,1)S(1)} collective-permute-done((bf16[4,128,768]{2,1,0:T(8,128)(2,1)S(1)}, bf16[4,128,768]{2,1,0:T(8,128)(2,1)S(1)}, u32[]{:S(2)}, u32[]{:S(2)}) %collective-permute-start.45) | collective-permute-done | bytes 786464 | tf_op jit(solution)/shard_map/rs_up_1/ppermute | solution.py:492
  158.0 1.0 collective-permute-start.50
  159.4 3.3 %collective-permute-start.53 = (bf16[128,768]{1,0:T(8,128)(2,1)S(1)}, bf16[128,768]{1,0:T(8,128)(2,1)S(1)}, u32[]{:S(2)}, u32[]{:S(2)}) collective-permute-start(bf16[128,768]{1,0:T(8,128)(2,1)S(1)} %get-tuple-element.334), channel_id=1, source_target_pairs={{0,8},{1,9},{2,10},{3,11},{4,12},{5,13},{6,14},{7,15},{8,0},{9,1},... | collective-permute-start | bytes 589832 | tf_op jit(solution)/shard_map/rs_up_z/ppermute | solution.py:492
  162.7 1.0 collective-permute-start.52
  163.7 1.0 input_grad.1
  164.8 2.1 %collective-permute-done.50 = bf16[4,80,768]{2,1,0:T(8,128)(2,1)S(1)} collective-permute-done((bf16[4,80,768]{2,1,0:T(8,128)(2,1)S(1)}, bf16[4,80,768]{2,1,0:T(8,128)(2,1)S(1)}, u32[]{:S(2)}, u32[]{:S(2)}) %collective-permute-start.50) | collective-permute-done | bytes 491552 | tf_op jit(solution)/shard_map/rs_qkv_3/ppermute | solution.py:492
  167.0 1.0 collective-permute-start.51
  168.0 1.4 collective-permute-done.53
  169.4 6.3 %collective-permute-done.54 = bf16[128,768]{1,0:T(8,128)(2,1)S(1)} collective-permute-done((bf16[128,768]{1,0:T(8,128)(2,1)S(1)}, bf16[128,768]{1,0:T(8,128)(2,1)S(1)}, u32[]{:S(2)}, u32[]{:S(2)}) %collective-permute-start.54) | collective-permute-done | bytes 196640 | tf_op jit(solution)/shard_map/rs_up_z/ppermute | solution.py:492
  177.3 6.1 %finish.1 = f32[256,768]{1,0:T(8,128)} custom-call(s32[4]{0:T(128)} %pad_add_fusion.place, bf16[256,3072]{1,0:T(8,128)(2,1)} %copy-done.32, f32[256,768]{1,0:T(8,128)} %copy-done.10, f32[8,768]{1,0:T(8,128)} %get-tuple-element.215.vectors, bf16[4,96,768]{2,1,0:T(8,128)(2,1)} %copy-done.5, bf16[4,96,768]{2,1,0:T(8,128)(2,1)} %copy-done.23, ...), custom_call_target="tpu_custom_call" | custom-call | flops 1207959552 | bytes 7888912 | tf_op jit(solution)/shard_map/finish/pallas_call | solution.py:595
  184.2 3.2 %collective-permute-start.57 = (bf16[80,768]{1,0:T(8,128)(2,1)S(1)}, bf16[80,768]{1,0:T(8,128)(2,1)S(1)}, u32[]{:S(2)}, u32[]{:S(2)}) collective-permute-start(bf16[80,768]{1,0:T(8,128)(2,1)S(1)} %get-tuple-element.343), channel_id=1, source_target_pairs={{0,16},{1,17},{2,18},{3,19},{4,20},{5,21},{6,22},{7,23},{8,24},{9,... | collective-permute-start | bytes 368648 | tf_op jit(solution)/shard_map/rs_qkv_z/ppermute | solution.py:492
  188.7 6.3 %collective-permute-done.57.z2 = bf16[80,768]{1,0:T(8,128)(2,1)S(1)} collective-permute-done((bf16[80,768]{1,0:T(8,128)(2,1)S(1)}, bf16[80,768]{1,0:T(8,128)(2,1)S(1)}, u32[]{:S(2)}, u32[]{:S(2)}) %collective-permute-start.57) | collective-permute-done | bytes 122912 | tf_op jit(solution)/shard_map/rs_qkv_z/ppermute | solution.py:492
  196.4 1.1 last.1
  (208 shorter events, 17.8 us)
Async XLA Ops:
  2.6 16.5 %collective-permute-start = (bf16[80,768]{1,0:T(8,128)(2,1)}, bf16[80,768]{1,0:T(8,128)(2,1)S(1)}, u32[]{:S(2)}, u32[]{:S(2)}) collective-permute-start(bf16[80,768]{1,0:T(8,128)(2,1)} %get-tuple-element.174), channel_id=1, source_target_pairs={{0,8},{1,9},{2,10},{3,11},{4,12},{5,13},{6,14},{7,15},{8,0},{9,1},... | collective-permute-start | bytes 368648 | tf_op jit(solution)/shard_map/qkv_z/ppermute | solution.py:492
  5.6 13.5 %collective-permute-start.1 = (bf16[80,768]{1,0:T(8,128)(2,1)}, bf16[80,768]{1,0:T(8,128)(2,1)S(1)}, u32[]{:S(2)}, u32[]{:S(2)}) collective-permute-start(bf16[80,768]{1,0:T(8,128)(2,1)} %get-tuple-element.174), channel_id=1, source_target_pairs={{0,16},{1,17},{2,18},{3,19},{4,20},{5,21},{6,22},{7,23},{8,24},{9,... | collective-permute-start | bytes 368648 | tf_op jit(solution)/shard_map/qkv_z/ppermute | solution.py:492
  8.2 10.9 %collective-permute-start.2 = (bf16[80,768]{1,0:T(8,128)(2,1)}, bf16[80,768]{1,0:T(8,128)(2,1)S(1)}, u32[]{:S(2)}, u32[]{:S(2)}) collective-permute-start(bf16[80,768]{1,0:T(8,128)(2,1)} %get-tuple-element.174), channel_id=1, source_target_pairs={{0,24},{1,25},{2,26},{3,27},{4,28},{5,29},{6,30},{7,31},{8,16},{9,... | collective-permute-start | bytes 368648 | tf_op jit(solution)/shard_map/qkv_z/ppermute | solution.py:492
  8.2 10.9 %collective-permute-start.3 = (bf16[256,768]{1,0:T(8,128)(2,1)}, bf16[256,768]{1,0:T(8,128)(2,1)S(1)}, u32[]{:S(2)}, u32[]{:S(2)}) collective-permute-start(bf16[256,768]{1,0:T(8,128)(2,1)} %frames.3), channel_id=1, source_target_pairs={{0,1},{1,0},{2,3},{3,2},{4,5},{5,4},{6,7},{7,6},{8,9},{9,8},{10,11... | collective-permute-start | bytes 1179656 | tf_op jit(solution)/shard_map/frames_pack/ppermute | solution.py:492
  19.1 31.8 %copy-start.8 = (bf16[256,768]{1,0:T(8,128)(2,1)}, bf16[256,768]{1,0:T(8,128)(2,1)S(1)}, u32[]{:S(2)}) copy-start(bf16[256,768]{1,0:T(8,128)(2,1)S(1)} %collective-permute-done.3.other.mate_frames) | copy-start | bytes 1179652
  19.2 31.7 %copy-start.43 = (bf16[4,80,768]{2,1,0:T(8,128)(2,1)}, bf16[4,80,768]{2,1,0:T(8,128)(2,1)S(1)}, u32[]{:S(2)}) copy-start(bf16[4,80,768]{2,1,0:T(8,128)(2,1)S(1)} %pad_maximum_fusion.2.p0) | copy-start | bytes 1474564
  19.2 14.8 %collective-permute-start.4 = (bf16[4,80,768]{2,1,0:T(8,128)(2,1)S(1)}, bf16[4,80,768]{2,1,0:T(8,128)(2,1)S(1)}, u32[]{:S(2)}, u32[]{:S(2)}) collective-permute-start(bf16[4,80,768]{2,1,0:T(8,128)(2,1)S(1)} %pad_maximum_fusion.2.p0), channel_id=1, source_target_pairs={{0,1},{1,0},{2,6},{3,7},{4,5},{5,4},{6,2},{7,3},{8,9},{9,8},{10,14... | collective-permute-start | bytes 1474568 | tf_op jit(solution)/shard_map/qkv_1/ppermute | solution.py:492
  20.4 5.7 %collective-permute-start.7 = (bf16[256,768]{1,0:T(8,128)(2,1)S(1)}, bf16[256,768]{1,0:T(8,128)(2,1)S(1)}, u32[]{:S(2)}, u32[]{:S(2)}) collective-permute-start(bf16[256,768]{1,0:T(8,128)(2,1)S(1)} %copy-done.36), channel_id=1, source_target_pairs={{0,2},{1,3},{2,0},{3,1},{4,6},{5,7},{6,4},{7,5},{8,10},{9,11},{10,... | collective-permute-start | bytes 1179656 | tf_op jit(solution)/shard_map/twin/ppermute | solution.py:492
  20.4 11.3 %collective-permute-start.5 = (bf16[128,768]{1,0:T(8,128)(2,1)S(1)}, bf16[128,768]{1,0:T(8,128)(2,1)S(1)}, u32[]{:S(2)}, u32[]{:S(2)}) collective-permute-start(bf16[128,768]{1,0:T(8,128)(2,1)S(1)} %copy-done.51), channel_id=1, source_target_pairs={{0,8},{1,9},{2,10},{3,11},{4,12},{5,13},{6,14},{7,15},{8,0},{9,1},... | collective-permute-start | bytes 589832 | tf_op jit(solution)/shard_map/up_z/ppermute | solution.py:492
  21.8 12.3 %collective-permute-start.6 = (bf16[128,768]{1,0:T(8,128)(2,1)S(1)}, bf16[128,768]{1,0:T(8,128)(2,1)S(1)}, u32[]{:S(2)}, u32[]{:S(2)}) collective-permute-start(bf16[128,768]{1,0:T(8,128)(2,1)S(1)} %copy-done.51), channel_id=1, source_target_pairs={{0,16},{1,17},{2,18},{3,19},{4,20},{5,21},{6,22},{7,23},{8,24},{9,... | collective-permute-start | bytes 589832 | tf_op jit(solution)/shard_map/up_z/ppermute | solution.py:492
  24.5 13.4 %collective-permute-start.9 = (bf16[4,80,768]{2,1,0:T(8,128)(2,1)S(1)}, bf16[4,80,768]{2,1,0:T(8,128)(2,1)S(1)}, u32[]{:S(2)}, u32[]{:S(2)}) collective-permute-start(bf16[4,80,768]{2,1,0:T(8,128)(2,1)S(1)} %pad_maximum_fusion.2.p0), channel_id=1, source_target_pairs={{0,4},{1,5},{2,3},{3,2},{4,0},{5,1},{6,7},{7,6},{8,12},{9,13},{10,... | collective-permute-start | bytes 1474568 | tf_op jit(solution)/shard_map/qkv_2/ppermute | solution.py:492
  34.0 9.1 %collective-permute-start.10 = (bf16[4,80,768]{2,1,0:T(8,128)(2,1)S(1)}, bf16[4,80,768]{2,1,0:T(8,128)(2,1)S(1)}, u32[]{:S(2)}, u32[]{:S(2)}) collective-permute-start(bf16[4,80,768]{2,1,0:T(8,128)(2,1)S(1)} %collective-permute-done.4.p1), channel_id=1, source_target_pairs={{0,4},{1,5},{2,3},{3,2},{4,0},{5,1},{6,7},{7,6},{8,12},{9,13},{10,... | collective-permute-start | bytes 1474568 | tf_op jit(solution)/shard_map/qkv_3/ppermute | solution.py:492
  35.5 7.6 %collective-permute-start.8 = (bf16[128,768]{1,0:T(8,128)(2,1)S(1)}, bf16[128,768]{1,0:T(8,128)(2,1)S(1)}, u32[]{:S(2)}, u32[]{:S(2)}) collective-permute-start(bf16[128,768]{1,0:T(8,128)(2,1)S(1)} %copy-done.51), channel_id=1, source_target_pairs={{0,24},{1,25},{2,26},{3,27},{4,28},{5,29},{6,30},{7,31},{8,16},{9,... | collective-permute-start | bytes 589832 | tf_op jit(solution)/shard_map/up_z/ppermute | solution.py:492
  43.2 32.0 %copy-start.3 = (bf16[4,128,768]{2,1,0:T(8,128)(2,1)}, bf16[4,128,768]{2,1,0:T(8,128)(2,1)S(1)}, u32[]{:S(2)}) copy-start(bf16[4,128,768]{2,1,0:T(8,128)(2,1)S(1)} %pad_maximum_fusion.p0.u0) | copy-start | bytes 2359300
  43.2 16.5 %collective-permute-start.12 = (bf16[4,128,768]{2,1,0:T(8,128)(2,1)S(1)}, bf16[4,128,768]{2,1,0:T(8,128)(2,1)S(1)}, u32[]{:S(2)}, u32[]{:S(2)}) collective-permute-start(bf16[4,128,768]{2,1,0:T(8,128)(2,1)S(1)} %pad_maximum_fusion.p0.u0), channel_id=1, source_target_pairs={{0,1},{1,0},{2,6},{3,7},{4,5},{5,4},{6,2},{7,3},{8,9},{9,8},{10,14... | collective-permute-start | bytes 2359304 | tf_op jit(solution)/shard_map/up_1/ppermute | solution.py:492
  44.7 1.9 collective-permute-start.13
  44.7 4.1 %collective-permute-start.14 = (bf16[4,80,768]{2,1,0:T(8,128)(2,1)S(1)}, bf16[4,80,768]{2,1,0:T(8,128)(2,1)S(1)}, u32[]{:S(2)}, u32[]{:S(2)}) collective-permute-start(bf16[4,80,768]{2,1,0:T(8,128)(2,1)S(1)} %collective-permute-done.4.p1), channel_id=1, source_target_pairs={{0,2},{1,3},{2,0},{3,1},{4,6},{5,7},{6,4},{7,5},{8,10},{9,11},{10,... | collective-permute-start | bytes 1474568 | tf_op jit(solution)/shard_map/twin/ppermute | solution.py:492
  45.2 4.1 %collective-permute-start.15 = (bf16[4,80,768]{2,1,0:T(8,128)(2,1)S(1)}, bf16[4,80,768]{2,1,0:T(8,128)(2,1)S(1)}, u32[]{:S(2)}, u32[]{:S(2)}) collective-permute-start(bf16[4,80,768]{2,1,0:T(8,128)(2,1)S(1)} %collective-permute-done.9.p2), channel_id=1, source_target_pairs={{0,2},{1,3},{2,0},{3,1},{4,6},{5,7},{6,4},{7,5},{8,10},{9,11},{10,... | collective-permute-start | bytes 1474568 | tf_op jit(solution)/shard_map/twin/ppermute | solution.py:492
  45.2 5.6 %collective-permute-start.16 = (bf16[4,80,768]{2,1,0:T(8,128)(2,1)S(1)}, bf16[4,80,768]{2,1,0:T(8,128)(2,1)S(1)}, u32[]{:S(2)}, u32[]{:S(2)}) collective-permute-start(bf16[4,80,768]{2,1,0:T(8,128)(2,1)S(1)} %collective-permute-done.10.p3), channel_id=1, source_target_pairs={{0,2},{1,3},{2,0},{3,1},{4,6},{5,7},{6,4},{7,5},{8,10},{9,11},{10,... | collective-permute-start | bytes 1474568 | tf_op jit(solution)/shard_map/twin/ppermute | solution.py:492
  46.6 13.1 %collective-permute-start.17 = (bf16[96,768]{1,0:T(8,128)(2,1)S(1)}, bf16[96,768]{1,0:T(8,128)(2,1)S(1)}, u32[]{:S(2)}, u32[]{:S(2)}) collective-permute-start(bf16[96,768]{1,0:T(8,128)(2,1)S(1)} %copy-done.52), channel_id=1, source_target_pairs={{0,8},{1,9},{2,10},{3,11},{4,12},{5,13},{6,14},{7,15},{8,0},{9,1},... | collective-permute-start | bytes 442376 | tf_op jit(solution)/shard_map/down_z/ppermute | solution.py:492
  48.8 10.9 %collective-permute-start.18 = (bf16[96,768]{1,0:T(8,128)(2,1)S(1)}, bf16[96,768]{1,0:T(8,128)(2,1)S(1)}, u32[]{:S(2)}, u32[]{:S(2)}) collective-permute-start(bf16[96,768]{1,0:T(8,128)(2,1)S(1)} %copy-done.52), channel_id=1, source_target_pairs={{0,16},{1,17},{2,18},{3,19},{4,20},{5,21},{6,22},{7,23},{8,24},{9,... | collective-permute-start | bytes 442376 | tf_op jit(solution)/shard_map/down_z/ppermute | solution.py:492
  49.4 21.5 %collective-permute-start.11 = (bf16[4,128,768]{2,1,0:T(8,128)(2,1)S(1)}, bf16[4,128,768]{2,1,0:T(8,128)(2,1)S(1)}, u32[]{:S(2)}, u32[]{:S(2)}) collective-permute-start(bf16[4,128,768]{2,1,0:T(8,128)(2,1)S(1)} %pad_maximum_fusion.p0.u0), channel_id=1, source_target_pairs={{0,4},{1,5},{2,3},{3,2},{4,0},{5,1},{6,7},{7,6},{8,12},{9,13},{10,... | collective-permute-start | bytes 2359304 | tf_op jit(solution)/shard_map/up_2/ppermute | solution.py:492
  59.8 12.1 %collective-permute-start.19 = (bf16[4,128,768]{2,1,0:T(8,128)(2,1)S(1)}, bf16[4,128,768]{2,1,0:T(8,128)(2,1)S(1)}, u32[]{:S(2)}, u32[]{:S(2)}) collective-permute-start(bf16[4,128,768]{2,1,0:T(8,128)(2,1)S(1)} %collective-permute-done.12.p1.u1), channel_id=1, source_target_pairs={{0,4},{1,5},{2,3},{3,2},{4,0},{5,1},{6,7},{7,6},{8,12},{9,13},{10,... | collective-permute-start | bytes 2359304 | tf_op jit(solution)/shard_map/up_3/ppermute | solution.py:492
  60.5 13.0 %collective-permute-start.23 = (bf16[4,128,768]{2,1,0:T(8,128)(2,1)S(1)}, bf16[4,128,768]{2,1,0:T(8,128)(2,1)S(1)}, u32[]{:S(2)}, u32[]{:S(2)}) collective-permute-start(bf16[4,128,768]{2,1,0:T(8,128)(2,1)S(1)} %pad_maximum_fusion.p0.u0), channel_id=1, source_target_pairs={{0,2},{1,3},{2,0},{3,1},{4,6},{5,7},{6,4},{7,5},{8,10},{9,11},{10,... | collective-permute-start | bytes 2359304 | tf_op jit(solution)/shard_map/twin/ppermute | solution.py:492
  60.5 10.3 %collective-permute-start.20 = (bf16[96,768]{1,0:T(8,128)(2,1)S(1)}, bf16[96,768]{1,0:T(8,128)(2,1)S(1)}, u32[]{:S(2)}, u32[]{:S(2)}) collective-permute-start(bf16[96,768]{1,0:T(8,128)(2,1)S(1)} %copy-done.52), channel_id=1, source_target_pairs={{0,24},{1,25},{2,26},{3,27},{4,28},{5,29},{6,30},{7,31},{8,16},{9,... | collective-permute-start | bytes 442376 | tf_op jit(solution)/shard_map/down_z/ppermute | solution.py:492
  63.1 11.8 %collective-permute-start.24 = (bf16[4,128,768]{2,1,0:T(8,128)(2,1)S(1)}, bf16[4,128,768]{2,1,0:T(8,128)(2,1)S(1)}, u32[]{:S(2)}, u32[]{:S(2)}) collective-permute-start(bf16[4,128,768]{2,1,0:T(8,128)(2,1)S(1)} %collective-permute-done.12.p1.u1), channel_id=1, source_target_pairs={{0,2},{1,3},{2,0},{3,1},{4,6},{5,7},{6,4},{7,5},{8,10},{9,11},{10,... | collective-permute-start | bytes 2359304 | tf_op jit(solution)/shard_map/twin/ppermute | solution.py:492
  71.8 3.0 %collective-permute-start.25 = (bf16[4,128,768]{2,1,0:T(8,128)(2,1)S(1)}, bf16[4,128,768]{2,1,0:T(8,128)(2,1)S(1)}, u32[]{:S(2)}, u32[]{:S(2)}) collective-permute-start(bf16[4,128,768]{2,1,0:T(8,128)(2,1)S(1)} %collective-permute-done.11.p2.u2), channel_id=1, source_target_pairs={{0,2},{1,3},{2,0},{3,1},{4,6},{5,7},{6,4},{7,5},{8,10},{9,11},{10,... | collective-permute-start | bytes 2359304 | tf_op jit(solution)/shard_map/twin/ppermute | solution.py:492
  72.0 3.3 %collective-permute-start.26 = (bf16[4,128,768]{2,1,0:T(8,128)(2,1)S(1)}, bf16[4,128,768]{2,1,0:T(8,128)(2,1)S(1)}, u32[]{:S(2)}, u32[]{:S(2)}) collective-permute-start(bf16[4,128,768]{2,1,0:T(8,128)(2,1)S(1)} %collective-permute-done.19.p3.u3), channel_id=1, source_target_pairs={{0,2},{1,3},{2,0},{3,1},{4,6},{5,7},{6,4},{7,5},{8,10},{9,11},{10,... | collective-permute-start | bytes 2359304 | tf_op jit(solution)/shard_map/twin/ppermute | solution.py:492
  72.4 29.2 %copy-start.5 = (bf16[4,96,768]{2,1,0:T(8,128)(2,1)}, bf16[4,96,768]{2,1,0:T(8,128)(2,1)S(1)}, u32[]{:S(2)}) copy-start(bf16[4,96,768]{2,1,0:T(8,128)(2,1)S(1)} %pad_maximum_fusion.1.p0) | copy-start | bytes 1769476
  72.4 16.1 %collective-permute-start.21 = (bf16[4,96,768]{2,1,0:T(8,128)(2,1)S(1)}, bf16[4,96,768]{2,1,0:T(8,128)(2,1)S(1)}, u32[]{:S(2)}, u32[]{:S(2)}) collective-permute-start(bf16[4,96,768]{2,1,0:T(8,128)(2,1)S(1)} %pad_maximum_fusion.1.p0), channel_id=1, source_target_pairs={{0,1},{1,0},{2,6},{3,7},{4,5},{5,4},{6,2},{7,3},{8,9},{9,8},{10,14... | collective-permute-start | bytes 1769480 | tf_op jit(solution)/shard_map/down_1/ppermute | solution.py:492
  73.6 15.0 %collective-permute-start.22 = (bf16[4,96,768]{2,1,0:T(8,128)(2,1)S(1)}, bf16[4,96,768]{2,1,0:T(8,128)(2,1)S(1)}, u32[]{:S(2)}, u32[]{:S(2)}) collective-permute-start(bf16[4,96,768]{2,1,0:T(8,128)(2,1)S(1)} %pad_maximum_fusion.1.p0), channel_id=1, source_target_pairs={{0,4},{1,5},{2,3},{3,2},{4,0},{5,1},{6,7},{7,6},{8,12},{9,13},{10,... | collective-permute-start | bytes 1769480 | tf_op jit(solution)/shard_map/down_2/ppermute | solution.py:492
  88.5 3.4 %collective-permute-start.28 = (bf16[256,3072]{1,0:T(8,128)(2,1)S(1)}, bf16[256,3072]{1,0:T(8,128)(2,1)S(1)}, u32[]{:S(2)}, u32[]{:S(2)}) collective-permute-start(bf16[256,3072]{1,0:T(8,128)(2,1)S(1)} %get-tuple-element.222.active), channel_id=1, source_target_pairs={{0,2},{1,3},{2,0},{3,1},{4,6},{5,7},{6,4},{7,5},{8,10},{9,11},{10,... | collective-permute-start | bytes 4718600 | tf_op jit(solution)/shard_map/twin/ppermute | solution.py:492
  88.6 9.9 %collective-permute-start.27 = (bf16[4,96,768]{2,1,0:T(8,128)(2,1)S(1)}, bf16[4,96,768]{2,1,0:T(8,128)(2,1)S(1)}, u32[]{:S(2)}, u32[]{:S(2)}) collective-permute-start(bf16[4,96,768]{2,1,0:T(8,128)(2,1)S(1)} %collective-permute-done.21.p1), channel_id=1, source_target_pairs={{0,4},{1,5},{2,3},{3,2},{4,0},{5,1},{6,7},{7,6},{8,12},{9,13},{10,... | collective-permute-start | bytes 1769480 | tf_op jit(solution)/shard_map/down_3/ppermute | solution.py:492
  89.7 9.4 %collective-permute-start.31 = (bf16[4,96,768]{2,1,0:T(8,128)(2,1)S(1)}, bf16[4,96,768]{2,1,0:T(8,128)(2,1)S(1)}, u32[]{:S(2)}, u32[]{:S(2)}) collective-permute-start(bf16[4,96,768]{2,1,0:T(8,128)(2,1)S(1)} %pad_maximum_fusion.1.p0), channel_id=1, source_target_pairs={{0,2},{1,3},{2,0},{3,1},{4,6},{5,7},{6,4},{7,5},{8,10},{9,11},{10,... | collective-permute-start | bytes 1769480 | tf_op jit(solution)/shard_map/twin/ppermute | solution.py:492
  89.7 10.4 %collective-permute-start.32 = (bf16[4,96,768]{2,1,0:T(8,128)(2,1)S(1)}, bf16[4,96,768]{2,1,0:T(8,128)(2,1)S(1)}, u32[]{:S(2)}, u32[]{:S(2)}) collective-permute-start(bf16[4,96,768]{2,1,0:T(8,128)(2,1)S(1)} %collective-permute-done.21.p1), channel_id=1, source_target_pairs={{0,2},{1,3},{2,0},{3,1},{4,6},{5,7},{6,4},{7,5},{8,10},{9,11},{10,... | collective-permute-start | bytes 1769480 | tf_op jit(solution)/shard_map/twin/ppermute | solution.py:492
  90.2 10.9 %collective-permute-start.33 = (bf16[4,96,768]{2,1,0:T(8,128)(2,1)S(1)}, bf16[4,96,768]{2,1,0:T(8,128)(2,1)S(1)}, u32[]{:S(2)}, u32[]{:S(2)}) collective-permute-start(bf16[4,96,768]{2,1,0:T(8,128)(2,1)S(1)} %collective-permute-done.22.p2), channel_id=1, source_target_pairs={{0,2},{1,3},{2,0},{3,1},{4,6},{5,7},{6,4},{7,5},{8,10},{9,11},{10,... | collective-permute-start | bytes 1769480 | tf_op jit(solution)/shard_map/twin/ppermute | solution.py:492
  98.5 2.6 %collective-permute-start.34 = (bf16[4,96,768]{2,1,0:T(8,128)(2,1)S(1)}, bf16[4,96,768]{2,1,0:T(8,128)(2,1)S(1)}, u32[]{:S(2)}, u32[]{:S(2)}) collective-permute-start(bf16[4,96,768]{2,1,0:T(8,128)(2,1)S(1)} %collective-permute-done.27.p3), channel_id=1, source_target_pairs={{0,2},{1,3},{2,0},{3,1},{4,6},{5,7},{6,4},{7,5},{8,10},{9,11},{10,... | collective-permute-start | bytes 1769480 | tf_op jit(solution)/shard_map/twin/ppermute | solution.py:492
  98.5 15.1 %collective-permute-start.37 = (bf16[512,768]{1,0:T(8,128)(2,1)S(1)}, bf16[512,768]{1,0:T(8,128)(2,1)S(1)}, u32[]{:S(2)}, u32[]{:S(2)}) collective-permute-start(bf16[512,768]{1,0:T(8,128)(2,1)S(1)} %copy-done.33), channel_id=1, source_target_pairs={{0,2},{1,3},{2,0},{3,1},{4,6},{5,7},{6,4},{7,5},{8,10},{9,11},{10,... | collective-permute-start | bytes 2359304 | tf_op jit(solution)/shard_map/twin/ppermute | solution.py:492
  99.1 14.6 %collective-permute-start.29 = (bf16[4,96,768]{2,1,0:T(8,128)(2,1)S(1)}, bf16[4,96,768]{2,1,0:T(8,128)(2,1)S(1)}, u32[]{:S(2)}, u32[]{:S(2)}) collective-permute-start(bf16[4,96,768]{2,1,0:T(8,128)(2,1)S(1)} %get-tuple-element.230), channel_id=1, source_target_pairs={{0,4},{1,5},{2,3},{3,2},{4,0},{5,1},{6,7},{7,6},{8,12},{9,13},{10,... | collective-permute-start | bytes 1769480 | tf_op jit(solution)/shard_map/rs_down_3/ppermute | solution.py:492
  100.1 15.2 %collective-permute-start.30 = (bf16[4,96,768]{2,1,0:T(8,128)(2,1)S(1)}, bf16[4,96,768]{2,1,0:T(8,128)(2,1)S(1)}, u32[]{:S(2)}, u32[]{:S(2)}) collective-permute-start(bf16[4,96,768]{2,1,0:T(8,128)(2,1)S(1)} %get-tuple-element.231), channel_id=1, source_target_pairs={{0,4},{1,5},{2,3},{3,2},{4,0},{5,1},{6,7},{7,6},{8,12},{9,13},{10,... | collective-permute-start | bytes 1769480 | tf_op jit(solution)/shard_map/rs_down_2/ppermute | solution.py:492
  101.1 12.5 %collective-permute-start.35 = (bf16[256,768]{1,0:T(8,128)(2,1)S(1)}, bf16[256,768]{1,0:T(8,128)(2,1)S(1)}, u32[]{:S(2)}, u32[]{:S(2)}) collective-permute-start(bf16[256,768]{1,0:T(8,128)(2,1)S(1)} %get-tuple-element.239.context), channel_id=1, source_target_pairs={{0,2},{1,3},{2,0},{3,1},{4,6},{5,7},{6,4},{7,5},{8,10},{9,11},{10,... | collective-permute-start | bytes 1179656 | tf_op jit(solution)/shard_map/twin/ppermute | solution.py:492
  101.1 12.5 %collective-permute-start.36 = (bf16[256,768]{1,0:T(8,128)(2,1)S(1)}, bf16[256,768]{1,0:T(8,128)(2,1)S(1)}, u32[]{:S(2)}, u32[]{:S(2)}) collective-permute-start(bf16[256,768]{1,0:T(8,128)(2,1)S(1)} %get-tuple-element.240.second), channel_id=1, source_target_pairs={{0,2},{1,3},{2,0},{3,1},{4,6},{5,7},{6,4},{7,5},{8,10},{9,11},{10,... | collective-permute-start | bytes 1179656 | tf_op jit(solution)/shard_map/twin/ppermute | solution.py:492
  115.3 4.0 %collective-permute-start.39 = (bf16[256,3072]{1,0:T(8,128)(2,1)}, bf16[256,3072]{1,0:T(8,128)(2,1)S(1)}, u32[]{:S(2)}, u32[]{:S(2)}) collective-permute-start(bf16[256,3072]{1,0:T(8,128)(2,1)} %get-tuple-element.245.hidden), channel_id=1, source_target_pairs={{0,2},{1,3},{2,0},{3,1},{4,6},{5,7},{6,4},{7,5},{8,10},{9,11},{10,... | collective-permute-start | bytes 4718600 | tf_op jit(solution)/shard_map/twin/ppermute | solution.py:492
  115.4 9.9 %collective-permute-start.38 = (bf16[4,96,768]{2,1,0:T(8,128)(2,1)S(1)}, bf16[4,96,768]{2,1,0:T(8,128)(2,1)S(1)}, u32[]{:S(2)}, u32[]{:S(2)}) collective-permute-start(bf16[4,96,768]{2,1,0:T(8,128)(2,1)S(1)} %add_convert_fusion.1), channel_id=1, source_target_pairs={{0,1},{1,0},{2,6},{3,7},{4,5},{5,4},{6,2},{7,3},{8,9},{9,8},{10,14... | collective-permute-start | bytes 1769480 | tf_op jit(solution)/shard_map/rs_down_1/ppermute | solution.py:492
  116.4 2.8 %collective-permute-start.40 = (bf16[256,768]{1,0:T(8,128)(2,1)S(1)}, bf16[256,768]{1,0:T(8,128)(2,1)S(1)}, u32[]{:S(2)}, u32[]{:S(2)}) collective-permute-start(bf16[256,768]{1,0:T(8,128)(2,1)S(1)} %get-tuple-element.247.branch), channel_id=1, source_target_pairs={{0,2},{1,3},{2,0},{3,1},{4,6},{5,7},{6,4},{7,5},{8,10},{9,11},{10,... | collective-permute-start | bytes 1179656 | tf_op jit(solution)/shard_map/twin/ppermute | solution.py:492
  125.4 16.2 %collective-permute-start.41 = (bf16[4,128,768]{2,1,0:T(8,128)(2,1)S(1)}, bf16[4,128,768]{2,1,0:T(8,128)(2,1)S(1)}, u32[]{:S(2)}, u32[]{:S(2)}) collective-permute-start(bf16[4,128,768]{2,1,0:T(8,128)(2,1)S(1)} %get-tuple-element.255), channel_id=1, source_target_pairs={{0,4},{1,5},{2,3},{3,2},{4,0},{5,1},{6,7},{7,6},{8,12},{9,13},{10,... | collective-permute-start | bytes 2359304 | tf_op jit(solution)/shard_map/rs_up_3/ppermute | solution.py:492
  126.4 15.2 %collective-permute-start.42 = (bf16[2,128,768]{2,1,0:T(8,128)(2,1)S(1)}, bf16[2,128,768]{2,1,0:T(8,128)(2,1)S(1)}, u32[]{:S(2)}, u32[]{:S(2)}) collective-permute-start(bf16[2,128,768]{2,1,0:T(8,128)(2,1)S(1)} %get-tuple-element.256), channel_id=1, source_target_pairs={{0,4},{1,5},{2,3},{3,2},{4,0},{5,1},{6,7},{7,6},{8,12},{9,13},{10,... | collective-permute-start | bytes 1179656 | tf_op jit(solution)/shard_map/rs_up_2a/ppermute | solution.py:492
  127.6 12.2 %collective-permute-start.43 = (bf16[96,768]{1,0:T(8,128)(2,1)S(1)}, bf16[96,768]{1,0:T(8,128)(2,1)S(1)}, u32[]{:S(2)}, u32[]{:S(2)}) collective-permute-start(bf16[96,768]{1,0:T(8,128)(2,1)S(1)} %get-tuple-element.341), channel_id=1, source_target_pairs={{0,8},{1,9},{2,10},{3,11},{4,12},{5,13},{6,14},{7,15},{8,0},{9,1},... | collective-permute-start | bytes 442376 | tf_op jit(solution)/shard_map/rs_down_z/ppermute | solution.py:492
  131.0 8.9 %collective-permute-start.44 = (bf16[96,768]{1,0:T(8,128)(2,1)S(1)}, bf16[96,768]{1,0:T(8,128)(2,1)S(1)}, u32[]{:S(2)}, u32[]{:S(2)}) collective-permute-start(bf16[96,768]{1,0:T(8,128)(2,1)S(1)} %get-tuple-element.340), channel_id=1, source_target_pairs={{0,16},{1,17},{2,18},{3,19},{4,20},{5,21},{6,22},{7,23},{8,24},{9,... | collective-permute-start | bytes 442376 | tf_op jit(solution)/shard_map/rs_down_z/ppermute | solution.py:492
  141.6 6.2 %collective-permute-start.47 = (bf16[3,512,768]{2,1,0:T(8,128)(2,1)S(1)}, bf16[3,512,768]{2,1,0:T(8,128)(2,1)S(1)}, u32[]{:S(2)}, u32[]{:S(2)}) collective-permute-start(bf16[3,512,768]{2,1,0:T(8,128)(2,1)S(1)} %get-tuple-element.267.grads), channel_id=1, source_target_pairs={{0,2},{1,3},{2,0},{3,1},{4,6},{5,7},{6,4},{7,5},{8,10},{9,11},{10,... | collective-permute-start | bytes 7077896 | tf_op jit(solution)/shard_map/twin/ppermute | solution.py:492
  141.8 16.3 %collective-permute-start.45 = (bf16[4,128,768]{2,1,0:T(8,128)(2,1)S(1)}, bf16[4,128,768]{2,1,0:T(8,128)(2,1)S(1)}, u32[]{:S(2)}, u32[]{:S(2)}) collective-permute-start(bf16[4,128,768]{2,1,0:T(8,128)(2,1)S(1)} %add_convert_fusion), channel_id=1, source_target_pairs={{0,1},{1,0},{2,6},{3,7},{4,5},{5,4},{6,2},{7,3},{8,9},{9,8},{10,14... | collective-permute-start | bytes 2359304 | tf_op jit(solution)/shard_map/rs_up_1/ppermute | solution.py:492
  142.8 13.1 %collective-permute-start.46 = (bf16[2,128,768]{2,1,0:T(8,128)(2,1)S(1)}, bf16[2,128,768]{2,1,0:T(8,128)(2,1)S(1)}, u32[]{:S(2)}, u32[]{:S(2)}) collective-permute-start(bf16[2,128,768]{2,1,0:T(8,128)(2,1)S(1)} %get-tuple-element.264), channel_id=1, source_target_pairs={{0,4},{1,5},{2,3},{3,2},{4,0},{5,1},{6,7},{7,6},{8,12},{9,13},{10,... | collective-permute-start | bytes 1179656 | tf_op jit(solution)/shard_map/rs_up_2b/ppermute | solution.py:492
  147.7 2.1 %collective-permute-start.49 = (f32[24,768]{1,0:T(8,128)S(1)}, f32[24,768]{1,0:T(8,128)S(1)}, u32[]{:S(2)}, u32[]{:S(2)}) collective-permute-start(f32[24,768]{1,0:T(8,128)S(1)} %get-tuple-element.275.small_own), channel_id=1, source_target_pairs={{0,2},{1,3},{2,0},{3,1},{4,6},{5,7},{6,4},{7,5},{8,10},{9,11},{10,... | collective-permute-start | bytes 221192 | tf_op jit(solution)/shard_map/twin/ppermute | solution.py:492
  147.8 10.2 %collective-permute-start.48 = (bf16[96,768]{1,0:T(8,128)(2,1)S(1)}, bf16[96,768]{1,0:T(8,128)(2,1)S(1)}, u32[]{:S(2)}, u32[]{:S(2)}) collective-permute-start(bf16[96,768]{1,0:T(8,128)(2,1)S(1)} %get-tuple-element.276), channel_id=1, source_target_pairs={{0,24},{1,25},{2,26},{3,27},{4,28},{5,29},{6,30},{7,31},{8,16},{9,... | collective-permute-start | bytes 442376 | tf_op jit(solution)/shard_map/rs_down_z/ppermute | solution.py:492
  158.0 8.8 %collective-permute-start.50 = (bf16[4,80,768]{2,1,0:T(8,128)(2,1)S(1)}, bf16[4,80,768]{2,1,0:T(8,128)(2,1)S(1)}, u32[]{:S(2)}, u32[]{:S(2)}) collective-permute-start(bf16[4,80,768]{2,1,0:T(8,128)(2,1)S(1)} %get-tuple-element.284), channel_id=1, source_target_pairs={{0,4},{1,5},{2,3},{3,2},{4,0},{5,1},{6,7},{7,6},{8,12},{9,13},{10,... | collective-permute-start | bytes 1474568 | tf_op jit(solution)/shard_map/rs_qkv_3/ppermute | solution.py:492
  159.4 10.0 %collective-permute-start.53 = (bf16[128,768]{1,0:T(8,128)(2,1)S(1)}, bf16[128,768]{1,0:T(8,128)(2,1)S(1)}, u32[]{:S(2)}, u32[]{:S(2)}) collective-permute-start(bf16[128,768]{1,0:T(8,128)(2,1)S(1)} %get-tuple-element.334), channel_id=1, source_target_pairs={{0,8},{1,9},{2,10},{3,11},{4,12},{5,13},{6,14},{7,15},{8,0},{9,1},... | collective-permute-start | bytes 589832 | tf_op jit(solution)/shard_map/rs_up_z/ppermute | solution.py:492
  162.7 13.0 %collective-permute-start.54 = (bf16[128,768]{1,0:T(8,128)(2,1)S(1)}, bf16[128,768]{1,0:T(8,128)(2,1)S(1)}, u32[]{:S(2)}, u32[]{:S(2)}) collective-permute-start(bf16[128,768]{1,0:T(8,128)(2,1)S(1)} %get-tuple-element.337), channel_id=1, source_target_pairs={{0,16},{1,17},{2,18},{3,19},{4,20},{5,21},{6,22},{7,23},{8,24},{9,... | collective-permute-start | bytes 589832 | tf_op jit(solution)/shard_map/rs_up_z/ppermute | solution.py:492
  162.7 20.6 %collective-permute-start.52 = (bf16[4,80,768]{2,1,0:T(8,128)(2,1)S(1)}, bf16[4,80,768]{2,1,0:T(8,128)(2,1)S(1)}, u32[]{:S(2)}, u32[]{:S(2)}) collective-permute-start(bf16[4,80,768]{2,1,0:T(8,128)(2,1)S(1)} %get-tuple-element.294), channel_id=1, source_target_pairs={{0,4},{1,5},{2,3},{3,2},{4,0},{5,1},{6,7},{7,6},{8,12},{9,13},{10,... | collective-permute-start | bytes 1474568 | tf_op jit(solution)/shard_map/rs_qkv_2/ppermute | solution.py:492
  167.0 16.4 %collective-permute-start.51 = (bf16[4,80,768]{2,1,0:T(8,128)(2,1)S(1)}, bf16[4,80,768]{2,1,0:T(8,128)(2,1)S(1)}, u32[]{:S(2)}, u32[]{:S(2)}) collective-permute-start(bf16[4,80,768]{2,1,0:T(8,128)(2,1)S(1)} %add_convert_fusion.2), channel_id=1, source_target_pairs={{0,1},{1,0},{2,6},{3,7},{4,5},{5,4},{6,2},{7,3},{8,9},{9,8},{10,14... | collective-permute-start | bytes 1474568 | tf_op jit(solution)/shard_map/rs_qkv_1/ppermute | solution.py:492
  175.7 7.6 %collective-permute-start.55 = (bf16[128,768]{1,0:T(8,128)(2,1)S(1)}, bf16[128,768]{1,0:T(8,128)(2,1)S(1)}, u32[]{:S(2)}, u32[]{:S(2)}) collective-permute-start(bf16[128,768]{1,0:T(8,128)(2,1)S(1)} %get-tuple-element.298), channel_id=1, source_target_pairs={{0,24},{1,25},{2,26},{3,27},{4,28},{5,29},{6,30},{7,31},{8,16},{9,... | collective-permute-start | bytes 589832 | tf_op jit(solution)/shard_map/rs_up_z/ppermute | solution.py:492
  183.6 12.8 %collective-permute-start.59 = (bf16[256,768]{1,0:T(8,128)(2,1)S(1)}, bf16[256,768]{1,0:T(8,128)(2,1)S(1)}, u32[]{:S(2)}, u32[]{:S(2)}) collective-permute-start(bf16[256,768]{1,0:T(8,128)(2,1)S(1)} %get-tuple-element.313), channel_id=1, source_target_pairs={{0,1},{1,0},{2,3},{3,2},{4,5},{5,4},{6,7},{7,6},{8,9},{9,8},{10,11... | collective-permute-start | bytes 1179656 | tf_op jit(solution)/shard_map/grad_pack/ppermute | solution.py:492
  183.8 4.9 %collective-permute-start.56 = (bf16[80,768]{1,0:T(8,128)(2,1)S(1)}, bf16[80,768]{1,0:T(8,128)(2,1)S(1)}, u32[]{:S(2)}, u32[]{:S(2)}) collective-permute-start(bf16[80,768]{1,0:T(8,128)(2,1)S(1)} %get-tuple-element.344), channel_id=1, source_target_pairs={{0,8},{1,9},{2,10},{3,11},{4,12},{5,13},{6,14},{7,15},{8,0},{9,1},... | collective-permute-start | bytes 368648 | tf_op jit(solution)/shard_map/rs_qkv_z/ppermute | solution.py:492
  184.2 10.8 %collective-permute-start.57 = (bf16[80,768]{1,0:T(8,128)(2,1)S(1)}, bf16[80,768]{1,0:T(8,128)(2,1)S(1)}, u32[]{:S(2)}, u32[]{:S(2)}) collective-permute-start(bf16[80,768]{1,0:T(8,128)(2,1)S(1)} %get-tuple-element.343), channel_id=1, source_target_pairs={{0,16},{1,17},{2,18},{3,19},{4,20},{5,21},{6,22},{7,23},{8,24},{9,... | collective-permute-start | bytes 368648 | tf_op jit(solution)/shard_map/rs_qkv_z/ppermute | solution.py:492
  187.4 7.6 %collective-permute-start.58 = (bf16[80,768]{1,0:T(8,128)(2,1)S(1)}, bf16[80,768]{1,0:T(8,128)(2,1)S(1)}, u32[]{:S(2)}, u32[]{:S(2)}) collective-permute-start(bf16[80,768]{1,0:T(8,128)(2,1)S(1)} %get-tuple-element.342), channel_id=1, source_target_pairs={{0,24},{1,25},{2,26},{3,27},{4,28},{5,29},{6,30},{7,31},{8,16},{9,... | collective-permute-start | bytes 368648 | tf_op jit(solution)/shard_map/rs_qkv_z/ppermute | solution.py:492
  (50 other events, 432.5 us)

commit v2 on v1

--- a/solution.py
+++ b/solution.py
@@ -1325,7 +1325,7 @@
         2 * shard_len * width * (ff + width),
         name="up_grad", limit=28,
     )
-    down_one, up_parts = joined(down_one, up_parts)
+    down_one = tied(down_one, up_parts[0])
     turned = shift(up_parts[4], OTHER_SIDE, "rs_up_3")
     up_two = shift(up_parts[2], OTHER_SIDE, "rs_up_2a")
     down_sum = down_sum + down_one.astype(F32)
@@ -1340,7 +1340,7 @@
         [shape(3, span, width), shape(H, span + shard_len, kind=F32)],
         [pl.BlockSpec((3, span, pair_lanes), lambda n: (0, 0, n)), whole(H, span + shard_len)],
         [],
-        (place, queries, keys, values, tied(context_grad, up_parts[0]), mixed, probs),
+        (place, queries, keys, values, tied(context_grad, up_parts[0], down_sum), mixed, probs),
         16 * shard_len * span * width,
         grid=(pairs,),
         name="attend_back", limit=24,
@@ -1383,7 +1383,7 @@
         2 * shard_len * width * 6 * width,
         name="qkv_grad", limit=28,
     )
-    up_one, up_rest, down_z, qkv_parts = joined(up_one, up_rest, down_z, qkv_parts)
+    up_one, up_rest, down_z = tied((up_one, up_rest, down_z), qkv_parts[0])
     turned = shift(qkv_parts[3], OTHER_SIDE, "rs_qkv_3")
     qkv_two = shift(qkv_parts[2], OTHER_SIDE, "rs_qkv_2")
     up_sum = [

time: 198 us -> 195 us (0.985)
  waiting for transfers between devices: 54.7 us -> 50.4 us
    ppermute x60, waiting for transfers between devices: 54.7 us -> 50.4 us  [shift(): return lax.ppermute(array, AXES, route(move))]
  transfers between devices with their start and end apart: 60 -> 60, of which waited for: 19 -> 20; matrix products, arithmetic and copies ran while one was open for 4% -> 4% of each run, Pallas kernels for 33% -> 34%
where the time goes in v2:
time: 195 us
  Pallas kernels  68.7 us (35%)
  starting transfers between devices  60.3 us (31%)
  waiting for transfers between devices  50.4 us (26%)
  other arithmetic  6.4 us (3%)
  local copies, waits for them, and re-layouts  6.18 us (3%)
    pallas_call x14, Pallas kernels, call(): pl.pallas_call(kernel, out_shape=outs, in_specs=in_specs, out_specs=out_s...  68.7 us
    ppermute x60, starting transfers between devices, shift(): return lax.ppermute(array, AXES, route(move))  60.3 us
    ppermute x60, waiting for transfers between devices, shift(): return lax.ppermute(array, AXES, route(move))  50.4 us
    unnamed x108, local copies, waits for them, and re-layouts  4.71 us
  transfers between devices with their start and end apart: 60, of which 20 were waited for; matrix products, arithmetic and copies ran while one was open for 4% of the time, Pallas kernels for 34%

profile of v2, /device:TPU:0, one launch (start us, length us, event | category | flops | bytes accessed | tf_op | source)
XLA Modules:
  0.0 194.7 jit_solution(12869896891622435406)
XLA Ops:
  0.7 1.9 pack.1
  2.6 3.0 %collective-permute-start = (bf16[80,768]{1,0:T(8,128)(2,1)}, bf16[80,768]{1,0:T(8,128)(2,1)S(1)}, u32[]{:S(2)}, u32[]{:S(2)}) collective-permute-start(bf16[80,768]{1,0:T(8,128)(2,1)} %get-tuple-element.163), channel_id=1, source_target_pairs={{0,8},{1,9},{2,10},{3,11},{4,12},{5,13},{6,14},{7,15},{8,0},{9,1},... | collective-permute-start | bytes 368648 | tf_op jit(solution)/shard_map/qkv_z/ppermute | solution.py:492
  5.6 2.6 %collective-permute-start.1 = (bf16[80,768]{1,0:T(8,128)(2,1)}, bf16[80,768]{1,0:T(8,128)(2,1)S(1)}, u32[]{:S(2)}, u32[]{:S(2)}) collective-permute-start(bf16[80,768]{1,0:T(8,128)(2,1)} %get-tuple-element.163), channel_id=1, source_target_pairs={{0,16},{1,17},{2,18},{3,19},{4,20},{5,21},{6,22},{7,23},{8,24},{9,... | collective-permute-start | bytes 368648 | tf_op jit(solution)/shard_map/qkv_z/ppermute | solution.py:492
  8.2 1.7 collective-permute-start.3
  10.0 1.5 convert_convert_fusion.wide_four
  11.5 1.1 convert_convert_fusion.1.wide_two
  12.6 0.9 convert_convert_fusion.2.wide_one
  13.5 1.0 fusion.2.curve
  14.5 4.0 %bias.1 = bf16[12,256,512]{2,1,0:T(8,128)(2,1)} custom-call(f32[12,768]{1,0:T(8,128)} %fusion.2.curve), custom_call_target="tpu_custom_call" | custom-call | bytes 3182592 | tf_op jit(solution)/shard_map/bias/pallas_call | solution.py:595
  19.2 1.1 collective-permute-start.4
  20.4 1.4 collective-permute-start.5
  21.8 2.8 %collective-permute-start.6 = (bf16[128,768]{1,0:T(8,128)(2,1)S(1)}, bf16[128,768]{1,0:T(8,128)(2,1)S(1)}, u32[]{:S(2)}, u32[]{:S(2)}) collective-permute-start(bf16[128,768]{1,0:T(8,128)(2,1)S(1)} %copy-done.51), channel_id=1, source_target_pairs={{0,16},{1,17},{2,18},{3,19},{4,20},{5,21},{6,22},{7,23},{8,24},{9,... | collective-permute-start | bytes 589832 | tf_op jit(solution)/shard_map/up_z/ppermute | solution.py:492
  24.5 1.5 collective-permute-start.9
  26.8 4.8 %collective-permute-done.5 = bf16[128,768]{1,0:T(8,128)(2,1)S(1)} collective-permute-done((bf16[128,768]{1,0:T(8,128)(2,1)S(1)}, bf16[128,768]{1,0:T(8,128)(2,1)S(1)}, u32[]{:S(2)}, u32[]{:S(2)}) %collective-permute-start.5) | collective-permute-done | bytes 196640 | tf_op jit(solution)/shard_map/up_z/ppermute | solution.py:492
  31.7 2.4 %collective-permute-done.6 = bf16[128,768]{1,0:T(8,128)(2,1)S(1)} collective-permute-done((bf16[128,768]{1,0:T(8,128)(2,1)S(1)}, bf16[128,768]{1,0:T(8,128)(2,1)S(1)}, u32[]{:S(2)}, u32[]{:S(2)}) %collective-permute-start.6) | collective-permute-done | bytes 196640 | tf_op jit(solution)/shard_map/up_z/ppermute | solution.py:492
  34.0 1.5 collective-permute-start.10
  35.5 2.4 %collective-permute-start.8 = (bf16[128,768]{1,0:T(8,128)(2,1)S(1)}, bf16[128,768]{1,0:T(8,128)(2,1)S(1)}, u32[]{:S(2)}, u32[]{:S(2)}) collective-permute-start(bf16[128,768]{1,0:T(8,128)(2,1)S(1)} %copy-done.51), channel_id=1, source_target_pairs={{0,24},{1,25},{2,26},{3,27},{4,28},{5,29},{6,30},{7,31},{8,16},{9,... | collective-permute-start | bytes 589832 | tf_op jit(solution)/shard_map/up_z/ppermute | solution.py:492
  37.9 5.2 %collective-permute-done.8 = bf16[128,768]{1,0:T(8,128)(2,1)S(1)} collective-permute-done((bf16[128,768]{1,0:T(8,128)(2,1)S(1)}, bf16[128,768]{1,0:T(8,128)(2,1)S(1)}, u32[]{:S(2)}, u32[]{:S(2)}) %collective-permute-start.8) | collective-permute-done | bytes 196640 | tf_op jit(solution)/shard_map/up_z/ppermute | solution.py:492
  43.2 1.5 collective-permute-start.12
  46.6 2.2 %collective-permute-start.17 = (bf16[96,768]{1,0:T(8,128)(2,1)S(1)}, bf16[96,768]{1,0:T(8,128)(2,1)S(1)}, u32[]{:S(2)}, u32[]{:S(2)}) collective-permute-start(bf16[96,768]{1,0:T(8,128)(2,1)S(1)} %copy-done.52), channel_id=1, source_target_pairs={{0,8},{1,9},{2,10},{3,11},{4,12},{5,13},{6,14},{7,15},{8,0},{9,1},... | collective-permute-start | bytes 442376 | tf_op jit(solution)/shard_map/down_z/ppermute | solution.py:492
  49.4 1.5 collective-permute-start.11
  51.7 8.0 %project.1 = (bf16[512,768]{1,0:T(8,128)(2,1)}, bf16[256,768]{1,0:T(8,128)(2,1)}, bf16[512,768]{1,0:T(8,128)(2,1)}, bf16[512,768]{1,0:T(8,128)(2,1)}, f32[8,768]...) custom-call(s32[4]{0:T(128)} %pad_add_fusion.place, bf16[256,768]{1,0:T(8,128)(2,1)} %frames.3, ...), custom_call_target="tpu_custom_call" | custom-call | flops 1509949440 | bytes 12861456 | tf_op jit(solution)/shard_map/project/pallas_call | solution.py:595
  60.5 2.5 %collective-permute-start.20 = (bf16[96,768]{1,0:T(8,128)(2,1)S(1)}, bf16[96,768]{1,0:T(8,128)(2,1)S(1)}, u32[]{:S(2)}, u32[]{:S(2)}) collective-permute-start(bf16[96,768]{1,0:T(8,128)(2,1)S(1)} %copy-done.52), channel_id=1, source_target_pairs={{0,24},{1,25},{2,26},{3,27},{4,28},{5,29},{6,30},{7,31},{8,16},{9,... | collective-permute-start | bytes 442376 | tf_op jit(solution)/shard_map/down_z/ppermute | solution.py:492
  63.3 7.5 %attend.1 = (bf16[12,256,512]{2,1,0:T(8,128)(2,1)}, f32[256,768]{1,0:T(8,128)}) custom-call(s32[4]{0:T(128)} %pad_add_fusion.place, s32[1,4]{1,0:T(1,128)} %lengths.1, bf16[256,768]{1,0:T(8,128)(2,1)} %get-tuple-element.192.queries, bf16[512,768]{1,0:T(8,128)(2,1)} %get-tuple-element.193.keys, bf16[512,768]{1,0:T(8,128)(2,1)} %get-tuple-element.194.values, ...), custom_call_target="tpu_custom_call" | custom-call | flops 805306368 | bytes 9053216 | tf_op jit(solution)/shard_map/attend/pallas_call | solution.py:595
  70.8 1.0 collective-permute-done.19.p3.u3
  72.4 1.2 collective-permute-start.21
  73.6 1.3 collective-permute-start.22
  75.3 4.0 %expand.1 = (f32[256,768]{1,0:T(8,128)S(1)}, bf16[256,768]{1,0:T(8,128)(2,1)S(1)}, bf16[256,768]{1,0:T(8,128)(2,1)S(1)}, bf16[256,3072]{1,0:T(8,128)(2,1)S(1)}, f32[256,3072]{1,0:T(8,128)S(1)}) custom-call(s32[4]{0:T(128)S(1)} %copy-done.39, bf16[256,768]{1,0:T(8,128)(2,1)S(1)} %copy-done.4, f32[256,768]{1,0:T(8,128)S(1)} %copy-done.21, ...), custom_call_target="tpu_custom_call" | custom-call | flops 1509949440 | bytes 13885456 | tf_op jit(solution)/shard_map/expand/pallas_call | solution.py:595
  79.4 9.1 %collective-permute-done.21.p1 = bf16[4,96,768]{2,1,0:T(8,128)(2,1)S(1)} collective-permute-done((bf16[4,96,768]{2,1,0:T(8,128)(2,1)S(1)}, bf16[4,96,768]{2,1,0:T(8,128)(2,1)S(1)}, u32[]{:S(2)}, u32[]{:S(2)}) %collective-permute-start.21) | collective-permute-done | bytes 589856 | tf_op jit(solution)/shard_map/down_1/ppermute | solution.py:492
  88.6 1.0 collective-permute-start.27
  90.2 1.8 collective-permute-done.28.active_twin
  92.0 3.1 %down_grad.1 = (bf16[4,96,768]{2,1,0:T(8,128)(2,1)S(1)}, bf16[4,96,768]{2,1,0:T(8,128)(2,1)S(1)}, bf16[4,96,768]{2,1,0:T(8,128)(2,1)S(1)}, bf16[4,96,768]{2,1,0:T(8,128)(2,1)S(1)}, f32[8,768]{1,0:T(8,128)S(1)}) custom-call(s32[4]{0:T(128)S(1)} %copy-done.39, bf16[256,3072]{1,0:T(8,128)(2,1)S(1)} %get-tuple-element.213.active, ...), custom_call_target="tpu_custom_call" | custom-call | flops 1207959552 | bytes 6316048 | tf_op jit(solution)/shard_map/down_grad/pallas_call | solution.py:595
  95.0 1.2 copy-done.32
  96.3 2.3 %collective-permute-done.27.p3 = bf16[4,96,768]{2,1,0:T(8,128)(2,1)S(1)} collective-permute-done((bf16[4,96,768]{2,1,0:T(8,128)(2,1)S(1)}, bf16[4,96,768]{2,1,0:T(8,128)(2,1)S(1)}, u32[]{:S(2)}, u32[]{:S(2)}) %collective-permute-start.27) | collective-permute-done | bytes 589856 | tf_op jit(solution)/shard_map/down_3/ppermute | solution.py:492
  99.1 1.0 collective-permute-start.29
  100.1 1.0 collective-permute-start.30
  101.6 10.2 %back.1 = (f32[256,768]{1,0:T(8,128)}, bf16[256,768]{1,0:T(8,128)(2,1)S(1)}, f32[8,768]{1,0:T(8,128)S(1)}, bf16[256,768]{1,0:T(8,128)(2,1)S(1)}, f32[8,3072]{1,0:T(8,128)S(1)}, /*index=5*/bf16[256,3072]{1,0:T(8,128)(2,1)}) custom-call(s32[4]{0:T(128)S(1)} %copy-done.39, bf16[256,768]{1,0:T(8,128)(2,1)S(1)} %copy-done.37, f32[256,3072]{1,0:T(8,128)} %copy-done.18, ...), custom_call_target="tpu_custom_call" | custom-call | flops 2717908992 | bytes 18628624 | tf_op jit(solution)/shard_map/back/pallas_call | solution.py:595
  112.7 0.9 copy-done.24
  113.7 1.6 collective-permute-done.30
  115.9 1.0 collective-permute-start.42
  116.9 1.9 collective-permute-done.39.branch_twin
  119.4 3.7 %up_grad.1 = (bf16[4,128,768]{2,1,0:T(8,128)(2,1)S(1)}, bf16[4,128,768]{2,1,0:T(8,128)(2,1)S(1)}, bf16[2,128,768]{2,1,0:T(8,128)(2,1)S(1)}, bf16[2,128,768]{2,1,0:T(8,128)(2,1)S(1)}, bf16[4,128,768]{2,1,0:T(8,128)(2,1)S(1)}) custom-call(s32[4]{0:T(128)S(1)} %copy-done.39, bf16[256,3072]{1,0:T(8,128)(2,1)S(1)} %copy-done.40, ...), custom_call_target="tpu_custom_call" | custom-call | flops 1509949440 | bytes 8650768 | tf_op jit(solution)/shard_map/up_grad/pallas_call | solution.py:595
  123.2 1.1 collective-permute-start.40
  124.2 1.6 collective-permute-done.42
  125.9 1.0 collective-permute-start.41
  127.1 3.3 %collective-permute-start.43 = (bf16[96,768]{1,0:T(8,128)(2,1)S(1)}, bf16[96,768]{1,0:T(8,128)(2,1)S(1)}, u32[]{:S(2)}, u32[]{:S(2)}) collective-permute-start(bf16[96,768]{1,0:T(8,128)(2,1)S(1)} %get-tuple-element.323), channel_id=1, source_target_pairs={{0,8},{1,9},{2,10},{3,11},{4,12},{5,13},{6,14},{7,15},{8,0},{9,1},... | collective-permute-start | bytes 442376 | tf_op jit(solution)/shard_map/rs_down_z/ppermute | solution.py:492
  130.5 8.8 %attend_back.1 = (bf16[3,512,768]{2,1,0:T(8,128)(2,1)S(1)}, f32[12,768]{1,0:T(8,128)S(1)}) custom-call(s32[4]{0:T(128)S(1)} %copy-done.39, bf16[256,768]{1,0:T(8,128)(2,1)S(1)} %copy-done.31, bf16[512,768]{1,0:T(8,128)(2,1)S(1)} %copy-done.19, bf16[512,768]{1,0:T(8,128)(2,1)S(1)} %copy-done.20, bf16[256,768]{1,0:T(8,128)(2,1)S(1)} %get-tuple-element.245.context_grad, ...), custom_call_target="tpu_custom_call" | custom-call | flops 1610612736 | bytes 8687632 | tf_op jit(solution)/shard_map/attend_back/pallas_call | solution.py:595
  139.7 1.0 collective-permute-start.48
  140.7 1.5 collective-permute-start.49
  142.2 3.4 %first_grad.1 = (f32[256,768]{1,0:T(8,128)S(1)}, f32[256,768]{1,0:T(8,128)S(1)}, f32[24,768]{1,0:T(8,128)S(1)}) custom-call(s32[4]{0:T(128)S(1)} %copy-done.39, bf16[256,768]{1,0:T(8,128)(2,1)S(1)} %copy-done.4, bf16[256,768]{1,0:T(8,128)(2,1)S(1)} %copy-done.9, bf16[3,512,768]{2,1,0:T(8,128)(2,1)S(1)} %get-tuple-element.248.grads, ...), custom_call_target="tpu_custom_call" | custom-call | flops 1509949440 | bytes 8515600 | tf_op jit(solution)/shard_map/first_grad/pallas_call | solution.py:595
  145.7 2.0 %collective-permute-start.50 = (bf16[96,768]{1,0:T(8,128)(2,1)S(1)}, bf16[96,768]{1,0:T(8,128)(2,1)S(1)}, u32[]{:S(2)}, u32[]{:S(2)}) collective-permute-start(bf16[96,768]{1,0:T(8,128)(2,1)S(1)} %get-tuple-element.268), channel_id=1, source_target_pairs={{0,24},{1,25},{2,26},{3,27},{4,28},{5,29},{6,30},{7,31},{8,16},{9,... | collective-permute-start | bytes 442376 | tf_op jit(solution)/shard_map/rs_down_z/ppermute | solution.py:492
  147.8 5.9 %qkv_grad.1 = (bf16[4,80,768]{2,1,0:T(8,128)(2,1)S(1)}, bf16[4,80,768]{2,1,0:T(8,128)(2,1)S(1)}, bf16[4,80,768]{2,1,0:T(8,128)(2,1)S(1)}, bf16[4,80,768]{2,1,0:T(8,128)(2,1)S(1)}) custom-call(s32[4]{0:T(128)S(1)} %copy-done.39, bf16[3,512,768]{2,1,0:T(8,128)(2,1)S(1)} %get-tuple-element.248.grads, ...), custom_call_target="tpu_custom_call" | custom-call | flops 1811939328 | bytes 10125328 | tf_op jit(solution)/shard_map/qkv_grad/pallas_call | solution.py:595
  153.7 1.3 collective-permute-start.47
  156.3 4.3 %collective-permute-start.53 = (bf16[128,768]{1,0:T(8,128)(2,1)S(1)}, bf16[128,768]{1,0:T(8,128)(2,1)S(1)}, u32[]{:S(2)}, u32[]{:S(2)}) collective-permute-start(bf16[128,768]{1,0:T(8,128)(2,1)S(1)} %get-tuple-element.316), channel_id=1, source_target_pairs={{0,8},{1,9},{2,10},{3,11},{4,12},{5,13},{6,14},{7,15},{8,0},{9,1},... | collective-permute-start | bytes 589832 | tf_op jit(solution)/shard_map/rs_up_z/ppermute | solution.py:492
  160.6 1.0 input_grad.1
  161.7 0.9 collective-permute-done.47
  162.7 1.2 collective-permute-start.51
  164.0 3.1 %collective-permute-done.53 = bf16[128,768]{1,0:T(8,128)(2,1)S(1)} collective-permute-done((bf16[128,768]{1,0:T(8,128)(2,1)S(1)}, bf16[128,768]{1,0:T(8,128)(2,1)S(1)}, u32[]{:S(2)}, u32[]{:S(2)}) %collective-permute-start.53) | collective-permute-done | bytes 196640 | tf_op jit(solution)/shard_map/rs_up_z/ppermute | solution.py:492
  167.1 6.4 %collective-permute-done.54 = bf16[128,768]{1,0:T(8,128)(2,1)S(1)} collective-permute-done((bf16[128,768]{1,0:T(8,128)(2,1)S(1)}, bf16[128,768]{1,0:T(8,128)(2,1)S(1)}, u32[]{:S(2)}, u32[]{:S(2)}) %collective-permute-start.54) | collective-permute-done | bytes 196640 | tf_op jit(solution)/shard_map/rs_up_z/ppermute | solution.py:492
  174.9 6.1 %finish.1 = f32[256,768]{1,0:T(8,128)} custom-call(s32[4]{0:T(128)} %pad_add_fusion.place, bf16[256,3072]{1,0:T(8,128)(2,1)} %copy-done.32, f32[256,768]{1,0:T(8,128)} %copy-done.10, f32[8,768]{1,0:T(8,128)} %get-tuple-element.206.vectors, bf16[4,96,768]{2,1,0:T(8,128)(2,1)} %copy-done.5, bf16[4,96,768]{2,1,0:T(8,128)(2,1)} %copy-done.23, ...), custom_call_target="tpu_custom_call" | custom-call | flops 1207959552 | bytes 7888912 | tf_op jit(solution)/shard_map/finish/pallas_call | solution.py:595
  181.4 3.7 %collective-permute-start.57 = (bf16[80,768]{1,0:T(8,128)(2,1)S(1)}, bf16[80,768]{1,0:T(8,128)(2,1)S(1)}, u32[]{:S(2)}, u32[]{:S(2)}) collective-permute-start(bf16[80,768]{1,0:T(8,128)(2,1)S(1)} %get-tuple-element.325), channel_id=1, source_target_pairs={{0,16},{1,17},{2,18},{3,19},{4,20},{5,21},{6,22},{7,23},{8,24},{9,... | collective-permute-start | bytes 368648 | tf_op jit(solution)/shard_map/rs_qkv_z/ppermute | solution.py:492
  185.8 3.0 %collective-permute-done.56.z1 = bf16[80,768]{1,0:T(8,128)(2,1)S(1)} collective-permute-done((bf16[80,768]{1,0:T(8,128)(2,1)S(1)}, bf16[80,768]{1,0:T(8,128)(2,1)S(1)}, u32[]{:S(2)}, u32[]{:S(2)}) %collective-permute-start.56) | collective-permute-done | bytes 122912 | tf_op jit(solution)/shard_map/rs_qkv_z/ppermute | solution.py:492
  188.8 3.2 %collective-permute-done.57.z2 = bf16[80,768]{1,0:T(8,128)(2,1)S(1)} collective-permute-done((bf16[80,768]{1,0:T(8,128)(2,1)S(1)}, bf16[80,768]{1,0:T(8,128)(2,1)S(1)}, u32[]{:S(2)}, u32[]{:S(2)}) %collective-permute-start.57) | collective-permute-done | bytes 122912 | tf_op jit(solution)/shard_map/rs_qkv_z/ppermute | solution.py:492
  193.4 1.1 last.1
  (208 shorter events, 16.7 us)
Async XLA Ops:
  2.6 16.5 %collective-permute-start = (bf16[80,768]{1,0:T(8,128)(2,1)}, bf16[80,768]{1,0:T(8,128)(2,1)S(1)}, u32[]{:S(2)}, u32[]{:S(2)}) collective-permute-start(bf16[80,768]{1,0:T(8,128)(2,1)} %get-tuple-element.163), channel_id=1, source_target_pairs={{0,8},{1,9},{2,10},{3,11},{4,12},{5,13},{6,14},{7,15},{8,0},{9,1},... | collective-permute-start | bytes 368648 | tf_op jit(solution)/shard_map/qkv_z/ppermute | solution.py:492
  5.6 13.5 %collective-permute-start.1 = (bf16[80,768]{1,0:T(8,128)(2,1)}, bf16[80,768]{1,0:T(8,128)(2,1)S(1)}, u32[]{:S(2)}, u32[]{:S(2)}) collective-permute-start(bf16[80,768]{1,0:T(8,128)(2,1)} %get-tuple-element.163), channel_id=1, source_target_pairs={{0,16},{1,17},{2,18},{3,19},{4,20},{5,21},{6,22},{7,23},{8,24},{9,... | collective-permute-start | bytes 368648 | tf_op jit(solution)/shard_map/qkv_z/ppermute | solution.py:492
  8.2 10.9 %collective-permute-start.2 = (bf16[80,768]{1,0:T(8,128)(2,1)}, bf16[80,768]{1,0:T(8,128)(2,1)S(1)}, u32[]{:S(2)}, u32[]{:S(2)}) collective-permute-start(bf16[80,768]{1,0:T(8,128)(2,1)} %get-tuple-element.163), channel_id=1, source_target_pairs={{0,24},{1,25},{2,26},{3,27},{4,28},{5,29},{6,30},{7,31},{8,16},{9,... | collective-permute-start | bytes 368648 | tf_op jit(solution)/shard_map/qkv_z/ppermute | solution.py:492
  8.2 10.9 %collective-permute-start.3 = (bf16[256,768]{1,0:T(8,128)(2,1)}, bf16[256,768]{1,0:T(8,128)(2,1)S(1)}, u32[]{:S(2)}, u32[]{:S(2)}) collective-permute-start(bf16[256,768]{1,0:T(8,128)(2,1)} %frames.3), channel_id=1, source_target_pairs={{0,1},{1,0},{2,3},{3,2},{4,5},{5,4},{6,7},{7,6},{8,9},{9,8},{10,11... | collective-permute-start | bytes 1179656 | tf_op jit(solution)/shard_map/frames_pack/ppermute | solution.py:492
  19.1 31.8 %copy-start.8 = (bf16[256,768]{1,0:T(8,128)(2,1)}, bf16[256,768]{1,0:T(8,128)(2,1)S(1)}, u32[]{:S(2)}) copy-start(bf16[256,768]{1,0:T(8,128)(2,1)S(1)} %collective-permute-done.3.other.mate_frames) | copy-start | bytes 1179652
  19.2 31.7 %copy-start.43 = (bf16[4,80,768]{2,1,0:T(8,128)(2,1)}, bf16[4,80,768]{2,1,0:T(8,128)(2,1)S(1)}, u32[]{:S(2)}) copy-start(bf16[4,80,768]{2,1,0:T(8,128)(2,1)S(1)} %pad_maximum_fusion.2.p0) | copy-start | bytes 1474564
  19.2 14.8 %collective-permute-start.4 = (bf16[4,80,768]{2,1,0:T(8,128)(2,1)S(1)}, bf16[4,80,768]{2,1,0:T(8,128)(2,1)S(1)}, u32[]{:S(2)}, u32[]{:S(2)}) collective-permute-start(bf16[4,80,768]{2,1,0:T(8,128)(2,1)S(1)} %pad_maximum_fusion.2.p0), channel_id=1, source_target_pairs={{0,1},{1,0},{2,6},{3,7},{4,5},{5,4},{6,2},{7,3},{8,9},{9,8},{10,14... | collective-permute-start | bytes 1474568 | tf_op jit(solution)/shard_map/qkv_1/ppermute | solution.py:492
  20.4 5.7 %collective-permute-start.7 = (bf16[256,768]{1,0:T(8,128)(2,1)S(1)}, bf16[256,768]{1,0:T(8,128)(2,1)S(1)}, u32[]{:S(2)}, u32[]{:S(2)}) collective-permute-start(bf16[256,768]{1,0:T(8,128)(2,1)S(1)} %copy-done.36), channel_id=1, source_target_pairs={{0,2},{1,3},{2,0},{3,1},{4,6},{5,7},{6,4},{7,5},{8,10},{9,11},{10,... | collective-permute-start | bytes 1179656 | tf_op jit(solution)/shard_map/twin/ppermute | solution.py:492
  20.4 11.3 %collective-permute-start.5 = (bf16[128,768]{1,0:T(8,128)(2,1)S(1)}, bf16[128,768]{1,0:T(8,128)(2,1)S(1)}, u32[]{:S(2)}, u32[]{:S(2)}) collective-permute-start(bf16[128,768]{1,0:T(8,128)(2,1)S(1)} %copy-done.51), channel_id=1, source_target_pairs={{0,8},{1,9},{2,10},{3,11},{4,12},{5,13},{6,14},{7,15},{8,0},{9,1},... | collective-permute-start | bytes 589832 | tf_op jit(solution)/shard_map/up_z/ppermute | solution.py:492
  21.8 12.3 %collective-permute-start.6 = (bf16[128,768]{1,0:T(8,128)(2,1)S(1)}, bf16[128,768]{1,0:T(8,128)(2,1)S(1)}, u32[]{:S(2)}, u32[]{:S(2)}) collective-permute-start(bf16[128,768]{1,0:T(8,128)(2,1)S(1)} %copy-done.51), channel_id=1, source_target_pairs={{0,16},{1,17},{2,18},{3,19},{4,20},{5,21},{6,22},{7,23},{8,24},{9,... | collective-permute-start | bytes 589832 | tf_op jit(solution)/shard_map/up_z/ppermute | solution.py:492
  24.5 13.4 %collective-permute-start.9 = (bf16[4,80,768]{2,1,0:T(8,128)(2,1)S(1)}, bf16[4,80,768]{2,1,0:T(8,128)(2,1)S(1)}, u32[]{:S(2)}, u32[]{:S(2)}) collective-permute-start(bf16[4,80,768]{2,1,0:T(8,128)(2,1)S(1)} %pad_maximum_fusion.2.p0), channel_id=1, source_target_pairs={{0,4},{1,5},{2,3},{3,2},{4,0},{5,1},{6,7},{7,6},{8,12},{9,13},{10,... | collective-permute-start | bytes 1474568 | tf_op jit(solution)/shard_map/qkv_2/ppermute | solution.py:492
  34.0 9.1 %collective-permute-start.10 = (bf16[4,80,768]{2,1,0:T(8,128)(2,1)S(1)}, bf16[4,80,768]{2,1,0:T(8,128)(2,1)S(1)}, u32[]{:S(2)}, u32[]{:S(2)}) collective-permute-start(bf16[4,80,768]{2,1,0:T(8,128)(2,1)S(1)} %collective-permute-done.4.p1), channel_id=1, source_target_pairs={{0,4},{1,5},{2,3},{3,2},{4,0},{5,1},{6,7},{7,6},{8,12},{9,13},{10,... | collective-permute-start | bytes 1474568 | tf_op jit(solution)/shard_map/qkv_3/ppermute | solution.py:492
  35.5 7.6 %collective-permute-start.8 = (bf16[128,768]{1,0:T(8,128)(2,1)S(1)}, bf16[128,768]{1,0:T(8,128)(2,1)S(1)}, u32[]{:S(2)}, u32[]{:S(2)}) collective-permute-start(bf16[128,768]{1,0:T(8,128)(2,1)S(1)} %copy-done.51), channel_id=1, source_target_pairs={{0,24},{1,25},{2,26},{3,27},{4,28},{5,29},{6,30},{7,31},{8,16},{9,... | collective-permute-start | bytes 589832 | tf_op jit(solution)/shard_map/up_z/ppermute | solution.py:492
  43.2 32.0 %copy-start.3 = (bf16[4,128,768]{2,1,0:T(8,128)(2,1)}, bf16[4,128,768]{2,1,0:T(8,128)(2,1)S(1)}, u32[]{:S(2)}) copy-start(bf16[4,128,768]{2,1,0:T(8,128)(2,1)S(1)} %pad_maximum_fusion.p0.u0) | copy-start | bytes 2359300
  43.2 16.5 %collective-permute-start.12 = (bf16[4,128,768]{2,1,0:T(8,128)(2,1)S(1)}, bf16[4,128,768]{2,1,0:T(8,128)(2,1)S(1)}, u32[]{:S(2)}, u32[]{:S(2)}) collective-permute-start(bf16[4,128,768]{2,1,0:T(8,128)(2,1)S(1)} %pad_maximum_fusion.p0.u0), channel_id=1, source_target_pairs={{0,1},{1,0},{2,6},{3,7},{4,5},{5,4},{6,2},{7,3},{8,9},{9,8},{10,14... | collective-permute-start | bytes 2359304 | tf_op jit(solution)/shard_map/up_1/ppermute | solution.py:492
  44.7 1.9 collective-permute-start.13
  44.7 4.1 %collective-permute-start.14 = (bf16[4,80,768]{2,1,0:T(8,128)(2,1)S(1)}, bf16[4,80,768]{2,1,0:T(8,128)(2,1)S(1)}, u32[]{:S(2)}, u32[]{:S(2)}) collective-permute-start(bf16[4,80,768]{2,1,0:T(8,128)(2,1)S(1)} %collective-permute-done.4.p1), channel_id=1, source_target_pairs={{0,2},{1,3},{2,0},{3,1},{4,6},{5,7},{6,4},{7,5},{8,10},{9,11},{10,... | collective-permute-start | bytes 1474568 | tf_op jit(solution)/shard_map/twin/ppermute | solution.py:492
  45.2 4.1 %collective-permute-start.15 = (bf16[4,80,768]{2,1,0:T(8,128)(2,1)S(1)}, bf16[4,80,768]{2,1,0:T(8,128)(2,1)S(1)}, u32[]{:S(2)}, u32[]{:S(2)}) collective-permute-start(bf16[4,80,768]{2,1,0:T(8,128)(2,1)S(1)} %collective-permute-done.9.p2), channel_id=1, source_target_pairs={{0,2},{1,3},{2,0},{3,1},{4,6},{5,7},{6,4},{7,5},{8,10},{9,11},{10,... | collective-permute-start | bytes 1474568 | tf_op jit(solution)/shard_map/twin/ppermute | solution.py:492
  45.2 5.6 %collective-permute-start.16 = (bf16[4,80,768]{2,1,0:T(8,128)(2,1)S(1)}, bf16[4,80,768]{2,1,0:T(8,128)(2,1)S(1)}, u32[]{:S(2)}, u32[]{:S(2)}) collective-permute-start(bf16[4,80,768]{2,1,0:T(8,128)(2,1)S(1)} %collective-permute-done.10.p3), channel_id=1, source_target_pairs={{0,2},{1,3},{2,0},{3,1},{4,6},{5,7},{6,4},{7,5},{8,10},{9,11},{10,... | collective-permute-start | bytes 1474568 | tf_op jit(solution)/shard_map/twin/ppermute | solution.py:492
  46.6 13.1 %collective-permute-start.17 = (bf16[96,768]{1,0:T(8,128)(2,1)S(1)}, bf16[96,768]{1,0:T(8,128)(2,1)S(1)}, u32[]{:S(2)}, u32[]{:S(2)}) collective-permute-start(bf16[96,768]{1,0:T(8,128)(2,1)S(1)} %copy-done.52), channel_id=1, source_target_pairs={{0,8},{1,9},{2,10},{3,11},{4,12},{5,13},{6,14},{7,15},{8,0},{9,1},... | collective-permute-start | bytes 442376 | tf_op jit(solution)/shard_map/down_z/ppermute | solution.py:492
  48.8 10.9 %collective-permute-start.18 = (bf16[96,768]{1,0:T(8,128)(2,1)S(1)}, bf16[96,768]{1,0:T(8,128)(2,1)S(1)}, u32[]{:S(2)}, u32[]{:S(2)}) collective-permute-start(bf16[96,768]{1,0:T(8,128)(2,1)S(1)} %copy-done.52), channel_id=1, source_target_pairs={{0,16},{1,17},{2,18},{3,19},{4,20},{5,21},{6,22},{7,23},{8,24},{9,... | collective-permute-start | bytes 442376 | tf_op jit(solution)/shard_map/down_z/ppermute | solution.py:492
  49.4 21.5 %collective-permute-start.11 = (bf16[4,128,768]{2,1,0:T(8,128)(2,1)S(1)}, bf16[4,128,768]{2,1,0:T(8,128)(2,1)S(1)}, u32[]{:S(2)}, u32[]{:S(2)}) collective-permute-start(bf16[4,128,768]{2,1,0:T(8,128)(2,1)S(1)} %pad_maximum_fusion.p0.u0), channel_id=1, source_target_pairs={{0,4},{1,5},{2,3},{3,2},{4,0},{5,1},{6,7},{7,6},{8,12},{9,13},{10,... | collective-permute-start | bytes 2359304 | tf_op jit(solution)/shard_map/up_2/ppermute | solution.py:492
  59.8 12.1 %collective-permute-start.19 = (bf16[4,128,768]{2,1,0:T(8,128)(2,1)S(1)}, bf16[4,128,768]{2,1,0:T(8,128)(2,1)S(1)}, u32[]{:S(2)}, u32[]{:S(2)}) collective-permute-start(bf16[4,128,768]{2,1,0:T(8,128)(2,1)S(1)} %collective-permute-done.12.p1.u1), channel_id=1, source_target_pairs={{0,4},{1,5},{2,3},{3,2},{4,0},{5,1},{6,7},{7,6},{8,12},{9,13},{10,... | collective-permute-start | bytes 2359304 | tf_op jit(solution)/shard_map/up_3/ppermute | solution.py:492
  60.5 13.0 %collective-permute-start.23 = (bf16[4,128,768]{2,1,0:T(8,128)(2,1)S(1)}, bf16[4,128,768]{2,1,0:T(8,128)(2,1)S(1)}, u32[]{:S(2)}, u32[]{:S(2)}) collective-permute-start(bf16[4,128,768]{2,1,0:T(8,128)(2,1)S(1)} %pad_maximum_fusion.p0.u0), channel_id=1, source_target_pairs={{0,2},{1,3},{2,0},{3,1},{4,6},{5,7},{6,4},{7,5},{8,10},{9,11},{10,... | collective-permute-start | bytes 2359304 | tf_op jit(solution)/shard_map/twin/ppermute | solution.py:492
  60.5 10.3 %collective-permute-start.20 = (bf16[96,768]{1,0:T(8,128)(2,1)S(1)}, bf16[96,768]{1,0:T(8,128)(2,1)S(1)}, u32[]{:S(2)}, u32[]{:S(2)}) collective-permute-start(bf16[96,768]{1,0:T(8,128)(2,1)S(1)} %copy-done.52), channel_id=1, source_target_pairs={{0,24},{1,25},{2,26},{3,27},{4,28},{5,29},{6,30},{7,31},{8,16},{9,... | collective-permute-start | bytes 442376 | tf_op jit(solution)/shard_map/down_z/ppermute | solution.py:492
  63.1 11.8 %collective-permute-start.24 = (bf16[4,128,768]{2,1,0:T(8,128)(2,1)S(1)}, bf16[4,128,768]{2,1,0:T(8,128)(2,1)S(1)}, u32[]{:S(2)}, u32[]{:S(2)}) collective-permute-start(bf16[4,128,768]{2,1,0:T(8,128)(2,1)S(1)} %collective-permute-done.12.p1.u1), channel_id=1, source_target_pairs={{0,2},{1,3},{2,0},{3,1},{4,6},{5,7},{6,4},{7,5},{8,10},{9,11},{10,... | collective-permute-start | bytes 2359304 | tf_op jit(solution)/shard_map/twin/ppermute | solution.py:492
  71.8 3.0 %collective-permute-start.25 = (bf16[4,128,768]{2,1,0:T(8,128)(2,1)S(1)}, bf16[4,128,768]{2,1,0:T(8,128)(2,1)S(1)}, u32[]{:S(2)}, u32[]{:S(2)}) collective-permute-start(bf16[4,128,768]{2,1,0:T(8,128)(2,1)S(1)} %collective-permute-done.11.p2.u2), channel_id=1, source_target_pairs={{0,2},{1,3},{2,0},{3,1},{4,6},{5,7},{6,4},{7,5},{8,10},{9,11},{10,... | collective-permute-start | bytes 2359304 | tf_op jit(solution)/shard_map/twin/ppermute | solution.py:492
  72.0 3.3 %collective-permute-start.26 = (bf16[4,128,768]{2,1,0:T(8,128)(2,1)S(1)}, bf16[4,128,768]{2,1,0:T(8,128)(2,1)S(1)}, u32[]{:S(2)}, u32[]{:S(2)}) collective-permute-start(bf16[4,128,768]{2,1,0:T(8,128)(2,1)S(1)} %collective-permute-done.19.p3.u3), channel_id=1, source_target_pairs={{0,2},{1,3},{2,0},{3,1},{4,6},{5,7},{6,4},{7,5},{8,10},{9,11},{10,... | collective-permute-start | bytes 2359304 | tf_op jit(solution)/shard_map/twin/ppermute | solution.py:492
  72.4 29.2 %copy-start.5 = (bf16[4,96,768]{2,1,0:T(8,128)(2,1)}, bf16[4,96,768]{2,1,0:T(8,128)(2,1)S(1)}, u32[]{:S(2)}) copy-start(bf16[4,96,768]{2,1,0:T(8,128)(2,1)S(1)} %pad_maximum_fusion.1.p0) | copy-start | bytes 1769476
  72.4 16.1 %collective-permute-start.21 = (bf16[4,96,768]{2,1,0:T(8,128)(2,1)S(1)}, bf16[4,96,768]{2,1,0:T(8,128)(2,1)S(1)}, u32[]{:S(2)}, u32[]{:S(2)}) collective-permute-start(bf16[4,96,768]{2,1,0:T(8,128)(2,1)S(1)} %pad_maximum_fusion.1.p0), channel_id=1, source_target_pairs={{0,1},{1,0},{2,6},{3,7},{4,5},{5,4},{6,2},{7,3},{8,9},{9,8},{10,14... | collective-permute-start | bytes 1769480 | tf_op jit(solution)/shard_map/down_1/ppermute | solution.py:492
  73.6 15.0 %collective-permute-start.22 = (bf16[4,96,768]{2,1,0:T(8,128)(2,1)S(1)}, bf16[4,96,768]{2,1,0:T(8,128)(2,1)S(1)}, u32[]{:S(2)}, u32[]{:S(2)}) collective-permute-start(bf16[4,96,768]{2,1,0:T(8,128)(2,1)S(1)} %pad_maximum_fusion.1.p0), channel_id=1, source_target_pairs={{0,4},{1,5},{2,3},{3,2},{4,0},{5,1},{6,7},{7,6},{8,12},{9,13},{10,... | collective-permute-start | bytes 1769480 | tf_op jit(solution)/shard_map/down_2/ppermute | solution.py:492
  88.5 3.4 %collective-permute-start.28 = (bf16[256,3072]{1,0:T(8,128)(2,1)S(1)}, bf16[256,3072]{1,0:T(8,128)(2,1)S(1)}, u32[]{:S(2)}, u32[]{:S(2)}) collective-permute-start(bf16[256,3072]{1,0:T(8,128)(2,1)S(1)} %get-tuple-element.213.active), channel_id=1, source_target_pairs={{0,2},{1,3},{2,0},{3,1},{4,6},{5,7},{6,4},{7,5},{8,10},{9,11},{10,... | collective-permute-start | bytes 4718600 | tf_op jit(solution)/shard_map/twin/ppermute | solution.py:492
  88.6 9.9 %collective-permute-start.27 = (bf16[4,96,768]{2,1,0:T(8,128)(2,1)S(1)}, bf16[4,96,768]{2,1,0:T(8,128)(2,1)S(1)}, u32[]{:S(2)}, u32[]{:S(2)}) collective-permute-start(bf16[4,96,768]{2,1,0:T(8,128)(2,1)S(1)} %collective-permute-done.21.p1), channel_id=1, source_target_pairs={{0,4},{1,5},{2,3},{3,2},{4,0},{5,1},{6,7},{7,6},{8,12},{9,13},{10,... | collective-permute-start | bytes 1769480 | tf_op jit(solution)/shard_map/down_3/ppermute | solution.py:492
  89.7 9.4 %collective-permute-start.31 = (bf16[4,96,768]{2,1,0:T(8,128)(2,1)S(1)}, bf16[4,96,768]{2,1,0:T(8,128)(2,1)S(1)}, u32[]{:S(2)}, u32[]{:S(2)}) collective-permute-start(bf16[4,96,768]{2,1,0:T(8,128)(2,1)S(1)} %pad_maximum_fusion.1.p0), channel_id=1, source_target_pairs={{0,2},{1,3},{2,0},{3,1},{4,6},{5,7},{6,4},{7,5},{8,10},{9,11},{10,... | collective-permute-start | bytes 1769480 | tf_op jit(solution)/shard_map/twin/ppermute | solution.py:492
  89.7 10.4 %collective-permute-start.32 = (bf16[4,96,768]{2,1,0:T(8,128)(2,1)S(1)}, bf16[4,96,768]{2,1,0:T(8,128)(2,1)S(1)}, u32[]{:S(2)}, u32[]{:S(2)}) collective-permute-start(bf16[4,96,768]{2,1,0:T(8,128)(2,1)S(1)} %collective-permute-done.21.p1), channel_id=1, source_target_pairs={{0,2},{1,3},{2,0},{3,1},{4,6},{5,7},{6,4},{7,5},{8,10},{9,11},{10,... | collective-permute-start | bytes 1769480 | tf_op jit(solution)/shard_map/twin/ppermute | solution.py:492
  90.2 10.9 %collective-permute-start.33 = (bf16[4,96,768]{2,1,0:T(8,128)(2,1)S(1)}, bf16[4,96,768]{2,1,0:T(8,128)(2,1)S(1)}, u32[]{:S(2)}, u32[]{:S(2)}) collective-permute-start(bf16[4,96,768]{2,1,0:T(8,128)(2,1)S(1)} %collective-permute-done.22.p2), channel_id=1, source_target_pairs={{0,2},{1,3},{2,0},{3,1},{4,6},{5,7},{6,4},{7,5},{8,10},{9,11},{10,... | collective-permute-start | bytes 1769480 | tf_op jit(solution)/shard_map/twin/ppermute | solution.py:492
  98.5 2.6 %collective-permute-start.34 = (bf16[4,96,768]{2,1,0:T(8,128)(2,1)S(1)}, bf16[4,96,768]{2,1,0:T(8,128)(2,1)S(1)}, u32[]{:S(2)}, u32[]{:S(2)}) collective-permute-start(bf16[4,96,768]{2,1,0:T(8,128)(2,1)S(1)} %collective-permute-done.27.p3), channel_id=1, source_target_pairs={{0,2},{1,3},{2,0},{3,1},{4,6},{5,7},{6,4},{7,5},{8,10},{9,11},{10,... | collective-permute-start | bytes 1769480 | tf_op jit(solution)/shard_map/twin/ppermute | solution.py:492
  98.5 15.1 %collective-permute-start.37 = (bf16[512,768]{1,0:T(8,128)(2,1)S(1)}, bf16[512,768]{1,0:T(8,128)(2,1)S(1)}, u32[]{:S(2)}, u32[]{:S(2)}) collective-permute-start(bf16[512,768]{1,0:T(8,128)(2,1)S(1)} %copy-done.33), channel_id=1, source_target_pairs={{0,2},{1,3},{2,0},{3,1},{4,6},{5,7},{6,4},{7,5},{8,10},{9,11},{10,... | collective-permute-start | bytes 2359304 | tf_op jit(solution)/shard_map/twin/ppermute | solution.py:492
  99.1 14.6 %collective-permute-start.29 = (bf16[4,96,768]{2,1,0:T(8,128)(2,1)S(1)}, bf16[4,96,768]{2,1,0:T(8,128)(2,1)S(1)}, u32[]{:S(2)}, u32[]{:S(2)}) collective-permute-start(bf16[4,96,768]{2,1,0:T(8,128)(2,1)S(1)} %get-tuple-element.221), channel_id=1, source_target_pairs={{0,4},{1,5},{2,3},{3,2},{4,0},{5,1},{6,7},{7,6},{8,12},{9,13},{10,... | collective-permute-start | bytes 1769480 | tf_op jit(solution)/shard_map/rs_down_3/ppermute | solution.py:492
  100.1 15.2 %collective-permute-start.30 = (bf16[4,96,768]{2,1,0:T(8,128)(2,1)S(1)}, bf16[4,96,768]{2,1,0:T(8,128)(2,1)S(1)}, u32[]{:S(2)}, u32[]{:S(2)}) collective-permute-start(bf16[4,96,768]{2,1,0:T(8,128)(2,1)S(1)} %get-tuple-element.222), channel_id=1, source_target_pairs={{0,4},{1,5},{2,3},{3,2},{4,0},{5,1},{6,7},{7,6},{8,12},{9,13},{10,... | collective-permute-start | bytes 1769480 | tf_op jit(solution)/shard_map/rs_down_2/ppermute | solution.py:492
  101.1 12.5 %collective-permute-start.35 = (bf16[256,768]{1,0:T(8,128)(2,1)S(1)}, bf16[256,768]{1,0:T(8,128)(2,1)S(1)}, u32[]{:S(2)}, u32[]{:S(2)}) collective-permute-start(bf16[256,768]{1,0:T(8,128)(2,1)S(1)} %get-tuple-element.229.context), channel_id=1, source_target_pairs={{0,2},{1,3},{2,0},{3,1},{4,6},{5,7},{6,4},{7,5},{8,10},{9,11},{10,... | collective-permute-start | bytes 1179656 | tf_op jit(solution)/shard_map/twin/ppermute | solution.py:492
  101.1 12.5 %collective-permute-start.36 = (bf16[256,768]{1,0:T(8,128)(2,1)S(1)}, bf16[256,768]{1,0:T(8,128)(2,1)S(1)}, u32[]{:S(2)}, u32[]{:S(2)}) collective-permute-start(bf16[256,768]{1,0:T(8,128)(2,1)S(1)} %get-tuple-element.230.second), channel_id=1, source_target_pairs={{0,2},{1,3},{2,0},{3,1},{4,6},{5,7},{6,4},{7,5},{8,10},{9,11},{10,... | collective-permute-start | bytes 1179656 | tf_op jit(solution)/shard_map/twin/ppermute | solution.py:492
  115.3 4.2 %collective-permute-start.38 = (bf16[256,3072]{1,0:T(8,128)(2,1)}, bf16[256,3072]{1,0:T(8,128)(2,1)S(1)}, u32[]{:S(2)}, u32[]{:S(2)}) collective-permute-start(bf16[256,3072]{1,0:T(8,128)(2,1)} %get-tuple-element.236.hidden), channel_id=1, source_target_pairs={{0,2},{1,3},{2,0},{3,1},{4,6},{5,7},{6,4},{7,5},{8,10},{9,11},{10,... | collective-permute-start | bytes 4718600 | tf_op jit(solution)/shard_map/twin/ppermute | solution.py:492
  115.3 3.6 %collective-permute-start.39 = (bf16[256,768]{1,0:T(8,128)(2,1)S(1)}, bf16[256,768]{1,0:T(8,128)(2,1)S(1)}, u32[]{:S(2)}, u32[]{:S(2)}) collective-permute-start(bf16[256,768]{1,0:T(8,128)(2,1)S(1)} %get-tuple-element.238.branch), channel_id=1, source_target_pairs={{0,2},{1,3},{2,0},{3,1},{4,6},{5,7},{6,4},{7,5},{8,10},{9,11},{10,... | collective-permute-start | bytes 1179656 | tf_op jit(solution)/shard_map/twin/ppermute | solution.py:492
  115.9 9.9 %collective-permute-start.42 = (bf16[4,96,768]{2,1,0:T(8,128)(2,1)S(1)}, bf16[4,96,768]{2,1,0:T(8,128)(2,1)S(1)}, u32[]{:S(2)}, u32[]{:S(2)}) collective-permute-start(bf16[4,96,768]{2,1,0:T(8,128)(2,1)S(1)} %add_convert_fusion.1), channel_id=1, source_target_pairs={{0,1},{1,0},{2,6},{3,7},{4,5},{5,4},{6,2},{7,3},{8,9},{9,8},{10,14... | collective-permute-start | bytes 1769480 | tf_op jit(solution)/shard_map/rs_down_1/ppermute | solution.py:492
  123.2 16.3 %collective-permute-start.40 = (bf16[4,128,768]{2,1,0:T(8,128)(2,1)S(1)}, bf16[4,128,768]{2,1,0:T(8,128)(2,1)S(1)}, u32[]{:S(2)}, u32[]{:S(2)}) collective-permute-start(bf16[4,128,768]{2,1,0:T(8,128)(2,1)S(1)} %get-tuple-element.240), channel_id=1, source_target_pairs={{0,4},{1,5},{2,3},{3,2},{4,0},{5,1},{6,7},{7,6},{8,12},{9,13},{10,... | collective-permute-start | bytes 2359304 | tf_op jit(solution)/shard_map/rs_up_3/ppermute | solution.py:492
  125.9 13.6 %collective-permute-start.41 = (bf16[2,128,768]{2,1,0:T(8,128)(2,1)S(1)}, bf16[2,128,768]{2,1,0:T(8,128)(2,1)S(1)}, u32[]{:S(2)}, u32[]{:S(2)}) collective-permute-start(bf16[2,128,768]{2,1,0:T(8,128)(2,1)S(1)} %get-tuple-element.241), channel_id=1, source_target_pairs={{0,4},{1,5},{2,3},{3,2},{4,0},{5,1},{6,7},{7,6},{8,12},{9,13},{10,... | collective-permute-start | bytes 1179656 | tf_op jit(solution)/shard_map/rs_up_2a/ppermute | solution.py:492
  127.1 12.2 %collective-permute-start.43 = (bf16[96,768]{1,0:T(8,128)(2,1)S(1)}, bf16[96,768]{1,0:T(8,128)(2,1)S(1)}, u32[]{:S(2)}, u32[]{:S(2)}) collective-permute-start(bf16[96,768]{1,0:T(8,128)(2,1)S(1)} %get-tuple-element.323), channel_id=1, source_target_pairs={{0,8},{1,9},{2,10},{3,11},{4,12},{5,13},{6,14},{7,15},{8,0},{9,1},... | collective-permute-start | bytes 442376 | tf_op jit(solution)/shard_map/rs_down_z/ppermute | solution.py:492
  130.5 8.9 %collective-permute-start.44 = (bf16[96,768]{1,0:T(8,128)(2,1)S(1)}, bf16[96,768]{1,0:T(8,128)(2,1)S(1)}, u32[]{:S(2)}, u32[]{:S(2)}) collective-permute-start(bf16[96,768]{1,0:T(8,128)(2,1)S(1)} %get-tuple-element.322), channel_id=1, source_target_pairs={{0,16},{1,17},{2,18},{3,19},{4,20},{5,21},{6,22},{7,23},{8,24},{9,... | collective-permute-start | bytes 442376 | tf_op jit(solution)/shard_map/rs_down_z/ppermute | solution.py:492
  139.4 6.2 %collective-permute-start.45 = (bf16[3,512,768]{2,1,0:T(8,128)(2,1)S(1)}, bf16[3,512,768]{2,1,0:T(8,128)(2,1)S(1)}, u32[]{:S(2)}, u32[]{:S(2)}) collective-permute-start(bf16[3,512,768]{2,1,0:T(8,128)(2,1)S(1)} %get-tuple-element.248.grads), channel_id=1, source_target_pairs={{0,2},{1,3},{2,0},{3,1},{4,6},{5,7},{6,4},{7,5},{8,10},{9,11},{10,... | collective-permute-start | bytes 7077896 | tf_op jit(solution)/shard_map/twin/ppermute | solution.py:492
  139.7 16.3 %collective-permute-start.48 = (bf16[4,128,768]{2,1,0:T(8,128)(2,1)S(1)}, bf16[4,128,768]{2,1,0:T(8,128)(2,1)S(1)}, u32[]{:S(2)}, u32[]{:S(2)}) collective-permute-start(bf16[4,128,768]{2,1,0:T(8,128)(2,1)S(1)} %add_convert_fusion), channel_id=1, source_target_pairs={{0,1},{1,0},{2,6},{3,7},{4,5},{5,4},{6,2},{7,3},{8,9},{9,8},{10,14... | collective-permute-start | bytes 2359304 | tf_op jit(solution)/shard_map/rs_up_1/ppermute | solution.py:492
  140.7 15.1 %collective-permute-start.49 = (bf16[2,128,768]{2,1,0:T(8,128)(2,1)S(1)}, bf16[2,128,768]{2,1,0:T(8,128)(2,1)S(1)}, u32[]{:S(2)}, u32[]{:S(2)}) collective-permute-start(bf16[2,128,768]{2,1,0:T(8,128)(2,1)S(1)} %get-tuple-element.265), channel_id=1, source_target_pairs={{0,4},{1,5},{2,3},{3,2},{4,0},{5,1},{6,7},{7,6},{8,12},{9,13},{10,... | collective-permute-start | bytes 1179656 | tf_op jit(solution)/shard_map/rs_up_2b/ppermute | solution.py:492
  145.6 2.1 %collective-permute-start.46 = (f32[24,768]{1,0:T(8,128)S(1)}, f32[24,768]{1,0:T(8,128)S(1)}, u32[]{:S(2)}, u32[]{:S(2)}) collective-permute-start(f32[24,768]{1,0:T(8,128)S(1)} %get-tuple-element.260.small_own), channel_id=1, source_target_pairs={{0,2},{1,3},{2,0},{3,1},{4,6},{5,7},{6,4},{7,5},{8,10},{9,11},{10,... | collective-permute-start | bytes 221192 | tf_op jit(solution)/shard_map/twin/ppermute | solution.py:492
  145.7 10.3 %collective-permute-start.50 = (bf16[96,768]{1,0:T(8,128)(2,1)S(1)}, bf16[96,768]{1,0:T(8,128)(2,1)S(1)}, u32[]{:S(2)}, u32[]{:S(2)}) collective-permute-start(bf16[96,768]{1,0:T(8,128)(2,1)S(1)} %get-tuple-element.268), channel_id=1, source_target_pairs={{0,24},{1,25},{2,26},{3,27},{4,28},{5,29},{6,30},{7,31},{8,16},{9,... | collective-permute-start | bytes 442376 | tf_op jit(solution)/shard_map/rs_down_z/ppermute | solution.py:492
  153.7 8.9 %collective-permute-start.47 = (bf16[4,80,768]{2,1,0:T(8,128)(2,1)S(1)}, bf16[4,80,768]{2,1,0:T(8,128)(2,1)S(1)}, u32[]{:S(2)}, u32[]{:S(2)}) collective-permute-start(bf16[4,80,768]{2,1,0:T(8,128)(2,1)S(1)} %get-tuple-element.262), channel_id=1, source_target_pairs={{0,4},{1,5},{2,3},{3,2},{4,0},{5,1},{6,7},{7,6},{8,12},{9,13},{10,... | collective-permute-start | bytes 1474568 | tf_op jit(solution)/shard_map/rs_qkv_3/ppermute | solution.py:492
  155.0 25.9 %collective-permute-start.52 = (bf16[4,80,768]{2,1,0:T(8,128)(2,1)S(1)}, bf16[4,80,768]{2,1,0:T(8,128)(2,1)S(1)}, u32[]{:S(2)}, u32[]{:S(2)}) collective-permute-start(bf16[4,80,768]{2,1,0:T(8,128)(2,1)S(1)} %get-tuple-element.277), channel_id=1, source_target_pairs={{0,4},{1,5},{2,3},{3,2},{4,0},{5,1},{6,7},{7,6},{8,12},{9,13},{10,... | collective-permute-start | bytes 1474568 | tf_op jit(solution)/shard_map/rs_qkv_2/ppermute | solution.py:492
  156.3 10.8 %collective-permute-start.53 = (bf16[128,768]{1,0:T(8,128)(2,1)S(1)}, bf16[128,768]{1,0:T(8,128)(2,1)S(1)}, u32[]{:S(2)}, u32[]{:S(2)}) collective-permute-start(bf16[128,768]{1,0:T(8,128)(2,1)S(1)} %get-tuple-element.316), channel_id=1, source_target_pairs={{0,8},{1,9},{2,10},{3,11},{4,12},{5,13},{6,14},{7,15},{8,0},{9,1},... | collective-permute-start | bytes 589832 | tf_op jit(solution)/shard_map/rs_up_z/ppermute | solution.py:492
  160.6 12.9 %collective-permute-start.54 = (bf16[128,768]{1,0:T(8,128)(2,1)S(1)}, bf16[128,768]{1,0:T(8,128)(2,1)S(1)}, u32[]{:S(2)}, u32[]{:S(2)}) collective-permute-start(bf16[128,768]{1,0:T(8,128)(2,1)S(1)} %get-tuple-element.319), channel_id=1, source_target_pairs={{0,16},{1,17},{2,18},{3,19},{4,20},{5,21},{6,22},{7,23},{8,24},{9,... | collective-permute-start | bytes 589832 | tf_op jit(solution)/shard_map/rs_up_z/ppermute | solution.py:492
  162.7 18.2 %collective-permute-start.51 = (bf16[4,80,768]{2,1,0:T(8,128)(2,1)S(1)}, bf16[4,80,768]{2,1,0:T(8,128)(2,1)S(1)}, u32[]{:S(2)}, u32[]{:S(2)}) collective-permute-start(bf16[4,80,768]{2,1,0:T(8,128)(2,1)S(1)} %add_convert_fusion.2), channel_id=1, source_target_pairs={{0,1},{1,0},{2,6},{3,7},{4,5},{5,4},{6,2},{7,3},{8,9},{9,8},{10,14... | collective-permute-start | bytes 1474568 | tf_op jit(solution)/shard_map/rs_qkv_1/ppermute | solution.py:492
  173.5 7.5 %collective-permute-start.55 = (bf16[128,768]{1,0:T(8,128)(2,1)S(1)}, bf16[128,768]{1,0:T(8,128)(2,1)S(1)}, u32[]{:S(2)}, u32[]{:S(2)}) collective-permute-start(bf16[128,768]{1,0:T(8,128)(2,1)S(1)} %get-tuple-element.281), channel_id=1, source_target_pairs={{0,24},{1,25},{2,26},{3,27},{4,28},{5,29},{6,30},{7,31},{8,16},{9,... | collective-permute-start | bytes 589832 | tf_op jit(solution)/shard_map/rs_up_z/ppermute | solution.py:492
  181.2 12.2 %collective-permute-start.59 = (bf16[256,768]{1,0:T(8,128)(2,1)S(1)}, bf16[256,768]{1,0:T(8,128)(2,1)S(1)}, u32[]{:S(2)}, u32[]{:S(2)}) collective-permute-start(bf16[256,768]{1,0:T(8,128)(2,1)S(1)} %get-tuple-element.295), channel_id=1, source_target_pairs={{0,1},{1,0},{2,3},{3,2},{4,5},{5,4},{6,7},{7,6},{8,9},{9,8},{10,11... | collective-permute-start | bytes 1179656 | tf_op jit(solution)/shard_map/grad_pack/ppermute | solution.py:492
  181.4 7.5 %collective-permute-start.56 = (bf16[80,768]{1,0:T(8,128)(2,1)S(1)}, bf16[80,768]{1,0:T(8,128)(2,1)S(1)}, u32[]{:S(2)}, u32[]{:S(2)}) collective-permute-start(bf16[80,768]{1,0:T(8,128)(2,1)S(1)} %get-tuple-element.326), channel_id=1, source_target_pairs={{0,8},{1,9},{2,10},{3,11},{4,12},{5,13},{6,14},{7,15},{8,0},{9,1},... | collective-permute-start | bytes 368648 | tf_op jit(solution)/shard_map/rs_qkv_z/ppermute | solution.py:492
  181.4 10.6 %collective-permute-start.57 = (bf16[80,768]{1,0:T(8,128)(2,1)S(1)}, bf16[80,768]{1,0:T(8,128)(2,1)S(1)}, u32[]{:S(2)}, u32[]{:S(2)}) collective-permute-start(bf16[80,768]{1,0:T(8,128)(2,1)S(1)} %get-tuple-element.325), channel_id=1, source_target_pairs={{0,16},{1,17},{2,18},{3,19},{4,20},{5,21},{6,22},{7,23},{8,24},{9,... | collective-permute-start | bytes 368648 | tf_op jit(solution)/shard_map/rs_qkv_z/ppermute | solution.py:492
  185.2 6.9 %collective-permute-start.58 = (bf16[80,768]{1,0:T(8,128)(2,1)S(1)}, bf16[80,768]{1,0:T(8,128)(2,1)S(1)}, u32[]{:S(2)}, u32[]{:S(2)}) collective-permute-start(bf16[80,768]{1,0:T(8,128)(2,1)S(1)} %get-tuple-element.324), channel_id=1, source_target_pairs={{0,24},{1,25},{2,26},{3,27},{4,28},{5,29},{6,30},{7,31},{8,16},{9,... | collective-permute-start | bytes 368648 | tf_op jit(solution)/shard_map/rs_qkv_z/ppermute | solution.py:492
  (50 other events, 424.1 us)

commit v3 on v2

--- a/solution.py
+++ b/solution.py
@@ -1423,7 +1423,6 @@
     qkv_z = z_sends(qkv_sum, "rs_qkv")
     up_sum = z_sum(tied(up_sum[:1], qkv_sum), up_z)
     mate_part = shift(tied(mate_part, up_sum), PACK, "grad_pack")
-    up_sum, qkv_z = joined(up_sum, qkv_z)
     last = call(
         last_kernel,
         [VMEM] * 6,

time: 195 us -> 194 us (level)
  no operation moved by 1% of the time
where the time goes in v3:
time: 194 us
  Pallas kernels  68.7 us (35%)
  starting transfers between devices  60.2 us (31%)
  waiting for transfers between devices  49.8 us (26%)
  other arithmetic  6.4 us (3%)
  local copies, waits for them, and re-layouts  6.18 us (3%)
    pallas_call x14, Pallas kernels, call(): pl.pallas_call(kernel, out_shape=outs, in_specs=in_specs, out_specs=out_s...  68.7 us
    ppermute x60, starting transfers between devices, shift(): return lax.ppermute(array, AXES, route(move))  60.2 us
    ppermute x60, waiting for transfers between devices, shift(): return lax.ppermute(array, AXES, route(move))  49.8 us
    unnamed x108, local copies, waits for them, and re-layouts  4.71 us
  transfers between devices with their start and end apart: 60, of which 20 were waited for; matrix products, arithmetic and copies ran while one was open for 4% of the time, Pallas kernels for 34%

profile of v3, /device:TPU:0, one launch (start us, length us, event | category | flops | bytes accessed | tf_op | source)
XLA Modules:
  0.0 194.0 jit_solution(5631506117493142324)
XLA Ops:
  0.7 1.9 pack.1
  2.6 3.0 %collective-permute-start = (bf16[80,768]{1,0:T(8,128)(2,1)}, bf16[80,768]{1,0:T(8,128)(2,1)S(1)}, u32[]{:S(2)}, u32[]{:S(2)}) collective-permute-start(bf16[80,768]{1,0:T(8,128)(2,1)} %get-tuple-element.159), channel_id=1, source_target_pairs={{0,8},{1,9},{2,10},{3,11},{4,12},{5,13},{6,14},{7,15},{8,0},{9,1},... | collective-permute-start | bytes 368648 | tf_op jit(solution)/shard_map/qkv_z/ppermute | solution.py:492
  5.6 2.6 %collective-permute-start.1 = (bf16[80,768]{1,0:T(8,128)(2,1)}, bf16[80,768]{1,0:T(8,128)(2,1)S(1)}, u32[]{:S(2)}, u32[]{:S(2)}) collective-permute-start(bf16[80,768]{1,0:T(8,128)(2,1)} %get-tuple-element.159), channel_id=1, source_target_pairs={{0,16},{1,17},{2,18},{3,19},{4,20},{5,21},{6,22},{7,23},{8,24},{9,... | collective-permute-start | bytes 368648 | tf_op jit(solution)/shard_map/qkv_z/ppermute | solution.py:492
  8.2 1.7 collective-permute-start.3
  10.0 1.5 convert_convert_fusion.wide_four
  11.5 1.1 convert_convert_fusion.1.wide_two
  12.6 0.9 convert_convert_fusion.2.wide_one
  13.5 1.0 fusion.2.curve
  14.5 4.0 %bias.1 = bf16[12,256,512]{2,1,0:T(8,128)(2,1)} custom-call(f32[12,768]{1,0:T(8,128)} %fusion.2.curve), custom_call_target="tpu_custom_call" | custom-call | bytes 3182592 | tf_op jit(solution)/shard_map/bias/pallas_call | solution.py:595
  19.2 1.1 collective-permute-start.4
  20.4 1.4 collective-permute-start.5
  21.8 2.8 %collective-permute-start.6 = (bf16[128,768]{1,0:T(8,128)(2,1)S(1)}, bf16[128,768]{1,0:T(8,128)(2,1)S(1)}, u32[]{:S(2)}, u32[]{:S(2)}) collective-permute-start(bf16[128,768]{1,0:T(8,128)(2,1)S(1)} %copy-done.51), channel_id=1, source_target_pairs={{0,16},{1,17},{2,18},{3,19},{4,20},{5,21},{6,22},{7,23},{8,24},{9,... | collective-permute-start | bytes 589832 | tf_op jit(solution)/shard_map/up_z/ppermute | solution.py:492
  24.5 1.5 collective-permute-start.9
  26.8 4.8 %collective-permute-done.5 = bf16[128,768]{1,0:T(8,128)(2,1)S(1)} collective-permute-done((bf16[128,768]{1,0:T(8,128)(2,1)S(1)}, bf16[128,768]{1,0:T(8,128)(2,1)S(1)}, u32[]{:S(2)}, u32[]{:S(2)}) %collective-permute-start.5) | collective-permute-done | bytes 196640 | tf_op jit(solution)/shard_map/up_z/ppermute | solution.py:492
  31.7 2.4 %collective-permute-done.6 = bf16[128,768]{1,0:T(8,128)(2,1)S(1)} collective-permute-done((bf16[128,768]{1,0:T(8,128)(2,1)S(1)}, bf16[128,768]{1,0:T(8,128)(2,1)S(1)}, u32[]{:S(2)}, u32[]{:S(2)}) %collective-permute-start.6) | collective-permute-done | bytes 196640 | tf_op jit(solution)/shard_map/up_z/ppermute | solution.py:492
  34.0 1.5 collective-permute-start.10
  35.5 2.4 %collective-permute-start.8 = (bf16[128,768]{1,0:T(8,128)(2,1)S(1)}, bf16[128,768]{1,0:T(8,128)(2,1)S(1)}, u32[]{:S(2)}, u32[]{:S(2)}) collective-permute-start(bf16[128,768]{1,0:T(8,128)(2,1)S(1)} %copy-done.51), channel_id=1, source_target_pairs={{0,24},{1,25},{2,26},{3,27},{4,28},{5,29},{6,30},{7,31},{8,16},{9,... | collective-permute-start | bytes 589832 | tf_op jit(solution)/shard_map/up_z/ppermute | solution.py:492
  37.9 5.2 %collective-permute-done.8 = bf16[128,768]{1,0:T(8,128)(2,1)S(1)} collective-permute-done((bf16[128,768]{1,0:T(8,128)(2,1)S(1)}, bf16[128,768]{1,0:T(8,128)(2,1)S(1)}, u32[]{:S(2)}, u32[]{:S(2)}) %collective-permute-start.8) | collective-permute-done | bytes 196640 | tf_op jit(solution)/shard_map/up_z/ppermute | solution.py:492
  43.2 1.5 collective-permute-start.12
  46.6 2.2 %collective-permute-start.17 = (bf16[96,768]{1,0:T(8,128)(2,1)S(1)}, bf16[96,768]{1,0:T(8,128)(2,1)S(1)}, u32[]{:S(2)}, u32[]{:S(2)}) collective-permute-start(bf16[96,768]{1,0:T(8,128)(2,1)S(1)} %copy-done.52), channel_id=1, source_target_pairs={{0,8},{1,9},{2,10},{3,11},{4,12},{5,13},{6,14},{7,15},{8,0},{9,1},... | collective-permute-start | bytes 442376 | tf_op jit(solution)/shard_map/down_z/ppermute | solution.py:492
  49.4 1.5 collective-permute-start.11
  51.7 8.0 %project.1 = (bf16[512,768]{1,0:T(8,128)(2,1)}, bf16[256,768]{1,0:T(8,128)(2,1)}, bf16[512,768]{1,0:T(8,128)(2,1)}, bf16[512,768]{1,0:T(8,128)(2,1)}, f32[8,768]...) custom-call(s32[4]{0:T(128)} %pad_add_fusion.place, bf16[256,768]{1,0:T(8,128)(2,1)} %frames.3, ...), custom_call_target="tpu_custom_call" | custom-call | flops 1509949440 | bytes 12861456 | tf_op jit(solution)/shard_map/project/pallas_call | solution.py:595
  60.5 2.5 %collective-permute-start.20 = (bf16[96,768]{1,0:T(8,128)(2,1)S(1)}, bf16[96,768]{1,0:T(8,128)(2,1)S(1)}, u32[]{:S(2)}, u32[]{:S(2)}) collective-permute-start(bf16[96,768]{1,0:T(8,128)(2,1)S(1)} %copy-done.52), channel_id=1, source_target_pairs={{0,24},{1,25},{2,26},{3,27},{4,28},{5,29},{6,30},{7,31},{8,16},{9,... | collective-permute-start | bytes 442376 | tf_op jit(solution)/shard_map/down_z/ppermute | solution.py:492
  63.3 7.5 %attend.1 = (bf16[12,256,512]{2,1,0:T(8,128)(2,1)}, f32[256,768]{1,0:T(8,128)}) custom-call(s32[4]{0:T(128)} %pad_add_fusion.place, s32[1,4]{1,0:T(1,128)} %lengths.1, bf16[256,768]{1,0:T(8,128)(2,1)} %get-tuple-element.188.queries, bf16[512,768]{1,0:T(8,128)(2,1)} %get-tuple-element.189.keys, bf16[512,768]{1,0:T(8,128)(2,1)} %get-tuple-element.190.values, ...), custom_call_target="tpu_custom_call" | custom-call | flops 805306368 | bytes 9053216 | tf_op jit(solution)/shard_map/attend/pallas_call | solution.py:595
  70.8 1.0 collective-permute-done.19.p3.u3
  72.4 1.2 collective-permute-start.21
  73.6 1.3 collective-permute-start.22
  75.3 4.0 %expand.1 = (f32[256,768]{1,0:T(8,128)S(1)}, bf16[256,768]{1,0:T(8,128)(2,1)S(1)}, bf16[256,768]{1,0:T(8,128)(2,1)S(1)}, bf16[256,3072]{1,0:T(8,128)(2,1)S(1)}, f32[256,3072]{1,0:T(8,128)S(1)}) custom-call(s32[4]{0:T(128)S(1)} %copy-done.39, bf16[256,768]{1,0:T(8,128)(2,1)S(1)} %copy-done.4, f32[256,768]{1,0:T(8,128)S(1)} %copy-done.21, ...), custom_call_target="tpu_custom_call" | custom-call | flops 1509949440 | bytes 13885456 | tf_op jit(solution)/shard_map/expand/pallas_call | solution.py:595
  79.4 9.1 %collective-permute-done.21.p1 = bf16[4,96,768]{2,1,0:T(8,128)(2,1)S(1)} collective-permute-done((bf16[4,96,768]{2,1,0:T(8,128)(2,1)S(1)}, bf16[4,96,768]{2,1,0:T(8,128)(2,1)S(1)}, u32[]{:S(2)}, u32[]{:S(2)}) %collective-permute-start.21) | collective-permute-done | bytes 589856 | tf_op jit(solution)/shard_map/down_1/ppermute | solution.py:492
  88.6 1.0 collective-permute-start.27
  90.2 1.8 collective-permute-done.28.active_twin
  92.0 3.1 %down_grad.1 = (bf16[4,96,768]{2,1,0:T(8,128)(2,1)S(1)}, bf16[4,96,768]{2,1,0:T(8,128)(2,1)S(1)}, bf16[4,96,768]{2,1,0:T(8,128)(2,1)S(1)}, bf16[4,96,768]{2,1,0:T(8,128)(2,1)S(1)}, f32[8,768]{1,0:T(8,128)S(1)}) custom-call(s32[4]{0:T(128)S(1)} %copy-done.39, bf16[256,3072]{1,0:T(8,128)(2,1)S(1)} %get-tuple-element.209.active, ...), custom_call_target="tpu_custom_call" | custom-call | flops 1207959552 | bytes 6316048 | tf_op jit(solution)/shard_map/down_grad/pallas_call | solution.py:595
  95.0 1.2 copy-done.32
  96.3 2.3 %collective-permute-done.27.p3 = bf16[4,96,768]{2,1,0:T(8,128)(2,1)S(1)} collective-permute-done((bf16[4,96,768]{2,1,0:T(8,128)(2,1)S(1)}, bf16[4,96,768]{2,1,0:T(8,128)(2,1)S(1)}, u32[]{:S(2)}, u32[]{:S(2)}) %collective-permute-start.27) | collective-permute-done | bytes 589856 | tf_op jit(solution)/shard_map/down_3/ppermute | solution.py:492
  99.1 1.0 collective-permute-start.29
  100.1 1.0 collective-permute-start.30
  101.6 10.2 %back.1 = (f32[256,768]{1,0:T(8,128)}, bf16[256,768]{1,0:T(8,128)(2,1)S(1)}, f32[8,768]{1,0:T(8,128)S(1)}, bf16[256,768]{1,0:T(8,128)(2,1)S(1)}, f32[8,3072]{1,0:T(8,128)S(1)}, /*index=5*/bf16[256,3072]{1,0:T(8,128)(2,1)}) custom-call(s32[4]{0:T(128)S(1)} %copy-done.39, bf16[256,768]{1,0:T(8,128)(2,1)S(1)} %copy-done.37, f32[256,3072]{1,0:T(8,128)} %copy-done.18, ...), custom_call_target="tpu_custom_call" | custom-call | flops 2717908992 | bytes 18628624 | tf_op jit(solution)/shard_map/back/pallas_call | solution.py:595
  112.7 0.9 copy-done.24
  113.7 1.6 collective-permute-done.30
  115.9 1.0 collective-permute-start.42
  116.9 1.9 collective-permute-done.39.branch_twin
  119.4 3.7 %up_grad.1 = (bf16[4,128,768]{2,1,0:T(8,128)(2,1)S(1)}, bf16[4,128,768]{2,1,0:T(8,128)(2,1)S(1)}, bf16[2,128,768]{2,1,0:T(8,128)(2,1)S(1)}, bf16[2,128,768]{2,1,0:T(8,128)(2,1)S(1)}, bf16[4,128,768]{2,1,0:T(8,128)(2,1)S(1)}) custom-call(s32[4]{0:T(128)S(1)} %copy-done.39, bf16[256,3072]{1,0:T(8,128)(2,1)S(1)} %copy-done.40, ...), custom_call_target="tpu_custom_call" | custom-call | flops 1509949440 | bytes 8650768 | tf_op jit(solution)/shard_map/up_grad/pallas_call | solution.py:595
  123.2 1.1 collective-permute-start.40
  124.2 1.6 collective-permute-done.42
  125.9 1.0 collective-permute-start.41
  127.1 3.3 %collective-permute-start.43 = (bf16[96,768]{1,0:T(8,128)(2,1)S(1)}, bf16[96,768]{1,0:T(8,128)(2,1)S(1)}, u32[]{:S(2)}, u32[]{:S(2)}) collective-permute-start(bf16[96,768]{1,0:T(8,128)(2,1)S(1)} %get-tuple-element.315), channel_id=1, source_target_pairs={{0,8},{1,9},{2,10},{3,11},{4,12},{5,13},{6,14},{7,15},{8,0},{9,1},... | collective-permute-start | bytes 442376 | tf_op jit(solution)/shard_map/rs_down_z/ppermute | solution.py:492
  130.5 8.8 %attend_back.1 = (bf16[3,512,768]{2,1,0:T(8,128)(2,1)S(1)}, f32[12,768]{1,0:T(8,128)S(1)}) custom-call(s32[4]{0:T(128)S(1)} %copy-done.39, bf16[256,768]{1,0:T(8,128)(2,1)S(1)} %copy-done.31, bf16[512,768]{1,0:T(8,128)(2,1)S(1)} %copy-done.19, bf16[512,768]{1,0:T(8,128)(2,1)S(1)} %copy-done.20, bf16[256,768]{1,0:T(8,128)(2,1)S(1)} %get-tuple-element.241.context_grad, ...), custom_call_target="tpu_custom_call" | custom-call | flops 1610612736 | bytes 8687632 | tf_op jit(solution)/shard_map/attend_back/pallas_call | solution.py:595
  139.7 1.0 collective-permute-start.48
  140.7 1.5 collective-permute-start.49
  142.2 3.4 %first_grad.1 = (f32[256,768]{1,0:T(8,128)S(1)}, f32[256,768]{1,0:T(8,128)S(1)}, f32[24,768]{1,0:T(8,128)S(1)}) custom-call(s32[4]{0:T(128)S(1)} %copy-done.39, bf16[256,768]{1,0:T(8,128)(2,1)S(1)} %copy-done.4, bf16[256,768]{1,0:T(8,128)(2,1)S(1)} %copy-done.9, bf16[3,512,768]{2,1,0:T(8,128)(2,1)S(1)} %get-tuple-element.244.grads, ...), custom_call_target="tpu_custom_call" | custom-call | flops 1509949440 | bytes 8515600 | tf_op jit(solution)/shard_map/first_grad/pallas_call | solution.py:595
  145.7 2.0 %collective-permute-start.50 = (bf16[96,768]{1,0:T(8,128)(2,1)S(1)}, bf16[96,768]{1,0:T(8,128)(2,1)S(1)}, u32[]{:S(2)}, u32[]{:S(2)}) collective-permute-start(bf16[96,768]{1,0:T(8,128)(2,1)S(1)} %get-tuple-element.264), channel_id=1, source_target_pairs={{0,24},{1,25},{2,26},{3,27},{4,28},{5,29},{6,30},{7,31},{8,16},{9,... | collective-permute-start | bytes 442376 | tf_op jit(solution)/shard_map/rs_down_z/ppermute | solution.py:492
  147.8 5.9 %qkv_grad.1 = (bf16[4,80,768]{2,1,0:T(8,128)(2,1)S(1)}, bf16[4,80,768]{2,1,0:T(8,128)(2,1)S(1)}, bf16[4,80,768]{2,1,0:T(8,128)(2,1)S(1)}, bf16[4,80,768]{2,1,0:T(8,128)(2,1)S(1)}) custom-call(s32[4]{0:T(128)S(1)} %copy-done.39, bf16[3,512,768]{2,1,0:T(8,128)(2,1)S(1)} %get-tuple-element.244.grads, ...), custom_call_target="tpu_custom_call" | custom-call | flops 1811939328 | bytes 10125328 | tf_op jit(solution)/shard_map/qkv_grad/pallas_call | solution.py:595
  153.7 1.3 collective-permute-start.47
  156.3 4.3 %collective-permute-start.53 = (bf16[128,768]{1,0:T(8,128)(2,1)S(1)}, bf16[128,768]{1,0:T(8,128)(2,1)S(1)}, u32[]{:S(2)}, u32[]{:S(2)}) collective-permute-start(bf16[128,768]{1,0:T(8,128)(2,1)S(1)} %get-tuple-element.308), channel_id=1, source_target_pairs={{0,8},{1,9},{2,10},{3,11},{4,12},{5,13},{6,14},{7,15},{8,0},{9,1},... | collective-permute-start | bytes 589832 | tf_op jit(solution)/shard_map/rs_up_z/ppermute | solution.py:492
  160.6 1.0 input_grad.1
  161.7 0.9 collective-permute-done.47
  162.7 1.2 collective-permute-start.51
  164.0 3.1 %collective-permute-done.53 = bf16[128,768]{1,0:T(8,128)(2,1)S(1)} collective-permute-done((bf16[128,768]{1,0:T(8,128)(2,1)S(1)}, bf16[128,768]{1,0:T(8,128)(2,1)S(1)}, u32[]{:S(2)}, u32[]{:S(2)}) %collective-permute-start.53) | collective-permute-done | bytes 196640 | tf_op jit(solution)/shard_map/rs_up_z/ppermute | solution.py:492
  167.1 6.4 %collective-permute-done.54 = bf16[128,768]{1,0:T(8,128)(2,1)S(1)} collective-permute-done((bf16[128,768]{1,0:T(8,128)(2,1)S(1)}, bf16[128,768]{1,0:T(8,128)(2,1)S(1)}, u32[]{:S(2)}, u32[]{:S(2)}) %collective-permute-start.54) | collective-permute-done | bytes 196640 | tf_op jit(solution)/shard_map/rs_up_z/ppermute | solution.py:492
  174.9 6.1 %finish.1 = f32[256,768]{1,0:T(8,128)} custom-call(s32[4]{0:T(128)} %pad_add_fusion.place, bf16[256,3072]{1,0:T(8,128)(2,1)} %copy-done.32, f32[256,768]{1,0:T(8,128)} %copy-done.10, f32[8,768]{1,0:T(8,128)} %get-tuple-element.202.vectors, bf16[4,96,768]{2,1,0:T(8,128)(2,1)} %copy-done.5, bf16[4,96,768]{2,1,0:T(8,128)(2,1)} %copy-done.23, ...), custom_call_target="tpu_custom_call" | custom-call | flops 1207959552 | bytes 7888912 | tf_op jit(solution)/shard_map/finish/pallas_call | solution.py:595
  182.1 3.7 %collective-permute-start.57 = (bf16[80,768]{1,0:T(8,128)(2,1)S(1)}, bf16[80,768]{1,0:T(8,128)(2,1)S(1)}, u32[]{:S(2)}, u32[]{:S(2)}) collective-permute-start(bf16[80,768]{1,0:T(8,128)(2,1)S(1)} %get-tuple-element.317), channel_id=1, source_target_pairs={{0,16},{1,17},{2,18},{3,19},{4,20},{5,21},{6,22},{7,23},{8,24},{9,... | collective-permute-start | bytes 368648 | tf_op jit(solution)/shard_map/rs_qkv_z/ppermute | solution.py:492
  187.1 2.4 %collective-permute-done.56.z1 = bf16[80,768]{1,0:T(8,128)(2,1)S(1)} collective-permute-done((bf16[80,768]{1,0:T(8,128)(2,1)S(1)}, bf16[80,768]{1,0:T(8,128)(2,1)S(1)}, u32[]{:S(2)}, u32[]{:S(2)}) %collective-permute-start.56) | collective-permute-done | bytes 122912 | tf_op jit(solution)/shard_map/rs_qkv_z/ppermute | solution.py:492
  189.5 3.2 %collective-permute-done.57.z2 = bf16[80,768]{1,0:T(8,128)(2,1)S(1)} collective-permute-done((bf16[80,768]{1,0:T(8,128)(2,1)S(1)}, bf16[80,768]{1,0:T(8,128)(2,1)S(1)}, u32[]{:S(2)}, u32[]{:S(2)}) %collective-permute-start.57) | collective-permute-done | bytes 122912 | tf_op jit(solution)/shard_map/rs_qkv_z/ppermute | solution.py:492
  192.7 1.1 last.1
  (208 shorter events, 16.6 us)
Async XLA Ops:
  2.6 16.5 %collective-permute-start = (bf16[80,768]{1,0:T(8,128)(2,1)}, bf16[80,768]{1,0:T(8,128)(2,1)S(1)}, u32[]{:S(2)}, u32[]{:S(2)}) collective-permute-start(bf16[80,768]{1,0:T(8,128)(2,1)} %get-tuple-element.159), channel_id=1, source_target_pairs={{0,8},{1,9},{2,10},{3,11},{4,12},{5,13},{6,14},{7,15},{8,0},{9,1},... | collective-permute-start | bytes 368648 | tf_op jit(solution)/shard_map/qkv_z/ppermute | solution.py:492
  5.6 13.5 %collective-permute-start.1 = (bf16[80,768]{1,0:T(8,128)(2,1)}, bf16[80,768]{1,0:T(8,128)(2,1)S(1)}, u32[]{:S(2)}, u32[]{:S(2)}) collective-permute-start(bf16[80,768]{1,0:T(8,128)(2,1)} %get-tuple-element.159), channel_id=1, source_target_pairs={{0,16},{1,17},{2,18},{3,19},{4,20},{5,21},{6,22},{7,23},{8,24},{9,... | collective-permute-start | bytes 368648 | tf_op jit(solution)/shard_map/qkv_z/ppermute | solution.py:492
  8.2 10.9 %collective-permute-start.2 = (bf16[80,768]{1,0:T(8,128)(2,1)}, bf16[80,768]{1,0:T(8,128)(2,1)S(1)}, u32[]{:S(2)}, u32[]{:S(2)}) collective-permute-start(bf16[80,768]{1,0:T(8,128)(2,1)} %get-tuple-element.159), channel_id=1, source_target_pairs={{0,24},{1,25},{2,26},{3,27},{4,28},{5,29},{6,30},{7,31},{8,16},{9,... | collective-permute-start | bytes 368648 | tf_op jit(solution)/shard_map/qkv_z/ppermute | solution.py:492
  8.2 10.9 %collective-permute-start.3 = (bf16[256,768]{1,0:T(8,128)(2,1)}, bf16[256,768]{1,0:T(8,128)(2,1)S(1)}, u32[]{:S(2)}, u32[]{:S(2)}) collective-permute-start(bf16[256,768]{1,0:T(8,128)(2,1)} %frames.3), channel_id=1, source_target_pairs={{0,1},{1,0},{2,3},{3,2},{4,5},{5,4},{6,7},{7,6},{8,9},{9,8},{10,11... | collective-permute-start | bytes 1179656 | tf_op jit(solution)/shard_map/frames_pack/ppermute | solution.py:492
  19.1 31.8 %copy-start.8 = (bf16[256,768]{1,0:T(8,128)(2,1)}, bf16[256,768]{1,0:T(8,128)(2,1)S(1)}, u32[]{:S(2)}) copy-start(bf16[256,768]{1,0:T(8,128)(2,1)S(1)} %collective-permute-done.3.other.mate_frames) | copy-start | bytes 1179652
  19.2 31.7 %copy-start.43 = (bf16[4,80,768]{2,1,0:T(8,128)(2,1)}, bf16[4,80,768]{2,1,0:T(8,128)(2,1)S(1)}, u32[]{:S(2)}) copy-start(bf16[4,80,768]{2,1,0:T(8,128)(2,1)S(1)} %pad_maximum_fusion.2.p0) | copy-start | bytes 1474564
  19.2 14.8 %collective-permute-start.4 = (bf16[4,80,768]{2,1,0:T(8,128)(2,1)S(1)}, bf16[4,80,768]{2,1,0:T(8,128)(2,1)S(1)}, u32[]{:S(2)}, u32[]{:S(2)}) collective-permute-start(bf16[4,80,768]{2,1,0:T(8,128)(2,1)S(1)} %pad_maximum_fusion.2.p0), channel_id=1, source_target_pairs={{0,1},{1,0},{2,6},{3,7},{4,5},{5,4},{6,2},{7,3},{8,9},{9,8},{10,14... | collective-permute-start | bytes 1474568 | tf_op jit(solution)/shard_map/qkv_1/ppermute | solution.py:492
  20.4 5.7 %collective-permute-start.7 = (bf16[256,768]{1,0:T(8,128)(2,1)S(1)}, bf16[256,768]{1,0:T(8,128)(2,1)S(1)}, u32[]{:S(2)}, u32[]{:S(2)}) collective-permute-start(bf16[256,768]{1,0:T(8,128)(2,1)S(1)} %copy-done.36), channel_id=1, source_target_pairs={{0,2},{1,3},{2,0},{3,1},{4,6},{5,7},{6,4},{7,5},{8,10},{9,11},{10,... | collective-permute-start | bytes 1179656 | tf_op jit(solution)/shard_map/twin/ppermute | solution.py:492
  20.4 11.3 %collective-permute-start.5 = (bf16[128,768]{1,0:T(8,128)(2,1)S(1)}, bf16[128,768]{1,0:T(8,128)(2,1)S(1)}, u32[]{:S(2)}, u32[]{:S(2)}) collective-permute-start(bf16[128,768]{1,0:T(8,128)(2,1)S(1)} %copy-done.51), channel_id=1, source_target_pairs={{0,8},{1,9},{2,10},{3,11},{4,12},{5,13},{6,14},{7,15},{8,0},{9,1},... | collective-permute-start | bytes 589832 | tf_op jit(solution)/shard_map/up_z/ppermute | solution.py:492
  21.8 12.3 %collective-permute-start.6 = (bf16[128,768]{1,0:T(8,128)(2,1)S(1)}, bf16[128,768]{1,0:T(8,128)(2,1)S(1)}, u32[]{:S(2)}, u32[]{:S(2)}) collective-permute-start(bf16[128,768]{1,0:T(8,128)(2,1)S(1)} %copy-done.51), channel_id=1, source_target_pairs={{0,16},{1,17},{2,18},{3,19},{4,20},{5,21},{6,22},{7,23},{8,24},{9,... | collective-permute-start | bytes 589832 | tf_op jit(solution)/shard_map/up_z/ppermute | solution.py:492
  24.5 13.4 %collective-permute-start.9 = (bf16[4,80,768]{2,1,0:T(8,128)(2,1)S(1)}, bf16[4,80,768]{2,1,0:T(8,128)(2,1)S(1)}, u32[]{:S(2)}, u32[]{:S(2)}) collective-permute-start(bf16[4,80,768]{2,1,0:T(8,128)(2,1)S(1)} %pad_maximum_fusion.2.p0), channel_id=1, source_target_pairs={{0,4},{1,5},{2,3},{3,2},{4,0},{5,1},{6,7},{7,6},{8,12},{9,13},{10,... | collective-permute-start | bytes 1474568 | tf_op jit(solution)/shard_map/qkv_2/ppermute | solution.py:492
  34.0 9.1 %collective-permute-start.10 = (bf16[4,80,768]{2,1,0:T(8,128)(2,1)S(1)}, bf16[4,80,768]{2,1,0:T(8,128)(2,1)S(1)}, u32[]{:S(2)}, u32[]{:S(2)}) collective-permute-start(bf16[4,80,768]{2,1,0:T(8,128)(2,1)S(1)} %collective-permute-done.4.p1), channel_id=1, source_target_pairs={{0,4},{1,5},{2,3},{3,2},{4,0},{5,1},{6,7},{7,6},{8,12},{9,13},{10,... | collective-permute-start | bytes 1474568 | tf_op jit(solution)/shard_map/qkv_3/ppermute | solution.py:492
  35.5 7.6 %collective-permute-start.8 = (bf16[128,768]{1,0:T(8,128)(2,1)S(1)}, bf16[128,768]{1,0:T(8,128)(2,1)S(1)}, u32[]{:S(2)}, u32[]{:S(2)}) collective-permute-start(bf16[128,768]{1,0:T(8,128)(2,1)S(1)} %copy-done.51), channel_id=1, source_target_pairs={{0,24},{1,25},{2,26},{3,27},{4,28},{5,29},{6,30},{7,31},{8,16},{9,... | collective-permute-start | bytes 589832 | tf_op jit(solution)/shard_map/up_z/ppermute | solution.py:492
  43.2 32.0 %copy-start.3 = (bf16[4,128,768]{2,1,0:T(8,128)(2,1)}, bf16[4,128,768]{2,1,0:T(8,128)(2,1)S(1)}, u32[]{:S(2)}) copy-start(bf16[4,128,768]{2,1,0:T(8,128)(2,1)S(1)} %pad_maximum_fusion.p0.u0) | copy-start | bytes 2359300
  43.2 16.5 %collective-permute-start.12 = (bf16[4,128,768]{2,1,0:T(8,128)(2,1)S(1)}, bf16[4,128,768]{2,1,0:T(8,128)(2,1)S(1)}, u32[]{:S(2)}, u32[]{:S(2)}) collective-permute-start(bf16[4,128,768]{2,1,0:T(8,128)(2,1)S(1)} %pad_maximum_fusion.p0.u0), channel_id=1, source_target_pairs={{0,1},{1,0},{2,6},{3,7},{4,5},{5,4},{6,2},{7,3},{8,9},{9,8},{10,14... | collective-permute-start | bytes 2359304 | tf_op jit(solution)/shard_map/up_1/ppermute | solution.py:492
  44.7 1.9 collective-permute-start.13
  44.7 4.1 %collective-permute-start.14 = (bf16[4,80,768]{2,1,0:T(8,128)(2,1)S(1)}, bf16[4,80,768]{2,1,0:T(8,128)(2,1)S(1)}, u32[]{:S(2)}, u32[]{:S(2)}) collective-permute-start(bf16[4,80,768]{2,1,0:T(8,128)(2,1)S(1)} %collective-permute-done.4.p1), channel_id=1, source_target_pairs={{0,2},{1,3},{2,0},{3,1},{4,6},{5,7},{6,4},{7,5},{8,10},{9,11},{10,... | collective-permute-start | bytes 1474568 | tf_op jit(solution)/shard_map/twin/ppermute | solution.py:492
  45.2 4.1 %collective-permute-start.15 = (bf16[4,80,768]{2,1,0:T(8,128)(2,1)S(1)}, bf16[4,80,768]{2,1,0:T(8,128)(2,1)S(1)}, u32[]{:S(2)}, u32[]{:S(2)}) collective-permute-start(bf16[4,80,768]{2,1,0:T(8,128)(2,1)S(1)} %collective-permute-done.9.p2), channel_id=1, source_target_pairs={{0,2},{1,3},{2,0},{3,1},{4,6},{5,7},{6,4},{7,5},{8,10},{9,11},{10,... | collective-permute-start | bytes 1474568 | tf_op jit(solution)/shard_map/twin/ppermute | solution.py:492
  45.2 5.6 %collective-permute-start.16 = (bf16[4,80,768]{2,1,0:T(8,128)(2,1)S(1)}, bf16[4,80,768]{2,1,0:T(8,128)(2,1)S(1)}, u32[]{:S(2)}, u32[]{:S(2)}) collective-permute-start(bf16[4,80,768]{2,1,0:T(8,128)(2,1)S(1)} %collective-permute-done.10.p3), channel_id=1, source_target_pairs={{0,2},{1,3},{2,0},{3,1},{4,6},{5,7},{6,4},{7,5},{8,10},{9,11},{10,... | collective-permute-start | bytes 1474568 | tf_op jit(solution)/shard_map/twin/ppermute | solution.py:492
  46.6 13.1 %collective-permute-start.17 = (bf16[96,768]{1,0:T(8,128)(2,1)S(1)}, bf16[96,768]{1,0:T(8,128)(2,1)S(1)}, u32[]{:S(2)}, u32[]{:S(2)}) collective-permute-start(bf16[96,768]{1,0:T(8,128)(2,1)S(1)} %copy-done.52), channel_id=1, source_target_pairs={{0,8},{1,9},{2,10},{3,11},{4,12},{5,13},{6,14},{7,15},{8,0},{9,1},... | collective-permute-start | bytes 442376 | tf_op jit(solution)/shard_map/down_z/ppermute | solution.py:492
  48.8 10.9 %collective-permute-start.18 = (bf16[96,768]{1,0:T(8,128)(2,1)S(1)}, bf16[96,768]{1,0:T(8,128)(2,1)S(1)}, u32[]{:S(2)}, u32[]{:S(2)}) collective-permute-start(bf16[96,768]{1,0:T(8,128)(2,1)S(1)} %copy-done.52), channel_id=1, source_target_pairs={{0,16},{1,17},{2,18},{3,19},{4,20},{5,21},{6,22},{7,23},{8,24},{9,... | collective-permute-start | bytes 442376 | tf_op jit(solution)/shard_map/down_z/ppermute | solution.py:492
  49.4 21.5 %collective-permute-start.11 = (bf16[4,128,768]{2,1,0:T(8,128)(2,1)S(1)}, bf16[4,128,768]{2,1,0:T(8,128)(2,1)S(1)}, u32[]{:S(2)}, u32[]{:S(2)}) collective-permute-start(bf16[4,128,768]{2,1,0:T(8,128)(2,1)S(1)} %pad_maximum_fusion.p0.u0), channel_id=1, source_target_pairs={{0,4},{1,5},{2,3},{3,2},{4,0},{5,1},{6,7},{7,6},{8,12},{9,13},{10,... | collective-permute-start | bytes 2359304 | tf_op jit(solution)/shard_map/up_2/ppermute | solution.py:492
  59.8 12.1 %collective-permute-start.19 = (bf16[4,128,768]{2,1,0:T(8,128)(2,1)S(1)}, bf16[4,128,768]{2,1,0:T(8,128)(2,1)S(1)}, u32[]{:S(2)}, u32[]{:S(2)}) collective-permute-start(bf16[4,128,768]{2,1,0:T(8,128)(2,1)S(1)} %collective-permute-done.12.p1.u1), channel_id=1, source_target_pairs={{0,4},{1,5},{2,3},{3,2},{4,0},{5,1},{6,7},{7,6},{8,12},{9,13},{10,... | collective-permute-start | bytes 2359304 | tf_op jit(solution)/shard_map/up_3/ppermute | solution.py:492
  60.5 13.0 %collective-permute-start.23 = (bf16[4,128,768]{2,1,0:T(8,128)(2,1)S(1)}, bf16[4,128,768]{2,1,0:T(8,128)(2,1)S(1)}, u32[]{:S(2)}, u32[]{:S(2)}) collective-permute-start(bf16[4,128,768]{2,1,0:T(8,128)(2,1)S(1)} %pad_maximum_fusion.p0.u0), channel_id=1, source_target_pairs={{0,2},{1,3},{2,0},{3,1},{4,6},{5,7},{6,4},{7,5},{8,10},{9,11},{10,... | collective-permute-start | bytes 2359304 | tf_op jit(solution)/shard_map/twin/ppermute | solution.py:492
  60.5 10.3 %collective-permute-start.20 = (bf16[96,768]{1,0:T(8,128)(2,1)S(1)}, bf16[96,768]{1,0:T(8,128)(2,1)S(1)}, u32[]{:S(2)}, u32[]{:S(2)}) collective-permute-start(bf16[96,768]{1,0:T(8,128)(2,1)S(1)} %copy-done.52), channel_id=1, source_target_pairs={{0,24},{1,25},{2,26},{3,27},{4,28},{5,29},{6,30},{7,31},{8,16},{9,... | collective-permute-start | bytes 442376 | tf_op jit(solution)/shard_map/down_z/ppermute | solution.py:492
  63.1 11.8 %collective-permute-start.24 = (bf16[4,128,768]{2,1,0:T(8,128)(2,1)S(1)}, bf16[4,128,768]{2,1,0:T(8,128)(2,1)S(1)}, u32[]{:S(2)}, u32[]{:S(2)}) collective-permute-start(bf16[4,128,768]{2,1,0:T(8,128)(2,1)S(1)} %collective-permute-done.12.p1.u1), channel_id=1, source_target_pairs={{0,2},{1,3},{2,0},{3,1},{4,6},{5,7},{6,4},{7,5},{8,10},{9,11},{10,... | collective-permute-start | bytes 2359304 | tf_op jit(solution)/shard_map/twin/ppermute | solution.py:492
  71.8 3.0 %collective-permute-start.25 = (bf16[4,128,768]{2,1,0:T(8,128)(2,1)S(1)}, bf16[4,128,768]{2,1,0:T(8,128)(2,1)S(1)}, u32[]{:S(2)}, u32[]{:S(2)}) collective-permute-start(bf16[4,128,768]{2,1,0:T(8,128)(2,1)S(1)} %collective-permute-done.11.p2.u2), channel_id=1, source_target_pairs={{0,2},{1,3},{2,0},{3,1},{4,6},{5,7},{6,4},{7,5},{8,10},{9,11},{10,... | collective-permute-start | bytes 2359304 | tf_op jit(solution)/shard_map/twin/ppermute | solution.py:492
  72.0 3.3 %collective-permute-start.26 = (bf16[4,128,768]{2,1,0:T(8,128)(2,1)S(1)}, bf16[4,128,768]{2,1,0:T(8,128)(2,1)S(1)}, u32[]{:S(2)}, u32[]{:S(2)}) collective-permute-start(bf16[4,128,768]{2,1,0:T(8,128)(2,1)S(1)} %collective-permute-done.19.p3.u3), channel_id=1, source_target_pairs={{0,2},{1,3},{2,0},{3,1},{4,6},{5,7},{6,4},{7,5},{8,10},{9,11},{10,... | collective-permute-start | bytes 2359304 | tf_op jit(solution)/shard_map/twin/ppermute | solution.py:492
  72.4 29.2 %copy-start.5 = (bf16[4,96,768]{2,1,0:T(8,128)(2,1)}, bf16[4,96,768]{2,1,0:T(8,128)(2,1)S(1)}, u32[]{:S(2)}) copy-start(bf16[4,96,768]{2,1,0:T(8,128)(2,1)S(1)} %pad_maximum_fusion.1.p0) | copy-start | bytes 1769476
  72.4 16.1 %collective-permute-start.21 = (bf16[4,96,768]{2,1,0:T(8,128)(2,1)S(1)}, bf16[4,96,768]{2,1,0:T(8,128)(2,1)S(1)}, u32[]{:S(2)}, u32[]{:S(2)}) collective-permute-start(bf16[4,96,768]{2,1,0:T(8,128)(2,1)S(1)} %pad_maximum_fusion.1.p0), channel_id=1, source_target_pairs={{0,1},{1,0},{2,6},{3,7},{4,5},{5,4},{6,2},{7,3},{8,9},{9,8},{10,14... | collective-permute-start | bytes 1769480 | tf_op jit(solution)/shard_map/down_1/ppermute | solution.py:492
  73.6 15.0 %collective-permute-start.22 = (bf16[4,96,768]{2,1,0:T(8,128)(2,1)S(1)}, bf16[4,96,768]{2,1,0:T(8,128)(2,1)S(1)}, u32[]{:S(2)}, u32[]{:S(2)}) collective-permute-start(bf16[4,96,768]{2,1,0:T(8,128)(2,1)S(1)} %pad_maximum_fusion.1.p0), channel_id=1, source_target_pairs={{0,4},{1,5},{2,3},{3,2},{4,0},{5,1},{6,7},{7,6},{8,12},{9,13},{10,... | collective-permute-start | bytes 1769480 | tf_op jit(solution)/shard_map/down_2/ppermute | solution.py:492
  88.5 3.4 %collective-permute-start.28 = (bf16[256,3072]{1,0:T(8,128)(2,1)S(1)}, bf16[256,3072]{1,0:T(8,128)(2,1)S(1)}, u32[]{:S(2)}, u32[]{:S(2)}) collective-permute-start(bf16[256,3072]{1,0:T(8,128)(2,1)S(1)} %get-tuple-element.209.active), channel_id=1, source_target_pairs={{0,2},{1,3},{2,0},{3,1},{4,6},{5,7},{6,4},{7,5},{8,10},{9,11},{10,... | collective-permute-start | bytes 4718600 | tf_op jit(solution)/shard_map/twin/ppermute | solution.py:492
  88.6 9.9 %collective-permute-start.27 = (bf16[4,96,768]{2,1,0:T(8,128)(2,1)S(1)}, bf16[4,96,768]{2,1,0:T(8,128)(2,1)S(1)}, u32[]{:S(2)}, u32[]{:S(2)}) collective-permute-start(bf16[4,96,768]{2,1,0:T(8,128)(2,1)S(1)} %collective-permute-done.21.p1), channel_id=1, source_target_pairs={{0,4},{1,5},{2,3},{3,2},{4,0},{5,1},{6,7},{7,6},{8,12},{9,13},{10,... | collective-permute-start | bytes 1769480 | tf_op jit(solution)/shard_map/down_3/ppermute | solution.py:492
  89.7 9.4 %collective-permute-start.31 = (bf16[4,96,768]{2,1,0:T(8,128)(2,1)S(1)}, bf16[4,96,768]{2,1,0:T(8,128)(2,1)S(1)}, u32[]{:S(2)}, u32[]{:S(2)}) collective-permute-start(bf16[4,96,768]{2,1,0:T(8,128)(2,1)S(1)} %pad_maximum_fusion.1.p0), channel_id=1, source_target_pairs={{0,2},{1,3},{2,0},{3,1},{4,6},{5,7},{6,4},{7,5},{8,10},{9,11},{10,... | collective-permute-start | bytes 1769480 | tf_op jit(solution)/shard_map/twin/ppermute | solution.py:492
  89.7 10.4 %collective-permute-start.32 = (bf16[4,96,768]{2,1,0:T(8,128)(2,1)S(1)}, bf16[4,96,768]{2,1,0:T(8,128)(2,1)S(1)}, u32[]{:S(2)}, u32[]{:S(2)}) collective-permute-start(bf16[4,96,768]{2,1,0:T(8,128)(2,1)S(1)} %collective-permute-done.21.p1), channel_id=1, source_target_pairs={{0,2},{1,3},{2,0},{3,1},{4,6},{5,7},{6,4},{7,5},{8,10},{9,11},{10,... | collective-permute-start | bytes 1769480 | tf_op jit(solution)/shard_map/twin/ppermute | solution.py:492
  90.2 10.9 %collective-permute-start.33 = (bf16[4,96,768]{2,1,0:T(8,128)(2,1)S(1)}, bf16[4,96,768]{2,1,0:T(8,128)(2,1)S(1)}, u32[]{:S(2)}, u32[]{:S(2)}) collective-permute-start(bf16[4,96,768]{2,1,0:T(8,128)(2,1)S(1)} %collective-permute-done.22.p2), channel_id=1, source_target_pairs={{0,2},{1,3},{2,0},{3,1},{4,6},{5,7},{6,4},{7,5},{8,10},{9,11},{10,... | collective-permute-start | bytes 1769480 | tf_op jit(solution)/shard_map/twin/ppermute | solution.py:492
  98.5 2.6 %collective-permute-start.34 = (bf16[4,96,768]{2,1,0:T(8,128)(2,1)S(1)}, bf16[4,96,768]{2,1,0:T(8,128)(2,1)S(1)}, u32[]{:S(2)}, u32[]{:S(2)}) collective-permute-start(bf16[4,96,768]{2,1,0:T(8,128)(2,1)S(1)} %collective-permute-done.27.p3), channel_id=1, source_target_pairs={{0,2},{1,3},{2,0},{3,1},{4,6},{5,7},{6,4},{7,5},{8,10},{9,11},{10,... | collective-permute-start | bytes 1769480 | tf_op jit(solution)/shard_map/twin/ppermute | solution.py:492
  98.5 15.1 %collective-permute-start.37 = (bf16[512,768]{1,0:T(8,128)(2,1)S(1)}, bf16[512,768]{1,0:T(8,128)(2,1)S(1)}, u32[]{:S(2)}, u32[]{:S(2)}) collective-permute-start(bf16[512,768]{1,0:T(8,128)(2,1)S(1)} %copy-done.33), channel_id=1, source_target_pairs={{0,2},{1,3},{2,0},{3,1},{4,6},{5,7},{6,4},{7,5},{8,10},{9,11},{10,... | collective-permute-start | bytes 2359304 | tf_op jit(solution)/shard_map/twin/ppermute | solution.py:492
  99.1 14.6 %collective-permute-start.29 = (bf16[4,96,768]{2,1,0:T(8,128)(2,1)S(1)}, bf16[4,96,768]{2,1,0:T(8,128)(2,1)S(1)}, u32[]{:S(2)}, u32[]{:S(2)}) collective-permute-start(bf16[4,96,768]{2,1,0:T(8,128)(2,1)S(1)} %get-tuple-element.217), channel_id=1, source_target_pairs={{0,4},{1,5},{2,3},{3,2},{4,0},{5,1},{6,7},{7,6},{8,12},{9,13},{10,... | collective-permute-start | bytes 1769480 | tf_op jit(solution)/shard_map/rs_down_3/ppermute | solution.py:492
  100.1 15.2 %collective-permute-start.30 = (bf16[4,96,768]{2,1,0:T(8,128)(2,1)S(1)}, bf16[4,96,768]{2,1,0:T(8,128)(2,1)S(1)}, u32[]{:S(2)}, u32[]{:S(2)}) collective-permute-start(bf16[4,96,768]{2,1,0:T(8,128)(2,1)S(1)} %get-tuple-element.218), channel_id=1, source_target_pairs={{0,4},{1,5},{2,3},{3,2},{4,0},{5,1},{6,7},{7,6},{8,12},{9,13},{10,... | collective-permute-start | bytes 1769480 | tf_op jit(solution)/shard_map/rs_down_2/ppermute | solution.py:492
  101.1 12.5 %collective-permute-start.35 = (bf16[256,768]{1,0:T(8,128)(2,1)S(1)}, bf16[256,768]{1,0:T(8,128)(2,1)S(1)}, u32[]{:S(2)}, u32[]{:S(2)}) collective-permute-start(bf16[256,768]{1,0:T(8,128)(2,1)S(1)} %get-tuple-element.225.context), channel_id=1, source_target_pairs={{0,2},{1,3},{2,0},{3,1},{4,6},{5,7},{6,4},{7,5},{8,10},{9,11},{10,... | collective-permute-start | bytes 1179656 | tf_op jit(solution)/shard_map/twin/ppermute | solution.py:492
  101.1 12.5 %collective-permute-start.36 = (bf16[256,768]{1,0:T(8,128)(2,1)S(1)}, bf16[256,768]{1,0:T(8,128)(2,1)S(1)}, u32[]{:S(2)}, u32[]{:S(2)}) collective-permute-start(bf16[256,768]{1,0:T(8,128)(2,1)S(1)} %get-tuple-element.226.second), channel_id=1, source_target_pairs={{0,2},{1,3},{2,0},{3,1},{4,6},{5,7},{6,4},{7,5},{8,10},{9,11},{10,... | collective-permute-start | bytes 1179656 | tf_op jit(solution)/shard_map/twin/ppermute | solution.py:492
  115.3 4.2 %collective-permute-start.38 = (bf16[256,3072]{1,0:T(8,128)(2,1)}, bf16[256,3072]{1,0:T(8,128)(2,1)S(1)}, u32[]{:S(2)}, u32[]{:S(2)}) collective-permute-start(bf16[256,3072]{1,0:T(8,128)(2,1)} %get-tuple-element.232.hidden), channel_id=1, source_target_pairs={{0,2},{1,3},{2,0},{3,1},{4,6},{5,7},{6,4},{7,5},{8,10},{9,11},{10,... | collective-permute-start | bytes 4718600 | tf_op jit(solution)/shard_map/twin/ppermute | solution.py:492
  115.3 3.6 %collective-permute-start.39 = (bf16[256,768]{1,0:T(8,128)(2,1)S(1)}, bf16[256,768]{1,0:T(8,128)(2,1)S(1)}, u32[]{:S(2)}, u32[]{:S(2)}) collective-permute-start(bf16[256,768]{1,0:T(8,128)(2,1)S(1)} %get-tuple-element.234.branch), channel_id=1, source_target_pairs={{0,2},{1,3},{2,0},{3,1},{4,6},{5,7},{6,4},{7,5},{8,10},{9,11},{10,... | collective-permute-start | bytes 1179656 | tf_op jit(solution)/shard_map/twin/ppermute | solution.py:492
  115.9 9.9 %collective-permute-start.42 = (bf16[4,96,768]{2,1,0:T(8,128)(2,1)S(1)}, bf16[4,96,768]{2,1,0:T(8,128)(2,1)S(1)}, u32[]{:S(2)}, u32[]{:S(2)}) collective-permute-start(bf16[4,96,768]{2,1,0:T(8,128)(2,1)S(1)} %add_convert_fusion.1), channel_id=1, source_target_pairs={{0,1},{1,0},{2,6},{3,7},{4,5},{5,4},{6,2},{7,3},{8,9},{9,8},{10,14... | collective-permute-start | bytes 1769480 | tf_op jit(solution)/shard_map/rs_down_1/ppermute | solution.py:492
  123.2 16.3 %collective-permute-start.40 = (bf16[4,128,768]{2,1,0:T(8,128)(2,1)S(1)}, bf16[4,128,768]{2,1,0:T(8,128)(2,1)S(1)}, u32[]{:S(2)}, u32[]{:S(2)}) collective-permute-start(bf16[4,128,768]{2,1,0:T(8,128)(2,1)S(1)} %get-tuple-element.236), channel_id=1, source_target_pairs={{0,4},{1,5},{2,3},{3,2},{4,0},{5,1},{6,7},{7,6},{8,12},{9,13},{10,... | collective-permute-start | bytes 2359304 | tf_op jit(solution)/shard_map/rs_up_3/ppermute | solution.py:492
  125.9 13.6 %collective-permute-start.41 = (bf16[2,128,768]{2,1,0:T(8,128)(2,1)S(1)}, bf16[2,128,768]{2,1,0:T(8,128)(2,1)S(1)}, u32[]{:S(2)}, u32[]{:S(2)}) collective-permute-start(bf16[2,128,768]{2,1,0:T(8,128)(2,1)S(1)} %get-tuple-element.237), channel_id=1, source_target_pairs={{0,4},{1,5},{2,3},{3,2},{4,0},{5,1},{6,7},{7,6},{8,12},{9,13},{10,... | collective-permute-start | bytes 1179656 | tf_op jit(solution)/shard_map/rs_up_2a/ppermute | solution.py:492
  127.1 12.2 %collective-permute-start.43 = (bf16[96,768]{1,0:T(8,128)(2,1)S(1)}, bf16[96,768]{1,0:T(8,128)(2,1)S(1)}, u32[]{:S(2)}, u32[]{:S(2)}) collective-permute-start(bf16[96,768]{1,0:T(8,128)(2,1)S(1)} %get-tuple-element.315), channel_id=1, source_target_pairs={{0,8},{1,9},{2,10},{3,11},{4,12},{5,13},{6,14},{7,15},{8,0},{9,1},... | collective-permute-start | bytes 442376 | tf_op jit(solution)/shard_map/rs_down_z/ppermute | solution.py:492
  130.5 8.9 %collective-permute-start.44 = (bf16[96,768]{1,0:T(8,128)(2,1)S(1)}, bf16[96,768]{1,0:T(8,128)(2,1)S(1)}, u32[]{:S(2)}, u32[]{:S(2)}) collective-permute-start(bf16[96,768]{1,0:T(8,128)(2,1)S(1)} %get-tuple-element.314), channel_id=1, source_target_pairs={{0,16},{1,17},{2,18},{3,19},{4,20},{5,21},{6,22},{7,23},{8,24},{9,... | collective-permute-start | bytes 442376 | tf_op jit(solution)/shard_map/rs_down_z/ppermute | solution.py:492
  139.4 6.2 %collective-permute-start.45 = (bf16[3,512,768]{2,1,0:T(8,128)(2,1)S(1)}, bf16[3,512,768]{2,1,0:T(8,128)(2,1)S(1)}, u32[]{:S(2)}, u32[]{:S(2)}) collective-permute-start(bf16[3,512,768]{2,1,0:T(8,128)(2,1)S(1)} %get-tuple-element.244.grads), channel_id=1, source_target_pairs={{0,2},{1,3},{2,0},{3,1},{4,6},{5,7},{6,4},{7,5},{8,10},{9,11},{10,... | collective-permute-start | bytes 7077896 | tf_op jit(solution)/shard_map/twin/ppermute | solution.py:492
  139.7 16.3 %collective-permute-start.48 = (bf16[4,128,768]{2,1,0:T(8,128)(2,1)S(1)}, bf16[4,128,768]{2,1,0:T(8,128)(2,1)S(1)}, u32[]{:S(2)}, u32[]{:S(2)}) collective-permute-start(bf16[4,128,768]{2,1,0:T(8,128)(2,1)S(1)} %add_convert_fusion), channel_id=1, source_target_pairs={{0,1},{1,0},{2,6},{3,7},{4,5},{5,4},{6,2},{7,3},{8,9},{9,8},{10,14... | collective-permute-start | bytes 2359304 | tf_op jit(solution)/shard_map/rs_up_1/ppermute | solution.py:492
  140.7 15.1 %collective-permute-start.49 = (bf16[2,128,768]{2,1,0:T(8,128)(2,1)S(1)}, bf16[2,128,768]{2,1,0:T(8,128)(2,1)S(1)}, u32[]{:S(2)}, u32[]{:S(2)}) collective-permute-start(bf16[2,128,768]{2,1,0:T(8,128)(2,1)S(1)} %get-tuple-element.261), channel_id=1, source_target_pairs={{0,4},{1,5},{2,3},{3,2},{4,0},{5,1},{6,7},{7,6},{8,12},{9,13},{10,... | collective-permute-start | bytes 1179656 | tf_op jit(solution)/shard_map/rs_up_2b/ppermute | solution.py:492
  145.6 2.1 %collective-permute-start.46 = (f32[24,768]{1,0:T(8,128)S(1)}, f32[24,768]{1,0:T(8,128)S(1)}, u32[]{:S(2)}, u32[]{:S(2)}) collective-permute-start(f32[24,768]{1,0:T(8,128)S(1)} %get-tuple-element.256.small_own), channel_id=1, source_target_pairs={{0,2},{1,3},{2,0},{3,1},{4,6},{5,7},{6,4},{7,5},{8,10},{9,11},{10,... | collective-permute-start | bytes 221192 | tf_op jit(solution)/shard_map/twin/ppermute | solution.py:492
  145.7 10.3 %collective-permute-start.50 = (bf16[96,768]{1,0:T(8,128)(2,1)S(1)}, bf16[96,768]{1,0:T(8,128)(2,1)S(1)}, u32[]{:S(2)}, u32[]{:S(2)}) collective-permute-start(bf16[96,768]{1,0:T(8,128)(2,1)S(1)} %get-tuple-element.264), channel_id=1, source_target_pairs={{0,24},{1,25},{2,26},{3,27},{4,28},{5,29},{6,30},{7,31},{8,16},{9,... | collective-permute-start | bytes 442376 | tf_op jit(solution)/shard_map/rs_down_z/ppermute | solution.py:492
  153.7 8.9 %collective-permute-start.47 = (bf16[4,80,768]{2,1,0:T(8,128)(2,1)S(1)}, bf16[4,80,768]{2,1,0:T(8,128)(2,1)S(1)}, u32[]{:S(2)}, u32[]{:S(2)}) collective-permute-start(bf16[4,80,768]{2,1,0:T(8,128)(2,1)S(1)} %get-tuple-element.258), channel_id=1, source_target_pairs={{0,4},{1,5},{2,3},{3,2},{4,0},{5,1},{6,7},{7,6},{8,12},{9,13},{10,... | collective-permute-start | bytes 1474568 | tf_op jit(solution)/shard_map/rs_qkv_3/ppermute | solution.py:492
  155.0 25.9 %collective-permute-start.52 = (bf16[4,80,768]{2,1,0:T(8,128)(2,1)S(1)}, bf16[4,80,768]{2,1,0:T(8,128)(2,1)S(1)}, u32[]{:S(2)}, u32[]{:S(2)}) collective-permute-start(bf16[4,80,768]{2,1,0:T(8,128)(2,1)S(1)} %get-tuple-element.273), channel_id=1, source_target_pairs={{0,4},{1,5},{2,3},{3,2},{4,0},{5,1},{6,7},{7,6},{8,12},{9,13},{10,... | collective-permute-start | bytes 1474568 | tf_op jit(solution)/shard_map/rs_qkv_2/ppermute | solution.py:492
  156.3 10.8 %collective-permute-start.53 = (bf16[128,768]{1,0:T(8,128)(2,1)S(1)}, bf16[128,768]{1,0:T(8,128)(2,1)S(1)}, u32[]{:S(2)}, u32[]{:S(2)}) collective-permute-start(bf16[128,768]{1,0:T(8,128)(2,1)S(1)} %get-tuple-element.308), channel_id=1, source_target_pairs={{0,8},{1,9},{2,10},{3,11},{4,12},{5,13},{6,14},{7,15},{8,0},{9,1},... | collective-permute-start | bytes 589832 | tf_op jit(solution)/shard_map/rs_up_z/ppermute | solution.py:492
  160.6 12.9 %collective-permute-start.54 = (bf16[128,768]{1,0:T(8,128)(2,1)S(1)}, bf16[128,768]{1,0:T(8,128)(2,1)S(1)}, u32[]{:S(2)}, u32[]{:S(2)}) collective-permute-start(bf16[128,768]{1,0:T(8,128)(2,1)S(1)} %get-tuple-element.311), channel_id=1, source_target_pairs={{0,16},{1,17},{2,18},{3,19},{4,20},{5,21},{6,22},{7,23},{8,24},{9,... | collective-permute-start | bytes 589832 | tf_op jit(solution)/shard_map/rs_up_z/ppermute | solution.py:492
  162.7 18.2 %collective-permute-start.51 = (bf16[4,80,768]{2,1,0:T(8,128)(2,1)S(1)}, bf16[4,80,768]{2,1,0:T(8,128)(2,1)S(1)}, u32[]{:S(2)}, u32[]{:S(2)}) collective-permute-start(bf16[4,80,768]{2,1,0:T(8,128)(2,1)S(1)} %add_convert_fusion.2), channel_id=1, source_target_pairs={{0,1},{1,0},{2,6},{3,7},{4,5},{5,4},{6,2},{7,3},{8,9},{9,8},{10,14... | collective-permute-start | bytes 1474568 | tf_op jit(solution)/shard_map/rs_qkv_1/ppermute | solution.py:492
  173.5 7.5 %collective-permute-start.55 = (bf16[128,768]{1,0:T(8,128)(2,1)S(1)}, bf16[128,768]{1,0:T(8,128)(2,1)S(1)}, u32[]{:S(2)}, u32[]{:S(2)}) collective-permute-start(bf16[128,768]{1,0:T(8,128)(2,1)S(1)} %get-tuple-element.277), channel_id=1, source_target_pairs={{0,24},{1,25},{2,26},{3,27},{4,28},{5,29},{6,30},{7,31},{8,16},{9,... | collective-permute-start | bytes 589832 | tf_op jit(solution)/shard_map/rs_up_z/ppermute | solution.py:492
  182.0 10.7 %collective-permute-start.59 = (bf16[256,768]{1,0:T(8,128)(2,1)S(1)}, bf16[256,768]{1,0:T(8,128)(2,1)S(1)}, u32[]{:S(2)}, u32[]{:S(2)}) collective-permute-start(bf16[256,768]{1,0:T(8,128)(2,1)S(1)} %get-tuple-element.288), channel_id=1, source_target_pairs={{0,1},{1,0},{2,3},{3,2},{4,5},{5,4},{6,7},{7,6},{8,9},{9,8},{10,11... | collective-permute-start | bytes 1179656 | tf_op jit(solution)/shard_map/grad_pack/ppermute | solution.py:492
  182.0 7.5 %collective-permute-start.56 = (bf16[80,768]{1,0:T(8,128)(2,1)S(1)}, bf16[80,768]{1,0:T(8,128)(2,1)S(1)}, u32[]{:S(2)}, u32[]{:S(2)}) collective-permute-start(bf16[80,768]{1,0:T(8,128)(2,1)S(1)} %get-tuple-element.318), channel_id=1, source_target_pairs={{0,8},{1,9},{2,10},{3,11},{4,12},{5,13},{6,14},{7,15},{8,0},{9,1},... | collective-permute-start | bytes 368648 | tf_op jit(solution)/shard_map/rs_qkv_z/ppermute | solution.py:492
  182.1 10.6 %collective-permute-start.57 = (bf16[80,768]{1,0:T(8,128)(2,1)S(1)}, bf16[80,768]{1,0:T(8,128)(2,1)S(1)}, u32[]{:S(2)}, u32[]{:S(2)}) collective-permute-start(bf16[80,768]{1,0:T(8,128)(2,1)S(1)} %get-tuple-element.317), channel_id=1, source_target_pairs={{0,16},{1,17},{2,18},{3,19},{4,20},{5,21},{6,22},{7,23},{8,24},{9,... | collective-permute-start | bytes 368648 | tf_op jit(solution)/shard_map/rs_qkv_z/ppermute | solution.py:492
  185.8 6.9 %collective-permute-start.58 = (bf16[80,768]{1,0:T(8,128)(2,1)S(1)}, bf16[80,768]{1,0:T(8,128)(2,1)S(1)}, u32[]{:S(2)}, u32[]{:S(2)}) collective-permute-start(bf16[80,768]{1,0:T(8,128)(2,1)S(1)} %get-tuple-element.316), channel_id=1, source_target_pairs={{0,24},{1,25},{2,26},{3,27},{4,28},{5,29},{6,30},{7,31},{8,16},{9,... | collective-permute-start | bytes 368648 | tf_op jit(solution)/shard_map/rs_qkv_z/ppermute | solution.py:492
  (50 other events, 422.7 us)

commit v4 on v3

--- a/solution.py
+++ b/solution.py
@@ -923,32 +923,37 @@
 def attend_back_kernel(
     place, queries, keys, values, context_grad, mixed, probs, grads, diagonals
 ):
-    q, k, v, dout = queries[...], keys[...], values[...], context_grad[...]
-    block_len, span = probs.shape[1:]
-    weighted = dout.astype(F32) * mixed[...]
-    row = lax.broadcasted_iota(jnp.int32, (block_len, block_len), 0)
-    lane = lax.broadcasted_iota(jnp.int32, (block_len, block_len), 1)
-    turn = (row + lane == block_len - 1).astype(LOW)
-    blank = jnp.zeros((block_len, block_len), F32)
-    dq, dk, dv = jnp.zeros(q.shape, F32), jnp.zeros(k.shape, F32), jnp.zeros(v.shape, F32)
-    for head in range(2):
-        mine = half_mask(q.shape, head)
-        dout_head = jnp.where(mine, dout, 0)
-        delta = jnp.sum(jnp.where(mine, weighted, 0.0), axis=1, keepdims=True)
-        prob = probs[head]
-        grad = prob.astype(F32) * (dot_nt(dout_head, v) - delta)
-        raw = (grad * (1.0 / math.sqrt(HD))).astype(LOW)
-        dq = dq + dot_nn(raw, jnp.where(half_mask(k.shape, head), k, 0))
-        dk = dk + dot_tn(raw, jnp.where(mine, q, 0))
-        dv = dv + dot_tn(prob, dout_head)
-        turned = jnp.concatenate([dot_nn(turn, raw), blank], axis=1)
-        sheared = pltpu.roll(turned, 0, 1, stride=1, stride_axis=0)
-        diagonals[pl.ds(2 * pl.program_id(0) + head, 1), :] = jnp.sum(sheared, axis=0, keepdims=True) * math.sqrt(HD)
-    own_at = pl.multiple_of(place[0] * block_len, block_len)
-    grads[0] = jnp.zeros(k.shape, LOW)
-    grads[0, pl.ds(own_at, block_len), :] = dq.astype(LOW)
-    grads[1] = dk.astype(LOW)
-    grads[2] = dv.astype(LOW)
+    def of_pair(pair, _):
+        lanes = pl.ds(pl.multiple_of(2 * HD * pair, 2 * HD), 2 * HD)
+        q, k, v, dout = queries[:, lanes], keys[:, lanes], values[:, lanes], context_grad[:, lanes]
+        block_len, span = probs.shape[1:]
+        weighted = dout.astype(F32) * mixed[:, lanes]
+        row = lax.broadcasted_iota(jnp.int32, (block_len, block_len), 0)
+        lane = lax.broadcasted_iota(jnp.int32, (block_len, block_len), 1)
+        turn = (row + lane == block_len - 1).astype(LOW)
+        blank = jnp.zeros((block_len, block_len), F32)
+        dq, dk, dv = jnp.zeros(q.shape, F32), jnp.zeros(k.shape, F32), jnp.zeros(v.shape, F32)
+        for head in range(2):
+            mine = half_mask(q.shape, head)
+            dout_head = jnp.where(mine, dout, 0)
+            delta = jnp.sum(jnp.where(mine, weighted, 0.0), axis=1, keepdims=True)
+            prob = probs[2 * pair + head]
+            grad = prob.astype(F32) * (dot_nt(dout_head, v) - delta)
+            raw = (grad * (1.0 / math.sqrt(HD))).astype(LOW)
+            dq = dq + dot_nn(raw, jnp.where(half_mask(k.shape, head), k, 0))
+            dk = dk + dot_tn(raw, jnp.where(mine, q, 0))
+            dv = dv + dot_tn(prob, dout_head)
+            turned = jnp.concatenate([dot_nn(turn, raw), blank], axis=1)
+            sheared = pltpu.roll(turned, 0, 1, stride=1, stride_axis=0)
+            diagonals[pl.ds(4 * pl.program_id(0) + 2 * pair + head, 1), :] = jnp.sum(sheared, axis=0, keepdims=True) * math.sqrt(HD)
+        own_at = pl.multiple_of(place[0] * block_len, block_len)
+        grads[0, :, lanes] = jnp.zeros(k.shape, LOW)
+        grads[0, pl.ds(own_at, block_len), lanes] = dq.astype(LOW)
+        grads[1, :, lanes] = dk.astype(LOW)
+        grads[2, :, lanes] = dv.astype(LOW)
+        return 0
+
+    lax.fori_loop(0, queries.shape[1] // (2 * HD), of_pair, 0)
 
 
 def total(array):
@@ -1334,15 +1339,15 @@
     grads, diagonals = call(
         attend_back_kernel,
         [
-            SMEM, lanes_of(shard_len), lanes_of(span), lanes_of(span), lanes_of(shard_len), lanes_of(shard_len),
-            heads_of(2, shard_len, span),
+            SMEM, lanes_of(shard_len, 2), lanes_of(span, 2), lanes_of(span, 2), lanes_of(shard_len, 2), lanes_of(shard_len, 2),
+            heads_of(4, shard_len, span),
         ],
         [shape(3, span, width), shape(H, span + shard_len, kind=F32)],
-        [pl.BlockSpec((3, span, pair_lanes), lambda n: (0, 0, n)), whole(H, span + shard_len)],
+        [pl.BlockSpec((3, span, 2 * pair_lanes), lambda n: (0, 0, n)), whole(H, span + shard_len)],
         [],
         (place, queries, keys, values, tied(context_grad, up_parts[0], down_sum), mixed, probs),
         16 * shard_len * span * width,
-        grid=(pairs,),
+        grid=(pairs // 2,),
         name="attend_back", limit=24,
     )
     turned, up_two, down_z, grads = joined(turned, up_two, down_z, grads)

time: 194 us -> 194 us (level)
  transfers between devices with their start and end apart: 60 -> 60, of which waited for: 20 -> 21; matrix products, arithmetic and copies ran while one was open for 4% -> 4% of each run, Pallas kernels for 34% -> 34%
where the time goes in v4:
time: 194 us
  Pallas kernels  68.4 us (35%)
  starting transfers between devices  59.6 us (31%)
  waiting for transfers between devices  50.9 us (26%)
  other arithmetic  6.39 us (3%)
  local copies, waits for them, and re-layouts  6.18 us (3%)
    pallas_call x14, Pallas kernels, call(): pl.pallas_call(kernel, out_shape=outs, in_specs=in_specs, out_specs=out_s...  68.4 us
    ppermute x60, starting transfers between devices, shift(): return lax.ppermute(array, AXES, route(move))  59.6 us
    ppermute x60, waiting for transfers between devices, shift(): return lax.ppermute(array, AXES, route(move))  50.9 us
    unnamed x108, local copies, waits for them, and re-layouts  4.71 us
  transfers between devices with their start and end apart: 60, of which 21 were waited for; matrix products, arithmetic and copies ran while one was open for 4% of the time, Pallas kernels for 34%

profile of v4, /device:TPU:0, one launch (start us, length us, event | category | flops | bytes accessed | tf_op | source)
XLA Modules:
  0.0 194.1 jit_solution(8577311947514820639)
XLA Ops:
  0.7 1.9 pack.1
  2.6 3.0 %collective-permute-start = (bf16[80,768]{1,0:T(8,128)(2,1)}, bf16[80,768]{1,0:T(8,128)(2,1)S(1)}, u32[]{:S(2)}, u32[]{:S(2)}) collective-permute-start(bf16[80,768]{1,0:T(8,128)(2,1)} %get-tuple-element.159), channel_id=1, source_target_pairs={{0,8},{1,9},{2,10},{3,11},{4,12},{5,13},{6,14},{7,15},{8,0},{9,1},... | collective-permute-start | bytes 368648 | tf_op jit(solution)/shard_map/qkv_z/ppermute | solution.py:492
  5.6 2.6 %collective-permute-start.1 = (bf16[80,768]{1,0:T(8,128)(2,1)}, bf16[80,768]{1,0:T(8,128)(2,1)S(1)}, u32[]{:S(2)}, u32[]{:S(2)}) collective-permute-start(bf16[80,768]{1,0:T(8,128)(2,1)} %get-tuple-element.159), channel_id=1, source_target_pairs={{0,16},{1,17},{2,18},{3,19},{4,20},{5,21},{6,22},{7,23},{8,24},{9,... | collective-permute-start | bytes 368648 | tf_op jit(solution)/shard_map/qkv_z/ppermute | solution.py:492
  8.2 1.7 collective-permute-start.3
  10.0 1.5 convert_convert_fusion.wide_four
  11.5 1.1 convert_convert_fusion.1.wide_two
  12.6 0.9 convert_convert_fusion.2.wide_one
  13.5 1.0 fusion.2.curve
  14.5 4.0 %bias.1 = bf16[12,256,512]{2,1,0:T(8,128)(2,1)} custom-call(f32[12,768]{1,0:T(8,128)} %fusion.2.curve), custom_call_target="tpu_custom_call" | custom-call | bytes 3182592 | tf_op jit(solution)/shard_map/bias/pallas_call | solution.py:595
  19.2 1.1 collective-permute-start.4
  20.4 1.4 collective-permute-start.5
  21.8 2.8 %collective-permute-start.6 = (bf16[128,768]{1,0:T(8,128)(2,1)S(1)}, bf16[128,768]{1,0:T(8,128)(2,1)S(1)}, u32[]{:S(2)}, u32[]{:S(2)}) collective-permute-start(bf16[128,768]{1,0:T(8,128)(2,1)S(1)} %copy-done.51), channel_id=1, source_target_pairs={{0,16},{1,17},{2,18},{3,19},{4,20},{5,21},{6,22},{7,23},{8,24},{9,... | collective-permute-start | bytes 589832 | tf_op jit(solution)/shard_map/up_z/ppermute | solution.py:492
  24.5 1.5 collective-permute-start.9
  26.8 4.8 %collective-permute-done.5 = bf16[128,768]{1,0:T(8,128)(2,1)S(1)} collective-permute-done((bf16[128,768]{1,0:T(8,128)(2,1)S(1)}, bf16[128,768]{1,0:T(8,128)(2,1)S(1)}, u32[]{:S(2)}, u32[]{:S(2)}) %collective-permute-start.5) | collective-permute-done | bytes 196640 | tf_op jit(solution)/shard_map/up_z/ppermute | solution.py:492
  31.7 2.4 %collective-permute-done.6 = bf16[128,768]{1,0:T(8,128)(2,1)S(1)} collective-permute-done((bf16[128,768]{1,0:T(8,128)(2,1)S(1)}, bf16[128,768]{1,0:T(8,128)(2,1)S(1)}, u32[]{:S(2)}, u32[]{:S(2)}) %collective-permute-start.6) | collective-permute-done | bytes 196640 | tf_op jit(solution)/shard_map/up_z/ppermute | solution.py:492
  34.0 1.5 collective-permute-start.10
  35.5 2.4 %collective-permute-start.8 = (bf16[128,768]{1,0:T(8,128)(2,1)S(1)}, bf16[128,768]{1,0:T(8,128)(2,1)S(1)}, u32[]{:S(2)}, u32[]{:S(2)}) collective-permute-start(bf16[128,768]{1,0:T(8,128)(2,1)S(1)} %copy-done.51), channel_id=1, source_target_pairs={{0,24},{1,25},{2,26},{3,27},{4,28},{5,29},{6,30},{7,31},{8,16},{9,... | collective-permute-start | bytes 589832 | tf_op jit(solution)/shard_map/up_z/ppermute | solution.py:492
  37.9 5.2 %collective-permute-done.8 = bf16[128,768]{1,0:T(8,128)(2,1)S(1)} collective-permute-done((bf16[128,768]{1,0:T(8,128)(2,1)S(1)}, bf16[128,768]{1,0:T(8,128)(2,1)S(1)}, u32[]{:S(2)}, u32[]{:S(2)}) %collective-permute-start.8) | collective-permute-done | bytes 196640 | tf_op jit(solution)/shard_map/up_z/ppermute | solution.py:492
  43.2 1.5 collective-permute-start.12
  46.6 2.2 %collective-permute-start.17 = (bf16[96,768]{1,0:T(8,128)(2,1)S(1)}, bf16[96,768]{1,0:T(8,128)(2,1)S(1)}, u32[]{:S(2)}, u32[]{:S(2)}) collective-permute-start(bf16[96,768]{1,0:T(8,128)(2,1)S(1)} %copy-done.52), channel_id=1, source_target_pairs={{0,8},{1,9},{2,10},{3,11},{4,12},{5,13},{6,14},{7,15},{8,0},{9,1},... | collective-permute-start | bytes 442376 | tf_op jit(solution)/shard_map/down_z/ppermute | solution.py:492
  49.4 1.5 collective-permute-start.11
  51.7 8.0 %project.1 = (bf16[512,768]{1,0:T(8,128)(2,1)}, bf16[256,768]{1,0:T(8,128)(2,1)}, bf16[512,768]{1,0:T(8,128)(2,1)}, bf16[512,768]{1,0:T(8,128)(2,1)}, f32[8,768]...) custom-call(s32[4]{0:T(128)} %pad_add_fusion.place, bf16[256,768]{1,0:T(8,128)(2,1)} %frames.3, ...), custom_call_target="tpu_custom_call" | custom-call | flops 1509949440 | bytes 12861456 | tf_op jit(solution)/shard_map/project/pallas_call | solution.py:595
  60.5 2.5 %collective-permute-start.20 = (bf16[96,768]{1,0:T(8,128)(2,1)S(1)}, bf16[96,768]{1,0:T(8,128)(2,1)S(1)}, u32[]{:S(2)}, u32[]{:S(2)}) collective-permute-start(bf16[96,768]{1,0:T(8,128)(2,1)S(1)} %copy-done.52), channel_id=1, source_target_pairs={{0,24},{1,25},{2,26},{3,27},{4,28},{5,29},{6,30},{7,31},{8,16},{9,... | collective-permute-start | bytes 442376 | tf_op jit(solution)/shard_map/down_z/ppermute | solution.py:492
  63.3 7.5 %attend.1 = (bf16[12,256,512]{2,1,0:T(8,128)(2,1)}, f32[256,768]{1,0:T(8,128)}) custom-call(s32[4]{0:T(128)} %pad_add_fusion.place, s32[1,4]{1,0:T(1,128)} %lengths.1, bf16[256,768]{1,0:T(8,128)(2,1)} %get-tuple-element.188.queries, bf16[512,768]{1,0:T(8,128)(2,1)} %get-tuple-element.189.keys, bf16[512,768]{1,0:T(8,128)(2,1)} %get-tuple-element.190.values, ...), custom_call_target="tpu_custom_call" | custom-call | flops 805306368 | bytes 9053216 | tf_op jit(solution)/shard_map/attend/pallas_call | solution.py:595
  70.8 1.0 collective-permute-done.19.p3.u3
  72.4 1.2 collective-permute-start.21
  73.6 1.3 collective-permute-start.22
  75.3 4.0 %expand.1 = (f32[256,768]{1,0:T(8,128)S(1)}, bf16[256,768]{1,0:T(8,128)(2,1)S(1)}, bf16[256,768]{1,0:T(8,128)(2,1)S(1)}, bf16[256,3072]{1,0:T(8,128)(2,1)S(1)}, f32[256,3072]{1,0:T(8,128)S(1)}) custom-call(s32[4]{0:T(128)S(1)} %copy-done.39, bf16[256,768]{1,0:T(8,128)(2,1)S(1)} %copy-done.4, f32[256,768]{1,0:T(8,128)S(1)} %copy-done.21, ...), custom_call_target="tpu_custom_call" | custom-call | flops 1509949440 | bytes 13885456 | tf_op jit(solution)/shard_map/expand/pallas_call | solution.py:595
  79.4 9.1 %collective-permute-done.21.p1 = bf16[4,96,768]{2,1,0:T(8,128)(2,1)S(1)} collective-permute-done((bf16[4,96,768]{2,1,0:T(8,128)(2,1)S(1)}, bf16[4,96,768]{2,1,0:T(8,128)(2,1)S(1)}, u32[]{:S(2)}, u32[]{:S(2)}) %collective-permute-start.21) | collective-permute-done | bytes 589856 | tf_op jit(solution)/shard_map/down_1/ppermute | solution.py:492
  88.6 1.0 collective-permute-start.27
  90.2 1.8 collective-permute-done.28.active_twin
  92.0 3.1 %down_grad.1 = (bf16[4,96,768]{2,1,0:T(8,128)(2,1)S(1)}, bf16[4,96,768]{2,1,0:T(8,128)(2,1)S(1)}, bf16[4,96,768]{2,1,0:T(8,128)(2,1)S(1)}, bf16[4,96,768]{2,1,0:T(8,128)(2,1)S(1)}, f32[8,768]{1,0:T(8,128)S(1)}) custom-call(s32[4]{0:T(128)S(1)} %copy-done.39, bf16[256,3072]{1,0:T(8,128)(2,1)S(1)} %get-tuple-element.209.active, ...), custom_call_target="tpu_custom_call" | custom-call | flops 1207959552 | bytes 6316048 | tf_op jit(solution)/shard_map/down_grad/pallas_call | solution.py:595
  95.0 1.2 copy-done.32
  96.3 2.3 %collective-permute-done.27.p3 = bf16[4,96,768]{2,1,0:T(8,128)(2,1)S(1)} collective-permute-done((bf16[4,96,768]{2,1,0:T(8,128)(2,1)S(1)}, bf16[4,96,768]{2,1,0:T(8,128)(2,1)S(1)}, u32[]{:S(2)}, u32[]{:S(2)}) %collective-permute-start.27) | collective-permute-done | bytes 589856 | tf_op jit(solution)/shard_map/down_3/ppermute | solution.py:492
  99.1 1.0 collective-permute-start.29
  100.1 1.0 collective-permute-start.30
  101.6 10.2 %back.1 = (f32[256,768]{1,0:T(8,128)}, bf16[256,768]{1,0:T(8,128)(2,1)S(1)}, f32[8,768]{1,0:T(8,128)S(1)}, bf16[256,768]{1,0:T(8,128)(2,1)S(1)}, f32[8,3072]{1,0:T(8,128)S(1)}, /*index=5*/bf16[256,3072]{1,0:T(8,128)(2,1)}) custom-call(s32[4]{0:T(128)S(1)} %copy-done.39, bf16[256,768]{1,0:T(8,128)(2,1)S(1)} %copy-done.37, f32[256,3072]{1,0:T(8,128)} %copy-done.18, ...), custom_call_target="tpu_custom_call" | custom-call | flops 2717908992 | bytes 18628624 | tf_op jit(solution)/shard_map/back/pallas_call | solution.py:595
  112.7 0.9 copy-done.24
  113.7 1.6 collective-permute-done.30
  115.9 1.0 collective-permute-start.42
  116.9 1.9 collective-permute-done.39.branch_twin
  119.4 3.7 %up_grad.1 = (bf16[4,128,768]{2,1,0:T(8,128)(2,1)S(1)}, bf16[4,128,768]{2,1,0:T(8,128)(2,1)S(1)}, bf16[2,128,768]{2,1,0:T(8,128)(2,1)S(1)}, bf16[2,128,768]{2,1,0:T(8,128)(2,1)S(1)}, bf16[4,128,768]{2,1,0:T(8,128)(2,1)S(1)}) custom-call(s32[4]{0:T(128)S(1)} %copy-done.39, bf16[256,3072]{1,0:T(8,128)(2,1)S(1)} %copy-done.40, ...), custom_call_target="tpu_custom_call" | custom-call | flops 1509949440 | bytes 8650768 | tf_op jit(solution)/shard_map/up_grad/pallas_call | solution.py:595
  123.2 1.1 collective-permute-start.40
  124.2 1.6 collective-permute-done.42
  125.9 1.0 collective-permute-start.41
  127.1 3.3 %collective-permute-start.43 = (bf16[96,768]{1,0:T(8,128)(2,1)S(1)}, bf16[96,768]{1,0:T(8,128)(2,1)S(1)}, u32[]{:S(2)}, u32[]{:S(2)}) collective-permute-start(bf16[96,768]{1,0:T(8,128)(2,1)S(1)} %get-tuple-element.315), channel_id=1, source_target_pairs={{0,8},{1,9},{2,10},{3,11},{4,12},{5,13},{6,14},{7,15},{8,0},{9,1},... | collective-permute-start | bytes 442376 | tf_op jit(solution)/shard_map/rs_down_z/ppermute | solution.py:492
  130.5 8.5 %attend_back.1 = (bf16[3,512,768]{2,1,0:T(8,128)(2,1)S(1)}, f32[12,768]{1,0:T(8,128)S(1)}) custom-call(s32[4]{0:T(128)S(1)} %copy-done.39, bf16[256,768]{1,0:T(8,128)(2,1)S(1)} %copy-done.31, bf16[512,768]{1,0:T(8,128)(2,1)S(1)} %copy-done.19, bf16[512,768]{1,0:T(8,128)(2,1)S(1)} %copy-done.20, bf16[256,768]{1,0:T(8,128)(2,1)S(1)} %get-tuple-element.241.context_grad, ...), custom_call_target="tpu_custom_call" | custom-call | flops 1610612736 | bytes 8687632 | tf_op jit(solution)/shard_map/attend_back/pallas_call | solution.py:595
  139.6 1.0 collective-permute-start.48
  140.7 1.5 collective-permute-start.49
  142.2 3.4 %first_grad.1 = (f32[256,768]{1,0:T(8,128)S(1)}, f32[256,768]{1,0:T(8,128)S(1)}, f32[24,768]{1,0:T(8,128)S(1)}) custom-call(s32[4]{0:T(128)S(1)} %copy-done.39, bf16[256,768]{1,0:T(8,128)(2,1)S(1)} %copy-done.4, bf16[256,768]{1,0:T(8,128)(2,1)S(1)} %copy-done.9, bf16[3,512,768]{2,1,0:T(8,128)(2,1)S(1)} %get-tuple-element.244.grads, ...), custom_call_target="tpu_custom_call" | custom-call | flops 1509949440 | bytes 8515600 | tf_op jit(solution)/shard_map/first_grad/pallas_call | solution.py:595
  145.7 2.0 %collective-permute-start.50 = (bf16[96,768]{1,0:T(8,128)(2,1)S(1)}, bf16[96,768]{1,0:T(8,128)(2,1)S(1)}, u32[]{:S(2)}, u32[]{:S(2)}) collective-permute-start(bf16[96,768]{1,0:T(8,128)(2,1)S(1)} %get-tuple-element.264), channel_id=1, source_target_pairs={{0,24},{1,25},{2,26},{3,27},{4,28},{5,29},{6,30},{7,31},{8,16},{9,... | collective-permute-start | bytes 442376 | tf_op jit(solution)/shard_map/rs_down_z/ppermute | solution.py:492
  147.8 5.9 %qkv_grad.1 = (bf16[4,80,768]{2,1,0:T(8,128)(2,1)S(1)}, bf16[4,80,768]{2,1,0:T(8,128)(2,1)S(1)}, bf16[4,80,768]{2,1,0:T(8,128)(2,1)S(1)}, bf16[4,80,768]{2,1,0:T(8,128)(2,1)S(1)}) custom-call(s32[4]{0:T(128)S(1)} %copy-done.39, bf16[3,512,768]{2,1,0:T(8,128)(2,1)S(1)} %get-tuple-element.244.grads, ...), custom_call_target="tpu_custom_call" | custom-call | flops 1811939328 | bytes 10125328 | tf_op jit(solution)/shard_map/qkv_grad/pallas_call | solution.py:595
  153.7 1.3 collective-permute-start.47
  156.2 4.3 %collective-permute-start.53 = (bf16[128,768]{1,0:T(8,128)(2,1)S(1)}, bf16[128,768]{1,0:T(8,128)(2,1)S(1)}, u32[]{:S(2)}, u32[]{:S(2)}) collective-permute-start(bf16[128,768]{1,0:T(8,128)(2,1)S(1)} %get-tuple-element.308), channel_id=1, source_target_pairs={{0,8},{1,9},{2,10},{3,11},{4,12},{5,13},{6,14},{7,15},{8,0},{9,1},... | collective-permute-start | bytes 589832 | tf_op jit(solution)/shard_map/rs_up_z/ppermute | solution.py:492
  160.6 1.0 input_grad.1
  161.7 0.9 collective-permute-done.47
  162.7 1.2 collective-permute-start.51
  164.0 2.7 %collective-permute-done.53 = bf16[128,768]{1,0:T(8,128)(2,1)S(1)} collective-permute-done((bf16[128,768]{1,0:T(8,128)(2,1)S(1)}, bf16[128,768]{1,0:T(8,128)(2,1)S(1)}, u32[]{:S(2)}, u32[]{:S(2)}) %collective-permute-start.53) | collective-permute-done | bytes 196640 | tf_op jit(solution)/shard_map/rs_up_z/ppermute | solution.py:492
  166.6 4.7 %collective-permute-done.54 = bf16[128,768]{1,0:T(8,128)(2,1)S(1)} collective-permute-done((bf16[128,768]{1,0:T(8,128)(2,1)S(1)}, bf16[128,768]{1,0:T(8,128)(2,1)S(1)}, u32[]{:S(2)}, u32[]{:S(2)}) %collective-permute-start.54) | collective-permute-done | bytes 196640 | tf_op jit(solution)/shard_map/rs_up_z/ppermute | solution.py:492
  172.1 6.1 %finish.1 = f32[256,768]{1,0:T(8,128)} custom-call(s32[4]{0:T(128)} %pad_add_fusion.place, bf16[256,3072]{1,0:T(8,128)(2,1)} %copy-done.32, f32[256,768]{1,0:T(8,128)} %copy-done.10, f32[8,768]{1,0:T(8,128)} %get-tuple-element.202.vectors, bf16[4,96,768]{2,1,0:T(8,128)(2,1)} %copy-done.5, bf16[4,96,768]{2,1,0:T(8,128)(2,1)} %copy-done.23, ...), custom_call_target="tpu_custom_call" | custom-call | flops 1207959552 | bytes 7888912 | tf_op jit(solution)/shard_map/finish/pallas_call | solution.py:595
  180.0 1.4 collective-permute-start.56
  181.4 2.3 %collective-permute-start.57 = (bf16[80,768]{1,0:T(8,128)(2,1)S(1)}, bf16[80,768]{1,0:T(8,128)(2,1)S(1)}, u32[]{:S(2)}, u32[]{:S(2)}) collective-permute-start(bf16[80,768]{1,0:T(8,128)(2,1)S(1)} %get-tuple-element.317), channel_id=1, source_target_pairs={{0,16},{1,17},{2,18},{3,19},{4,20},{5,21},{6,22},{7,23},{8,24},{9,... | collective-permute-start | bytes 368648 | tf_op jit(solution)/shard_map/rs_qkv_z/ppermute | solution.py:492
  185.2 7.5 %collective-permute-done.57.z2 = bf16[80,768]{1,0:T(8,128)(2,1)S(1)} collective-permute-done((bf16[80,768]{1,0:T(8,128)(2,1)S(1)}, bf16[80,768]{1,0:T(8,128)(2,1)S(1)}, u32[]{:S(2)}, u32[]{:S(2)}) %collective-permute-start.57) | collective-permute-done | bytes 122912 | tf_op jit(solution)/shard_map/rs_qkv_z/ppermute | solution.py:492
  192.8 1.1 last.1
  (208 shorter events, 17.1 us)
Async XLA Ops:
  2.6 16.5 %collective-permute-start = (bf16[80,768]{1,0:T(8,128)(2,1)}, bf16[80,768]{1,0:T(8,128)(2,1)S(1)}, u32[]{:S(2)}, u32[]{:S(2)}) collective-permute-start(bf16[80,768]{1,0:T(8,128)(2,1)} %get-tuple-element.159), channel_id=1, source_target_pairs={{0,8},{1,9},{2,10},{3,11},{4,12},{5,13},{6,14},{7,15},{8,0},{9,1},... | collective-permute-start | bytes 368648 | tf_op jit(solution)/shard_map/qkv_z/ppermute | solution.py:492
  5.6 13.5 %collective-permute-start.1 = (bf16[80,768]{1,0:T(8,128)(2,1)}, bf16[80,768]{1,0:T(8,128)(2,1)S(1)}, u32[]{:S(2)}, u32[]{:S(2)}) collective-permute-start(bf16[80,768]{1,0:T(8,128)(2,1)} %get-tuple-element.159), channel_id=1, source_target_pairs={{0,16},{1,17},{2,18},{3,19},{4,20},{5,21},{6,22},{7,23},{8,24},{9,... | collective-permute-start | bytes 368648 | tf_op jit(solution)/shard_map/qkv_z/ppermute | solution.py:492
  8.2 10.9 %collective-permute-start.2 = (bf16[80,768]{1,0:T(8,128)(2,1)}, bf16[80,768]{1,0:T(8,128)(2,1)S(1)}, u32[]{:S(2)}, u32[]{:S(2)}) collective-permute-start(bf16[80,768]{1,0:T(8,128)(2,1)} %get-tuple-element.159), channel_id=1, source_target_pairs={{0,24},{1,25},{2,26},{3,27},{4,28},{5,29},{6,30},{7,31},{8,16},{9,... | collective-permute-start | bytes 368648 | tf_op jit(solution)/shard_map/qkv_z/ppermute | solution.py:492
  8.2 10.9 %collective-permute-start.3 = (bf16[256,768]{1,0:T(8,128)(2,1)}, bf16[256,768]{1,0:T(8,128)(2,1)S(1)}, u32[]{:S(2)}, u32[]{:S(2)}) collective-permute-start(bf16[256,768]{1,0:T(8,128)(2,1)} %frames.3), channel_id=1, source_target_pairs={{0,1},{1,0},{2,3},{3,2},{4,5},{5,4},{6,7},{7,6},{8,9},{9,8},{10,11... | collective-permute-start | bytes 1179656 | tf_op jit(solution)/shard_map/frames_pack/ppermute | solution.py:492
  19.1 31.8 %copy-start.8 = (bf16[256,768]{1,0:T(8,128)(2,1)}, bf16[256,768]{1,0:T(8,128)(2,1)S(1)}, u32[]{:S(2)}) copy-start(bf16[256,768]{1,0:T(8,128)(2,1)S(1)} %collective-permute-done.3.other.mate_frames) | copy-start | bytes 1179652
  19.2 31.7 %copy-start.43 = (bf16[4,80,768]{2,1,0:T(8,128)(2,1)}, bf16[4,80,768]{2,1,0:T(8,128)(2,1)S(1)}, u32[]{:S(2)}) copy-start(bf16[4,80,768]{2,1,0:T(8,128)(2,1)S(1)} %pad_maximum_fusion.2.p0) | copy-start | bytes 1474564
  19.2 14.8 %collective-permute-start.4 = (bf16[4,80,768]{2,1,0:T(8,128)(2,1)S(1)}, bf16[4,80,768]{2,1,0:T(8,128)(2,1)S(1)}, u32[]{:S(2)}, u32[]{:S(2)}) collective-permute-start(bf16[4,80,768]{2,1,0:T(8,128)(2,1)S(1)} %pad_maximum_fusion.2.p0), channel_id=1, source_target_pairs={{0,1},{1,0},{2,6},{3,7},{4,5},{5,4},{6,2},{7,3},{8,9},{9,8},{10,14... | collective-permute-start | bytes 1474568 | tf_op jit(solution)/shard_map/qkv_1/ppermute | solution.py:492
  20.4 5.7 %collective-permute-start.7 = (bf16[256,768]{1,0:T(8,128)(2,1)S(1)}, bf16[256,768]{1,0:T(8,128)(2,1)S(1)}, u32[]{:S(2)}, u32[]{:S(2)}) collective-permute-start(bf16[256,768]{1,0:T(8,128)(2,1)S(1)} %copy-done.36), channel_id=1, source_target_pairs={{0,2},{1,3},{2,0},{3,1},{4,6},{5,7},{6,4},{7,5},{8,10},{9,11},{10,... | collective-permute-start | bytes 1179656 | tf_op jit(solution)/shard_map/twin/ppermute | solution.py:492
  20.4 11.3 %collective-permute-start.5 = (bf16[128,768]{1,0:T(8,128)(2,1)S(1)}, bf16[128,768]{1,0:T(8,128)(2,1)S(1)}, u32[]{:S(2)}, u32[]{:S(2)}) collective-permute-start(bf16[128,768]{1,0:T(8,128)(2,1)S(1)} %copy-done.51), channel_id=1, source_target_pairs={{0,8},{1,9},{2,10},{3,11},{4,12},{5,13},{6,14},{7,15},{8,0},{9,1},... | collective-permute-start | bytes 589832 | tf_op jit(solution)/shard_map/up_z/ppermute | solution.py:492
  21.8 12.3 %collective-permute-start.6 = (bf16[128,768]{1,0:T(8,128)(2,1)S(1)}, bf16[128,768]{1,0:T(8,128)(2,1)S(1)}, u32[]{:S(2)}, u32[]{:S(2)}) collective-permute-start(bf16[128,768]{1,0:T(8,128)(2,1)S(1)} %copy-done.51), channel_id=1, source_target_pairs={{0,16},{1,17},{2,18},{3,19},{4,20},{5,21},{6,22},{7,23},{8,24},{9,... | collective-permute-start | bytes 589832 | tf_op jit(solution)/shard_map/up_z/ppermute | solution.py:492
  24.5 13.4 %collective-permute-start.9 = (bf16[4,80,768]{2,1,0:T(8,128)(2,1)S(1)}, bf16[4,80,768]{2,1,0:T(8,128)(2,1)S(1)}, u32[]{:S(2)}, u32[]{:S(2)}) collective-permute-start(bf16[4,80,768]{2,1,0:T(8,128)(2,1)S(1)} %pad_maximum_fusion.2.p0), channel_id=1, source_target_pairs={{0,4},{1,5},{2,3},{3,2},{4,0},{5,1},{6,7},{7,6},{8,12},{9,13},{10,... | collective-permute-start | bytes 1474568 | tf_op jit(solution)/shard_map/qkv_2/ppermute | solution.py:492
  34.0 9.1 %collective-permute-start.10 = (bf16[4,80,768]{2,1,0:T(8,128)(2,1)S(1)}, bf16[4,80,768]{2,1,0:T(8,128)(2,1)S(1)}, u32[]{:S(2)}, u32[]{:S(2)}) collective-permute-start(bf16[4,80,768]{2,1,0:T(8,128)(2,1)S(1)} %collective-permute-done.4.p1), channel_id=1, source_target_pairs={{0,4},{1,5},{2,3},{3,2},{4,0},{5,1},{6,7},{7,6},{8,12},{9,13},{10,... | collective-permute-start | bytes 1474568 | tf_op jit(solution)/shard_map/qkv_3/ppermute | solution.py:492
  35.5 7.6 %collective-permute-start.8 = (bf16[128,768]{1,0:T(8,128)(2,1)S(1)}, bf16[128,768]{1,0:T(8,128)(2,1)S(1)}, u32[]{:S(2)}, u32[]{:S(2)}) collective-permute-start(bf16[128,768]{1,0:T(8,128)(2,1)S(1)} %copy-done.51), channel_id=1, source_target_pairs={{0,24},{1,25},{2,26},{3,27},{4,28},{5,29},{6,30},{7,31},{8,16},{9,... | collective-permute-start | bytes 589832 | tf_op jit(solution)/shard_map/up_z/ppermute | solution.py:492
  43.2 32.0 %copy-start.3 = (bf16[4,128,768]{2,1,0:T(8,128)(2,1)}, bf16[4,128,768]{2,1,0:T(8,128)(2,1)S(1)}, u32[]{:S(2)}) copy-start(bf16[4,128,768]{2,1,0:T(8,128)(2,1)S(1)} %pad_maximum_fusion.p0.u0) | copy-start | bytes 2359300
  43.2 16.5 %collective-permute-start.12 = (bf16[4,128,768]{2,1,0:T(8,128)(2,1)S(1)}, bf16[4,128,768]{2,1,0:T(8,128)(2,1)S(1)}, u32[]{:S(2)}, u32[]{:S(2)}) collective-permute-start(bf16[4,128,768]{2,1,0:T(8,128)(2,1)S(1)} %pad_maximum_fusion.p0.u0), channel_id=1, source_target_pairs={{0,1},{1,0},{2,6},{3,7},{4,5},{5,4},{6,2},{7,3},{8,9},{9,8},{10,14... | collective-permute-start | bytes 2359304 | tf_op jit(solution)/shard_map/up_1/ppermute | solution.py:492
  44.7 1.9 collective-permute-start.13
  44.7 4.1 %collective-permute-start.14 = (bf16[4,80,768]{2,1,0:T(8,128)(2,1)S(1)}, bf16[4,80,768]{2,1,0:T(8,128)(2,1)S(1)}, u32[]{:S(2)}, u32[]{:S(2)}) collective-permute-start(bf16[4,80,768]{2,1,0:T(8,128)(2,1)S(1)} %collective-permute-done.4.p1), channel_id=1, source_target_pairs={{0,2},{1,3},{2,0},{3,1},{4,6},{5,7},{6,4},{7,5},{8,10},{9,11},{10,... | collective-permute-start | bytes 1474568 | tf_op jit(solution)/shard_map/twin/ppermute | solution.py:492
  45.2 4.1 %collective-permute-start.15 = (bf16[4,80,768]{2,1,0:T(8,128)(2,1)S(1)}, bf16[4,80,768]{2,1,0:T(8,128)(2,1)S(1)}, u32[]{:S(2)}, u32[]{:S(2)}) collective-permute-start(bf16[4,80,768]{2,1,0:T(8,128)(2,1)S(1)} %collective-permute-done.9.p2), channel_id=1, source_target_pairs={{0,2},{1,3},{2,0},{3,1},{4,6},{5,7},{6,4},{7,5},{8,10},{9,11},{10,... | collective-permute-start | bytes 1474568 | tf_op jit(solution)/shard_map/twin/ppermute | solution.py:492
  45.2 5.6 %collective-permute-start.16 = (bf16[4,80,768]{2,1,0:T(8,128)(2,1)S(1)}, bf16[4,80,768]{2,1,0:T(8,128)(2,1)S(1)}, u32[]{:S(2)}, u32[]{:S(2)}) collective-permute-start(bf16[4,80,768]{2,1,0:T(8,128)(2,1)S(1)} %collective-permute-done.10.p3), channel_id=1, source_target_pairs={{0,2},{1,3},{2,0},{3,1},{4,6},{5,7},{6,4},{7,5},{8,10},{9,11},{10,... | collective-permute-start | bytes 1474568 | tf_op jit(solution)/shard_map/twin/ppermute | solution.py:492
  46.6 13.1 %collective-permute-start.17 = (bf16[96,768]{1,0:T(8,128)(2,1)S(1)}, bf16[96,768]{1,0:T(8,128)(2,1)S(1)}, u32[]{:S(2)}, u32[]{:S(2)}) collective-permute-start(bf16[96,768]{1,0:T(8,128)(2,1)S(1)} %copy-done.52), channel_id=1, source_target_pairs={{0,8},{1,9},{2,10},{3,11},{4,12},{5,13},{6,14},{7,15},{8,0},{9,1},... | collective-permute-start | bytes 442376 | tf_op jit(solution)/shard_map/down_z/ppermute | solution.py:492
  48.8 10.9 %collective-permute-start.18 = (bf16[96,768]{1,0:T(8,128)(2,1)S(1)}, bf16[96,768]{1,0:T(8,128)(2,1)S(1)}, u32[]{:S(2)}, u32[]{:S(2)}) collective-permute-start(bf16[96,768]{1,0:T(8,128)(2,1)S(1)} %copy-done.52), channel_id=1, source_target_pairs={{0,16},{1,17},{2,18},{3,19},{4,20},{5,21},{6,22},{7,23},{8,24},{9,... | collective-permute-start | bytes 442376 | tf_op jit(solution)/shard_map/down_z/ppermute | solution.py:492
  49.4 21.5 %collective-permute-start.11 = (bf16[4,128,768]{2,1,0:T(8,128)(2,1)S(1)}, bf16[4,128,768]{2,1,0:T(8,128)(2,1)S(1)}, u32[]{:S(2)}, u32[]{:S(2)}) collective-permute-start(bf16[4,128,768]{2,1,0:T(8,128)(2,1)S(1)} %pad_maximum_fusion.p0.u0), channel_id=1, source_target_pairs={{0,4},{1,5},{2,3},{3,2},{4,0},{5,1},{6,7},{7,6},{8,12},{9,13},{10,... | collective-permute-start | bytes 2359304 | tf_op jit(solution)/shard_map/up_2/ppermute | solution.py:492
  59.8 12.1 %collective-permute-start.19 = (bf16[4,128,768]{2,1,0:T(8,128)(2,1)S(1)}, bf16[4,128,768]{2,1,0:T(8,128)(2,1)S(1)}, u32[]{:S(2)}, u32[]{:S(2)}) collective-permute-start(bf16[4,128,768]{2,1,0:T(8,128)(2,1)S(1)} %collective-permute-done.12.p1.u1), channel_id=1, source_target_pairs={{0,4},{1,5},{2,3},{3,2},{4,0},{5,1},{6,7},{7,6},{8,12},{9,13},{10,... | collective-permute-start | bytes 2359304 | tf_op jit(solution)/shard_map/up_3/ppermute | solution.py:492
  60.5 13.0 %collective-permute-start.23 = (bf16[4,128,768]{2,1,0:T(8,128)(2,1)S(1)}, bf16[4,128,768]{2,1,0:T(8,128)(2,1)S(1)}, u32[]{:S(2)}, u32[]{:S(2)}) collective-permute-start(bf16[4,128,768]{2,1,0:T(8,128)(2,1)S(1)} %pad_maximum_fusion.p0.u0), channel_id=1, source_target_pairs={{0,2},{1,3},{2,0},{3,1},{4,6},{5,7},{6,4},{7,5},{8,10},{9,11},{10,... | collective-permute-start | bytes 2359304 | tf_op jit(solution)/shard_map/twin/ppermute | solution.py:492
  60.5 10.3 %collective-permute-start.20 = (bf16[96,768]{1,0:T(8,128)(2,1)S(1)}, bf16[96,768]{1,0:T(8,128)(2,1)S(1)}, u32[]{:S(2)}, u32[]{:S(2)}) collective-permute-start(bf16[96,768]{1,0:T(8,128)(2,1)S(1)} %copy-done.52), channel_id=1, source_target_pairs={{0,24},{1,25},{2,26},{3,27},{4,28},{5,29},{6,30},{7,31},{8,16},{9,... | collective-permute-start | bytes 442376 | tf_op jit(solution)/shard_map/down_z/ppermute | solution.py:492
  63.1 11.8 %collective-permute-start.24 = (bf16[4,128,768]{2,1,0:T(8,128)(2,1)S(1)}, bf16[4,128,768]{2,1,0:T(8,128)(2,1)S(1)}, u32[]{:S(2)}, u32[]{:S(2)}) collective-permute-start(bf16[4,128,768]{2,1,0:T(8,128)(2,1)S(1)} %collective-permute-done.12.p1.u1), channel_id=1, source_target_pairs={{0,2},{1,3},{2,0},{3,1},{4,6},{5,7},{6,4},{7,5},{8,10},{9,11},{10,... | collective-permute-start | bytes 2359304 | tf_op jit(solution)/shard_map/twin/ppermute | solution.py:492
  71.8 3.0 %collective-permute-start.25 = (bf16[4,128,768]{2,1,0:T(8,128)(2,1)S(1)}, bf16[4,128,768]{2,1,0:T(8,128)(2,1)S(1)}, u32[]{:S(2)}, u32[]{:S(2)}) collective-permute-start(bf16[4,128,768]{2,1,0:T(8,128)(2,1)S(1)} %collective-permute-done.11.p2.u2), channel_id=1, source_target_pairs={{0,2},{1,3},{2,0},{3,1},{4,6},{5,7},{6,4},{7,5},{8,10},{9,11},{10,... | collective-permute-start | bytes 2359304 | tf_op jit(solution)/shard_map/twin/ppermute | solution.py:492
  72.0 3.3 %collective-permute-start.26 = (bf16[4,128,768]{2,1,0:T(8,128)(2,1)S(1)}, bf16[4,128,768]{2,1,0:T(8,128)(2,1)S(1)}, u32[]{:S(2)}, u32[]{:S(2)}) collective-permute-start(bf16[4,128,768]{2,1,0:T(8,128)(2,1)S(1)} %collective-permute-done.19.p3.u3), channel_id=1, source_target_pairs={{0,2},{1,3},{2,0},{3,1},{4,6},{5,7},{6,4},{7,5},{8,10},{9,11},{10,... | collective-permute-start | bytes 2359304 | tf_op jit(solution)/shard_map/twin/ppermute | solution.py:492
  72.4 29.2 %copy-start.5 = (bf16[4,96,768]{2,1,0:T(8,128)(2,1)}, bf16[4,96,768]{2,1,0:T(8,128)(2,1)S(1)}, u32[]{:S(2)}) copy-start(bf16[4,96,768]{2,1,0:T(8,128)(2,1)S(1)} %pad_maximum_fusion.1.p0) | copy-start | bytes 1769476
  72.4 16.1 %collective-permute-start.21 = (bf16[4,96,768]{2,1,0:T(8,128)(2,1)S(1)}, bf16[4,96,768]{2,1,0:T(8,128)(2,1)S(1)}, u32[]{:S(2)}, u32[]{:S(2)}) collective-permute-start(bf16[4,96,768]{2,1,0:T(8,128)(2,1)S(1)} %pad_maximum_fusion.1.p0), channel_id=1, source_target_pairs={{0,1},{1,0},{2,6},{3,7},{4,5},{5,4},{6,2},{7,3},{8,9},{9,8},{10,14... | collective-permute-start | bytes 1769480 | tf_op jit(solution)/shard_map/down_1/ppermute | solution.py:492
  73.6 15.0 %collective-permute-start.22 = (bf16[4,96,768]{2,1,0:T(8,128)(2,1)S(1)}, bf16[4,96,768]{2,1,0:T(8,128)(2,1)S(1)}, u32[]{:S(2)}, u32[]{:S(2)}) collective-permute-start(bf16[4,96,768]{2,1,0:T(8,128)(2,1)S(1)} %pad_maximum_fusion.1.p0), channel_id=1, source_target_pairs={{0,4},{1,5},{2,3},{3,2},{4,0},{5,1},{6,7},{7,6},{8,12},{9,13},{10,... | collective-permute-start | bytes 1769480 | tf_op jit(solution)/shard_map/down_2/ppermute | solution.py:492
  88.5 3.4 %collective-permute-start.28 = (bf16[256,3072]{1,0:T(8,128)(2,1)S(1)}, bf16[256,3072]{1,0:T(8,128)(2,1)S(1)}, u32[]{:S(2)}, u32[]{:S(2)}) collective-permute-start(bf16[256,3072]{1,0:T(8,128)(2,1)S(1)} %get-tuple-element.209.active), channel_id=1, source_target_pairs={{0,2},{1,3},{2,0},{3,1},{4,6},{5,7},{6,4},{7,5},{8,10},{9,11},{10,... | collective-permute-start | bytes 4718600 | tf_op jit(solution)/shard_map/twin/ppermute | solution.py:492
  88.6 9.9 %collective-permute-start.27 = (bf16[4,96,768]{2,1,0:T(8,128)(2,1)S(1)}, bf16[4,96,768]{2,1,0:T(8,128)(2,1)S(1)}, u32[]{:S(2)}, u32[]{:S(2)}) collective-permute-start(bf16[4,96,768]{2,1,0:T(8,128)(2,1)S(1)} %collective-permute-done.21.p1), channel_id=1, source_target_pairs={{0,4},{1,5},{2,3},{3,2},{4,0},{5,1},{6,7},{7,6},{8,12},{9,13},{10,... | collective-permute-start | bytes 1769480 | tf_op jit(solution)/shard_map/down_3/ppermute | solution.py:492
  89.7 9.4 %collective-permute-start.31 = (bf16[4,96,768]{2,1,0:T(8,128)(2,1)S(1)}, bf16[4,96,768]{2,1,0:T(8,128)(2,1)S(1)}, u32[]{:S(2)}, u32[]{:S(2)}) collective-permute-start(bf16[4,96,768]{2,1,0:T(8,128)(2,1)S(1)} %pad_maximum_fusion.1.p0), channel_id=1, source_target_pairs={{0,2},{1,3},{2,0},{3,1},{4,6},{5,7},{6,4},{7,5},{8,10},{9,11},{10,... | collective-permute-start | bytes 1769480 | tf_op jit(solution)/shard_map/twin/ppermute | solution.py:492
  89.7 10.4 %collective-permute-start.32 = (bf16[4,96,768]{2,1,0:T(8,128)(2,1)S(1)}, bf16[4,96,768]{2,1,0:T(8,128)(2,1)S(1)}, u32[]{:S(2)}, u32[]{:S(2)}) collective-permute-start(bf16[4,96,768]{2,1,0:T(8,128)(2,1)S(1)} %collective-permute-done.21.p1), channel_id=1, source_target_pairs={{0,2},{1,3},{2,0},{3,1},{4,6},{5,7},{6,4},{7,5},{8,10},{9,11},{10,... | collective-permute-start | bytes 1769480 | tf_op jit(solution)/shard_map/twin/ppermute | solution.py:492
  90.2 10.9 %collective-permute-start.33 = (bf16[4,96,768]{2,1,0:T(8,128)(2,1)S(1)}, bf16[4,96,768]{2,1,0:T(8,128)(2,1)S(1)}, u32[]{:S(2)}, u32[]{:S(2)}) collective-permute-start(bf16[4,96,768]{2,1,0:T(8,128)(2,1)S(1)} %collective-permute-done.22.p2), channel_id=1, source_target_pairs={{0,2},{1,3},{2,0},{3,1},{4,6},{5,7},{6,4},{7,5},{8,10},{9,11},{10,... | collective-permute-start | bytes 1769480 | tf_op jit(solution)/shard_map/twin/ppermute | solution.py:492
  98.5 2.6 %collective-permute-start.34 = (bf16[4,96,768]{2,1,0:T(8,128)(2,1)S(1)}, bf16[4,96,768]{2,1,0:T(8,128)(2,1)S(1)}, u32[]{:S(2)}, u32[]{:S(2)}) collective-permute-start(bf16[4,96,768]{2,1,0:T(8,128)(2,1)S(1)} %collective-permute-done.27.p3), channel_id=1, source_target_pairs={{0,2},{1,3},{2,0},{3,1},{4,6},{5,7},{6,4},{7,5},{8,10},{9,11},{10,... | collective-permute-start | bytes 1769480 | tf_op jit(solution)/shard_map/twin/ppermute | solution.py:492
  98.5 15.1 %collective-permute-start.37 = (bf16[512,768]{1,0:T(8,128)(2,1)S(1)}, bf16[512,768]{1,0:T(8,128)(2,1)S(1)}, u32[]{:S(2)}, u32[]{:S(2)}) collective-permute-start(bf16[512,768]{1,0:T(8,128)(2,1)S(1)} %copy-done.33), channel_id=1, source_target_pairs={{0,2},{1,3},{2,0},{3,1},{4,6},{5,7},{6,4},{7,5},{8,10},{9,11},{10,... | collective-permute-start | bytes 2359304 | tf_op jit(solution)/shard_map/twin/ppermute | solution.py:492
  99.1 14.6 %collective-permute-start.29 = (bf16[4,96,768]{2,1,0:T(8,128)(2,1)S(1)}, bf16[4,96,768]{2,1,0:T(8,128)(2,1)S(1)}, u32[]{:S(2)}, u32[]{:S(2)}) collective-permute-start(bf16[4,96,768]{2,1,0:T(8,128)(2,1)S(1)} %get-tuple-element.217), channel_id=1, source_target_pairs={{0,4},{1,5},{2,3},{3,2},{4,0},{5,1},{6,7},{7,6},{8,12},{9,13},{10,... | collective-permute-start | bytes 1769480 | tf_op jit(solution)/shard_map/rs_down_3/ppermute | solution.py:492
  100.1 15.2 %collective-permute-start.30 = (bf16[4,96,768]{2,1,0:T(8,128)(2,1)S(1)}, bf16[4,96,768]{2,1,0:T(8,128)(2,1)S(1)}, u32[]{:S(2)}, u32[]{:S(2)}) collective-permute-start(bf16[4,96,768]{2,1,0:T(8,128)(2,1)S(1)} %get-tuple-element.218), channel_id=1, source_target_pairs={{0,4},{1,5},{2,3},{3,2},{4,0},{5,1},{6,7},{7,6},{8,12},{9,13},{10,... | collective-permute-start | bytes 1769480 | tf_op jit(solution)/shard_map/rs_down_2/ppermute | solution.py:492
  101.1 12.5 %collective-permute-start.35 = (bf16[256,768]{1,0:T(8,128)(2,1)S(1)}, bf16[256,768]{1,0:T(8,128)(2,1)S(1)}, u32[]{:S(2)}, u32[]{:S(2)}) collective-permute-start(bf16[256,768]{1,0:T(8,128)(2,1)S(1)} %get-tuple-element.225.context), channel_id=1, source_target_pairs={{0,2},{1,3},{2,0},{3,1},{4,6},{5,7},{6,4},{7,5},{8,10},{9,11},{10,... | collective-permute-start | bytes 1179656 | tf_op jit(solution)/shard_map/twin/ppermute | solution.py:492
  101.1 12.5 %collective-permute-start.36 = (bf16[256,768]{1,0:T(8,128)(2,1)S(1)}, bf16[256,768]{1,0:T(8,128)(2,1)S(1)}, u32[]{:S(2)}, u32[]{:S(2)}) collective-permute-start(bf16[256,768]{1,0:T(8,128)(2,1)S(1)} %get-tuple-element.226.second), channel_id=1, source_target_pairs={{0,2},{1,3},{2,0},{3,1},{4,6},{5,7},{6,4},{7,5},{8,10},{9,11},{10,... | collective-permute-start | bytes 1179656 | tf_op jit(solution)/shard_map/twin/ppermute | solution.py:492
  115.3 4.2 %collective-permute-start.38 = (bf16[256,3072]{1,0:T(8,128)(2,1)}, bf16[256,3072]{1,0:T(8,128)(2,1)S(1)}, u32[]{:S(2)}, u32[]{:S(2)}) collective-permute-start(bf16[256,3072]{1,0:T(8,128)(2,1)} %get-tuple-element.232.hidden), channel_id=1, source_target_pairs={{0,2},{1,3},{2,0},{3,1},{4,6},{5,7},{6,4},{7,5},{8,10},{9,11},{10,... | collective-permute-start | bytes 4718600 | tf_op jit(solution)/shard_map/twin/ppermute | solution.py:492
  115.3 3.6 %collective-permute-start.39 = (bf16[256,768]{1,0:T(8,128)(2,1)S(1)}, bf16[256,768]{1,0:T(8,128)(2,1)S(1)}, u32[]{:S(2)}, u32[]{:S(2)}) collective-permute-start(bf16[256,768]{1,0:T(8,128)(2,1)S(1)} %get-tuple-element.234.branch), channel_id=1, source_target_pairs={{0,2},{1,3},{2,0},{3,1},{4,6},{5,7},{6,4},{7,5},{8,10},{9,11},{10,... | collective-permute-start | bytes 1179656 | tf_op jit(solution)/shard_map/twin/ppermute | solution.py:492
  115.9 9.9 %collective-permute-start.42 = (bf16[4,96,768]{2,1,0:T(8,128)(2,1)S(1)}, bf16[4,96,768]{2,1,0:T(8,128)(2,1)S(1)}, u32[]{:S(2)}, u32[]{:S(2)}) collective-permute-start(bf16[4,96,768]{2,1,0:T(8,128)(2,1)S(1)} %add_convert_fusion.1), channel_id=1, source_target_pairs={{0,1},{1,0},{2,6},{3,7},{4,5},{5,4},{6,2},{7,3},{8,9},{9,8},{10,14... | collective-permute-start | bytes 1769480 | tf_op jit(solution)/shard_map/rs_down_1/ppermute | solution.py:492
  123.2 16.3 %collective-permute-start.40 = (bf16[4,128,768]{2,1,0:T(8,128)(2,1)S(1)}, bf16[4,128,768]{2,1,0:T(8,128)(2,1)S(1)}, u32[]{:S(2)}, u32[]{:S(2)}) collective-permute-start(bf16[4,128,768]{2,1,0:T(8,128)(2,1)S(1)} %get-tuple-element.236), channel_id=1, source_target_pairs={{0,4},{1,5},{2,3},{3,2},{4,0},{5,1},{6,7},{7,6},{8,12},{9,13},{10,... | collective-permute-start | bytes 2359304 | tf_op jit(solution)/shard_map/rs_up_3/ppermute | solution.py:492
  125.9 13.6 %collective-permute-start.41 = (bf16[2,128,768]{2,1,0:T(8,128)(2,1)S(1)}, bf16[2,128,768]{2,1,0:T(8,128)(2,1)S(1)}, u32[]{:S(2)}, u32[]{:S(2)}) collective-permute-start(bf16[2,128,768]{2,1,0:T(8,128)(2,1)S(1)} %get-tuple-element.237), channel_id=1, source_target_pairs={{0,4},{1,5},{2,3},{3,2},{4,0},{5,1},{6,7},{7,6},{8,12},{9,13},{10,... | collective-permute-start | bytes 1179656 | tf_op jit(solution)/shard_map/rs_up_2a/ppermute | solution.py:492
  127.1 11.9 %collective-permute-start.43 = (bf16[96,768]{1,0:T(8,128)(2,1)S(1)}, bf16[96,768]{1,0:T(8,128)(2,1)S(1)}, u32[]{:S(2)}, u32[]{:S(2)}) collective-permute-start(bf16[96,768]{1,0:T(8,128)(2,1)S(1)} %get-tuple-element.315), channel_id=1, source_target_pairs={{0,8},{1,9},{2,10},{3,11},{4,12},{5,13},{6,14},{7,15},{8,0},{9,1},... | collective-permute-start | bytes 442376 | tf_op jit(solution)/shard_map/rs_down_z/ppermute | solution.py:492
  130.5 8.6 %collective-permute-start.44 = (bf16[96,768]{1,0:T(8,128)(2,1)S(1)}, bf16[96,768]{1,0:T(8,128)(2,1)S(1)}, u32[]{:S(2)}, u32[]{:S(2)}) collective-permute-start(bf16[96,768]{1,0:T(8,128)(2,1)S(1)} %get-tuple-element.314), channel_id=1, source_target_pairs={{0,16},{1,17},{2,18},{3,19},{4,20},{5,21},{6,22},{7,23},{8,24},{9,... | collective-permute-start | bytes 442376 | tf_op jit(solution)/shard_map/rs_down_z/ppermute | solution.py:492
  139.4 6.2 %collective-permute-start.45 = (bf16[3,512,768]{2,1,0:T(8,128)(2,1)S(1)}, bf16[3,512,768]{2,1,0:T(8,128)(2,1)S(1)}, u32[]{:S(2)}, u32[]{:S(2)}) collective-permute-start(bf16[3,512,768]{2,1,0:T(8,128)(2,1)S(1)} %get-tuple-element.244.grads), channel_id=1, source_target_pairs={{0,2},{1,3},{2,0},{3,1},{4,6},{5,7},{6,4},{7,5},{8,10},{9,11},{10,... | collective-permute-start | bytes 7077896 | tf_op jit(solution)/shard_map/twin/ppermute | solution.py:492
  139.6 16.3 %collective-permute-start.48 = (bf16[4,128,768]{2,1,0:T(8,128)(2,1)S(1)}, bf16[4,128,768]{2,1,0:T(8,128)(2,1)S(1)}, u32[]{:S(2)}, u32[]{:S(2)}) collective-permute-start(bf16[4,128,768]{2,1,0:T(8,128)(2,1)S(1)} %add_convert_fusion), channel_id=1, source_target_pairs={{0,1},{1,0},{2,6},{3,7},{4,5},{5,4},{6,2},{7,3},{8,9},{9,8},{10,14... | collective-permute-start | bytes 2359304 | tf_op jit(solution)/shard_map/rs_up_1/ppermute | solution.py:492
  140.7 15.1 %collective-permute-start.49 = (bf16[2,128,768]{2,1,0:T(8,128)(2,1)S(1)}, bf16[2,128,768]{2,1,0:T(8,128)(2,1)S(1)}, u32[]{:S(2)}, u32[]{:S(2)}) collective-permute-start(bf16[2,128,768]{2,1,0:T(8,128)(2,1)S(1)} %get-tuple-element.261), channel_id=1, source_target_pairs={{0,4},{1,5},{2,3},{3,2},{4,0},{5,1},{6,7},{7,6},{8,12},{9,13},{10,... | collective-permute-start | bytes 1179656 | tf_op jit(solution)/shard_map/rs_up_2b/ppermute | solution.py:492
  145.6 2.1 %collective-permute-start.46 = (f32[24,768]{1,0:T(8,128)S(1)}, f32[24,768]{1,0:T(8,128)S(1)}, u32[]{:S(2)}, u32[]{:S(2)}) collective-permute-start(f32[24,768]{1,0:T(8,128)S(1)} %get-tuple-element.256.small_own), channel_id=1, source_target_pairs={{0,2},{1,3},{2,0},{3,1},{4,6},{5,7},{6,4},{7,5},{8,10},{9,11},{10,... | collective-permute-start | bytes 221192 | tf_op jit(solution)/shard_map/twin/ppermute | solution.py:492
  145.7 10.2 %collective-permute-start.50 = (bf16[96,768]{1,0:T(8,128)(2,1)S(1)}, bf16[96,768]{1,0:T(8,128)(2,1)S(1)}, u32[]{:S(2)}, u32[]{:S(2)}) collective-permute-start(bf16[96,768]{1,0:T(8,128)(2,1)S(1)} %get-tuple-element.264), channel_id=1, source_target_pairs={{0,24},{1,25},{2,26},{3,27},{4,28},{5,29},{6,30},{7,31},{8,16},{9,... | collective-permute-start | bytes 442376 | tf_op jit(solution)/shard_map/rs_down_z/ppermute | solution.py:492
  153.7 8.9 %collective-permute-start.47 = (bf16[4,80,768]{2,1,0:T(8,128)(2,1)S(1)}, bf16[4,80,768]{2,1,0:T(8,128)(2,1)S(1)}, u32[]{:S(2)}, u32[]{:S(2)}) collective-permute-start(bf16[4,80,768]{2,1,0:T(8,128)(2,1)S(1)} %get-tuple-element.258), channel_id=1, source_target_pairs={{0,4},{1,5},{2,3},{3,2},{4,0},{5,1},{6,7},{7,6},{8,12},{9,13},{10,... | collective-permute-start | bytes 1474568 | tf_op jit(solution)/shard_map/rs_qkv_3/ppermute | solution.py:492
  155.0 23.2 %collective-permute-start.52 = (bf16[4,80,768]{2,1,0:T(8,128)(2,1)S(1)}, bf16[4,80,768]{2,1,0:T(8,128)(2,1)S(1)}, u32[]{:S(2)}, u32[]{:S(2)}) collective-permute-start(bf16[4,80,768]{2,1,0:T(8,128)(2,1)S(1)} %get-tuple-element.273), channel_id=1, source_target_pairs={{0,4},{1,5},{2,3},{3,2},{4,0},{5,1},{6,7},{7,6},{8,12},{9,13},{10,... | collective-permute-start | bytes 1474568 | tf_op jit(solution)/shard_map/rs_qkv_2/ppermute | solution.py:492
  156.2 10.4 %collective-permute-start.53 = (bf16[128,768]{1,0:T(8,128)(2,1)S(1)}, bf16[128,768]{1,0:T(8,128)(2,1)S(1)}, u32[]{:S(2)}, u32[]{:S(2)}) collective-permute-start(bf16[128,768]{1,0:T(8,128)(2,1)S(1)} %get-tuple-element.308), channel_id=1, source_target_pairs={{0,8},{1,9},{2,10},{3,11},{4,12},{5,13},{6,14},{7,15},{8,0},{9,1},... | collective-permute-start | bytes 589832 | tf_op jit(solution)/shard_map/rs_up_z/ppermute | solution.py:492
  160.6 10.8 %collective-permute-start.54 = (bf16[128,768]{1,0:T(8,128)(2,1)S(1)}, bf16[128,768]{1,0:T(8,128)(2,1)S(1)}, u32[]{:S(2)}, u32[]{:S(2)}) collective-permute-start(bf16[128,768]{1,0:T(8,128)(2,1)S(1)} %get-tuple-element.311), channel_id=1, source_target_pairs={{0,16},{1,17},{2,18},{3,19},{4,20},{5,21},{6,22},{7,23},{8,24},{9,... | collective-permute-start | bytes 589832 | tf_op jit(solution)/shard_map/rs_up_z/ppermute | solution.py:492
  162.7 16.2 %collective-permute-start.51 = (bf16[4,80,768]{2,1,0:T(8,128)(2,1)S(1)}, bf16[4,80,768]{2,1,0:T(8,128)(2,1)S(1)}, u32[]{:S(2)}, u32[]{:S(2)}) collective-permute-start(bf16[4,80,768]{2,1,0:T(8,128)(2,1)S(1)} %add_convert_fusion.2), channel_id=1, source_target_pairs={{0,1},{1,0},{2,6},{3,7},{4,5},{5,4},{6,2},{7,3},{8,9},{9,8},{10,14... | collective-permute-start | bytes 1474568 | tf_op jit(solution)/shard_map/rs_qkv_1/ppermute | solution.py:492
  171.4 7.6 %collective-permute-start.55 = (bf16[128,768]{1,0:T(8,128)(2,1)S(1)}, bf16[128,768]{1,0:T(8,128)(2,1)S(1)}, u32[]{:S(2)}, u32[]{:S(2)}) collective-permute-start(bf16[128,768]{1,0:T(8,128)(2,1)S(1)} %get-tuple-element.277), channel_id=1, source_target_pairs={{0,24},{1,25},{2,26},{3,27},{4,28},{5,29},{6,30},{7,31},{8,16},{9,... | collective-permute-start | bytes 589832 | tf_op jit(solution)/shard_map/rs_up_z/ppermute | solution.py:492
  179.9 12.8 %collective-permute-start.59 = (bf16[256,768]{1,0:T(8,128)(2,1)S(1)}, bf16[256,768]{1,0:T(8,128)(2,1)S(1)}, u32[]{:S(2)}, u32[]{:S(2)}) collective-permute-start(bf16[256,768]{1,0:T(8,128)(2,1)S(1)} %get-tuple-element.288), channel_id=1, source_target_pairs={{0,1},{1,0},{2,3},{3,2},{4,5},{5,4},{6,7},{7,6},{8,9},{9,8},{10,11... | collective-permute-start | bytes 1179656 | tf_op jit(solution)/shard_map/grad_pack/ppermute | solution.py:492
  180.0 5.3 %collective-permute-start.56 = (bf16[80,768]{1,0:T(8,128)(2,1)S(1)}, bf16[80,768]{1,0:T(8,128)(2,1)S(1)}, u32[]{:S(2)}, u32[]{:S(2)}) collective-permute-start(bf16[80,768]{1,0:T(8,128)(2,1)S(1)} %get-tuple-element.318), channel_id=1, source_target_pairs={{0,8},{1,9},{2,10},{3,11},{4,12},{5,13},{6,14},{7,15},{8,0},{9,1},... | collective-permute-start | bytes 368648 | tf_op jit(solution)/shard_map/rs_qkv_z/ppermute | solution.py:492
  181.4 11.4 %collective-permute-start.57 = (bf16[80,768]{1,0:T(8,128)(2,1)S(1)}, bf16[80,768]{1,0:T(8,128)(2,1)S(1)}, u32[]{:S(2)}, u32[]{:S(2)}) collective-permute-start(bf16[80,768]{1,0:T(8,128)(2,1)S(1)} %get-tuple-element.317), channel_id=1, source_target_pairs={{0,16},{1,17},{2,18},{3,19},{4,20},{5,21},{6,22},{7,23},{8,24},{9,... | collective-permute-start | bytes 368648 | tf_op jit(solution)/shard_map/rs_qkv_z/ppermute | solution.py:492
  183.7 9.1 %collective-permute-start.58 = (bf16[80,768]{1,0:T(8,128)(2,1)S(1)}, bf16[80,768]{1,0:T(8,128)(2,1)S(1)}, u32[]{:S(2)}, u32[]{:S(2)}) collective-permute-start(bf16[80,768]{1,0:T(8,128)(2,1)S(1)} %get-tuple-element.316), channel_id=1, source_target_pairs={{0,24},{1,25},{2,26},{3,27},{4,28},{5,29},{6,30},{7,31},{8,16},{9,... | collective-permute-start | bytes 368648 | tf_op jit(solution)/shard_map/rs_qkv_z/ppermute | solution.py:492
  (50 other events, 425.2 us)
